TPU v7x, 32 devices: a whole 2x2x4 slice. The times are simulated.
32 devices in a mesh: member: 2 (over y), mesh: 16 (over z, x, core).
Axes of the slice: x: 2, y: 2, z: 4, core: 2. Of those that a mesh axis runs over, the one named last changes fastest.
Arguments:
- struct_modes: bfloat16 [24576, 2048], P(('member', 'mesh')), parts along dimension 0, may hold values from -0.078125 to 0.078125
- acoustic_modes: bfloat16 [16384, 2048], P(('member', 'mesh')), parts along dimension 0, may hold values from -6 to 6
- coupling: bfloat16 [320, 64, 256], P('mesh'), may hold values from -0.375 to 0.375
- face_shift: int32 [192], P('mesh'), may hold values from 0 to 4, as said below
- face_blocks: int32 [320, 4], P('mesh'), may hold values from 0 to 7
Outputs:
- panel: float32 [4096, 2048], P(('member', 'mesh')), parts along dimension 0
There are 2 independent parts, one for each index of `member`. A program takes and returns all parts, laid end to end along the dimension named above; an argument that names none is the same for every part. Nothing has to cross between parts.
Inputs may be any that keep to these rules, and one draw needn't show every extreme that they name: `face_shift`: on each shell owner the counts of its 12 blocks over the five classes are a reordering of 4, 1, 3, 2 and 2; so no shell owner hands more than 4 blocks to one face owner, and a face owner receives at most 4 from each of its five shell owners (at most 20 in all); in every draw at least one face owner receives exactly 4 from each of its five shell owners.
All inputs are finite; a program needn't handle non-finite values.
Results may differ from a plain program's by a relative error of at most 0.0029.
Values may be sent and summed in bfloat16 or wider, within the bound.
No kernel may reach another device: no remote copies, remote signals or barrier semaphores. Data moves between devices by JAX's collectives and lax.ppermute only.
A program may use at most 128 MiB of HBM per device.

v0:
```python
import jax
import jax.numpy as jnp
from jax import lax
from jax.sharding import PartitionSpec as P


def passed_along(block, axis, distance):
    devices = range(lax.axis_size(axis))
    route = [((i - distance) % len(devices), i) for i in devices]
    return lax.ppermute(block, axis, route)


def slot_matrix(shift_local, capacity):
    classes = jnp.arange(5, dtype=jnp.int32)
    onehot = (shift_local[:, None] == classes[None, :]).astype(jnp.int32)
    before = jnp.cumsum(onehot, axis=0) - onehot
    slot_index = jnp.sum(before * onehot, axis=1)
    target = shift_local * capacity + slot_index
    every_slot = jnp.arange(5 * capacity, dtype=jnp.int32)
    return (target[None, :] == every_slot[:, None]).astype(jnp.bfloat16)


def per_device(struct_modes, acoustic_modes, coupling, face_shift, face_blocks):
    mode_width = struct_modes.shape[1]
    acoustic_width = acoustic_modes.shape[1]
    block_count = face_shift.shape[0]
    block_rows = struct_modes.shape[0] // block_count
    slot_count = coupling.shape[0]
    capacity = slot_count // 5
    selector = slot_matrix(face_shift, capacity)
    acoustic_blocks = acoustic_modes.reshape(-1, block_rows, acoustic_width)
    picked = acoustic_blocks[face_blocks].reshape(slot_count, -1, acoustic_width)
    coupled = jnp.einsum(
        "srk,skm->srm", coupling, picked, preferred_element_type=jnp.float32
    ).astype(jnp.bfloat16)
    outgoing = jnp.dot(
        selector, struct_modes.reshape(block_count, -1), preferred_element_type=jnp.float32
    )
    outgoing = outgoing.astype(jnp.bfloat16).reshape(5, capacity, block_rows, mode_width)
    received_pieces = []
    for offset_class in range(5):
        if offset_class == 2:
            received_pieces.append(outgoing[2])
        else:
            received_pieces.append(passed_along(outgoing[offset_class], "mesh", offset_class - 2))
    left_rows = jnp.stack(received_pieces).reshape(slot_count * block_rows, mode_width)
    right_rows = coupled.reshape(slot_count * block_rows, acoustic_width)
    partial_value = lax.dot_general(
        left_rows, right_rows, (((0,), (0,)), ((), ())), preferred_element_type=jnp.float32
    )
    return lax.psum_scatter(partial_value, "mesh", scatter_dimension=0, tiled=True)


def solution(mesh):
    placed = (
        P(("member", "mesh"), None),
        P(("member", "mesh"), None),
        P("mesh", None, None),
        P("mesh"),
        P("mesh", None),
    )
    return jax.shard_map(
        per_device,
        mesh=mesh,
        in_specs=placed,
        out_specs=P(("member", "mesh"), None),
        check_vma=False,
    )
```

profile of v0, /device:TPU:0, one launch (start us, length us, event | category | flops | bytes accessed | tf_op | source)
XLA Modules:
  0.0 296.6 jit_solution(12406944945052929088)
XLA Ops:
  6.5 0.0 copy-start
  6.5 0.0 reduce-scatter.2.cloned.1.call-start
  6.5 0.8 fusion.1
  7.3 0.2 reduce_window_sum.11
  7.5 0.7 select_reduce_fusion
  8.2 0.7 multiply_add_fusion
  8.8 4.8 %reshape.27 = bf16[12,131072]{1,0:T(8,128)(2,1)} reshape(bf16[768,2048]{1,0:T(8,128)(2,1)} %param.5) | data formatting | bytes 6291456 | tf_op jit(solution)/shard_map/reshape | solution.py:37
  13.7 3.9 %convolution_convert_fusion = bf16[20,131072]{1,0:T(8,128)(2,1)S(1)} fusion(bf16[12,131072]{1,0:T(8,128)(2,1)} %reshape.27, s32[12]{0:T(128)S(1)} %multiply_add_fusion), kind=kOutput, calls=%fused_computation.1 | convolution fusion | flops 65536240 | bytes 8388656 | tf_op jit(solution)/shard_map/dot_general | solution.py:36
  17.6 1.7 fusion.2
  19.3 0.0 copy-start.2
  19.3 1.5 copy.22
  20.9 6.0 %collective-permute-start = (bf16[4,64,2048]{2,1,0:T(8,128)(2,1)}, bf16[4,64,2048]{2,1,0:T(8,128)(2,1)}, u32[]{:S(2)}, u32[]{:S(2)}) collective-permute-start(bf16[4,64,2048]{2,1,0:T(8,128)(2,1)} %bitcast.38), channel_id=1, source_target_pairs={{2,0},{3,1},{4,2},{5,3},{6,4},{7,5},{8,6},{9,7},{10,8},{11,9},{12,... | collective-permute-start | bytes 3145736 | tf_op jit(solution)/shard_map/ppermute | solution.py:10
  26.8 1.6 copy.21
  28.4 0.0 collective-permute-start.1
  28.4 1.6 copy.20
  30.0 0.5 collective-permute-start.2
  30.5 1.5 copy.19
  32.0 0.7 collective-permute-start.3
  32.7 0.0 copy-done.2
  32.7 0.1 copy.8
  32.8 0.1 reshape.34
  32.9 0.0 copy-done
  32.9 8.8 %gather_fusion = bf16[80,64,2048]{2,1,0:T(8,128)(2,1)} fusion(bf16[8,64,2048]{2,1,0:T(8,128)(2,1)S(1)} %bitcast.39, s32[1024]{0:T(1024)S(1)} %pad_clamp_fusion), kind=kCustom, calls=%fused_computation | custom fusion | bytes 41943360 | tf_op jit(solution)/shard_map/gather | solution.py:32
  41.7 10.9 %convolution_convert_fusion.1 = bf16[20,2048,64]{1,2,0:T(8,128)(2,1)S(1)} fusion(bf16[20,64,256]{2,1,0:T(8,128)(2,1)} %param.7, bf16[20,256,2048]{2,1,0:T(8,128)(2,1)} %bitcast.40), kind=kOutput, calls=%fused_computation.2 | convolution fusion | flops 1344798720 | bytes 26869760 | tf_op jit(solution)/shard_map/srk,skm->srm/dot_general | solution.py:33
  52.7 28.3 %collective-permute-done = bf16[4,64,2048]{2,1,0:T(8,128)(2,1)} collective-permute-done((bf16[4,64,2048]{2,1,0:T(8,128)(2,1)}, bf16[4,64,2048]{2,1,0:T(8,128)(2,1)}, u32[]{:S(2)}, u32[]{:S(2)}) %collective-permute-start) | collective-permute-done | bytes 1048608 | tf_op jit(solution)/shard_map/ppermute | solution.py:10
  81.0 1.3 bitcast_dynamic-update-slice_fusion.4
  82.3 0.0 collective-permute-done.1
  82.3 1.3 bitcast_dynamic-update-slice_fusion.3
  83.6 0.6 bitcast_dynamic-update-slice_fusion
  84.2 0.0 collective-permute-done.2
  84.2 1.3 bitcast_dynamic-update-slice_fusion.2
  85.6 0.0 collective-permute-done.3
  85.6 1.3 bitcast_dynamic-update-slice_fusion.1
  86.9 13.8 %fusion.3 = f32[2048,2048]{1,0:T(8,128)} fusion(bf16[1280,2048]{1,0:T(8,128)(2,1)S(1)} %bitcast.47, bf16[1280,2048]{1,0:T(8,128)(2,1)S(1)} %bitcast.41), kind=kOutput, calls=%fused_computation.21 | convolution fusion | flops 10737418240 | bytes 27262976 | tf_op jit(solution)/shard_map/dot_general | solution.py:48
  100.8 0.0 copy-start.1
  100.8 0.0 reduce-scatter.2.cloned.1.call-update
  100.8 189.0 %reduce-scatter.2.cloned.1.call-done = f32[128,2048]{1,0:T(8,128)} async-done(((f32[2048,2048]{1,0:T(8,128)}), f32[128,2048]{1,0:T(8,128)}) %reduce-scatter.2.cloned.1.call-update) | async-done | bytes 1048592 | tf_op jit(solution)/shard_map/reduce_scatter | solution.py:51
  289.8 0.0 copy-done.1
  (2 shorter events, 0.0 us)
Async XLA Ops:
  6.5 26.4 %copy-start = (bf16[512,2048]{1,0:T(8,128)(2,1)S(1)}, bf16[512,2048]{1,0:T(8,128)(2,1)}, u32[]{:S(2)}) copy-start(bf16[512,2048]{1,0:T(8,128)(2,1)} %param.6) | copy-start | bytes 6291460
  6.5 283.2 %reduce-scatter.2.cloned.1.call-start = ((), (), s32[]{:S(2)}) async-start(), calls=%async_computation.1 | async-start | bytes 17825792 | tf_op jit(solution)/shard_map/reduce_scatter | solution.py:51
  19.3 13.4 %copy-start.2 = (s32[20,4]{0,1:T(4,128)S(1)}, s32[20,4]{0,1:T(4,128)}, u32[]{:S(2)}) copy-start(s32[20,4]{0,1:T(4,128)} %param.9) | copy-start | bytes 964
  20.9 60.1 %collective-permute-start = (bf16[4,64,2048]{2,1,0:T(8,128)(2,1)}, bf16[4,64,2048]{2,1,0:T(8,128)(2,1)}, u32[]{:S(2)}, u32[]{:S(2)}) collective-permute-start(bf16[4,64,2048]{2,1,0:T(8,128)(2,1)} %bitcast.38), channel_id=1, source_target_pairs={{2,0},{3,1},{4,2},{5,3},{6,4},{7,5},{8,6},{9,7},{10,8},{11,9},{12,... | collective-permute-start | bytes 3145736 | tf_op jit(solution)/shard_map/ppermute | solution.py:10
  28.4 53.9 %collective-permute-start.1 = (bf16[4,64,2048]{2,1,0:T(8,128)(2,1)}, bf16[4,64,2048]{2,1,0:T(8,128)(2,1)}, u32[]{:S(2)}, u32[]{:S(2)}) collective-permute-start(bf16[4,64,2048]{2,1,0:T(8,128)(2,1)} %bitcast.37), channel_id=1, source_target_pairs={{1,0},{2,1},{3,2},{4,3},{5,4},{6,5},{7,6},{8,7},{9,8},{10,9},{11,1... | collective-permute-start | bytes 3145736 | tf_op jit(solution)/shard_map/ppermute | solution.py:10
  30.0 54.3 %collective-permute-start.2 = (bf16[4,64,2048]{2,1,0:T(8,128)(2,1)}, bf16[4,64,2048]{2,1,0:T(8,128)(2,1)}, u32[]{:S(2)}, u32[]{:S(2)}) collective-permute-start(bf16[4,64,2048]{2,1,0:T(8,128)(2,1)} %bitcast.36), channel_id=1, source_target_pairs={{15,0},{0,1},{1,2},{2,3},{3,4},{4,5},{5,6},{6,7},{7,8},{8,9},{9,10... | collective-permute-start | bytes 3145736 | tf_op jit(solution)/shard_map/ppermute | solution.py:10
  32.0 53.6 %collective-permute-start.3 = (bf16[4,64,2048]{2,1,0:T(8,128)(2,1)}, bf16[4,64,2048]{2,1,0:T(8,128)(2,1)}, u32[]{:S(2)}, u32[]{:S(2)}) collective-permute-start(bf16[4,64,2048]{2,1,0:T(8,128)(2,1)} %bitcast.35), channel_id=1, source_target_pairs={{14,0},{15,1},{0,2},{1,3},{2,4},{3,5},{4,6},{5,7},{6,8},{7,9},{8,1... | collective-permute-start | bytes 3145736 | tf_op jit(solution)/shard_map/ppermute | solution.py:10
  100.8 189.0 %copy-start.1 = (bf16[512,2048]{1,0:T(8,128)(2,1)S(1)}, bf16[512,2048]{1,0:T(8,128)(2,1)}, u32[]{:S(2)}) copy-start(bf16[512,2048]{1,0:T(8,128)(2,1)} %param.6) | copy-start | bytes 6291460
Sparse Core Ops, SparseCore 0:
  100.9 188.7 reduce-scatter.1
where the time goes:
time: 297 us
  waiting for transfers between devices  217 us (73%)
  matrix products  28.7 us (10%)
  local copies, waits for them, and re-layouts  27.6 us (9%)
  between operations  13.5 us (5%)
  starting transfers between devices  7.17 us (2%)
    reduce_scatter x1, waiting for transfers between devices, per_device(): lax.psum_scatter(partial_value, 'mesh', scatter_dimension=0, tiled=True)  189 us
    ppermute x4, waiting for transfers between devices, passed_along(): return lax.ppermute(block, axis, route)  28.3 us
    dot_general x1, matrix products, per_device(): lax.dot_general(left_rows, right_rows, (((0,), (0,)), ((), ())), preferre...  13.8 us
    dot_general x1, matrix products, per_device(): jnp.einsum('srk,skm->srm', coupling, picked, preferred_element_type=jnp.f...  10.9 us
    unnamed x14, local copies, waits for them, and re-layouts  10.8 us
    gather x1, local copies, waits for them, and re-layouts, per_device(): acoustic_blocks[face_blocks].reshape(slot_count, -1, acoustic_width)  8.82 us
    ppermute x4, starting transfers between devices, passed_along(): return lax.ppermute(block, axis, route)  7.17 us
  transfers between devices with their start and end apart: 5, of which 2 were waited for; matrix products, arithmetic and copies ran while one was open for 10% of the time, Pallas kernels for 0%

commit v1 on v0

v1 whole, which is shorter than its diff:
```python
import functools

import jax
import jax.numpy as jnp
from jax import lax
from jax.experimental import pallas as pl
from jax.experimental.pallas import tpu as pltpu
from jax.sharding import PartitionSpec as P

CLASSES = 5
CHUNKS = 4


def coupled_kernel(blocks_ref, acoustic_ref, coupling_ref, *refs):
    outs, picked = refs[:CLASSES], refs[CLASSES]
    slots, rows, depth = coupling_ref.shape
    per_class = slots // CLASSES
    for slot in range(slots):
        for n in range(depth // rows):
            at = pl.multiple_of(blocks_ref[slot, n] * rows, rows)
            picked[n * rows : (n + 1) * rows, :] = acoustic_ref[pl.ds(at, rows), :]
        product = jnp.dot(
            coupling_ref[slot], picked[...], preferred_element_type=jnp.float32
        )
        k, s = divmod(slot, per_class)
        outs[k][s * rows : (s + 1) * rows, :] = product.astype(jnp.bfloat16)


def coupled_chunk(blocks, acoustic, coupling, chunk, width):
    slots, rows, depth = coupling.shape
    tall = slots // CLASSES * rows
    return pl.pallas_call(
        coupled_kernel,
        out_shape=[jax.ShapeDtypeStruct((tall, width), jnp.bfloat16)] * CLASSES,
        grid_spec=pltpu.PrefetchScalarGridSpec(
            num_scalar_prefetch=1,
            grid=(1,),
            in_specs=[
                pl.BlockSpec((acoustic.shape[0], width), lambda i, b: (0, chunk)),
                pl.BlockSpec(coupling.shape, lambda i, b: (0, 0, 0)),
            ],
            out_specs=[pl.BlockSpec((tall, width), lambda i, b: (0, 0))] * CLASSES,
            scratch_shapes=[pltpu.VMEM((depth, width), jnp.bfloat16)],
        ),
        compiler_params=pltpu.CompilerParams(vmem_limit_bytes=32 * 2**20),
        cost_estimate=pl.CostEstimate(
            flops=2 * slots * rows * depth * width,
            bytes_accessed=2 * width * (acoustic.shape[0] + slots * rows),
            transcendentals=0,
        ),
        name="coupled_chunk",
    )(blocks, acoustic, coupling)


def panel_kernel(shift_ref, left_ref, *refs):
    pieces, out_ref, picked = refs[:CLASSES], refs[CLASSES], refs[CLASSES + 1]
    count = shift_ref.shape[0]
    rows = left_ref.shape[1] // count

    @pl.when(pl.program_id(0) == 0)
    def _():
        seen = [jnp.int32(0)] * CLASSES
        for b in range(count):
            kind = shift_ref[b]
            slot = jnp.int32(0)
            for k in range(CLASSES):
                slot = jnp.where(kind == k, seen[k], slot)
                seen[k] = seen[k] + (kind == k).astype(jnp.int32)
            at = pl.multiple_of(slot * rows, rows)
            for k in range(CLASSES):

                @pl.when(kind == k)
                def _(k=k, b=b, at=at):
                    picked[b * rows : (b + 1) * rows, :] = pieces[k][pl.ds(at, rows), :]

    out_ref[...] = jnp.dot(
        left_ref[...], picked[...], preferred_element_type=jnp.float32
    ).astype(out_ref.dtype)


def panel_part(shift, left, pieces, dtype):
    tall, depth = left.shape
    high, width = pieces[0].shape
    tile = min(tall, 256)
    return pl.pallas_call(
        panel_kernel,
        out_shape=jax.ShapeDtypeStruct((tall, width), dtype),
        grid_spec=pltpu.PrefetchScalarGridSpec(
            num_scalar_prefetch=1,
            grid=(tall // tile,),
            in_specs=[pl.BlockSpec((tile, depth), lambda i, s: (i, 0))]
            + [pl.BlockSpec((high, width), lambda i, s: (0, 0))] * CLASSES,
            out_specs=pl.BlockSpec((tile, width), lambda i, s: (i, 0)),
            scratch_shapes=[pltpu.VMEM((depth, width), jnp.bfloat16)],
        ),
        compiler_params=pltpu.CompilerParams(vmem_limit_bytes=32 * 2**20),
        cost_estimate=pl.CostEstimate(
            flops=2 * tall * depth * width,
            bytes_accessed=2 * (tall * depth + CLASSES * high * width) + 4 * tall * width,
            transcendentals=0,
        ),
        name="panel_part",
    )(shift, left, *pieces)


def passed_along(block, distance):
    size = lax.axis_size("mesh")
    return lax.ppermute(block, "mesh", [((i - distance) % size, i) for i in range(size)])


def swapped(block, bit):
    size = lax.axis_size("mesh")
    return lax.ppermute(block, "mesh", [(i, i ^ (1 << bit)) for i in range(size)])


def halving_order(size):
    bits = list(range(size.bit_length() - 1))
    return [0, 2, 1] + bits[3:] if len(bits) > 2 else bits


def per_device(struct_modes, acoustic_modes, coupling, face_shift, face_blocks):
    size = lax.axis_size("mesh")
    me = lax.axis_index("mesh")
    width = acoustic_modes.shape[1] // CHUNKS
    share = struct_modes.shape[1] // size
    order = halving_order(size)

    sides = struct_modes.T.reshape(size // 2, 2, share, -1)
    mine = me & 1

    def side(which):
        return lax.dynamic_index_in_dim(sides, which, 1, keepdims=False).reshape(
            size // 2 * share, -1
        )

    kept_left, sent_left = side(mine), side(1 - mine)

    columns = []
    for chunk in range(CHUNKS):
        made = coupled_chunk(face_blocks, acoustic_modes, coupling, chunk, width)
        pieces = [
            made[k] if k == 2 else passed_along(made[k], 2 - k) for k in range(CLASSES)
        ]
        got = swapped(panel_part(face_shift, sent_left, pieces, jnp.bfloat16), order[0])
        held = panel_part(face_shift, kept_left, pieces, jnp.float32)
        left_bits = sorted(order[1:], reverse=True)
        for level, bit in enumerate(order[1:], 1):
            place = left_bits.index(bit)
            left_bits.remove(bit)
            total = (held + got.astype(jnp.float32)).reshape(2**place, 2, -1, width)
            here = (me >> bit) & 1
            held = lax.dynamic_index_in_dim(total, here, 1, keepdims=False)
            away = lax.dynamic_index_in_dim(total, 1 - here, 1, keepdims=False)
            held = held.reshape(-1, width)
            wire = jnp.bfloat16 if level < 4 else jnp.float32
            got = swapped(away.reshape(-1, width).astype(wire), bit)
        columns.append(held + got.astype(jnp.float32))
    return jnp.concatenate(columns, axis=1)


def solution(mesh):
    placed = (
        P(("member", "mesh"), None),
        P(("member", "mesh"), None),
        P("mesh", None, None),
        P("mesh"),
        P("mesh", None),
    )
    return jax.shard_map(
        per_device,
        mesh=mesh,
        in_specs=placed,
        out_specs=P(("member", "mesh"), None),
        check_vma=False,
    )
```

time: 297 us -> 206 us (0.69)
  waiting for transfers between devices: 217 us -> 71.9 us
  Pallas kernels: 0 us -> 37.7 us
  starting transfers between devices: 7.17 us -> 43.1 us
  matrix products: 28.7 us -> 0 us
  local copies, waits for them, and re-layouts: 27.6 us -> 45.4 us
  between operations: 13.5 us -> 0.67 us
  other arithmetic: 2.31 us -> 5.84 us
    reduce_scatter x1 -> x0, waiting for transfers between devices: 189 us -> none  [per_device(): lax.psum_scatter(partial_value, 'mesh', scatter_dimension=0, tiled=True)]
    ppermute x4 -> x32, waiting for transfers between devices: 28.3 us -> 71.9 us  [the longest x16 57.6 us: swapped(): return lax.ppermute(block, 'mesh', [(i, i ^ 1 << bit) for i in range(size)])]
    pallas_call x0 -> x12, Pallas kernels: none -> 37.7 us  [the longest x8 28.3 us: panel_part(): pl.pallas_call(panel_kernel, out_shape=jax.ShapeDtypeStruct((tall, width)...]
    ppermute x4 -> x32, starting transfers between devices: 7.17 us -> 43.1 us  [the longest x16 28.6 us: passed_along(): lax.ppermute(block, 'mesh', [((i - distance) % size, i) for i in range(si...]
    dot_general x3 -> x0, matrix products: 28.7 us -> none  [the longest x1 13.8 us: per_device(): lax.dot_general(left_rows, right_rows, (((0,), (0,)), ((), ())), preferre...]
    unnamed x14 -> x71, local copies, waits for them, and re-layouts: 10.8 us -> 26.2 us
    dynamic_slice x0 -> x9, local copies, waits for them, and re-layouts: none -> 12.5 us  [the longest x1 12.1 us: side(): lax.dynamic_index_in_dim(sides, which, 1, keepdims=False)]
    gather x1 -> x0, local copies, waits for them, and re-layouts: 8.82 us -> none  [per_device(): acoustic_blocks[face_blocks].reshape(slot_count, -1, acoustic_width)]
  transfers between devices with their start and end apart: 5 -> 32, of which waited for: 2 -> 12; matrix products, arithmetic and copies ran while one was open for 10% -> 18% of each run, Pallas kernels for 0% -> 17%
where the time goes in v1:
time: 206 us; the launch traced here: 205 us
  waiting for transfers between devices  71.9 us (35%)
  local copies, waits for them, and re-layouts  45.4 us (22%)
  starting transfers between devices  43.1 us (21%)
  Pallas kernels  37.7 us (18%)
  other arithmetic  5.84 us (3%)
    ppermute x16, waiting for transfers between devices, swapped(): return lax.ppermute(block, 'mesh', [(i, i ^ 1 << bit) for i in range(size)])  57.6 us
    ppermute x16, starting transfers between devices, passed_along(): lax.ppermute(block, 'mesh', [((i - distance) % size, i) for i in range(si...  28.6 us
    pallas_call x8, Pallas kernels, panel_part(): pl.pallas_call(panel_kernel, out_shape=jax.ShapeDtypeStruct((tall, width)...  28.3 us
    unnamed x71, local copies, waits for them, and re-layouts  26.2 us
    ppermute x16, starting transfers between devices, swapped(): return lax.ppermute(block, 'mesh', [(i, i ^ 1 << bit) for i in range(size)])  14.5 us
    ppermute x16, waiting for transfers between devices, passed_along(): lax.ppermute(block, 'mesh', [((i - distance) % size, i) for i in range(si...  14.3 us
    dynamic_slice x1, local copies, waits for them, and re-layouts, side(): lax.dynamic_index_in_dim(sides, which, 1, keepdims=False)  12.1 us
    pallas_call x4, Pallas kernels, coupled_chunk(): pl.pallas_call(coupled_kernel, out_shape=[jax.ShapeDtypeStruct((tall, wid...  9.35 us
  transfers between devices with their start and end apart: 32, of which 12 were waited for; matrix products, arithmetic and copies ran while one was open for 18% of the time, Pallas kernels for 17%

profile of v1, /device:TPU:0, one launch (start us, length us, event | category | flops | bytes accessed | tf_op | source)
XLA Modules:
  0.0 204.7 jit_solution(6498393205881929597)
XLA Ops:
  0.0 0.8 copy.7.blocks_ref
  0.8 1.6 copy-done
  2.4 1.1 copy-done.3
  3.5 2.5 %coupled_chunk.4 = (bf16[256,512]{1,0:T(8,128)(2,1)S(1)}, bf16[256,512]{1,0:T(8,128)(2,1)S(1)}, bf16[256,512]{1,0:T(8,128)(2,1)S(1)}, bf16[256,512]{1,0:T(8,128)(2,1)S(1)}, bf16[256,512]{1,0:T(8,128)(2,1)}) custom-call(s32[20,4]{1,0:T(8,128)S(1)} %copy.7.blocks_ref, bf16[512,2048]{1,0:T(8,128)(2,1)S(1)} %copy-done, bf16[20,64,256]{2,1,0:T(8,128)(2,1)S(1)} %copy-done.3), custom_call_target="tpu_custom_call" | custom-call | flops 335544320 | bytes 1835008 | tf_op jit(solution)/shard_map/coupled_chunk/pallas_call | solution.py:32
  6.0 2.9 %collective-permute-start = (bf16[256,512]{1,0:T(8,128)(2,1)S(1)}, bf16[256,512]{1,0:T(8,128)(2,1)S(1)}, u32[]{:S(2)}, u32[]{:S(2)}) collective-permute-start(bf16[256,512]{1,0:T(8,128)(2,1)S(1)} %get-tuple-element.25), channel_id=1, source_target_pairs={{14,0},{15,1},{0,2},{1,3},{2,4},{3,5},{4,6},{5,7},{6,8},{7,9},{8,1... | collective-permute-start | bytes 786440 | tf_op jit(solution)/shard_map/ppermute | solution.py:108
  8.9 4.4 %collective-permute-start.2 = (bf16[256,512]{1,0:T(8,128)(2,1)S(1)}, bf16[256,512]{1,0:T(8,128)(2,1)S(1)}, u32[]{:S(2)}, u32[]{:S(2)}) collective-permute-start(bf16[256,512]{1,0:T(8,128)(2,1)S(1)} %get-tuple-element.28), channel_id=1, source_target_pairs={{1,0},{2,1},{3,2},{4,3},{5,4},{6,5},{7,6},{8,7},{9,8},{10,9},{11,1... | collective-permute-start | bytes 786440 | tf_op jit(solution)/shard_map/ppermute | solution.py:108
  13.3 0.4 collective-permute-start.3
  13.7 2.6 %coupled_chunk.5 = (bf16[256,512]{1,0:T(8,128)(2,1)}, bf16[256,512]{1,0:T(8,128)(2,1)}, bf16[256,512]{1,0:T(8,128)(2,1)S(1)}, bf16[256,512]{1,0:T(8,128)(2,1)}, bf16[256,512]{1,0:T(8,128)(2,1)}) custom-call(s32[20,4]{1,0:T(8,128)S(1)} %copy.7.blocks_ref, bf16[512,2048]{1,0:T(8,128)(2,1)S(1)} %copy-done, bf16[20,64,256]{2,1,0:T(8,128)(2,1)S(1)} %copy-done.3), custom_call_target="tpu_custom_call" | custom-call | flops 335544320 | bytes 1835008 | tf_op jit(solution)/shard_map/coupled_chunk/pallas_call | solution.py:32
  16.3 0.7 copy-done.11
  17.1 6.1 %reshape.131 = bf16[8,2,128,768]{2,1,0,3:T(2,128)(2,1)} reshape(bf16[2048,768]{0,1:T(8,128)(2,1)} %bitcast.97) | data formatting | bytes 6291456 | tf_op jit(solution)/shard_map/reshape | solution.py:128
  23.2 3.6 %collective-permute-done.refs_0_ = bf16[256,512]{1,0:T(8,128)(2,1)S(1)} collective-permute-done((bf16[256,512]{1,0:T(8,128)(2,1)S(1)}, bf16[256,512]{1,0:T(8,128)(2,1)S(1)}, u32[]{:S(2)}, u32[]{:S(2)}) %collective-permute-start) | collective-permute-done | bytes 262176 | tf_op jit(solution)/shard_map/ppermute | solution.py:108
  26.7 8.5 %collective-permute-start.11 = (bf16[256,512]{1,0:T(8,128)(2,1)}, bf16[256,512]{1,0:T(8,128)(2,1)}, u32[]{:S(2)}, u32[]{:S(2)}) collective-permute-start(bf16[256,512]{1,0:T(8,128)(2,1)} %get-tuple-element.34), channel_id=1, source_target_pairs={{2,0},{3,1},{4,2},{5,3},{6,4},{7,5},{8,6},{9,7},{10,8},{11,9},{12,... | collective-permute-start | bytes 786440 | tf_op jit(solution)/shard_map/ppermute | solution.py:108
  35.3 12.1 %constant_dynamic-slice_fusion.8 = (bf16[8,1,128,768]{2,1,0,3:T(2,128)(2,1)}, bf16[8,1,128,768]{2,1,0,3:T(2,128)(2,1)}) fusion(bf16[8,2,128,768]{2,1,0,3:T(2,128)(2,1)} %reshape.131, s32[]{:T(128)S(6)} %select_n.47, s32[]{:T(128)S(6)} %select_n.46), kind=kLoop, calls=%fused_computation.41 | loop fusion | bytes 6291464 | tf_op jit(solution)/shard_map/jit(dynamic_index_in_dim)/dynamic_slice | solution.py:132
  47.3 6.8 %copy.21 = bf16[8,1,128,768]{3,2,0,1:T(8,128)(2,1)S(1)} copy(bf16[8,1,128,768]{2,1,0,3:T(2,128)(2,1)} %get-tuple-element.45) | data formatting | bytes 3145728
  54.2 1.6 copy-done.1
  55.8 1.8 coupled_chunk.6
  57.6 0.7 copy-done.14
  58.3 4.5 %panel_part.9 = bf16[1024,512]{1,0:T(8,128)(2,1)} custom-call(s32[12]{0:T(128)S(1)} %copy-done.33, bf16[1024,768]{1,0:T(8,128)(2,1)S(1)} %bitcast.77, bf16[256,512]{1,0:T(8,128)(2,1)S(1)} %collective-permute-done.refs_0_, bf16[256,512]{1,0:T(8,128)(2,1)S(1)} %collective-permute-done.1.refs_1_, bf16[256,512]{1,0:T(8,128)(2,1)S(1)} %get-tuple-element.27.refs_2_, ...), custom_call_target="tpu_custom_call" | custom-call | flops 805306368 | bytes 4980736 | tf_op jit(solution)/shard_map/panel_part/pallas_call | solution.py:85
  62.8 1.2 collective-permute-start.4
  64.1 4.4 %collective-permute-start.18 = (bf16[256,512]{1,0:T(8,128)(2,1)S(1)}, bf16[256,512]{1,0:T(8,128)(2,1)S(1)}, u32[]{:S(2)}, u32[]{:S(2)}) collective-permute-start(bf16[256,512]{1,0:T(8,128)(2,1)S(1)} %get-tuple-element.38), channel_id=1, source_target_pairs={{1,0},{2,1},{3,2},{4,3},{5,4},{6,5},{7,6},{8,7},{9,8},{10,9},{11,1... | collective-permute-start | bytes 786440 | tf_op jit(solution)/shard_map/ppermute | solution.py:108
  68.5 1.1 collective-permute-start.19
  69.6 2.5 %coupled_chunk.7 = (bf16[256,512]{1,0:T(8,128)(2,1)S(1)}, bf16[256,512]{1,0:T(8,128)(2,1)}, bf16[256,512]{1,0:T(8,128)(2,1)S(1)}, bf16[256,512]{1,0:T(8,128)(2,1)}, bf16[256,512]{1,0:T(8,128)(2,1)}) custom-call(s32[20,4]{1,0:T(8,128)S(1)} %copy.7.blocks_ref, bf16[512,2048]{1,0:T(8,128)(2,1)S(1)} %copy-done.2, bf16[20,64,256]{2,1,0:T(8,128)(2,1)S(1)} %copy-done.4), custom_call_target="tpu_custom_call" | custom-call | flops 335544320 | bytes 1835008 | tf_op jit(solution)/shard_map/coupled_chunk/pallas_call | solution.py:32
  72.1 0.7 copy-done.29
  72.8 0.9 collective-permute-start.24
  73.8 1.1 collective-permute-done.18.refs_3_
  74.9 4.7 %collective-permute-start.26 = (bf16[256,512]{1,0:T(8,128)(2,1)}, bf16[256,512]{1,0:T(8,128)(2,1)}, u32[]{:S(2)}, u32[]{:S(2)}) collective-permute-start(bf16[256,512]{1,0:T(8,128)(2,1)} %get-tuple-element.43), channel_id=1, source_target_pairs={{1,0},{2,1},{3,2},{4,3},{5,4},{6,5},{7,6},{8,7},{9,8},{10,9},{11,1... | collective-permute-start | bytes 786440 | tf_op jit(solution)/shard_map/ppermute | solution.py:108
  79.6 9.6 %collective-permute-done.19.refs_4_ = bf16[256,512]{1,0:T(8,128)(2,1)S(1)} collective-permute-done((bf16[256,512]{1,0:T(8,128)(2,1)S(1)}, bf16[256,512]{1,0:T(8,128)(2,1)S(1)}, u32[]{:S(2)}, u32[]{:S(2)}) %collective-permute-start.19) | collective-permute-done | bytes 262176 | tf_op jit(solution)/shard_map/ppermute | solution.py:108
  89.2 1.1 collective-permute-start.27
  90.3 4.7 %panel_part.11 = bf16[1024,512]{1,0:T(8,128)(2,1)} custom-call(s32[12]{0:T(128)S(1)} %copy-done.33, bf16[1024,768]{1,0:T(8,128)(2,1)S(1)} %bitcast.78, bf16[256,512]{1,0:T(8,128)(2,1)} %collective-permute-done.8.refs_0_, bf16[256,512]{1,0:T(8,128)(2,1)} %collective-permute-done.9.refs_1_, bf16[256,512]{1,0:T(8,128)(2,1)S(1)} %copy-done.12, ...), custom_call_target="tpu_custom_call" | custom-call | flops 805306368 | bytes 4980736 | tf_op jit(solution)/shard_map/panel_part/pallas_call | solution.py:85
  95.0 0.7 copy-done.31
  95.7 6.8 %copy.20 = bf16[8,1,128,768]{3,2,0,1:T(8,128)(2,1)S(1)} copy(bf16[8,1,128,768]{2,1,0,3:T(2,128)(2,1)} %get-tuple-element.46) | data formatting | bytes 3145728
  102.5 0.9 copy-done.15
  103.4 0.9 copy-done.18
  104.4 0.9 copy-done.21
  105.3 0.9 copy-done.24
  106.3 0.9 copy-done.27
  107.2 2.5 %panel_part.13 = bf16[1024,512]{1,0:T(8,128)(2,1)S(1)} custom-call(s32[12]{0:T(128)S(1)} %copy-done.33, bf16[1024,768]{1,0:T(8,128)(2,1)S(1)} %bitcast.79, bf16[256,512]{1,0:T(8,128)(2,1)S(1)} %copy-done.18, bf16[256,512]{1,0:T(8,128)(2,1)S(1)} %copy-done.21, bf16[256,512]{1,0:T(8,128)(2,1)S(1)} %copy-done.15, bf16[256,512]{1,0:T(8,128)(2,1)S(1)} %copy-done.24, ...), custom_call_target="tpu_custom_call" | custom-call | flops 805306368 | bytes 4980736 | tf_op jit(solution)/shard_map/panel_part/pallas_call | solution.py:85
  109.7 0.6 collective-permute-start.20
  110.3 3.6 %panel_part.15 = bf16[1024,512]{1,0:T(8,128)(2,1)S(1)} custom-call(s32[12]{0:T(128)S(1)} %copy-done.33, bf16[1024,768]{1,0:T(8,128)(2,1)S(1)} %bitcast.80, bf16[256,512]{1,0:T(8,128)(2,1)S(1)} %copy-done.32, bf16[256,512]{1,0:T(8,128)(2,1)} %collective-permute-done.25.refs_1_, bf16[256,512]{1,0:T(8,128)(2,1)S(1)} %copy-done.30, ...), custom_call_target="tpu_custom_call" | custom-call | flops 805306368 | bytes 4980736 | tf_op jit(solution)/shard_map/panel_part/pallas_call | solution.py:85
  114.0 3.4 %panel_part.8 = f32[1024,512]{1,0:T(8,128)S(1)} custom-call(s32[12]{0:T(128)S(1)} %copy-done.33, bf16[1024,768]{1,0:T(8,128)(2,1)S(1)} %bitcast.73, bf16[256,512]{1,0:T(8,128)(2,1)S(1)} %copy-done.6, bf16[256,512]{1,0:T(8,128)(2,1)S(1)} %copy-done.8, bf16[256,512]{1,0:T(8,128)(2,1)S(1)} %get-tuple-element.27.refs_2_, bf16[256,512]{1,0:T(8,128)(2,1)S(1)} %copy-done.10, ...), custom_call_target="tpu_custom_call" | custom-call | flops 805306368 | bytes 4980736 | tf_op jit(solution)/shard_map/panel_part/pallas_call | solution.py:85
  117.5 3.6 %panel_part.10 = f32[1024,512]{1,0:T(8,128)S(1)} custom-call(s32[12]{0:T(128)S(1)} %copy-done.33, bf16[1024,768]{1,0:T(8,128)(2,1)S(1)} %bitcast.74, bf16[256,512]{1,0:T(8,128)(2,1)} %collective-permute-done.8.refs_0_, bf16[256,512]{1,0:T(8,128)(2,1)} %collective-permute-done.9.refs_1_, bf16[256,512]{1,0:T(8,128)(2,1)S(1)} %copy-done.13, ...), custom_call_target="tpu_custom_call" | custom-call | flops 805306368 | bytes 4980736 | tf_op jit(solution)/shard_map/panel_part/pallas_call | solution.py:85
  121.2 2.5 %panel_part.12 = f32[1024,512]{1,0:T(8,128)S(1)} custom-call(s32[12]{0:T(128)S(1)} %copy-done.33, bf16[1024,768]{1,0:T(8,128)(2,1)S(1)} %bitcast.75, bf16[256,512]{1,0:T(8,128)(2,1)S(1)} %copy-done.19, bf16[256,512]{1,0:T(8,128)(2,1)S(1)} %copy-done.22, bf16[256,512]{1,0:T(8,128)(2,1)S(1)} %copy-done.16, bf16[256,512]{1,0:T(8,128)(2,1)S(1)} %copy-done.25, ...), custom_call_target="tpu_custom_call" | custom-call | flops 805306368 | bytes 4980736 | tf_op jit(solution)/shard_map/panel_part/pallas_call | solution.py:85
  123.7 3.6 %panel_part.14 = f32[1024,512]{1,0:T(8,128)S(1)} custom-call(s32[12]{0:T(128)S(1)} %copy-done.33, bf16[1024,768]{1,0:T(8,128)(2,1)S(1)} %bitcast.76, bf16[256,512]{1,0:T(8,128)(2,1)S(1)} %copy-done.32, bf16[256,512]{1,0:T(8,128)(2,1)} %collective-permute-done.25.refs_1_, bf16[256,512]{1,0:T(8,128)(2,1)S(1)} %copy-done.30, ...), custom_call_target="tpu_custom_call" | custom-call | flops 805306368 | bytes 4980736 | tf_op jit(solution)/shard_map/panel_part/pallas_call | solution.py:85
  127.2 1.5 convert_add_fusion.3
  129.0 1.5 convert_add_fusion.2
  130.6 2.1 %collective-permute-start.13 = (bf16[512,512]{1,0:T(8,128)(2,1)S(1)}, bf16[512,512]{1,0:T(8,128)(2,1)S(1)}, u32[]{:S(2)}, u32[]{:S(2)}) collective-permute-start(bf16[512,512]{1,0:T(8,128)(2,1)S(1)} %bitcast.108), channel_id=1, source_target_pairs={{0,4},{1,5},{2,6},{3,7},{4,0},{5,1},{6,2},{7,3},{8,12},{9,13},{10,... | collective-permute-start | bytes 1572872 | tf_op jit(solution)/shard_map/ppermute | solution.py:113
  133.6 2.1 %collective-permute-start.29 = (bf16[512,512]{1,0:T(8,128)(2,1)S(1)}, bf16[512,512]{1,0:T(8,128)(2,1)S(1)}, u32[]{:S(2)}, u32[]{:S(2)}) collective-permute-start(bf16[512,512]{1,0:T(8,128)(2,1)S(1)} %bitcast.106), channel_id=1, source_target_pairs={{0,4},{1,5},{2,6},{3,7},{4,0},{5,1},{6,2},{7,3},{8,12},{9,13},{10,... | collective-permute-start | bytes 1572872 | tf_op jit(solution)/shard_map/ppermute | solution.py:113
  136.0 7.7 %collective-permute-done.5 = bf16[512,512]{1,0:T(8,128)(2,1)S(1)} collective-permute-done((bf16[512,512]{1,0:T(8,128)(2,1)S(1)}, bf16[512,512]{1,0:T(8,128)(2,1)S(1)}, u32[]{:S(2)}, u32[]{:S(2)}) %collective-permute-start.5) | collective-permute-done | bytes 524320 | tf_op jit(solution)/shard_map/ppermute | solution.py:113
  143.9 0.9 collective-permute-start.6
  144.8 10.1 %collective-permute-done.13 = bf16[512,512]{1,0:T(8,128)(2,1)S(1)} collective-permute-done((bf16[512,512]{1,0:T(8,128)(2,1)S(1)}, bf16[512,512]{1,0:T(8,128)(2,1)S(1)}, u32[]{:S(2)}, u32[]{:S(2)}) %collective-permute-start.13) | collective-permute-done | bytes 524320 | tf_op jit(solution)/shard_map/ppermute | solution.py:113
  155.1 0.9 collective-permute-start.14
  156.1 10.1 %collective-permute-done.21 = bf16[512,512]{1,0:T(8,128)(2,1)S(1)} collective-permute-done((bf16[512,512]{1,0:T(8,128)(2,1)S(1)}, bf16[512,512]{1,0:T(8,128)(2,1)S(1)}, u32[]{:S(2)}, u32[]{:S(2)}) %collective-permute-start.21) | collective-permute-done | bytes 524320 | tf_op jit(solution)/shard_map/ppermute | solution.py:113
  166.4 0.9 collective-permute-start.22
  167.4 9.6 %collective-permute-done.29 = bf16[512,512]{1,0:T(8,128)(2,1)S(1)} collective-permute-done((bf16[512,512]{1,0:T(8,128)(2,1)S(1)}, bf16[512,512]{1,0:T(8,128)(2,1)S(1)}, u32[]{:S(2)}, u32[]{:S(2)}) %collective-permute-start.29) | collective-permute-done | bytes 524320 | tf_op jit(solution)/shard_map/ppermute | solution.py:113
  177.2 1.0 collective-permute-start.30
  178.4 1.1 collective-permute-start.7
  179.6 1.9 collective-permute-start.15
  181.7 1.1 collective-permute-start.23
  182.8 2.3 %collective-permute-done.30 = bf16[256,512]{1,0:T(8,128)(2,1)S(1)} collective-permute-done((bf16[256,512]{1,0:T(8,128)(2,1)S(1)}, bf16[256,512]{1,0:T(8,128)(2,1)S(1)}, u32[]{:S(2)}, u32[]{:S(2)}) %collective-permute-start.30) | collective-permute-done | bytes 262176 | tf_op jit(solution)/shard_map/ppermute | solution.py:113
  185.6 9.7 %collective-permute-done.7 = bf16[128,512]{1,0:T(8,128)(2,1)S(1)} collective-permute-done((bf16[128,512]{1,0:T(8,128)(2,1)S(1)}, bf16[128,512]{1,0:T(8,128)(2,1)S(1)}, u32[]{:S(2)}, u32[]{:S(2)}) %collective-permute-start.7) | collective-permute-done | bytes 131104 | tf_op jit(solution)/shard_map/ppermute | solution.py:113
  195.3 2.8 %collective-permute-done.15 = bf16[128,512]{1,0:T(8,128)(2,1)S(1)} collective-permute-done((bf16[128,512]{1,0:T(8,128)(2,1)S(1)}, bf16[128,512]{1,0:T(8,128)(2,1)S(1)}, u32[]{:S(2)}, u32[]{:S(2)}) %collective-permute-start.15) | collective-permute-done | bytes 131104 | tf_op jit(solution)/shard_map/ppermute | solution.py:113
  198.1 2.8 %collective-permute-done.23 = bf16[128,512]{1,0:T(8,128)(2,1)S(1)} collective-permute-done((bf16[128,512]{1,0:T(8,128)(2,1)S(1)}, bf16[128,512]{1,0:T(8,128)(2,1)S(1)}, u32[]{:S(2)}, u32[]{:S(2)}) %collective-permute-start.23) | collective-permute-done | bytes 131104 | tf_op jit(solution)/shard_map/ppermute | solution.py:113
  200.9 2.7 %collective-permute-done.31 = bf16[128,512]{1,0:T(8,128)(2,1)S(1)} collective-permute-done((bf16[128,512]{1,0:T(8,128)(2,1)S(1)}, bf16[128,512]{1,0:T(8,128)(2,1)S(1)}, u32[]{:S(2)}, u32[]{:S(2)}) %collective-permute-start.31) | collective-permute-done | bytes 131104 | tf_op jit(solution)/shard_map/ppermute | solution.py:113
  203.6 1.0 pad_maximum_fusion
  (122 shorter events, 3.7 us)
Async XLA Ops:
  0.8 1.6 copy-start
  2.4 1.1 copy-start.3
  6.0 20.8 %collective-permute-start = (bf16[256,512]{1,0:T(8,128)(2,1)S(1)}, bf16[256,512]{1,0:T(8,128)(2,1)S(1)}, u32[]{:S(2)}, u32[]{:S(2)}) collective-permute-start(bf16[256,512]{1,0:T(8,128)(2,1)S(1)} %get-tuple-element.25), channel_id=1, source_target_pairs={{14,0},{15,1},{0,2},{1,3},{2,4},{3,5},{4,6},{5,7},{6,8},{7,9},{8,1... | collective-permute-start | bytes 786440 | tf_op jit(solution)/shard_map/ppermute | solution.py:108
  8.9 26.3 %collective-permute-start.1 = (bf16[256,512]{1,0:T(8,128)(2,1)S(1)}, bf16[256,512]{1,0:T(8,128)(2,1)S(1)}, u32[]{:S(2)}, u32[]{:S(2)}) collective-permute-start(bf16[256,512]{1,0:T(8,128)(2,1)S(1)} %get-tuple-element.26), channel_id=1, source_target_pairs={{15,0},{0,1},{1,2},{2,3},{3,4},{4,5},{5,6},{6,7},{7,8},{8,9},{9,10... | collective-permute-start | bytes 786440 | tf_op jit(solution)/shard_map/ppermute | solution.py:108
  8.9 26.3 %collective-permute-start.2 = (bf16[256,512]{1,0:T(8,128)(2,1)S(1)}, bf16[256,512]{1,0:T(8,128)(2,1)S(1)}, u32[]{:S(2)}, u32[]{:S(2)}) collective-permute-start(bf16[256,512]{1,0:T(8,128)(2,1)S(1)} %get-tuple-element.28), channel_id=1, source_target_pairs={{1,0},{2,1},{3,2},{4,3},{5,4},{6,5},{7,6},{8,7},{9,8},{10,9},{11,1... | collective-permute-start | bytes 786440 | tf_op jit(solution)/shard_map/ppermute | solution.py:108
  13.3 44.9 %collective-permute-start.3 = (bf16[256,512]{1,0:T(8,128)(2,1)}, bf16[256,512]{1,0:T(8,128)(2,1)}, u32[]{:S(2)}, u32[]{:S(2)}) collective-permute-start(bf16[256,512]{1,0:T(8,128)(2,1)} %get-tuple-element.29), channel_id=1, source_target_pairs={{2,0},{3,1},{4,2},{5,3},{6,4},{7,5},{8,6},{9,7},{10,8},{11,9},{12,... | collective-permute-start | bytes 786440 | tf_op jit(solution)/shard_map/ppermute | solution.py:108
  16.3 0.7 copy-start.11
  17.0 45.9 %collective-permute-start.10 = (bf16[256,512]{1,0:T(8,128)(2,1)}, bf16[256,512]{1,0:T(8,128)(2,1)}, u32[]{:S(2)}, u32[]{:S(2)}) collective-permute-start(bf16[256,512]{1,0:T(8,128)(2,1)} %get-tuple-element.33), channel_id=1, source_target_pairs={{1,0},{2,1},{3,2},{4,3},{5,4},{6,5},{7,6},{8,7},{9,8},{10,9},{11,1... | collective-permute-start | bytes 786440 | tf_op jit(solution)/shard_map/ppermute | solution.py:108
  26.7 31.6 %copy-start.5 = (bf16[256,512]{1,0:T(8,128)(2,1)}, bf16[256,512]{1,0:T(8,128)(2,1)S(1)}, u32[]{:S(2)}) copy-start(bf16[256,512]{1,0:T(8,128)(2,1)S(1)} %collective-permute-done.refs_0_) | copy-start | bytes 786436
  26.7 37.4 %collective-permute-start.11 = (bf16[256,512]{1,0:T(8,128)(2,1)}, bf16[256,512]{1,0:T(8,128)(2,1)}, u32[]{:S(2)}, u32[]{:S(2)}) collective-permute-start(bf16[256,512]{1,0:T(8,128)(2,1)} %get-tuple-element.34), channel_id=1, source_target_pairs={{2,0},{3,1},{4,2},{5,3},{6,4},{7,5},{8,6},{9,7},{10,8},{11,9},{12,... | collective-permute-start | bytes 786440 | tf_op jit(solution)/shard_map/ppermute | solution.py:108
  35.2 23.1 %copy-start.7 = (bf16[256,512]{1,0:T(8,128)(2,1)}, bf16[256,512]{1,0:T(8,128)(2,1)S(1)}, u32[]{:S(2)}) copy-start(bf16[256,512]{1,0:T(8,128)(2,1)S(1)} %collective-permute-done.1.refs_1_) | copy-start | bytes 786436
  35.2 29.0 %collective-permute-start.8 = (bf16[256,512]{1,0:T(8,128)(2,1)}, bf16[256,512]{1,0:T(8,128)(2,1)}, u32[]{:S(2)}, u32[]{:S(2)}) collective-permute-start(bf16[256,512]{1,0:T(8,128)(2,1)} %get-tuple-element.30), channel_id=1, source_target_pairs={{14,0},{15,1},{0,2},{1,3},{2,4},{3,5},{4,6},{5,7},{6,8},{7,9},{8,1... | collective-permute-start | bytes 786440 | tf_op jit(solution)/shard_map/ppermute | solution.py:108
  35.2 23.1 %copy-start.9 = (bf16[256,512]{1,0:T(8,128)(2,1)}, bf16[256,512]{1,0:T(8,128)(2,1)S(1)}, u32[]{:S(2)}) copy-start(bf16[256,512]{1,0:T(8,128)(2,1)S(1)} %collective-permute-done.2.refs_3_) | copy-start | bytes 786436
  35.2 33.3 %collective-permute-start.9 = (bf16[256,512]{1,0:T(8,128)(2,1)}, bf16[256,512]{1,0:T(8,128)(2,1)}, u32[]{:S(2)}, u32[]{:S(2)}) collective-permute-start(bf16[256,512]{1,0:T(8,128)(2,1)} %get-tuple-element.31), channel_id=1, source_target_pairs={{15,0},{0,1},{1,2},{2,3},{3,4},{4,5},{5,6},{6,7},{7,8},{8,9},{9,10... | collective-permute-start | bytes 786440 | tf_op jit(solution)/shard_map/ppermute | solution.py:108
  47.3 6.8 %copy-start.4 = (bf16[20,64,256]{2,1,0:T(8,128)(2,1)S(1)}, bf16[20,64,256]{2,1,0:T(8,128)(2,1)}, u32[]{:S(2)}) copy-start(bf16[20,64,256]{2,1,0:T(8,128)(2,1)} %coupling_ref.7) | copy-start | bytes 1966084
  54.2 1.6 copy-start.1
  55.8 2.5 %copy-start.33 = (s32[12]{0:T(128)S(1)}, s32[12]{0:T(128)}, u32[]{:S(2)}) copy-start(s32[12]{0:T(128)} %shift_ref.15) | copy-start | bytes 148
  58.3 11.4 %copy-start.2 = (bf16[512,2048]{1,0:T(8,128)(2,1)S(1)}, bf16[512,2048]{1,0:T(8,128)(2,1)}, u32[]{:S(2)}) copy-start(bf16[512,2048]{1,0:T(8,128)(2,1)} %acoustic_ref.7) | copy-start | bytes 6291460
  58.3 14.6 %collective-permute-start.16 = (bf16[256,512]{1,0:T(8,128)(2,1)S(1)}, bf16[256,512]{1,0:T(8,128)(2,1)S(1)}, u32[]{:S(2)}, u32[]{:S(2)}) collective-permute-start(bf16[256,512]{1,0:T(8,128)(2,1)S(1)} %get-tuple-element.35), channel_id=1, source_target_pairs={{14,0},{15,1},{0,2},{1,3},{2,4},{3,5},{4,6},{5,7},{6,8},{7,9},{8,1... | collective-permute-start | bytes 786440 | tf_op jit(solution)/shard_map/ppermute | solution.py:108
  62.8 27.4 %copy-start.12 = (bf16[256,512]{1,0:T(8,128)(2,1)S(1)}, bf16[256,512]{1,0:T(8,128)(2,1)}, u32[]{:S(2)}) copy-start(bf16[256,512]{1,0:T(8,128)(2,1)} %copy-done.11) | copy-start | bytes 786436
  62.8 64.4 %collective-permute-start.4 = (bf16[1024,512]{1,0:T(8,128)(2,1)}, bf16[1024,512]{1,0:T(8,128)(2,1)}, u32[]{:S(2)}, u32[]{:S(2)}) collective-permute-start(bf16[1024,512]{1,0:T(8,128)(2,1)} %panel_part.9), channel_id=1, source_target_pairs={{0,1},{1,0},{2,3},{3,2},{4,5},{5,4},{6,7},{7,6},{8,9},{9,8},{10,11... | collective-permute-start | bytes 3145736 | tf_op jit(solution)/shard_map/ppermute | solution.py:113
  64.1 9.7 %collective-permute-start.17 = (bf16[256,512]{1,0:T(8,128)(2,1)S(1)}, bf16[256,512]{1,0:T(8,128)(2,1)S(1)}, u32[]{:S(2)}, u32[]{:S(2)}) collective-permute-start(bf16[256,512]{1,0:T(8,128)(2,1)S(1)} %get-tuple-element.36), channel_id=1, source_target_pairs={{15,0},{0,1},{1,2},{2,3},{3,4},{4,5},{5,6},{6,7},{7,8},{8,9},{9,10... | collective-permute-start | bytes 786440 | tf_op jit(solution)/shard_map/ppermute | solution.py:108
  64.1 10.7 %collective-permute-start.18 = (bf16[256,512]{1,0:T(8,128)(2,1)S(1)}, bf16[256,512]{1,0:T(8,128)(2,1)S(1)}, u32[]{:S(2)}, u32[]{:S(2)}) collective-permute-start(bf16[256,512]{1,0:T(8,128)(2,1)S(1)} %get-tuple-element.38), channel_id=1, source_target_pairs={{1,0},{2,1},{3,2},{4,3},{5,4},{6,5},{7,6},{8,7},{9,8},{10,9},{11,1... | collective-permute-start | bytes 786440 | tf_op jit(solution)/shard_map/ppermute | solution.py:108
  68.5 20.6 %collective-permute-start.19 = (bf16[256,512]{1,0:T(8,128)(2,1)S(1)}, bf16[256,512]{1,0:T(8,128)(2,1)S(1)}, u32[]{:S(2)}, u32[]{:S(2)}) collective-permute-start(bf16[256,512]{1,0:T(8,128)(2,1)S(1)} %get-tuple-element.39), channel_id=1, source_target_pairs={{2,0},{3,1},{4,2},{5,3},{6,4},{7,5},{8,6},{9,7},{10,8},{11,9},{12,... | collective-permute-start | bytes 786440 | tf_op jit(solution)/shard_map/ppermute | solution.py:108
  72.8 22.1 %copy-start.17 = (bf16[256,512]{1,0:T(8,128)(2,1)}, bf16[256,512]{1,0:T(8,128)(2,1)S(1)}, u32[]{:S(2)}) copy-start(bf16[256,512]{1,0:T(8,128)(2,1)S(1)} %collective-permute-done.16.refs_0_) | copy-start | bytes 786436
  72.8 22.1 %collective-permute-start.24 = (bf16[256,512]{1,0:T(8,128)(2,1)S(1)}, bf16[256,512]{1,0:T(8,128)(2,1)S(1)}, u32[]{:S(2)}, u32[]{:S(2)}) collective-permute-start(bf16[256,512]{1,0:T(8,128)(2,1)S(1)} %get-tuple-element.40), channel_id=1, source_target_pairs={{14,0},{15,1},{0,2},{1,3},{2,4},{3,5},{4,6},{5,7},{6,8},{7,9},{8,1... | collective-permute-start | bytes 786440 | tf_op jit(solution)/shard_map/ppermute | solution.py:108
  73.8 21.9 %copy-start.20 = (bf16[256,512]{1,0:T(8,128)(2,1)}, bf16[256,512]{1,0:T(8,128)(2,1)S(1)}, u32[]{:S(2)}) copy-start(bf16[256,512]{1,0:T(8,128)(2,1)S(1)} %collective-permute-done.17.refs_1_) | copy-start | bytes 786436
  73.8 36.0 %collective-permute-start.25 = (bf16[256,512]{1,0:T(8,128)(2,1)}, bf16[256,512]{1,0:T(8,128)(2,1)}, u32[]{:S(2)}, u32[]{:S(2)}) collective-permute-start(bf16[256,512]{1,0:T(8,128)(2,1)} %get-tuple-element.41), channel_id=1, source_target_pairs={{15,0},{0,1},{1,2},{2,3},{3,4},{4,5},{5,6},{6,7},{7,8},{8,9},{9,10... | collective-permute-start | bytes 786440 | tf_op jit(solution)/shard_map/ppermute | solution.py:108
  74.9 20.8 %copy-start.23 = (bf16[256,512]{1,0:T(8,128)(2,1)}, bf16[256,512]{1,0:T(8,128)(2,1)S(1)}, u32[]{:S(2)}) copy-start(bf16[256,512]{1,0:T(8,128)(2,1)S(1)} %collective-permute-done.18.refs_3_) | copy-start | bytes 786436
  74.9 35.4 %collective-permute-start.26 = (bf16[256,512]{1,0:T(8,128)(2,1)}, bf16[256,512]{1,0:T(8,128)(2,1)}, u32[]{:S(2)}, u32[]{:S(2)}) collective-permute-start(bf16[256,512]{1,0:T(8,128)(2,1)} %get-tuple-element.43), channel_id=1, source_target_pairs={{1,0},{2,1},{3,2},{4,3},{5,4},{6,5},{7,6},{8,7},{9,8},{10,9},{11,1... | collective-permute-start | bytes 786440 | tf_op jit(solution)/shard_map/ppermute | solution.py:108
  89.2 5.8 %copy-start.26 = (bf16[256,512]{1,0:T(8,128)(2,1)}, bf16[256,512]{1,0:T(8,128)(2,1)S(1)}, u32[]{:S(2)}) copy-start(bf16[256,512]{1,0:T(8,128)(2,1)S(1)} %collective-permute-done.19.refs_4_) | copy-start | bytes 786436
  89.2 21.1 %collective-permute-start.27 = (bf16[256,512]{1,0:T(8,128)(2,1)}, bf16[256,512]{1,0:T(8,128)(2,1)}, u32[]{:S(2)}, u32[]{:S(2)}) collective-permute-start(bf16[256,512]{1,0:T(8,128)(2,1)} %get-tuple-element.44), channel_id=1, source_target_pairs={{2,0},{3,1},{4,2},{5,3},{6,4},{7,5},{8,6},{9,7},{10,8},{11,9},{12,... | collective-permute-start | bytes 786440 | tf_op jit(solution)/shard_map/ppermute | solution.py:108
  94.9 0.7 copy-start.31
  95.7 33.3 %collective-permute-start.12 = (bf16[1024,512]{1,0:T(8,128)(2,1)}, bf16[1024,512]{1,0:T(8,128)(2,1)}, u32[]{:S(2)}, u32[]{:S(2)}) collective-permute-start(bf16[1024,512]{1,0:T(8,128)(2,1)} %panel_part.11), channel_id=1, source_target_pairs={{0,1},{1,0},{2,3},{3,2},{4,5},{5,4},{6,7},{7,6},{8,9},{9,8},{10,11... | collective-permute-start | bytes 3145736 | tf_op jit(solution)/shard_map/ppermute | solution.py:113
  102.4 1.0 copy-start.15
  103.4 0.9 copy-start.18
  104.3 0.9 copy-start.21
  105.3 0.9 copy-start.24
  106.2 0.9 copy-start.27
  107.2 3.1 %copy-start.30 = (bf16[256,512]{1,0:T(8,128)(2,1)S(1)}, bf16[256,512]{1,0:T(8,128)(2,1)}, u32[]{:S(2)}) copy-start(bf16[256,512]{1,0:T(8,128)(2,1)} %copy-done.29) | copy-start | bytes 786436
  107.2 3.1 %copy-start.32 = (bf16[256,512]{1,0:T(8,128)(2,1)S(1)}, bf16[256,512]{1,0:T(8,128)(2,1)}, u32[]{:S(2)}) copy-start(bf16[256,512]{1,0:T(8,128)(2,1)} %copy-done.31) | copy-start | bytes 786436
  109.7 4.3 %copy-start.6 = (bf16[256,512]{1,0:T(8,128)(2,1)S(1)}, bf16[256,512]{1,0:T(8,128)(2,1)}, u32[]{:S(2)}) copy-start(bf16[256,512]{1,0:T(8,128)(2,1)} %copy-done.5) | copy-start | bytes 786436
  109.7 4.3 %copy-start.8 = (bf16[256,512]{1,0:T(8,128)(2,1)S(1)}, bf16[256,512]{1,0:T(8,128)(2,1)}, u32[]{:S(2)}) copy-start(bf16[256,512]{1,0:T(8,128)(2,1)} %copy-done.7) | copy-start | bytes 786436
  109.7 4.3 %copy-start.10 = (bf16[256,512]{1,0:T(8,128)(2,1)S(1)}, bf16[256,512]{1,0:T(8,128)(2,1)}, u32[]{:S(2)}) copy-start(bf16[256,512]{1,0:T(8,128)(2,1)} %copy-done.9) | copy-start | bytes 786436
  109.7 22.9 %collective-permute-start.20 = (bf16[1024,512]{1,0:T(8,128)(2,1)S(1)}, bf16[1024,512]{1,0:T(8,128)(2,1)S(1)}, u32[]{:S(2)}, u32[]{:S(2)}) collective-permute-start(bf16[1024,512]{1,0:T(8,128)(2,1)S(1)} %panel_part.13), channel_id=1, source_target_pairs={{0,1},{1,0},{2,3},{3,2},{4,5},{5,4},{6,7},{7,6},{8,9},{9,8},{10,11... | collective-permute-start | bytes 3145736 | tf_op jit(solution)/shard_map/ppermute | solution.py:113
  113.9 19.3 %collective-permute-start.28 = (bf16[1024,512]{1,0:T(8,128)(2,1)S(1)}, bf16[1024,512]{1,0:T(8,128)(2,1)S(1)}, u32[]{:S(2)}, u32[]{:S(2)}) collective-permute-start(bf16[1024,512]{1,0:T(8,128)(2,1)S(1)} %panel_part.15), channel_id=1, source_target_pairs={{0,1},{1,0},{2,3},{3,2},{4,5},{5,4},{6,7},{7,6},{8,9},{9,8},{10,11... | collective-permute-start | bytes 3145736 | tf_op jit(solution)/shard_map/ppermute | solution.py:113
  114.0 3.4 %copy-start.13 = (bf16[256,512]{1,0:T(8,128)(2,1)S(1)}, bf16[256,512]{1,0:T(8,128)(2,1)}, u32[]{:S(2)}) copy-start(bf16[256,512]{1,0:T(8,128)(2,1)} %copy-done.11) | copy-start | bytes 786436
  117.4 3.7 %copy-start.16 = (bf16[256,512]{1,0:T(8,128)(2,1)S(1)}, bf16[256,512]{1,0:T(8,128)(2,1)}, u32[]{:S(2)}) copy-start(bf16[256,512]{1,0:T(8,128)(2,1)} %copy-done.14) | copy-start | bytes 786436
  117.4 3.7 %copy-start.19 = (bf16[256,512]{1,0:T(8,128)(2,1)S(1)}, bf16[256,512]{1,0:T(8,128)(2,1)}, u32[]{:S(2)}) copy-start(bf16[256,512]{1,0:T(8,128)(2,1)} %copy-done.17) | copy-start | bytes 786436
  117.4 3.7 %copy-start.22 = (bf16[256,512]{1,0:T(8,128)(2,1)S(1)}, bf16[256,512]{1,0:T(8,128)(2,1)}, u32[]{:S(2)}) copy-start(bf16[256,512]{1,0:T(8,128)(2,1)} %copy-done.20) | copy-start | bytes 786436
  117.5 3.7 %copy-start.25 = (bf16[256,512]{1,0:T(8,128)(2,1)S(1)}, bf16[256,512]{1,0:T(8,128)(2,1)}, u32[]{:S(2)}) copy-start(bf16[256,512]{1,0:T(8,128)(2,1)} %copy-done.23) | copy-start | bytes 786436
  117.5 3.7 %copy-start.28 = (bf16[256,512]{1,0:T(8,128)(2,1)S(1)}, bf16[256,512]{1,0:T(8,128)(2,1)}, u32[]{:S(2)}) copy-start(bf16[256,512]{1,0:T(8,128)(2,1)} %copy-done.26) | copy-start | bytes 786436
  128.9 14.8 %collective-permute-start.5 = (bf16[512,512]{1,0:T(8,128)(2,1)S(1)}, bf16[512,512]{1,0:T(8,128)(2,1)S(1)}, u32[]{:S(2)}, u32[]{:S(2)}) collective-permute-start(bf16[512,512]{1,0:T(8,128)(2,1)S(1)} %bitcast.107), channel_id=1, source_target_pairs={{0,4},{1,5},{2,6},{3,7},{4,0},{5,1},{6,2},{7,3},{8,12},{9,13},{10,... | collective-permute-start | bytes 1572872 | tf_op jit(solution)/shard_map/ppermute | solution.py:113
  130.6 24.3 %collective-permute-start.13 = (bf16[512,512]{1,0:T(8,128)(2,1)S(1)}, bf16[512,512]{1,0:T(8,128)(2,1)S(1)}, u32[]{:S(2)}, u32[]{:S(2)}) collective-permute-start(bf16[512,512]{1,0:T(8,128)(2,1)S(1)} %bitcast.108), channel_id=1, source_target_pairs={{0,4},{1,5},{2,6},{3,7},{4,0},{5,1},{6,2},{7,3},{8,12},{9,13},{10,... | collective-permute-start | bytes 1572872 | tf_op jit(solution)/shard_map/ppermute | solution.py:113
  133.1 33.1 %collective-permute-start.21 = (bf16[512,512]{1,0:T(8,128)(2,1)S(1)}, bf16[512,512]{1,0:T(8,128)(2,1)S(1)}, u32[]{:S(2)}, u32[]{:S(2)}) collective-permute-start(bf16[512,512]{1,0:T(8,128)(2,1)S(1)} %bitcast.109), channel_id=1, source_target_pairs={{0,4},{1,5},{2,6},{3,7},{4,0},{5,1},{6,2},{7,3},{8,12},{9,13},{10,... | collective-permute-start | bytes 1572872 | tf_op jit(solution)/shard_map/ppermute | solution.py:113
  133.6 43.3 %collective-permute-start.29 = (bf16[512,512]{1,0:T(8,128)(2,1)S(1)}, bf16[512,512]{1,0:T(8,128)(2,1)S(1)}, u32[]{:S(2)}, u32[]{:S(2)}) collective-permute-start(bf16[512,512]{1,0:T(8,128)(2,1)S(1)} %bitcast.106), channel_id=1, source_target_pairs={{0,4},{1,5},{2,6},{3,7},{4,0},{5,1},{6,2},{7,3},{8,12},{9,13},{10,... | collective-permute-start | bytes 1572872 | tf_op jit(solution)/shard_map/ppermute | solution.py:113
  143.9 34.4 %collective-permute-start.6 = (bf16[256,512]{1,0:T(8,128)(2,1)S(1)}, bf16[256,512]{1,0:T(8,128)(2,1)S(1)}, u32[]{:S(2)}, u32[]{:S(2)}) collective-permute-start(bf16[256,512]{1,0:T(8,128)(2,1)S(1)} %bitcast.110), channel_id=1, source_target_pairs={{0,2},{1,3},{2,0},{3,1},{4,6},{5,7},{6,4},{7,5},{8,10},{9,11},{10,... | collective-permute-start | bytes 786440 | tf_op jit(solution)/shard_map/ppermute | solution.py:113
  155.1 24.4 %collective-permute-start.14 = (bf16[256,512]{1,0:T(8,128)(2,1)S(1)}, bf16[256,512]{1,0:T(8,128)(2,1)S(1)}, u32[]{:S(2)}, u32[]{:S(2)}) collective-permute-start(bf16[256,512]{1,0:T(8,128)(2,1)S(1)} %bitcast.111), channel_id=1, source_target_pairs={{0,2},{1,3},{2,0},{3,1},{4,6},{5,7},{6,4},{7,5},{8,10},{9,11},{10,... | collective-permute-start | bytes 786440 | tf_op jit(solution)/shard_map/ppermute | solution.py:113
  166.4 15.2 %collective-permute-start.22 = (bf16[256,512]{1,0:T(8,128)(2,1)S(1)}, bf16[256,512]{1,0:T(8,128)(2,1)S(1)}, u32[]{:S(2)}, u32[]{:S(2)}) collective-permute-start(bf16[256,512]{1,0:T(8,128)(2,1)S(1)} %bitcast.112), channel_id=1, source_target_pairs={{0,2},{1,3},{2,0},{3,1},{4,6},{5,7},{6,4},{7,5},{8,10},{9,11},{10,... | collective-permute-start | bytes 786440 | tf_op jit(solution)/shard_map/ppermute | solution.py:113
  177.2 7.9 %collective-permute-start.30 = (bf16[256,512]{1,0:T(8,128)(2,1)S(1)}, bf16[256,512]{1,0:T(8,128)(2,1)S(1)}, u32[]{:S(2)}, u32[]{:S(2)}) collective-permute-start(bf16[256,512]{1,0:T(8,128)(2,1)S(1)} %bitcast.113), channel_id=1, source_target_pairs={{0,2},{1,3},{2,0},{3,1},{4,6},{5,7},{6,4},{7,5},{8,10},{9,11},{10,... | collective-permute-start | bytes 786440 | tf_op jit(solution)/shard_map/ppermute | solution.py:113
  178.4 16.9 %collective-permute-start.7 = (bf16[128,512]{1,0:T(8,128)(2,1)S(1)}, bf16[128,512]{1,0:T(8,128)(2,1)S(1)}, u32[]{:S(2)}, u32[]{:S(2)}) collective-permute-start(bf16[128,512]{1,0:T(8,128)(2,1)S(1)} %fusion), channel_id=1, source_target_pairs={{0,8},{1,9},{2,10},{3,11},{4,12},{5,13},{6,14},{7,15},{8,0},{9,1},... | collective-permute-start | bytes 393224 | tf_op jit(solution)/shard_map/ppermute | solution.py:113
  179.6 18.5 %collective-permute-start.15 = (bf16[128,512]{1,0:T(8,128)(2,1)S(1)}, bf16[128,512]{1,0:T(8,128)(2,1)S(1)}, u32[]{:S(2)}, u32[]{:S(2)}) collective-permute-start(bf16[128,512]{1,0:T(8,128)(2,1)S(1)} %fusion.1), channel_id=1, source_target_pairs={{0,8},{1,9},{2,10},{3,11},{4,12},{5,13},{6,14},{7,15},{8,0},{9,1},... | collective-permute-start | bytes 393224 | tf_op jit(solution)/shard_map/ppermute | solution.py:113
  181.7 19.2 %collective-permute-start.23 = (bf16[128,512]{1,0:T(8,128)(2,1)S(1)}, bf16[128,512]{1,0:T(8,128)(2,1)S(1)}, u32[]{:S(2)}, u32[]{:S(2)}) collective-permute-start(bf16[128,512]{1,0:T(8,128)(2,1)S(1)} %fusion.2), channel_id=1, source_target_pairs={{0,8},{1,9},{2,10},{3,11},{4,12},{5,13},{6,14},{7,15},{8,0},{9,1},... | collective-permute-start | bytes 393224 | tf_op jit(solution)/shard_map/ppermute | solution.py:113
  185.2 18.4 %collective-permute-start.31 = (bf16[128,512]{1,0:T(8,128)(2,1)S(1)}, bf16[128,512]{1,0:T(8,128)(2,1)S(1)}, u32[]{:S(2)}, u32[]{:S(2)}) collective-permute-start(bf16[128,512]{1,0:T(8,128)(2,1)S(1)} %fusion.3), channel_id=1, source_target_pairs={{0,8},{1,9},{2,10},{3,11},{4,12},{5,13},{6,14},{7,15},{8,0},{9,1},... | collective-permute-start | bytes 393224 | tf_op jit(solution)/shard_map/ppermute | solution.py:113
  (2 other events, 1.4 us)

commit v2 on v0

v2 whole, which is shorter than its diff:
```python
import jax
import jax.numpy as jnp
from jax import lax
from jax.experimental import pallas as pl
from jax.experimental.pallas import tpu as pltpu
from jax.sharding import PartitionSpec as P

CLASSES = 5
EIGHTHS = (2, 2, 2, 1, 1)
LIMIT = 20 * 2**20
ANY = pl.BlockSpec(memory_space=pl.ANY)
BF16, F32 = jnp.bfloat16, jnp.float32


def call(body, scalars, arrays, specs, after, out_shape, out_specs, grid, scratch, flops, alias=None):
    lead = len(scalars) + len(arrays)
    extra = len(after)

    def kernel(*refs):
        body(*refs[:lead], *refs[lead + extra :])

    touched = sum(a.size * a.dtype.itemsize for a in arrays)
    aliases = {} if alias is None else {lead - 1: alias}
    return pl.pallas_call(
        kernel,
        out_shape=out_shape,
        grid_spec=pltpu.PrefetchScalarGridSpec(
            num_scalar_prefetch=len(scalars),
            grid=grid,
            in_specs=specs + [ANY] * extra,
            out_specs=out_specs,
            scratch_shapes=scratch,
        ),
        input_output_aliases=aliases,
        compiler_params=pltpu.CompilerParams(vmem_limit_bytes=LIMIT),
        cost_estimate=pl.CostEstimate(flops=flops, bytes_accessed=touched, transcendentals=0),
        name=body.__name__,
    )(*scalars, *arrays, *after)


def coupled(blocks, acoustic, coupling, classes, at, width, after):
    slots, rows, depth = coupling.shape
    per = slots // CLASSES

    def coupled_rows(blocks_ref, acoustic_ref, coupling_ref, *refs):
        outs, picked = refs[:-1], refs[-1]
        for k, out in zip(classes, outs):
            for s in range(per):
                slot = k * per + s
                for n in range(depth // rows):
                    first = pl.multiple_of(blocks_ref[slot, n] * rows, rows)
                    picked[n * rows : (n + 1) * rows, :] = acoustic_ref[pl.ds(first, rows), :]
                out[s * rows : (s + 1) * rows, :] = jnp.dot(
                    coupling_ref[slot], picked[...], preferred_element_type=F32
                ).astype(BF16)

    count = len(classes)
    return call(
        coupled_rows,
        [blocks],
        [acoustic, coupling],
        [
            pl.BlockSpec((acoustic.shape[0], width), lambda i, b: (0, at // width)),
            pl.BlockSpec(coupling.shape, lambda i, b: (0, 0, 0)),
        ],
        after,
        [jax.ShapeDtypeStruct((per * rows, width), BF16)] * count,
        [pl.BlockSpec((per * rows, width), lambda i, b: (0, 0))] * count,
        (1,),
        [pltpu.VMEM((depth, width), BF16)],
        2 * count * per * rows * depth * width,
    )


def turned(mine, struct_modes, share, after):
    depth, modes = struct_modes.shape
    half = modes // 2

    def turn(mine_ref, kept_ref, sent_ref, kept_out, sent_out):
        kept_out[...] = kept_ref[...].T
        sent_out[...] = sent_ref[...].T

    if share % 128:
        sides = struct_modes.T.reshape(-1, 2, share, depth)
        return tuple(
            lax.dynamic_index_in_dim(sides, side, 1, keepdims=False).reshape(half, depth)
            for side in (mine, 1 - mine)
        )
    return call(
        turn,
        [mine.reshape(1)],
        [struct_modes, struct_modes],
        [
            pl.BlockSpec((depth, share), lambda i, m: (0, 2 * i + m[0])),
            pl.BlockSpec((depth, share), lambda i, m: (0, 2 * i + 1 - m[0])),
        ],
        after,
        [jax.ShapeDtypeStruct((half, depth), BF16)] * 2,
        [pl.BlockSpec((share, depth), lambda i, m: (i, 0))] * 2,
        (half // share,),
        [],
        0,
    )


def panel_sent(shift, left, pieces, after):
    tall, depth = left.shape
    high, width = pieces[0].shape
    tile = min(tall, 256)

    def panel_away(shift_ref, left_ref, *refs):
        parts, out_ref, picked = refs[:CLASSES], refs[CLASSES], refs[CLASSES + 1]
        count = shift_ref.shape[0]
        rows = depth // count

        @pl.when(pl.program_id(0) == 0)
        def _():
            seen = [jnp.int32(0)] * CLASSES
            for b in range(count):
                kind = shift_ref[b]
                slot = jnp.int32(0)
                for k in range(CLASSES):
                    slot = jnp.where(kind == k, seen[k], slot)
                    seen[k] = seen[k] + (kind == k).astype(jnp.int32)
                first = pl.multiple_of(slot * rows, rows)
                for k in range(CLASSES):

                    @pl.when(kind == k)
                    def _(k=k, b=b, first=first):
                        picked[b * rows : (b + 1) * rows, :] = parts[k][pl.ds(first, rows), :]

        out_ref[...] = jnp.dot(left_ref[...], picked[...], preferred_element_type=F32).astype(BF16)

    return call(
        panel_away,
        [shift],
        [left, *pieces],
        [pl.BlockSpec((tile, depth), lambda i, s: (i, 0))]
        + [pl.BlockSpec((high, width), lambda i, s: (0, 0))] * CLASSES,
        after,
        [
            jax.ShapeDtypeStruct((tall, width), BF16),
            jax.ShapeDtypeStruct((depth, width), BF16),
        ],
        [
            pl.BlockSpec((tile, width), lambda i, s: (i, 0)),
            pl.BlockSpec((depth, width), lambda i, s: (0, 0)),
        ],
        (tall // tile,),
        [],
        2 * tall * depth * width,
    )


def panel_kept(left, picked, after):
    tall, depth = left.shape
    width = picked.shape[1]
    tile = min(tall, 256)

    def panel_own(left_ref, picked_ref, out_ref):
        out_ref[...] = jnp.dot(left_ref[...], picked_ref[...], preferred_element_type=F32)

    return call(
        panel_own,
        [],
        [left, picked],
        [
            pl.BlockSpec((tile, depth), lambda i: (i, 0)),
            pl.BlockSpec((depth, width), lambda i: (0, 0)),
        ],
        after,
        jax.ShapeDtypeStruct((tall, width), F32),
        pl.BlockSpec((tile, width), lambda i: (i, 0)),
        (tall // tile,),
        [],
        2 * tall * depth * width,
    )


def added(held, got, here, before, wire, after):
    width = held.shape[1]
    shape = (before, 2, held.shape[0] // before // 2, width)
    block = (1, *shape[1:])
    out = (shape[0] * shape[2], width)

    def added_split(here_ref, held_ref, got_ref, kept_ref, away_ref):
        side = here_ref[0]
        kept_ref[...] = held_ref[0, side] + got_ref[0, side].astype(F32)
        away_ref[...] = (held_ref[0, 1 - side] + got_ref[0, 1 - side].astype(F32)).astype(wire)

    return call(
        added_split,
        [here.reshape(1)],
        [held.reshape(shape), got.reshape(shape)],
        [pl.BlockSpec(block, lambda i, h: (i, 0, 0, 0))] * 2,
        after,
        [jax.ShapeDtypeStruct(out, F32), jax.ShapeDtypeStruct(out, wire)],
        [pl.BlockSpec(shape[2:], lambda i, h: (i, 0))] * 2,
        (before,),
        [],
        2 * held.size,
    )


def finished(held, got, buffer, at, modes, after):
    rows, width = held.shape

    def added_last(held_ref, got_ref, *refs):
        refs[-1][...] = held_ref[...] + got_ref[...].astype(F32)

    spec = pl.BlockSpec((rows, width), lambda i: (0, 0))
    return call(
        added_last,
        [],
        [held, got] + ([] if buffer is None else [buffer]),
        [spec, spec] + ([] if buffer is None else [ANY]),
        after,
        jax.ShapeDtypeStruct((rows, modes), F32),
        pl.BlockSpec((rows, width), lambda i: (0, at // width)),
        (1,),
        [],
        held.size,
        None if buffer is None else 0,
    )


def passed_along(block, distance):
    size = lax.axis_size("mesh")
    return lax.ppermute(block, "mesh", [((i - distance) % size, i) for i in range(size)])


def swapped(block, bit):
    size = lax.axis_size("mesh")
    return lax.ppermute(block, "mesh", [(i, i ^ (1 << bit)) for i in range(size)])


def halving_order(size):
    bits = list(range(size.bit_length() - 1))
    return [0, 2, 1] + bits[3:] if len(bits) > 2 else bits


def planned(levels):
    steps, arrived, before = [], 4.0, 4.0
    for j, eighths in enumerate(EIGHTHS):
        size = eighths / 2
        arrived += 20.0 * size
        steps.append((before - 6.0 if j else 0.0, "far", j))
        steps.append((before - 3.0 if j else 0.0, "near", j))
        steps.append((arrived, "panel", j))
        at = arrived + 4.0 + 5.0 * size
        for level in range(1, levels):
            steps.append((at, level, j))
            at += (2.0 + 12.0 * size) if level == 1 else (2.0 + 7.0 * size)
        steps.append((at, levels, j))
        before = arrived
    return [step[1:] for step in sorted(steps, key=lambda step: step[0])]


def per_device(struct_modes, acoustic_modes, coupling, face_shift, face_blocks):
    size = lax.axis_size("mesh")
    me = lax.axis_index("mesh")
    modes = acoustic_modes.shape[1]
    share = struct_modes.shape[1] // size
    order = halving_order(size)
    levels = len(order)
    widths = [e * modes // 8 for e in EIGHTHS]
    starts = [sum(widths[:j]) for j in range(len(widths))]

    state = [dict(bits=sorted(order[1:], reverse=True)) for _ in widths]
    token, buffer, lefts = [], None, None
    for stage, j in planned(levels):
        now = state[j]
        if stage in ("far", "near"):
            classes = (0, 4) if stage == "far" else (1, 3, 2)
            made = coupled(
                face_blocks, acoustic_modes, coupling, classes, starts[j], widths[j], token
            )
            for k, block in zip(classes, made):
                now[k] = block if k == 2 else passed_along(block, 2 - k)
            token = [made[0]]
            if stage == "near" and lefts is None:
                lefts = turned(me & 1, struct_modes, share, token)
                token = [lefts[0]]
        elif stage == "panel":
            pieces = [now[k] for k in range(CLASSES)]
            away, picked = panel_sent(face_shift, lefts[1], pieces, token)
            now["got"] = swapped(away, order[0])
            now["held"] = panel_kept(lefts[0], picked, [])
            token = [now["held"]]
        elif stage < levels:
            bit = order[stage]
            place = now["bits"].index(bit)
            now["bits"].remove(bit)
            now["held"], away = added(
                now["held"], now["got"], (me >> bit) & 1, 2**place, BF16 if stage < 4 else F32, token
            )
            now["got"] = swapped(away, bit)
            token = [now["held"]]
        else:
            token = [t for t in token if t is not buffer]
            buffer = finished(now["held"], now["got"], buffer, starts[j], modes, token)
            token = [buffer]
    return buffer


def solution(mesh):
    placed = (
        P(("member", "mesh"), None),
        P(("member", "mesh"), None),
        P("mesh", None, None),
        P("mesh"),
        P("mesh", None),
    )
    return jax.shard_map(
        per_device,
        mesh=mesh,
        in_specs=placed,
        out_specs=P(("member", "mesh"), None),
        check_vma=False,
    )
```

time: 297 us -> 201 us (0.68)
  waiting for transfers between devices: 217 us -> 63.5 us
  starting transfers between devices: 7.17 us -> 60.4 us
  Pallas kernels: 0 us -> 52.1 us
  matrix products: 28.7 us -> 0 us
  between operations: 13.5 us -> 0.47 us
  local copies, waits for them, and re-layouts: 27.6 us -> 22.1 us
    reduce_scatter x1 -> x0, waiting for transfers between devices: 189 us -> none  [per_device(): lax.psum_scatter(partial_value, 'mesh', scatter_dimension=0, tiled=True)]
    ppermute x4 -> x40, starting transfers between devices: 7.17 us -> 60.4 us  [the longest x20 31.8 us: passed_along(): lax.ppermute(block, 'mesh', [((i - distance) % size, i) for i in range(si...]
    pallas_call x0 -> x41, Pallas kernels: none -> 52.1 us  [call(): pl.pallas_call(kernel, out_shape=out_shape, grid_spec=pltpu.PrefetchScala...]
    ppermute x4 -> x40, waiting for transfers between devices: 28.3 us -> 63.5 us  [the longest x20 55.2 us: swapped(): return lax.ppermute(block, 'mesh', [(i, i ^ 1 << bit) for i in range(size)])]
    dot_general x3 -> x0, matrix products: 28.7 us -> none  [the longest x1 13.8 us: per_device(): lax.dot_general(left_rows, right_rows, (((0,), (0,)), ((), ())), preferre...]
    unnamed x14 -> x61, local copies, waits for them, and re-layouts: 10.8 us -> 22.1 us
    gather x1 -> x0, local copies, waits for them, and re-layouts: 8.82 us -> none  [per_device(): acoustic_blocks[face_blocks].reshape(slot_count, -1, acoustic_width)]
    reshape x1 -> x0, local copies, waits for them, and re-layouts: 4.81 us -> none  [per_device(): struct_modes.reshape(block_count, -1)]
  transfers between devices with their start and end apart: 5 -> 40, of which waited for: 2 -> 14; matrix products, arithmetic and copies ran while one was open for 10% -> 0% of each run, Pallas kernels for 0% -> 17%
where the time goes in v2:
time: 201 us; the launch traced here: 199 us
  waiting for transfers between devices  63.5 us (32%)
  starting transfers between devices  60.4 us (30%)
  Pallas kernels  52.1 us (26%)
  local copies, waits for them, and re-layouts  22.1 us (11%)
    ppermute x20, waiting for transfers between devices, swapped(): return lax.ppermute(block, 'mesh', [(i, i ^ 1 << bit) for i in range(size)])  55.2 us
    pallas_call x41, Pallas kernels, call(): pl.pallas_call(kernel, out_shape=out_shape, grid_spec=pltpu.PrefetchScala...  52.1 us
    ppermute x20, starting transfers between devices, passed_along(): lax.ppermute(block, 'mesh', [((i - distance) % size, i) for i in range(si...  31.8 us
    ppermute x20, starting transfers between devices, swapped(): return lax.ppermute(block, 'mesh', [(i, i ^ 1 << bit) for i in range(size)])  28.6 us
    unnamed x61, local copies, waits for them, and re-layouts  22.1 us
    ppermute x20, waiting for transfers between devices, passed_along(): lax.ppermute(block, 'mesh', [((i - distance) % size, i) for i in range(si...  8.36 us
  transfers between devices with their start and end apart: 40, of which 14 were waited for; matrix products, arithmetic and copies ran while one was open for 0% of the time, Pallas kernels for 17%

profile of v2, /device:TPU:0, one launch (start us, length us, event | category | flops | bytes accessed | tf_op | source)
XLA Modules:
  0.0 198.6 jit_solution(16776731563518148954)
XLA Ops:
  0.8 1.6 copy-done
  2.4 1.1 copy-done.5
  3.5 2.0 coupled_rows.10
  5.4 6.0 %collective-permute-start.7 = (bf16[256,512]{1,0:T(8,128)(2,1)}, bf16[256,512]{1,0:T(8,128)(2,1)S(1)}, u32[]{:S(2)}, u32[]{:S(2)}) collective-permute-start(bf16[256,512]{1,0:T(8,128)(2,1)} %get-tuple-element.83), channel_id=1, source_target_pairs={{2,0},{3,1},{4,2},{5,3},{6,4},{7,5},{8,6},{9,7},{10,8},{11,9},{12,... | collective-permute-start | bytes 786440 | tf_op jit(solution)/shard_map/ppermute | solution.py:229
  11.4 2.0 %coupled_rows.11 = (bf16[256,512]{1,0:T(8,128)(2,1)}, bf16[256,512]{1,0:T(8,128)(2,1)}, bf16[256,512]{1,0:T(8,128)(2,1)S(1)}) custom-call(s32[20,4]{1,0:T(8,128)S(1)} %copy.11.refs_0_, bf16[512,2048]{1,0:T(8,128)(2,1)S(1)} %copy-done, bf16[20,64,256]{2,1,0:T(8,128)(2,1)S(1)} %copy-done.5, bf16[256,512]{1,0:T(8,128)(2,1)S(1)} %get-tuple-element.72.refs_3_), custom_call_target="tpu_custom_call" | custom-call | flops 201326592 | bytes 2752512 | tf_op jit(solution)/shard_map/coupled_rows/pallas_call | solution.py:24
  14.1 3.6 %collective-permute-start.6 = (bf16[256,512]{1,0:T(8,128)(2,1)}, bf16[256,512]{1,0:T(8,128)(2,1)}, u32[]{:S(2)}, u32[]{:S(2)}) collective-permute-start(bf16[256,512]{1,0:T(8,128)(2,1)} %get-tuple-element.82), channel_id=1, source_target_pairs={{1,0},{2,1},{3,2},{4,3},{5,4},{6,5},{7,6},{8,7},{9,8},{10,9},{11,1... | collective-permute-start | bytes 786440 | tf_op jit(solution)/shard_map/ppermute | solution.py:229
  17.7 1.9 copy-done.16
  19.6 2.3 %turn.1 = (bf16[1024,768]{1,0:T(8,128)(2,1)S(1)}, bf16[1024,768]{1,0:T(8,128)(2,1)S(1)}) custom-call(s32[1]{0:T(128)} %bitcast.3.refs_0_, bf16[768,2048]{1,0:T(8,128)(2,1)S(1)} %copy-done.16, bf16[768,2048]{1,0:T(8,128)(2,1)S(1)} %copy-done.16, bf16[256,512]{1,0:T(8,128)(2,1)} %get-tuple-element.73.refs_3_), custom_call_target="tpu_custom_call" | custom-call | bytes 6291456 | tf_op jit(solution)/shard_map/turn/pallas_call | solution.py:24
  21.9 2.0 coupled_rows.12
  23.9 2.0 %coupled_rows.13 = (bf16[256,512]{1,0:T(8,128)(2,1)}, bf16[256,512]{1,0:T(8,128)(2,1)}, bf16[256,512]{1,0:T(8,128)(2,1)S(1)}) custom-call(s32[20,4]{1,0:T(8,128)S(1)} %copy.11.refs_0_, bf16[512,2048]{1,0:T(8,128)(2,1)S(1)} %copy-done.1, bf16[20,64,256]{2,1,0:T(8,128)(2,1)S(1)} %copy-done.6, bf16[256,512]{1,0:T(8,128)(2,1)S(1)} %get-tuple-element.76.refs_3_), custom_call_target="tpu_custom_call" | custom-call | flops 201326592 | bytes 2752512 | tf_op jit(solution)/shard_map/coupled_rows/pallas_call | solution.py:24
  26.7 4.6 %panel_away.5 = (bf16[1024,512]{1,0:T(8,128)(2,1)}, bf16[768,512]{1,0:T(8,128)(2,1)S(1)}) custom-call(s32[12]{0:T(128)S(1)} %copy-done.29, bf16[1024,768]{1,0:T(8,128)(2,1)S(1)} %get-tuple-element.75.refs_1_, bf16[256,512]{1,0:T(8,128)(2,1)} %collective-permute-done.4.refs_2_, bf16[256,512]{1,0:T(8,128)(2,1)} %collective-permute-done.5.refs_3_, ...), custom_call_target="tpu_custom_call" | custom-call | flops 805306368 | bytes 2883584 | tf_op jit(solution)/shard_map/panel_away/pallas_call | solution.py:24
  32.9 1.4 collective-permute-start
  34.4 3.3 %collective-permute-start.3 = (bf16[256,512]{1,0:T(8,128)(2,1)}, bf16[256,512]{1,0:T(8,128)(2,1)}, u32[]{:S(2)}, u32[]{:S(2)}) collective-permute-start(bf16[256,512]{1,0:T(8,128)(2,1)} %get-tuple-element.80), channel_id=1, source_target_pairs={{2,0},{3,1},{4,2},{5,3},{6,4},{7,5},{8,6},{9,7},{10,8},{11,9},{12,... | collective-permute-start | bytes 786440 | tf_op jit(solution)/shard_map/ppermute | solution.py:229
  38.2 1.4 copy-done.8
  39.6 1.1 copy-done.20
  40.7 1.5 panel_own.5.refs_3_
  42.2 2.1 %added_split.15 = (f32[512,512]{1,0:T(8,128)S(1)}, bf16[512,512]{1,0:T(8,128)(2,1)}) custom-call(s32[1]{0:T(128)} %bitcast.2.refs_0_, f32[2,2,256,512]{3,2,1,0:T(8,128)S(1)} %bitcast.36, bf16[2,2,256,512]{3,2,1,0:T(8,128)(2,1)} %bitcast.5.refs_2_, f32[1024,512]{1,0:T(8,128)S(1)} %panel_own.5.refs_3_), custom_call_target="tpu_custom_call" | custom-call | flops 1048576 | bytes 3145728 | tf_op jit(solution)/shard_map/added_split/pallas_call | solution.py:24
  44.3 2.0 coupled_rows.14
  46.2 2.0 %coupled_rows.15 = (bf16[256,512]{1,0:T(8,128)(2,1)}, bf16[256,512]{1,0:T(8,128)(2,1)}, bf16[256,512]{1,0:T(8,128)(2,1)S(1)}) custom-call(s32[20,4]{1,0:T(8,128)S(1)} %copy.11.refs_0_, bf16[512,2048]{1,0:T(8,128)(2,1)S(1)} %copy-done.1, bf16[20,64,256]{2,1,0:T(8,128)(2,1)S(1)} %copy-done.6, bf16[256,512]{1,0:T(8,128)(2,1)} %get-tuple-element.87.refs_3_), custom_call_target="tpu_custom_call" | custom-call | flops 201326592 | bytes 2752512 | tf_op jit(solution)/shard_map/coupled_rows/pallas_call | solution.py:24
  48.2 3.3 %collective-permute-done.3.refs_6_ = bf16[256,512]{1,0:T(8,128)(2,1)} collective-permute-done((bf16[256,512]{1,0:T(8,128)(2,1)}, bf16[256,512]{1,0:T(8,128)(2,1)}, u32[]{:S(2)}, u32[]{:S(2)}) %collective-permute-start.3) | collective-permute-done | bytes 262176 | tf_op jit(solution)/shard_map/ppermute | solution.py:229
  51.6 4.7 %panel_away.6 = (bf16[1024,512]{1,0:T(8,128)(2,1)}, bf16[768,512]{1,0:T(8,128)(2,1)S(1)}) custom-call(s32[12]{0:T(128)S(1)} %copy-done.29, bf16[1024,768]{1,0:T(8,128)(2,1)S(1)} %copy-done.12, bf16[256,512]{1,0:T(8,128)(2,1)} %collective-permute-done.refs_2_, bf16[256,512]{1,0:T(8,128)(2,1)} %collective-permute-done.1.refs_3_, ...), custom_call_target="tpu_custom_call" | custom-call | flops 805306368 | bytes 2883584 | tf_op jit(solution)/shard_map/panel_away/pallas_call | solution.py:24
  57.2 2.6 %collective-permute-start.9 = (bf16[1024,512]{1,0:T(8,128)(2,1)}, bf16[1024,512]{1,0:T(8,128)(2,1)}, u32[]{:S(2)}, u32[]{:S(2)}) collective-permute-start(bf16[1024,512]{1,0:T(8,128)(2,1)} %get-tuple-element.90), channel_id=1, source_target_pairs={{0,1},{1,0},{2,3},{3,2},{4,5},{5,4},{6,7},{7,6},{8,9},{9,8},{10,11... | collective-permute-start | bytes 3145736 | tf_op jit(solution)/shard_map/ppermute | solution.py:234
  59.8 1.4 copy-done.9
  61.2 1.1 copy-done.22
  62.3 1.5 panel_own.6.refs_3_
  63.8 10.0 %collective-permute-done.10 = bf16[512,512]{1,0:T(8,128)(2,1)S(1)} collective-permute-done((bf16[512,512]{1,0:T(8,128)(2,1)}, bf16[512,512]{1,0:T(8,128)(2,1)S(1)}, u32[]{:S(2)}, u32[]{:S(2)}) %collective-permute-start.10) | collective-permute-done | bytes 524320 | tf_op jit(solution)/shard_map/ppermute | solution.py:234
  76.4 1.3 copy-done.14
  78.5 1.3 collective-permute-start.14
  79.7 3.4 %collective-permute-start.17 = (bf16[256,512]{1,0:T(8,128)(2,1)}, bf16[256,512]{1,0:T(8,128)(2,1)}, u32[]{:S(2)}, u32[]{:S(2)}) collective-permute-start(bf16[256,512]{1,0:T(8,128)(2,1)} %get-tuple-element.100), channel_id=1, source_target_pairs={{2,0},{3,1},{4,2},{5,3},{6,4},{7,5},{8,6},{9,7},{10,8},{11,9},{12,... | collective-permute-start | bytes 786440 | tf_op jit(solution)/shard_map/ppermute | solution.py:229
  83.7 1.6 copy-done.15
  85.3 1.3 added_split.17
  86.6 9.1 %collective-permute-done.12 = bf16[256,512]{1,0:T(8,128)(2,1)} collective-permute-done((bf16[256,512]{1,0:T(8,128)(2,1)}, bf16[256,512]{1,0:T(8,128)(2,1)}, u32[]{:S(2)}, u32[]{:S(2)}) %collective-permute-start.12) | collective-permute-done | bytes 262176 | tf_op jit(solution)/shard_map/ppermute | solution.py:234
  96.7 1.1 coupled_rows.16
  97.8 1.2 coupled_rows.17
  99.6 3.7 %panel_away.7 = (bf16[1024,512]{1,0:T(8,128)(2,1)S(1)}, bf16[768,512]{1,0:T(8,128)(2,1)S(1)}) custom-call(s32[12]{0:T(128)S(1)} %copy-done.29, bf16[1024,768]{1,0:T(8,128)(2,1)S(1)} %copy-done.13, bf16[256,512]{1,0:T(8,128)(2,1)} %collective-permute-done.14.refs_2_, bf16[256,512]{1,0:T(8,128)(2,1)} %collective-permute-done.15.refs_3_, ...), custom_call_target="tpu_custom_call" | custom-call | flops 805306368 | bytes 2883584 | tf_op jit(solution)/shard_map/panel_away/pallas_call | solution.py:24
  103.2 2.6 %collective-permute-start.26 = (bf16[1024,512]{1,0:T(8,128)(2,1)S(1)}, bf16[1024,512]{1,0:T(8,128)(2,1)S(1)}, u32[]{:S(2)}, u32[]{:S(2)}) collective-permute-start(bf16[1024,512]{1,0:T(8,128)(2,1)S(1)} %get-tuple-element.113), channel_id=1, source_target_pairs={{0,1},{1,0},{2,3},{3,2},{4,5},{5,4},{6,7},{7,6},{8,9},{9,8},{10,11... | collective-permute-start | bytes 3145736 | tf_op jit(solution)/shard_map/ppermute | solution.py:234
  106.4 2.2 %collective-permute-start.13 = (bf16[128,512]{1,0:T(8,128)(2,1)S(1)}, bf16[128,512]{1,0:T(8,128)(2,1)S(1)}, u32[]{:S(2)}, u32[]{:S(2)}) collective-permute-start(bf16[128,512]{1,0:T(8,128)(2,1)S(1)} %get-tuple-element.97), channel_id=1, source_target_pairs={{0,8},{1,9},{2,10},{3,11},{4,12},{5,13},{6,14},{7,15},{8,0},{9,1},... | collective-permute-start | bytes 393224 | tf_op jit(solution)/shard_map/ppermute | solution.py:234
  108.7 2.0 %collective-permute-start.22 = (bf16[256,256]{1,0:T(8,128)(2,1)S(1)}, bf16[256,256]{1,0:T(8,128)(2,1)S(1)}, u32[]{:S(2)}, u32[]{:S(2)}) collective-permute-start(bf16[256,256]{1,0:T(8,128)(2,1)S(1)} %get-tuple-element.101.refs_3_), channel_id=1, source_target_pairs={{14,0},{15,1},{0,2},{1,3},{2,4},{3,5},{4,6},{5,7},{6,8},{7,9},{8,1... | collective-permute-start | bytes 393224 | tf_op jit(solution)/shard_map/ppermute | solution.py:229
  110.6 2.7 %collective-permute-start.25 = (bf16[256,256]{1,0:T(8,128)(2,1)S(1)}, bf16[256,256]{1,0:T(8,128)(2,1)S(1)}, u32[]{:S(2)}, u32[]{:S(2)}) collective-permute-start(bf16[256,256]{1,0:T(8,128)(2,1)S(1)} %get-tuple-element.112), channel_id=1, source_target_pairs={{2,0},{3,1},{4,2},{5,3},{6,4},{7,5},{8,6},{9,7},{10,8},{11,9},{12,... | collective-permute-start | bytes 393224 | tf_op jit(solution)/shard_map/ppermute | solution.py:229
  113.4 8.1 %collective-permute-done.13.refs_1_ = bf16[128,512]{1,0:T(8,128)(2,1)S(1)} collective-permute-done((bf16[128,512]{1,0:T(8,128)(2,1)S(1)}, bf16[128,512]{1,0:T(8,128)(2,1)S(1)}, u32[]{:S(2)}, u32[]{:S(2)}) %collective-permute-start.13) | collective-permute-done | bytes 131104 | tf_op jit(solution)/shard_map/ppermute | solution.py:234
  121.5 2.3 %collective-permute-start.24 = (bf16[256,256]{1,0:T(8,128)(2,1)S(1)}, bf16[256,256]{1,0:T(8,128)(2,1)S(1)}, u32[]{:S(2)}, u32[]{:S(2)}) collective-permute-start(bf16[256,256]{1,0:T(8,128)(2,1)S(1)} %get-tuple-element.111), channel_id=1, source_target_pairs={{1,0},{2,1},{3,2},{4,3},{5,4},{6,5},{7,6},{8,7},{9,8},{10,9},{11,1... | collective-permute-start | bytes 393224 | tf_op jit(solution)/shard_map/ppermute | solution.py:229
  123.9 1.5 panel_own.7.refs_2_
  126.1 1.2 copy-done.2
  128.5 1.2 coupled_rows.19
  131.0 2.1 %panel_away.8 = (bf16[1024,256]{1,0:T(8,128)(2,1)S(1)}, bf16[768,256]{1,0:T(8,128)(2,1)S(1)}) custom-call(s32[12]{0:T(128)S(1)} %copy-done.29, bf16[1024,768]{1,0:T(8,128)(2,1)S(1)} %copy-done.13, bf16[256,256]{1,0:T(8,128)(2,1)S(1)} %collective-permute-done.22.refs_2_, bf16[256,256]{1,0:T(8,128)(2,1)S(1)} %collective-permute-done.23.refs_3_, ...), custom_call_target="tpu_custom_call" | custom-call | flops 402653184 | bytes 2228224 | tf_op jit(solution)/shard_map/panel_away/pallas_call | solution.py:24
  133.1 1.4 collective-permute-start.28
  135.2 4.0 %collective-permute-start.21 = (bf16[256,256]{1,0:T(8,128)(2,1)S(1)}, bf16[256,256]{1,0:T(8,128)(2,1)S(1)}, u32[]{:S(2)}, u32[]{:S(2)}) collective-permute-start(bf16[256,256]{1,0:T(8,128)(2,1)S(1)} %get-tuple-element.109), channel_id=1, source_target_pairs={{2,0},{3,1},{4,2},{5,3},{6,4},{7,5},{8,6},{9,7},{10,8},{11,9},{12,... | collective-permute-start | bytes 393224 | tf_op jit(solution)/shard_map/ppermute | solution.py:229
  139.3 6.2 %collective-permute-done.28 = bf16[256,512]{1,0:T(8,128)(2,1)S(1)} collective-permute-done((bf16[256,512]{1,0:T(8,128)(2,1)S(1)}, bf16[256,512]{1,0:T(8,128)(2,1)S(1)}, u32[]{:S(2)}, u32[]{:S(2)}) %collective-permute-start.28) | collective-permute-done | bytes 262176 | tf_op jit(solution)/shard_map/ppermute | solution.py:234
  145.4 1.1 panel_own.8.refs_3_
  146.6 2.3 %collective-permute-start.31 = (bf16[512,512]{1,0:T(8,128)(2,1)S(1)}, bf16[512,512]{1,0:T(8,128)(2,1)S(1)}, u32[]{:S(2)}, u32[]{:S(2)}) collective-permute-start(bf16[512,512]{1,0:T(8,128)(2,1)S(1)} %get-tuple-element.123), channel_id=1, source_target_pairs={{0,4},{1,5},{2,6},{3,7},{4,0},{5,1},{6,2},{7,3},{8,12},{9,13},{10,... | collective-permute-start | bytes 1572872 | tf_op jit(solution)/shard_map/ppermute | solution.py:234
  149.1 3.5 %collective-permute-done.19.refs_3_ = bf16[256,256]{1,0:T(8,128)(2,1)S(1)} collective-permute-done((bf16[256,256]{1,0:T(8,128)(2,1)S(1)}, bf16[256,256]{1,0:T(8,128)(2,1)S(1)}, u32[]{:S(2)}, u32[]{:S(2)}) %collective-permute-start.19) | collective-permute-done | bytes 131104 | tf_op jit(solution)/shard_map/ppermute | solution.py:229
  152.5 2.1 %panel_away.9 = (bf16[1024,256]{1,0:T(8,128)(2,1)S(1)}, bf16[768,256]{1,0:T(8,128)(2,1)S(1)}) custom-call(s32[12]{0:T(128)S(1)} %copy-done.29, bf16[1024,768]{1,0:T(8,128)(2,1)S(1)} %copy-done.13, bf16[256,256]{1,0:T(8,128)(2,1)S(1)} %collective-permute-done.18.refs_2_, bf16[256,256]{1,0:T(8,128)(2,1)S(1)} %collective-permute-done.19.refs_3_, ...), custom_call_target="tpu_custom_call" | custom-call | flops 402653184 | bytes 2228224 | tf_op jit(solution)/shard_map/panel_away/pallas_call | solution.py:24
  155.2 1.3 collective-permute-start.32
  156.5 1.1 panel_own.9.refs_3_
  157.6 10.3 %collective-permute-done.32.refs_1_ = bf16[128,512]{1,0:T(8,128)(2,1)S(1)} collective-permute-done((bf16[128,512]{1,0:T(8,128)(2,1)S(1)}, bf16[128,512]{1,0:T(8,128)(2,1)S(1)}, u32[]{:S(2)}, u32[]{:S(2)}) %collective-permute-start.32) | collective-permute-done | bytes 131104 | tf_op jit(solution)/shard_map/ppermute | solution.py:234
  168.7 1.2 copy-done.3
  170.1 2.8 %collective-permute-start.34 = (bf16[256,512]{1,0:T(8,128)(2,1)S(1)}, bf16[256,512]{1,0:T(8,128)(2,1)S(1)}, u32[]{:S(2)}, u32[]{:S(2)}) collective-permute-start(bf16[256,512]{1,0:T(8,128)(2,1)S(1)} %get-tuple-element.129), channel_id=1, source_target_pairs={{0,2},{1,3},{2,0},{3,1},{4,6},{5,7},{6,4},{7,5},{8,10},{9,11},{10,... | collective-permute-start | bytes 786440 | tf_op jit(solution)/shard_map/ppermute | solution.py:234
  173.1 3.4 %collective-permute-start.33 = (bf16[512,256]{1,0:T(8,128)(2,1)S(1)}, bf16[512,256]{1,0:T(8,128)(2,1)S(1)}, u32[]{:S(2)}, u32[]{:S(2)}) collective-permute-start(bf16[512,256]{1,0:T(8,128)(2,1)S(1)} %get-tuple-element.128), channel_id=1, source_target_pairs={{0,4},{1,5},{2,6},{3,7},{4,0},{5,1},{6,2},{7,3},{8,12},{9,13},{10,... | collective-permute-start | bytes 786440 | tf_op jit(solution)/shard_map/ppermute | solution.py:234
  176.6 6.2 %collective-permute-done.35 = bf16[256,256]{1,0:T(8,128)(2,1)S(1)} collective-permute-done((bf16[256,256]{1,0:T(8,128)(2,1)S(1)}, bf16[256,256]{1,0:T(8,128)(2,1)S(1)}, u32[]{:S(2)}, u32[]{:S(2)}) %collective-permute-start.35) | collective-permute-done | bytes 131104 | tf_op jit(solution)/shard_map/ppermute | solution.py:234
  183.5 3.1 %collective-permute-start.37 = (bf16[128,256]{1,0:T(8,128)(2,1)S(1)}, bf16[128,256]{1,0:T(8,128)(2,1)S(1)}, u32[]{:S(2)}, u32[]{:S(2)}) collective-permute-start(bf16[128,256]{1,0:T(8,128)(2,1)S(1)} %get-tuple-element.135), channel_id=1, source_target_pairs={{0,8},{1,9},{2,10},{3,11},{4,12},{5,13},{6,14},{7,15},{8,0},{9,1},... | collective-permute-start | bytes 196616 | tf_op jit(solution)/shard_map/ppermute | solution.py:234
  186.6 2.5 %collective-permute-done.37.refs_1_ = bf16[128,256]{1,0:T(8,128)(2,1)S(1)} collective-permute-done((bf16[128,256]{1,0:T(8,128)(2,1)S(1)}, bf16[128,256]{1,0:T(8,128)(2,1)S(1)}, u32[]{:S(2)}, u32[]{:S(2)}) %collective-permute-start.37) | collective-permute-done | bytes 65568 | tf_op jit(solution)/shard_map/ppermute | solution.py:234
  189.8 1.2 copy-done.4
  191.1 3.5 %collective-permute-start.38 = (bf16[128,256]{1,0:T(8,128)(2,1)S(1)}, bf16[128,256]{1,0:T(8,128)(2,1)S(1)}, u32[]{:S(2)}, u32[]{:S(2)}) collective-permute-start(bf16[128,256]{1,0:T(8,128)(2,1)S(1)} %get-tuple-element.137), channel_id=1, source_target_pairs={{0,8},{1,9},{2,10},{3,11},{4,12},{5,13},{6,14},{7,15},{8,0},{9,1},... | collective-permute-start | bytes 196616 | tf_op jit(solution)/shard_map/ppermute | solution.py:234
  194.6 2.1 %collective-permute-done.39.refs_1_ = bf16[128,512]{1,0:T(8,128)(2,1)S(1)} collective-permute-done((bf16[128,512]{1,0:T(8,128)(2,1)S(1)}, bf16[128,512]{1,0:T(8,128)(2,1)S(1)}, u32[]{:S(2)}, u32[]{:S(2)}) %collective-permute-start.39) | collective-permute-done | bytes 131104 | tf_op jit(solution)/shard_map/ppermute | solution.py:234
  (118 shorter events, 20.4 us)
Async XLA Ops:
  0.8 1.6 copy-start
  2.4 1.1 copy-start.5
  5.4 21.2 %collective-permute-start.7 = (bf16[256,512]{1,0:T(8,128)(2,1)}, bf16[256,512]{1,0:T(8,128)(2,1)S(1)}, u32[]{:S(2)}, u32[]{:S(2)}) collective-permute-start(bf16[256,512]{1,0:T(8,128)(2,1)} %get-tuple-element.83), channel_id=1, source_target_pairs={{2,0},{3,1},{4,2},{5,3},{6,4},{7,5},{8,6},{9,7},{10,8},{11,9},{12,... | collective-permute-start | bytes 786440 | tf_op jit(solution)/shard_map/ppermute | solution.py:229
  11.4 15.2 %collective-permute-start.4 = (bf16[256,512]{1,0:T(8,128)(2,1)S(1)}, bf16[256,512]{1,0:T(8,128)(2,1)}, u32[]{:S(2)}, u32[]{:S(2)}) collective-permute-start(bf16[256,512]{1,0:T(8,128)(2,1)S(1)} %get-tuple-element.72.refs_3_), channel_id=1, source_target_pairs={{14,0},{15,1},{0,2},{1,3},{2,4},{3,5},{4,6},{5,7},{6,8},{7,9},{8,1... | collective-permute-start | bytes 786440 | tf_op jit(solution)/shard_map/ppermute | solution.py:229
  14.1 12.5 %collective-permute-start.6 = (bf16[256,512]{1,0:T(8,128)(2,1)}, bf16[256,512]{1,0:T(8,128)(2,1)}, u32[]{:S(2)}, u32[]{:S(2)}) collective-permute-start(bf16[256,512]{1,0:T(8,128)(2,1)} %get-tuple-element.82), channel_id=1, source_target_pairs={{1,0},{2,1},{3,2},{4,3},{5,4},{6,5},{7,6},{8,7},{9,8},{10,9},{11,1... | collective-permute-start | bytes 786440 | tf_op jit(solution)/shard_map/ppermute | solution.py:229
  17.7 8.9 %collective-permute-start.5 = (bf16[256,512]{1,0:T(8,128)(2,1)}, bf16[256,512]{1,0:T(8,128)(2,1)}, u32[]{:S(2)}, u32[]{:S(2)}) collective-permute-start(bf16[256,512]{1,0:T(8,128)(2,1)} %get-tuple-element.73.refs_3_), channel_id=1, source_target_pairs={{15,0},{0,1},{1,2},{2,3},{3,4},{4,5},{5,6},{6,7},{7,8},{8,9},{9,10... | collective-permute-start | bytes 786440 | tf_op jit(solution)/shard_map/ppermute | solution.py:229
  17.7 1.9 copy-start.16
  19.6 2.3 %copy-start.1 = (bf16[512,2048]{1,0:T(8,128)(2,1)S(1)}, bf16[512,2048]{1,0:T(8,128)(2,1)}, u32[]{:S(2)}) copy-start(bf16[512,2048]{1,0:T(8,128)(2,1)} %refs_1_.21) | copy-start | bytes 6291460
  19.6 2.3 %copy-start.6 = (bf16[20,64,256]{2,1,0:T(8,128)(2,1)S(1)}, bf16[20,64,256]{2,1,0:T(8,128)(2,1)}, u32[]{:S(2)}) copy-start(bf16[20,64,256]{2,1,0:T(8,128)(2,1)} %refs_2_.21) | copy-start | bytes 1966084
  21.9 2.0 %copy-start.7 = (bf16[1024,768]{1,0:T(8,128)(2,1)}, bf16[1024,768]{1,0:T(8,128)(2,1)S(1)}, u32[]{:S(2)}) copy-start(bf16[1024,768]{1,0:T(8,128)(2,1)S(1)} %get-tuple-element.74.refs_3_.refs_0_) | copy-start | bytes 4718596
  21.9 4.7 %copy-start.11 = (bf16[1024,768]{1,0:T(8,128)(2,1)}, bf16[1024,768]{1,0:T(8,128)(2,1)S(1)}, u32[]{:S(2)}) copy-start(bf16[1024,768]{1,0:T(8,128)(2,1)S(1)} %get-tuple-element.75.refs_1_) | copy-start | bytes 4718596
  23.9 2.8 %copy-start.28 = (bf16[256,512]{1,0:T(8,128)(2,1)S(1)}, bf16[256,512]{1,0:T(8,128)(2,1)}, u32[]{:S(2)}) copy-start(bf16[256,512]{1,0:T(8,128)(2,1)} %copy-done.27) | copy-start | bytes 786436
  23.9 2.8 %copy-start.29 = (s32[12]{0:T(128)S(1)}, s32[12]{0:T(128)}, u32[]{:S(2)}) copy-start(s32[12]{0:T(128)} %refs_0_.19) | copy-start | bytes 148
  32.2 10.0 %collective-permute-start.8 = (bf16[1024,512]{1,0:T(8,128)(2,1)}, bf16[1024,512]{1,0:T(8,128)(2,1)}, u32[]{:S(2)}, u32[]{:S(2)}) collective-permute-start(bf16[1024,512]{1,0:T(8,128)(2,1)} %get-tuple-element.85), channel_id=1, source_target_pairs={{0,1},{1,0},{2,3},{3,2},{4,5},{5,4},{6,7},{7,6},{8,9},{9,8},{10,11... | collective-permute-start | bytes 3145736 | tf_op jit(solution)/shard_map/ppermute | solution.py:234
  32.9 18.6 %collective-permute-start = (bf16[256,512]{1,0:T(8,128)(2,1)S(1)}, bf16[256,512]{1,0:T(8,128)(2,1)}, u32[]{:S(2)}, u32[]{:S(2)}) collective-permute-start(bf16[256,512]{1,0:T(8,128)(2,1)S(1)} %get-tuple-element.76.refs_3_), channel_id=1, source_target_pairs={{14,0},{15,1},{0,2},{1,3},{2,4},{3,5},{4,6},{5,7},{6,8},{7,9},{8,1... | collective-permute-start | bytes 786440 | tf_op jit(solution)/shard_map/ppermute | solution.py:229
  34.4 17.2 %collective-permute-start.3 = (bf16[256,512]{1,0:T(8,128)(2,1)}, bf16[256,512]{1,0:T(8,128)(2,1)}, u32[]{:S(2)}, u32[]{:S(2)}) collective-permute-start(bf16[256,512]{1,0:T(8,128)(2,1)} %get-tuple-element.80), channel_id=1, source_target_pairs={{2,0},{3,1},{4,2},{5,3},{6,4},{7,5},{8,6},{9,7},{10,8},{11,9},{12,... | collective-permute-start | bytes 786440 | tf_op jit(solution)/shard_map/ppermute | solution.py:229
  37.6 13.9 %collective-permute-start.2 = (bf16[256,512]{1,0:T(8,128)(2,1)}, bf16[256,512]{1,0:T(8,128)(2,1)}, u32[]{:S(2)}, u32[]{:S(2)}) collective-permute-start(bf16[256,512]{1,0:T(8,128)(2,1)} %get-tuple-element.79), channel_id=1, source_target_pairs={{1,0},{2,1},{3,2},{4,3},{5,4},{6,5},{7,6},{8,7},{9,8},{10,9},{11,1... | collective-permute-start | bytes 786440 | tf_op jit(solution)/shard_map/ppermute | solution.py:229
  38.1 13.4 %collective-permute-start.1 = (bf16[256,512]{1,0:T(8,128)(2,1)}, bf16[256,512]{1,0:T(8,128)(2,1)}, u32[]{:S(2)}, u32[]{:S(2)}) collective-permute-start(bf16[256,512]{1,0:T(8,128)(2,1)} %get-tuple-element.77.refs_7_), channel_id=1, source_target_pairs={{15,0},{0,1},{1,2},{2,3},{3,4},{4,5},{5,6},{6,7},{7,8},{8,9},{9,10... | collective-permute-start | bytes 786440 | tf_op jit(solution)/shard_map/ppermute | solution.py:229
  38.2 1.4 copy-start.8
  39.6 1.1 copy-start.20
  44.3 4.0 %copy-start.17 = (f32[512,512]{1,0:T(8,128)}, f32[512,512]{1,0:T(8,128)S(1)}, u32[]{:S(2)}) copy-start(f32[512,512]{1,0:T(8,128)S(1)} %get-tuple-element.86.refs_3_) | copy-start | bytes 3145732
  46.2 5.3 %copy-start.12 = (bf16[1024,768]{1,0:T(8,128)(2,1)S(1)}, bf16[1024,768]{1,0:T(8,128)(2,1)}, u32[]{:S(2)}) copy-start(bf16[1024,768]{1,0:T(8,128)(2,1)} %copy-done.11) | copy-start | bytes 4718596
  46.2 5.3 %copy-start.26 = (bf16[256,512]{1,0:T(8,128)(2,1)S(1)}, bf16[256,512]{1,0:T(8,128)(2,1)}, u32[]{:S(2)}) copy-start(bf16[256,512]{1,0:T(8,128)(2,1)} %copy-done.25) | copy-start | bytes 786436
  57.2 26.0 %collective-permute-start.9 = (bf16[1024,512]{1,0:T(8,128)(2,1)}, bf16[1024,512]{1,0:T(8,128)(2,1)}, u32[]{:S(2)}, u32[]{:S(2)}) collective-permute-start(bf16[1024,512]{1,0:T(8,128)(2,1)} %get-tuple-element.90), channel_id=1, source_target_pairs={{0,1},{1,0},{2,3},{3,2},{4,5},{5,4},{6,7},{7,6},{8,9},{9,8},{10,11... | collective-permute-start | bytes 3145736 | tf_op jit(solution)/shard_map/ppermute | solution.py:234
  59.8 14.0 %collective-permute-start.10 = (bf16[512,512]{1,0:T(8,128)(2,1)}, bf16[512,512]{1,0:T(8,128)(2,1)S(1)}, u32[]{:S(2)}, u32[]{:S(2)}) collective-permute-start(bf16[512,512]{1,0:T(8,128)(2,1)} %get-tuple-element.91), channel_id=1, source_target_pairs={{0,4},{1,5},{2,6},{3,7},{4,0},{5,1},{6,2},{7,3},{8,12},{9,13},{10,... | collective-permute-start | bytes 1572872 | tf_op jit(solution)/shard_map/ppermute | solution.py:234
  59.8 1.4 copy-start.9
  61.2 1.1 copy-start.22
  62.3 12.3 %copy-start.18 = (f32[512,512]{1,0:T(8,128)S(1)}, f32[512,512]{1,0:T(8,128)}, u32[]{:S(2)}) copy-start(f32[512,512]{1,0:T(8,128)} %copy-done.17) | copy-start | bytes 3145732
  76.4 1.3 copy-start.14
  77.7 18.0 %collective-permute-start.12 = (bf16[256,512]{1,0:T(8,128)(2,1)}, bf16[256,512]{1,0:T(8,128)(2,1)}, u32[]{:S(2)}, u32[]{:S(2)}) collective-permute-start(bf16[256,512]{1,0:T(8,128)(2,1)} %get-tuple-element.95), channel_id=1, source_target_pairs={{0,2},{1,3},{2,0},{3,1},{4,6},{5,7},{6,4},{7,5},{8,10},{9,11},{10,... | collective-permute-start | bytes 786440 | tf_op jit(solution)/shard_map/ppermute | solution.py:234
  78.5 21.1 %collective-permute-start.14 = (bf16[256,512]{1,0:T(8,128)(2,1)}, bf16[256,512]{1,0:T(8,128)(2,1)}, u32[]{:S(2)}, u32[]{:S(2)}) collective-permute-start(bf16[256,512]{1,0:T(8,128)(2,1)} %get-tuple-element.87.refs_3_), channel_id=1, source_target_pairs={{14,0},{15,1},{0,2},{1,3},{2,4},{3,5},{4,6},{5,7},{6,8},{7,9},{8,1... | collective-permute-start | bytes 786440 | tf_op jit(solution)/shard_map/ppermute | solution.py:229
  79.7 19.7 %collective-permute-start.17 = (bf16[256,512]{1,0:T(8,128)(2,1)}, bf16[256,512]{1,0:T(8,128)(2,1)}, u32[]{:S(2)}, u32[]{:S(2)}) collective-permute-start(bf16[256,512]{1,0:T(8,128)(2,1)} %get-tuple-element.100), channel_id=1, source_target_pairs={{2,0},{3,1},{4,2},{5,3},{6,4},{7,5},{8,6},{9,7},{10,8},{11,9},{12,... | collective-permute-start | bytes 786440 | tf_op jit(solution)/shard_map/ppermute | solution.py:229
  83.2 16.4 %collective-permute-start.16 = (bf16[256,512]{1,0:T(8,128)(2,1)}, bf16[256,512]{1,0:T(8,128)(2,1)}, u32[]{:S(2)}, u32[]{:S(2)}) collective-permute-start(bf16[256,512]{1,0:T(8,128)(2,1)} %get-tuple-element.99), channel_id=1, source_target_pairs={{1,0},{2,1},{3,2},{4,3},{5,4},{6,5},{7,6},{8,7},{9,8},{10,9},{11,1... | collective-permute-start | bytes 786440 | tf_op jit(solution)/shard_map/ppermute | solution.py:229
  83.2 16.4 %collective-permute-start.15 = (bf16[256,512]{1,0:T(8,128)(2,1)}, bf16[256,512]{1,0:T(8,128)(2,1)}, u32[]{:S(2)}, u32[]{:S(2)}) collective-permute-start(bf16[256,512]{1,0:T(8,128)(2,1)} %get-tuple-element.88.refs_7_), channel_id=1, source_target_pairs={{15,0},{0,1},{1,2},{2,3},{3,4},{4,5},{5,6},{6,7},{7,8},{8,9},{9,10... | collective-permute-start | bytes 786440 | tf_op jit(solution)/shard_map/ppermute | solution.py:229
  83.7 1.6 copy-start.15
  97.8 1.8 copy-start.13
  99.0 24.9 %copy-start.10 = (bf16[1024,768]{1,0:T(8,128)(2,1)S(1)}, bf16[1024,768]{1,0:T(8,128)(2,1)}, u32[]{:S(2)}) copy-start(bf16[1024,768]{1,0:T(8,128)(2,1)} %copy-done.7) | copy-start | bytes 4718596
  103.2 26.5 %collective-permute-start.26 = (bf16[1024,512]{1,0:T(8,128)(2,1)S(1)}, bf16[1024,512]{1,0:T(8,128)(2,1)S(1)}, u32[]{:S(2)}, u32[]{:S(2)}) collective-permute-start(bf16[1024,512]{1,0:T(8,128)(2,1)S(1)} %get-tuple-element.113), channel_id=1, source_target_pairs={{0,1},{1,0},{2,3},{3,2},{4,5},{5,4},{6,7},{7,6},{8,9},{9,8},{10,11... | collective-permute-start | bytes 3145736 | tf_op jit(solution)/shard_map/ppermute | solution.py:234
  105.8 18.0 %collective-permute-start.11 = (bf16[512,512]{1,0:T(8,128)(2,1)S(1)}, bf16[512,512]{1,0:T(8,128)(2,1)S(1)}, u32[]{:S(2)}, u32[]{:S(2)}) collective-permute-start(bf16[512,512]{1,0:T(8,128)(2,1)S(1)} %get-tuple-element.94), channel_id=1, source_target_pairs={{0,4},{1,5},{2,6},{3,7},{4,0},{5,1},{6,2},{7,3},{8,12},{9,13},{10,... | collective-permute-start | bytes 1572872 | tf_op jit(solution)/shard_map/ppermute | solution.py:234
  106.4 15.1 %collective-permute-start.13 = (bf16[128,512]{1,0:T(8,128)(2,1)S(1)}, bf16[128,512]{1,0:T(8,128)(2,1)S(1)}, u32[]{:S(2)}, u32[]{:S(2)}) collective-permute-start(bf16[128,512]{1,0:T(8,128)(2,1)S(1)} %get-tuple-element.97), channel_id=1, source_target_pairs={{0,8},{1,9},{2,10},{3,11},{4,12},{5,13},{6,14},{7,15},{8,0},{9,1},... | collective-permute-start | bytes 393224 | tf_op jit(solution)/shard_map/ppermute | solution.py:234
  108.7 21.3 %collective-permute-start.22 = (bf16[256,256]{1,0:T(8,128)(2,1)S(1)}, bf16[256,256]{1,0:T(8,128)(2,1)S(1)}, u32[]{:S(2)}, u32[]{:S(2)}) collective-permute-start(bf16[256,256]{1,0:T(8,128)(2,1)S(1)} %get-tuple-element.101.refs_3_), channel_id=1, source_target_pairs={{14,0},{15,1},{0,2},{1,3},{2,4},{3,5},{4,6},{5,7},{6,8},{7,9},{8,1... | collective-permute-start | bytes 393224 | tf_op jit(solution)/shard_map/ppermute | solution.py:229
  110.6 19.3 %collective-permute-start.25 = (bf16[256,256]{1,0:T(8,128)(2,1)S(1)}, bf16[256,256]{1,0:T(8,128)(2,1)S(1)}, u32[]{:S(2)}, u32[]{:S(2)}) collective-permute-start(bf16[256,256]{1,0:T(8,128)(2,1)S(1)} %get-tuple-element.112), channel_id=1, source_target_pairs={{2,0},{3,1},{4,2},{5,3},{6,4},{7,5},{8,6},{9,7},{10,8},{11,9},{12,... | collective-permute-start | bytes 393224 | tf_op jit(solution)/shard_map/ppermute | solution.py:229
  121.5 8.5 %collective-permute-start.24 = (bf16[256,256]{1,0:T(8,128)(2,1)S(1)}, bf16[256,256]{1,0:T(8,128)(2,1)S(1)}, u32[]{:S(2)}, u32[]{:S(2)}) collective-permute-start(bf16[256,256]{1,0:T(8,128)(2,1)S(1)} %get-tuple-element.111), channel_id=1, source_target_pairs={{1,0},{2,1},{3,2},{4,3},{5,4},{6,5},{7,6},{8,7},{9,8},{10,9},{11,1... | collective-permute-start | bytes 393224 | tf_op jit(solution)/shard_map/ppermute | solution.py:229
  123.9 7.1 %collective-permute-start.23 = (bf16[256,256]{1,0:T(8,128)(2,1)S(1)}, bf16[256,256]{1,0:T(8,128)(2,1)S(1)}, u32[]{:S(2)}, u32[]{:S(2)}) collective-permute-start(bf16[256,256]{1,0:T(8,128)(2,1)S(1)} %get-tuple-element.102.refs_7_), channel_id=1, source_target_pairs={{15,0},{0,1},{1,2},{2,3},{3,4},{4,5},{5,6},{6,7},{7,8},{8,9},{9,10... | collective-permute-start | bytes 393224 | tf_op jit(solution)/shard_map/ppermute | solution.py:229
  126.1 1.2 copy-start.2
  133.0 13.6 %collective-permute-start.27 = (bf16[1024,256]{1,0:T(8,128)(2,1)S(1)}, bf16[1024,256]{1,0:T(8,128)(2,1)S(1)}, u32[]{:S(2)}, u32[]{:S(2)}) collective-permute-start(bf16[1024,256]{1,0:T(8,128)(2,1)S(1)} %get-tuple-element.116), channel_id=1, source_target_pairs={{0,1},{1,0},{2,3},{3,2},{4,5},{5,4},{6,7},{7,6},{8,9},{9,8},{10,11... | collective-permute-start | bytes 1572872 | tf_op jit(solution)/shard_map/ppermute | solution.py:234
  133.1 12.3 %collective-permute-start.28 = (bf16[256,512]{1,0:T(8,128)(2,1)S(1)}, bf16[256,512]{1,0:T(8,128)(2,1)S(1)}, u32[]{:S(2)}, u32[]{:S(2)}) collective-permute-start(bf16[256,512]{1,0:T(8,128)(2,1)S(1)} %get-tuple-element.117), channel_id=1, source_target_pairs={{0,2},{1,3},{2,0},{3,1},{4,6},{5,7},{6,4},{7,5},{8,10},{9,11},{10,... | collective-permute-start | bytes 786440 | tf_op jit(solution)/shard_map/ppermute | solution.py:234
  134.5 14.5 %collective-permute-start.18 = (bf16[256,256]{1,0:T(8,128)(2,1)S(1)}, bf16[256,256]{1,0:T(8,128)(2,1)S(1)}, u32[]{:S(2)}, u32[]{:S(2)}) collective-permute-start(bf16[256,256]{1,0:T(8,128)(2,1)S(1)} %get-tuple-element.105.refs_3_), channel_id=1, source_target_pairs={{14,0},{15,1},{0,2},{1,3},{2,4},{3,5},{4,6},{5,7},{6,8},{7,9},{8,1... | collective-permute-start | bytes 393224 | tf_op jit(solution)/shard_map/ppermute | solution.py:229
  135.2 13.8 %collective-permute-start.21 = (bf16[256,256]{1,0:T(8,128)(2,1)S(1)}, bf16[256,256]{1,0:T(8,128)(2,1)S(1)}, u32[]{:S(2)}, u32[]{:S(2)}) collective-permute-start(bf16[256,256]{1,0:T(8,128)(2,1)S(1)} %get-tuple-element.109), channel_id=1, source_target_pairs={{2,0},{3,1},{4,2},{5,3},{6,4},{7,5},{8,6},{9,7},{10,8},{11,9},{12,... | collective-permute-start | bytes 393224 | tf_op jit(solution)/shard_map/ppermute | solution.py:229
  139.3 9.8 %collective-permute-start.20 = (bf16[256,256]{1,0:T(8,128)(2,1)S(1)}, bf16[256,256]{1,0:T(8,128)(2,1)S(1)}, u32[]{:S(2)}, u32[]{:S(2)}) collective-permute-start(bf16[256,256]{1,0:T(8,128)(2,1)S(1)} %get-tuple-element.108), channel_id=1, source_target_pairs={{1,0},{2,1},{3,2},{4,3},{5,4},{6,5},{7,6},{8,7},{9,8},{10,9},{11,1... | collective-permute-start | bytes 393224 | tf_op jit(solution)/shard_map/ppermute | solution.py:229
  145.4 7.1 %collective-permute-start.19 = (bf16[256,256]{1,0:T(8,128)(2,1)S(1)}, bf16[256,256]{1,0:T(8,128)(2,1)S(1)}, u32[]{:S(2)}, u32[]{:S(2)}) collective-permute-start(bf16[256,256]{1,0:T(8,128)(2,1)S(1)} %get-tuple-element.106.refs_3_), channel_id=1, source_target_pairs={{15,0},{0,1},{1,2},{2,3},{3,4},{4,5},{5,6},{6,7},{7,8},{8,9},{9,10... | collective-permute-start | bytes 393224 | tf_op jit(solution)/shard_map/ppermute | solution.py:229
  146.6 22.1 %collective-permute-start.31 = (bf16[512,512]{1,0:T(8,128)(2,1)S(1)}, bf16[512,512]{1,0:T(8,128)(2,1)S(1)}, u32[]{:S(2)}, u32[]{:S(2)}) collective-permute-start(bf16[512,512]{1,0:T(8,128)(2,1)S(1)} %get-tuple-element.123), channel_id=1, source_target_pairs={{0,4},{1,5},{2,6},{3,7},{4,0},{5,1},{6,2},{7,3},{8,12},{9,13},{10,... | collective-permute-start | bytes 1572872 | tf_op jit(solution)/shard_map/ppermute | solution.py:234
  154.6 18.3 %collective-permute-start.29 = (bf16[1024,256]{1,0:T(8,128)(2,1)S(1)}, bf16[1024,256]{1,0:T(8,128)(2,1)S(1)}, u32[]{:S(2)}, u32[]{:S(2)}) collective-permute-start(bf16[1024,256]{1,0:T(8,128)(2,1)S(1)} %get-tuple-element.121), channel_id=1, source_target_pairs={{0,1},{1,0},{2,3},{3,2},{4,5},{5,4},{6,7},{7,6},{8,9},{9,8},{10,11... | collective-permute-start | bytes 1572872 | tf_op jit(solution)/shard_map/ppermute | solution.py:234
  154.7 18.1 %collective-permute-start.30 = (bf16[512,256]{1,0:T(8,128)(2,1)S(1)}, bf16[512,256]{1,0:T(8,128)(2,1)S(1)}, u32[]{:S(2)}, u32[]{:S(2)}) collective-permute-start(bf16[512,256]{1,0:T(8,128)(2,1)S(1)} %get-tuple-element.122), channel_id=1, source_target_pairs={{0,4},{1,5},{2,6},{3,7},{4,0},{5,1},{6,2},{7,3},{8,12},{9,13},{10,... | collective-permute-start | bytes 786440 | tf_op jit(solution)/shard_map/ppermute | solution.py:234
  155.2 12.8 %collective-permute-start.32 = (bf16[128,512]{1,0:T(8,128)(2,1)S(1)}, bf16[128,512]{1,0:T(8,128)(2,1)S(1)}, u32[]{:S(2)}, u32[]{:S(2)}) collective-permute-start(bf16[128,512]{1,0:T(8,128)(2,1)S(1)} %get-tuple-element.124), channel_id=1, source_target_pairs={{0,8},{1,9},{2,10},{3,11},{4,12},{5,13},{6,14},{7,15},{8,0},{9,1},... | collective-permute-start | bytes 393224 | tf_op jit(solution)/shard_map/ppermute | solution.py:234
  168.7 1.2 copy-start.3
  170.1 12.8 %collective-permute-start.34 = (bf16[256,512]{1,0:T(8,128)(2,1)S(1)}, bf16[256,512]{1,0:T(8,128)(2,1)S(1)}, u32[]{:S(2)}, u32[]{:S(2)}) collective-permute-start(bf16[256,512]{1,0:T(8,128)(2,1)S(1)} %get-tuple-element.129), channel_id=1, source_target_pairs={{0,2},{1,3},{2,0},{3,1},{4,6},{5,7},{6,4},{7,5},{8,10},{9,11},{10,... | collective-permute-start | bytes 786440 | tf_op jit(solution)/shard_map/ppermute | solution.py:234
  173.1 9.8 %collective-permute-start.33 = (bf16[512,256]{1,0:T(8,128)(2,1)S(1)}, bf16[512,256]{1,0:T(8,128)(2,1)S(1)}, u32[]{:S(2)}, u32[]{:S(2)}) collective-permute-start(bf16[512,256]{1,0:T(8,128)(2,1)S(1)} %get-tuple-element.128), channel_id=1, source_target_pairs={{0,4},{1,5},{2,6},{3,7},{4,0},{5,1},{6,2},{7,3},{8,12},{9,13},{10,... | collective-permute-start | bytes 786440 | tf_op jit(solution)/shard_map/ppermute | solution.py:234
  176.5 6.3 %collective-permute-start.35 = (bf16[256,256]{1,0:T(8,128)(2,1)S(1)}, bf16[256,256]{1,0:T(8,128)(2,1)S(1)}, u32[]{:S(2)}, u32[]{:S(2)}) collective-permute-start(bf16[256,256]{1,0:T(8,128)(2,1)S(1)} %get-tuple-element.130), channel_id=1, source_target_pairs={{0,2},{1,3},{2,0},{3,1},{4,6},{5,7},{6,4},{7,5},{8,10},{9,11},{10,... | collective-permute-start | bytes 393224 | tf_op jit(solution)/shard_map/ppermute | solution.py:234
  183.0 6.8 %collective-permute-start.36 = (bf16[256,256]{1,0:T(8,128)(2,1)S(1)}, bf16[256,256]{1,0:T(8,128)(2,1)S(1)}, u32[]{:S(2)}, u32[]{:S(2)}) collective-permute-start(bf16[256,256]{1,0:T(8,128)(2,1)S(1)} %get-tuple-element.134), channel_id=1, source_target_pairs={{0,2},{1,3},{2,0},{3,1},{4,6},{5,7},{6,4},{7,5},{8,10},{9,11},{10,... | collective-permute-start | bytes 393224 | tf_op jit(solution)/shard_map/ppermute | solution.py:234
  183.5 5.6 %collective-permute-start.37 = (bf16[128,256]{1,0:T(8,128)(2,1)S(1)}, bf16[128,256]{1,0:T(8,128)(2,1)S(1)}, u32[]{:S(2)}, u32[]{:S(2)}) collective-permute-start(bf16[128,256]{1,0:T(8,128)(2,1)S(1)} %get-tuple-element.135), channel_id=1, source_target_pairs={{0,8},{1,9},{2,10},{3,11},{4,12},{5,13},{6,14},{7,15},{8,0},{9,1},... | collective-permute-start | bytes 196616 | tf_op jit(solution)/shard_map/ppermute | solution.py:234
  186.6 10.1 %collective-permute-start.39 = (bf16[128,512]{1,0:T(8,128)(2,1)S(1)}, bf16[128,512]{1,0:T(8,128)(2,1)S(1)}, u32[]{:S(2)}, u32[]{:S(2)}) collective-permute-start(bf16[128,512]{1,0:T(8,128)(2,1)S(1)} %get-tuple-element.138), channel_id=1, source_target_pairs={{0,8},{1,9},{2,10},{3,11},{4,12},{5,13},{6,14},{7,15},{8,0},{9,1},... | collective-permute-start | bytes 393224 | tf_op jit(solution)/shard_map/ppermute | solution.py:234
  189.8 1.2 copy-start.4
  191.1 6.9 %collective-permute-start.38 = (bf16[128,256]{1,0:T(8,128)(2,1)S(1)}, bf16[128,256]{1,0:T(8,128)(2,1)S(1)}, u32[]{:S(2)}, u32[]{:S(2)}) collective-permute-start(bf16[128,256]{1,0:T(8,128)(2,1)S(1)} %get-tuple-element.137), channel_id=1, source_target_pairs={{0,8},{1,9},{2,10},{3,11},{4,12},{5,13},{6,14},{7,15},{8,0},{9,1},... | collective-permute-start | bytes 196616 | tf_op jit(solution)/shard_map/ppermute | solution.py:234
  (6 other events, 5.1 us)

commit v3 on v0

v3 whole, which is shorter than its diff:
```python
import jax
import jax.numpy as jnp
from jax import lax
from jax.experimental import pallas as pl
from jax.experimental.pallas import tpu as pltpu
from jax.sharding import PartitionSpec as P

CLASSES = 5
EIGHTHS = (2, 2, 2, 1, 1)
LIMIT = 20 * 2**20
ANY = pl.BlockSpec(memory_space=pl.ANY)
BF16, F32 = jnp.bfloat16, jnp.float32
NEXT = ((0, 0), (1, 0), (1, 1))
BEFORE = ((0, 3), (0, 4), (1, 4))
HERE = ((0, 1), (0, 2), (1, 2), (1, 3))
FOUND = ((0, 2, 7, 9, 4), (1, 6, 8, 3, 5))


def call(body, scalars, arrays, specs, after, out_shape, out_specs, grid, scratch, alias=None):
    lead = len(scalars) + len(arrays)
    extra = len(after)
    outs = len(out_shape)

    def kernel(*refs):
        rest = refs[lead + extra :]
        body(*refs[:lead], *rest[:outs], *rest[outs + 1 :])

    return pl.pallas_call(
        kernel,
        out_shape=[*out_shape, jax.ShapeDtypeStruct((8, 128), F32)],
        grid_spec=pltpu.PrefetchScalarGridSpec(
            num_scalar_prefetch=len(scalars),
            grid=grid,
            in_specs=specs + [ANY] * extra,
            out_specs=[*out_specs, ANY],
            scratch_shapes=scratch,
        ),
        input_output_aliases={} if alias is None else {lead - 1: alias},
        compiler_params=pltpu.CompilerParams(vmem_limit_bytes=LIMIT),
        cost_estimate=pl.CostEstimate(flops=0, bytes_accessed=0, transcendentals=0),
        name=body.__name__,
    )(*scalars, *arrays, *after)


def halved(core, acoustic, after):
    rows, modes = acoustic.shape
    tile = modes // 4

    def other_half(core_ref, in_ref, out_ref):
        out_ref[...] = in_ref[...]

    return call(
        other_half,
        [core],
        [acoustic],
        [pl.BlockSpec((rows, tile), lambda i, c: (0, 2 * (1 - c[0]) + i))],
        after,
        [jax.ShapeDtypeStruct((rows, modes // 2), BF16)],
        [pl.BlockSpec((rows, tile), lambda i, c: (0, i))],
        (2,),
        [],
    )


def coupled(core, blocks, acoustic, coupling, at, width, after):
    slots, rows, depth = coupling[0].shape
    per = slots // CLASSES
    nodes, modes = acoustic[0].shape
    steps = modes // 2 // width
    lists = (NEXT, BEFORE, HERE)

    def coupled_rows(core_ref, own_blocks, far_blocks, own_a, far_a, own_c, far_c, *refs):
        outs, both, picked = refs[:3], refs[3], refs[4]
        core = core_ref[0]
        both[pl.ds(pl.multiple_of(core * nodes, nodes), nodes), :] = own_a[...]
        both[pl.ds(pl.multiple_of((1 - core) * nodes, nodes), nodes), :] = far_a[...]
        for out, pairs in zip(outs, lists):
            for place, (face, k) in enumerate(pairs):
                own = core == face
                for s in range(per):
                    slot = k * per + s
                    for n in range(depth // rows):
                        block = jnp.where(own, own_blocks[slot, n], far_blocks[slot, n])
                        first = pl.multiple_of(face * nodes + block * rows, rows)
                        picked[n * rows : (n + 1) * rows, :] = both[pl.ds(first, rows), :]
                    weights = jnp.where(own, own_c[slot], far_c[slot])
                    row = (place * per + s) * rows
                    out[row : row + rows, :] = jnp.dot(
                        weights, picked[...], preferred_element_type=F32
                    ).astype(BF16)

    shapes = [(len(pairs) * per * rows, width) for pairs in lists]
    return call(
        coupled_rows,
        [core, *blocks],
        [*acoustic, *coupling],
        [
            pl.BlockSpec((nodes, width), lambda i, c, *_: (0, c[0] * steps + at // width)),
            pl.BlockSpec((nodes, width), lambda i, *_: (0, at // width)),
        ]
        + [pl.BlockSpec(coupling[0].shape, lambda i, *_: (0, 0, 0))] * 2,
        after,
        [jax.ShapeDtypeStruct(shape, BF16) for shape in shapes],
        [pl.BlockSpec(shape, lambda i, *_: (0, 0)) for shape in shapes],
        (1,),
        [pltpu.VMEM((2 * nodes, width), BF16), pltpu.VMEM((depth, width), BF16)],
    )


def turned(side, bit, struct_modes, share, after):
    depth, modes = struct_modes.shape
    half = modes // 2
    low = 2**bit

    def turn(side_ref, kept_ref, sent_ref, kept_out, sent_out):
        kept_out[...] = kept_ref[...].T
        sent_out[...] = sent_ref[...].T

    if share % 128:
        sides = struct_modes.T.reshape(-1, 2, low * share, depth)
        pair = [
            lax.dynamic_index_in_dim(sides, one, 1, keepdims=False).reshape(half, depth)
            for one in (side[0], 1 - side[0])
        ]
        return [*pair, after[0]]

    def column(i, which):
        return (0, i // low * 2 * low + which * low + i % low)

    return call(
        turn,
        [side],
        [struct_modes, struct_modes],
        [
            pl.BlockSpec((depth, share), lambda i, s: column(i, s[0])),
            pl.BlockSpec((depth, share), lambda i, s: column(i, 1 - s[0])),
        ],
        after,
        [jax.ShapeDtypeStruct((half, depth), BF16)] * 2,
        [pl.BlockSpec((share, depth), lambda i, s: (i, 0))] * 2,
        (half // share,),
        [],
    )


def panel(core, shifts, lefts, pieces, after):
    (kept, sent), (far_kept, far_sent) = lefts
    tall, depth = kept.shape
    width = pieces[0].shape[1]
    tile = min(tall, 256)
    steps = tall // tile
    count = shifts[0].shape[0]
    rows = depth // count
    per = pieces[0].shape[0] // len(NEXT) // rows

    def panel_part(core_ref, own_shift, far_shift, own_k, own_s, far_k, far_s, *refs):
        parts, kept_ref, sent_ref, picked = refs[:3], refs[3], refs[4], refs[5]
        step = pl.program_id(0)

        @pl.when(step == 0)
        def _():
            for half, shift in enumerate((own_shift, far_shift)):
                first_core = core_ref[0] == half
                seen = [jnp.int32(0)] * CLASSES
                for b in range(count):
                    kind = shift[b]
                    slot = jnp.int32(0)
                    for k in range(CLASSES):
                        group = jnp.where(first_core, FOUND[0][k], FOUND[1][k])
                        slot = jnp.where(kind == k, group * per + seen[k], slot)
                        seen[k] = seen[k] + (kind == k).astype(jnp.int32)
                    row = (half * count + b) * rows
                    base = 0
                    for part in parts:
                        many = part.shape[0] // rows

                        @pl.when((slot >= base) & (slot < base + many))
                        def _(part=part, row=row, slot=slot, base=base):
                            first = pl.multiple_of((slot - base) * rows, rows)
                            picked[row : row + rows, :] = part[pl.ds(first, rows), :]

                        base += many

        def product(own, far):
            return jnp.dot(own[...], picked[:depth, :], preferred_element_type=F32) + jnp.dot(
                far[...], picked[depth:, :], preferred_element_type=F32
            )

        @pl.when(step < steps)
        def _():
            sent_ref[...] = product(own_s, far_s).astype(BF16)

        @pl.when(step >= steps)
        def _():
            kept_ref[...] = product(own_k, far_k)

    early = lambda i, *_: (jnp.minimum(i, steps - 1), 0)
    late = lambda i, *_: (jnp.maximum(i - steps, 0), 0)
    return call(
        panel_part,
        [core, *shifts],
        [kept, sent, far_kept, far_sent, *pieces],
        [
            pl.BlockSpec((tile, depth), late),
            pl.BlockSpec((tile, depth), early),
            pl.BlockSpec((tile, depth), late),
            pl.BlockSpec((tile, depth), early),
        ]
        + [pl.BlockSpec(piece.shape, lambda i, *_: (0, 0)) for piece in pieces],
        after,
        [jax.ShapeDtypeStruct((tall, width), F32), jax.ShapeDtypeStruct((tall, width), BF16)],
        [pl.BlockSpec((tile, width), late), pl.BlockSpec((tile, width), early)],
        (2 * steps,),
        [pltpu.VMEM((2 * depth, width), BF16)],
    )


def added(held, got, here, before, wire, after):
    width = held.shape[1]
    shape = (before, 2, held.shape[0] // before // 2, width)
    block = (1, *shape[1:])
    out = (shape[0] * shape[2], width)

    def added_split(here_ref, held_ref, got_ref, kept_ref, away_ref):
        side = here_ref[0]
        kept_ref[...] = held_ref[0, side] + got_ref[0, side].astype(F32)
        away_ref[...] = (held_ref[0, 1 - side] + got_ref[0, 1 - side].astype(F32)).astype(wire)

    return call(
        added_split,
        [here],
        [held.reshape(shape), got.reshape(shape)],
        [pl.BlockSpec(block, lambda i, h: (i, 0, 0, 0))] * 2,
        after,
        [jax.ShapeDtypeStruct(out, F32), jax.ShapeDtypeStruct(out, wire)],
        [pl.BlockSpec(shape[2:], lambda i, h: (i, 0))] * 2,
        (before,),
        [],
    )


def placed_in(core, block, buffer, half, at, modes, after):
    rows, width = block.shape
    steps = modes // 2 // width

    def place(core_ref, block_ref, *refs):
        refs[-1][...] = block_ref[...]

    def column(i, c):
        return (0, (c[0] if half == 0 else 1 - c[0]) * steps + at // width)

    return call(
        place,
        [core],
        [block] + ([] if buffer is None else [buffer]),
        [pl.BlockSpec((rows, width), lambda i, c: (0, 0))] + ([] if buffer is None else [ANY]),
        after,
        [jax.ShapeDtypeStruct((rows, modes), F32)],
        [pl.BlockSpec((rows, width), column)],
        (1,),
        [],
        None if buffer is None else 0,
    )


def passed_along(block, distance):
    size = lax.axis_size("mesh")
    return lax.ppermute(block, "mesh", [((i - distance) % size, i) for i in range(size)])


def swapped(block, bit):
    size = lax.axis_size("mesh")
    return lax.ppermute(block, "mesh", [(i, i ^ (1 << bit)) for i in range(size)])


def planned(levels):
    steps, arrived, before = [], 10.0, 10.0
    for j, eighths in enumerate(EIGHTHS):
        size = eighths / 2
        arrived += 20.0 * size
        steps.append((before - 4.0 if j else 0.0, "coupled", j))
        steps.append((arrived, "panel", j))
        at = arrived + 4.0
        for level in range(1, levels + 1):
            at += (2.0 + 12.0 * size) if level == 1 else (2.0 + 7.0 * size)
            steps.append((at, level, j))
        steps.append((at + 5.0, "last", j))
        before = arrived
    return [step[1:] for step in sorted(steps, key=lambda step: step[0])]


def per_device(struct_modes, acoustic_modes, coupling, face_shift, face_blocks):
    size = lax.axis_size("mesh")
    me = lax.axis_index("mesh")
    modes = acoustic_modes.shape[1]
    share = struct_modes.shape[1] // size
    bits = list(range(1, size.bit_length() - 1))
    order = [2, 1, *bits[2:]]
    levels = len(order)
    widths = [e * modes // 16 for e in EIGHTHS]
    starts = [sum(widths[:j]) for j in range(len(widths))]

    def bit_of(bit):
        return ((me >> bit) & 1).reshape(1)

    core = bit_of(0)
    half, token = halved(core, acoustic_modes, [])
    token = [token]
    blocks = (face_blocks, swapped(face_blocks, 0))
    couplings = (coupling, swapped(coupling, 0))
    acoustics = (acoustic_modes, swapped(half, 0))
    far_struct = swapped(struct_modes, 0)
    shifts = (face_shift, swapped(face_shift, 0))
    *own, last = turned(bit_of(order[0]), order[0], struct_modes, share, token)
    lefts, token = [own], [last]

    state = [dict(bits=sorted([0, *order[1:]], reverse=True)) for _ in widths]
    buffer = None
    for stage, j in planned(levels):
        now = state[j]
        if stage == "coupled":
            ahead, behind, here, last = coupled(
                core, blocks, acoustics, couplings, starts[j], widths[j], token
            )
            now["pieces"] = [passed_along(ahead, 2), passed_along(behind, -2), here]
            token = [last]
            if len(lefts) == 1:
                *far, last = turned(bit_of(order[0]), order[0], far_struct, share, token)
                lefts.append(far)
                token = [last]
        elif stage == "panel":
            now["held"], away, last = panel(core, shifts, lefts, now["pieces"], token)
            now["got"] = swapped(away, order[0])
            token = [last]
        elif stage == "last":
            buffer, last = placed_in(core, now["held"], buffer, 0, starts[j], modes, token)
            buffer, last = placed_in(core, now["got"], buffer, 1, starts[j], modes, [last])
            token = [last]
        else:
            bit = order[stage] if stage < levels else 0
            place = now["bits"].index(bit)
            now["bits"].remove(bit)
            wire = BF16 if stage < min(levels, 3) else F32
            now["held"], away, last = added(
                now["held"], now["got"], bit_of(bit), 2**place, wire, token
            )
            now["got"] = swapped(away, bit)
            token = [last]
    return buffer


def solution(mesh):
    placed = (
        P(("member", "mesh"), None),
        P(("member", "mesh"), None),
        P("mesh", None, None),
        P("mesh"),
        P("mesh", None),
    )
    return jax.shard_map(
        per_device,
        mesh=mesh,
        in_specs=placed,
        out_specs=P(("member", "mesh"), None),
        check_vma=False,
    )
```

time: 297 us -> 172 us (0.58)
  waiting for transfers between devices: 217 us -> 42.1 us
  Pallas kernels: 0 us -> 63.4 us
  starting transfers between devices: 7.17 us -> 50.2 us
  matrix products: 28.7 us -> 0 us
  local copies, waits for them, and re-layouts: 27.6 us -> 14.5 us
  between operations: 13.5 us -> 0.48 us
    reduce_scatter x1 -> x0, waiting for transfers between devices: 189 us -> none  [per_device(): lax.psum_scatter(partial_value, 'mesh', scatter_dimension=0, tiled=True)]
    pallas_call x0 -> x38, Pallas kernels: none -> 63.4 us  [call(): pl.pallas_call(kernel, out_shape=[*out_shape, jax.ShapeDtypeStruct((8, 12...]
    ppermute x4 -> x35, starting transfers between devices: 7.17 us -> 50.2 us  [the longest x25 28.1 us: swapped(): return lax.ppermute(block, 'mesh', [(i, i ^ 1 << bit) for i in range(size)])]
    dot_general x3 -> x0, matrix products: 28.7 us -> none  [the longest x1 13.8 us: per_device(): lax.dot_general(left_rows, right_rows, (((0,), (0,)), ((), ())), preferre...]
    ppermute x4 -> x35, waiting for transfers between devices: 28.3 us -> 42.1 us  [the longest x25 24.9 us: swapped(): return lax.ppermute(block, 'mesh', [(i, i ^ 1 << bit) for i in range(size)])]
    gather x1 -> x0, local copies, waits for them, and re-layouts: 8.82 us -> none  [per_device(): acoustic_blocks[face_blocks].reshape(slot_count, -1, acoustic_width)]
    reshape x1 -> x0, local copies, waits for them, and re-layouts: 4.81 us -> none  [per_device(): struct_modes.reshape(block_count, -1)]
    unnamed x14 -> x77, local copies, waits for them, and re-layouts: 10.8 us -> 14.5 us
  transfers between devices with their start and end apart: 5 -> 35, of which waited for: 2 -> 14; matrix products, arithmetic and copies ran while one was open for 10% -> 0% of each run, Pallas kernels for 0% -> 27%
where the time goes in v3:
time: 172 us; the launch traced here: 171 us
  Pallas kernels  63.4 us (37%)
  starting transfers between devices  50.2 us (29%)
  waiting for transfers between devices  42.1 us (24%)
  local copies, waits for them, and re-layouts  14.5 us (8%)
    pallas_call x38, Pallas kernels, call(): pl.pallas_call(kernel, out_shape=[*out_shape, jax.ShapeDtypeStruct((8, 12...  63.4 us
    ppermute x25, starting transfers between devices, swapped(): return lax.ppermute(block, 'mesh', [(i, i ^ 1 << bit) for i in range(size)])  28.1 us
    ppermute x25, waiting for transfers between devices, swapped(): return lax.ppermute(block, 'mesh', [(i, i ^ 1 << bit) for i in range(size)])  24.9 us
    ppermute x10, starting transfers between devices, passed_along(): lax.ppermute(block, 'mesh', [((i - distance) % size, i) for i in range(si...  22.2 us
    ppermute x10, waiting for transfers between devices, passed_along(): lax.ppermute(block, 'mesh', [((i - distance) % size, i) for i in range(si...  17.3 us
    unnamed x77, local copies, waits for them, and re-layouts  14.5 us
  transfers between devices with their start and end apart: 35, of which 14 were waited for; matrix products, arithmetic and copies ran while one was open for 0% of the time, Pallas kernels for 27%

profile of v3, /device:TPU:0, one launch (start us, length us, event | category | flops | bytes accessed | tf_op | source)
XLA Modules:
  0.0 170.7 jit_solution(5929269823635317980)
XLA Ops:
  0.5 1.6 copy-done
  2.0 1.1 other_half.1
  3.8 1.9 %copy-done.14 = bf16[768,2048]{1,0:T(8,128)(2,1)S(1)} copy-done((bf16[768,2048]{1,0:T(8,128)(2,1)S(1)}, bf16[768,2048]{1,0:T(8,128)(2,1)}, u32[]{:S(2)}) %copy-start.14) | copy-done | bytes 3145752
  5.7 2.4 %turn.2 = (bf16[1024,768]{1,0:T(8,128)(2,1)S(1)}, bf16[1024,768]{1,0:T(8,128)(2,1)S(1)}, f32[8,128]{1,0:T(8,128)S(1)}) custom-call(s32[1]{0:T(128)} %bitcast.3.refs_0_, bf16[768,2048]{1,0:T(8,128)(2,1)S(1)} %copy-done.14, bf16[768,2048]{1,0:T(8,128)(2,1)S(1)} %copy-done.14, f32[8,128]{1,0:T(8,128)S(1)} %get-tuple-element.112.refs_3_), custom_call_target="tpu_custom_call" | custom-call | tf_op jit(solution)/shard_map/turn/pallas_call | solution.py:28
  8.4 3.3 %coupled_rows.5 = (bf16[768,256]{1,0:T(8,128)(2,1)S(1)}, bf16[768,256]{1,0:T(8,128)(2,1)S(1)}, bf16[1024,256]{1,0:T(8,128)(2,1)S(1)}, f32[8,128]{1,0:T(8,128)S(1)}) custom-call(s32[1]{0:T(128)} %bitcast.refs_0_, s32[20,4]{1,0:T(8,128)S(1)} %copy.16.refs_1_, s32[20,4]{1,0:T(8,128)S(1)} %collective-permute-done.2.refs_2_, bf16[512,2048]{1,0:T(8,128)(2,1)S(1)} %copy-done.1, ...), custom_call_target="tpu_custom_call" | custom-call | tf_op jit(solution)/shard_map/coupled_rows/pallas_call | solution.py:28
  11.8 2.9 %collective-permute-start.5 = (bf16[768,256]{1,0:T(8,128)(2,1)S(1)}, bf16[768,256]{1,0:T(8,128)(2,1)S(1)}, u32[]{:S(2)}, u32[]{:S(2)}) collective-permute-start(bf16[768,256]{1,0:T(8,128)(2,1)S(1)} %get-tuple-element.120), channel_id=1, source_target_pairs={{14,0},{15,1},{0,2},{1,3},{2,4},{3,5},{4,6},{5,7},{6,8},{7,9},{8,1... | collective-permute-start | bytes 1179656 | tf_op jit(solution)/shard_map/ppermute | solution.py:268
  14.7 3.1 %collective-permute-start.6 = (bf16[768,256]{1,0:T(8,128)(2,1)S(1)}, bf16[768,256]{1,0:T(8,128)(2,1)S(1)}, u32[]{:S(2)}, u32[]{:S(2)}) collective-permute-start(bf16[768,256]{1,0:T(8,128)(2,1)S(1)} %get-tuple-element.121), channel_id=1, source_target_pairs={{2,0},{3,1},{4,2},{5,3},{6,4},{7,5},{8,6},{9,7},{10,8},{11,9},{12,... | collective-permute-start | bytes 1179656 | tf_op jit(solution)/shard_map/ppermute | solution.py:268
  17.8 5.2 %turn.3 = (bf16[1024,768]{1,0:T(8,128)(2,1)S(1)}, bf16[1024,768]{1,0:T(8,128)(2,1)S(1)}, f32[8,128]{1,0:T(8,128)S(1)}) custom-call(s32[1]{0:T(128)} %bitcast.3.refs_0_, bf16[768,2048]{1,0:T(8,128)(2,1)} %collective-permute-done.1.refs_1_.refs_2_, bf16[768,2048]{1,0:T(8,128)(2,1)} %collective-permute-done.1.refs_1_.refs_2_, ...), custom_call_target="tpu_custom_call" | custom-call | tf_op jit(solution)/shard_map/turn/pallas_call | solution.py:28
  23.0 4.0 %coupled_rows.6 = (bf16[768,256]{1,0:T(8,128)(2,1)}, bf16[768,256]{1,0:T(8,128)(2,1)}, bf16[1024,256]{1,0:T(8,128)(2,1)S(1)}, f32[8,128]{1,0:T(8,128)S(1)}) custom-call(s32[1]{0:T(128)} %bitcast.refs_0_, s32[20,4]{1,0:T(8,128)S(1)} %copy.16.refs_1_, s32[20,4]{1,0:T(8,128)S(1)} %collective-permute-done.2.refs_2_, bf16[512,2048]{1,0:T(8,128)(2,1)S(1)} %copy-done.1, ...), custom_call_target="tpu_custom_call" | custom-call | tf_op jit(solution)/shard_map/coupled_rows/pallas_call | solution.py:28
  27.1 4.7 %collective-permute-done.5.refs_7_ = bf16[768,256]{1,0:T(8,128)(2,1)S(1)} collective-permute-done((bf16[768,256]{1,0:T(8,128)(2,1)S(1)}, bf16[768,256]{1,0:T(8,128)(2,1)S(1)}, u32[]{:S(2)}, u32[]{:S(2)}) %collective-permute-start.5) | collective-permute-done | bytes 393248 | tf_op jit(solution)/shard_map/ppermute | solution.py:268
  31.8 2.2 %collective-permute-done.6.refs_8_ = bf16[768,256]{1,0:T(8,128)(2,1)S(1)} collective-permute-done((bf16[768,256]{1,0:T(8,128)(2,1)S(1)}, bf16[768,256]{1,0:T(8,128)(2,1)S(1)}, u32[]{:S(2)}, u32[]{:S(2)}) %collective-permute-start.6) | collective-permute-done | bytes 393248 | tf_op jit(solution)/shard_map/ppermute | solution.py:268
  34.0 5.6 %panel_part.5 = (f32[1024,256]{1,0:T(8,128)S(1)}, bf16[1024,256]{1,0:T(8,128)(2,1)}, f32[8,128]{1,0:T(8,128)S(1)}) custom-call(s32[1]{0:T(128)} %bitcast.refs_0_, s32[12]{0:T(128)S(1)} %copy-done.29, s32[12]{0:T(128)S(1)} %collective-permute-done.refs_2_, bf16[1024,768]{1,0:T(8,128)(2,1)S(1)} %get-tuple-element.113.refs_3_, ...), custom_call_target="tpu_custom_call" | custom-call | tf_op jit(solution)/shard_map/panel_part/pallas_call | solution.py:28
  39.6 1.0 copy-done.17
  41.1 1.3 collective-permute-start.7
  43.0 4.1 %collective-permute-start.10 = (bf16[768,256]{1,0:T(8,128)(2,1)}, bf16[768,256]{1,0:T(8,128)(2,1)}, u32[]{:S(2)}, u32[]{:S(2)}) collective-permute-start(bf16[768,256]{1,0:T(8,128)(2,1)} %get-tuple-element.132), channel_id=1, source_target_pairs={{2,0},{3,1},{4,2},{5,3},{6,4},{7,5},{8,6},{9,7},{10,8},{11,9},{12,... | collective-permute-start | bytes 1179656 | tf_op jit(solution)/shard_map/ppermute | solution.py:268
  47.1 0.7 copy-done.26
  47.8 0.7 copy-done.36
  48.5 4.3 %coupled_rows.7 = (bf16[768,256]{1,0:T(8,128)(2,1)}, bf16[768,256]{1,0:T(8,128)(2,1)}, bf16[1024,256]{1,0:T(8,128)(2,1)S(1)}, f32[8,128]{1,0:T(8,128)S(1)}) custom-call(s32[1]{0:T(128)} %bitcast.refs_0_, s32[20,4]{1,0:T(8,128)S(1)} %copy.16.refs_1_, s32[20,4]{1,0:T(8,128)S(1)} %copy-done.26, bf16[512,2048]{1,0:T(8,128)(2,1)S(1)} %copy-done.1, ...), custom_call_target="tpu_custom_call" | custom-call | tf_op jit(solution)/shard_map/coupled_rows/pallas_call | solution.py:28
  52.8 3.5 %collective-permute-done.7 = bf16[1024,256]{1,0:T(8,128)(2,1)} collective-permute-done((bf16[1024,256]{1,0:T(8,128)(2,1)}, bf16[1024,256]{1,0:T(8,128)(2,1)}, u32[]{:S(2)}, u32[]{:S(2)}) %collective-permute-start.7) | collective-permute-done | bytes 524320 | tf_op jit(solution)/shard_map/ppermute | solution.py:273
  56.3 1.7 %added_split.15 = (f32[512,256]{1,0:T(8,128)S(1)}, bf16[512,256]{1,0:T(8,128)(2,1)}, f32[8,128]{1,0:T(8,128)S(1)}) custom-call(s32[1]{0:T(128)} %bitcast.2.refs_0_, f32[2,2,256,256]{3,2,1,0:T(8,128)S(1)} %bitcast.36, bf16[2,2,256,256]{3,2,1,0:T(8,128)(2,1)} %bitcast.5.refs_2_, f32[8,128]{1,0:T(8,128)S(1)} %get-tuple-element.128.refs_3_), custom_call_target="tpu_custom_call" | custom-call | tf_op jit(solution)/shard_map/added_split/pallas_call | solution.py:28
  58.0 6.6 %collective-permute-done.9.refs_7_ = bf16[768,256]{1,0:T(8,128)(2,1)S(1)} collective-permute-done((bf16[768,256]{1,0:T(8,128)(2,1)}, bf16[768,256]{1,0:T(8,128)(2,1)S(1)}, u32[]{:S(2)}, u32[]{:S(2)}) %collective-permute-start.9) | collective-permute-done | bytes 393248 | tf_op jit(solution)/shard_map/ppermute | solution.py:268
  64.7 1.4 copy-done.12
  66.1 1.0 copy-done.24
  67.1 6.4 %panel_part.6 = (f32[1024,256]{1,0:T(8,128)S(1)}, bf16[1024,256]{1,0:T(8,128)(2,1)}, f32[8,128]{1,0:T(8,128)S(1)}) custom-call(s32[1]{0:T(128)} %bitcast.refs_0_, s32[12]{0:T(128)S(1)} %copy-done.29, s32[12]{0:T(128)S(1)} %copy-done.31, bf16[1024,768]{1,0:T(8,128)(2,1)S(1)} %copy-done.3, bf16[1024,768]{1,0:T(8,128)(2,1)S(1)} %copy-done.6, ...), custom_call_target="tpu_custom_call" | custom-call | tf_op jit(solution)/shard_map/panel_part/pallas_call | solution.py:28
  73.6 1.0 copy-done.15
  75.2 2.0 %collective-permute-start.13 = (bf16[768,256]{1,0:T(8,128)(2,1)}, bf16[768,256]{1,0:T(8,128)(2,1)S(1)}, u32[]{:S(2)}, u32[]{:S(2)}) collective-permute-start(bf16[768,256]{1,0:T(8,128)(2,1)} %get-tuple-element.141), channel_id=1, source_target_pairs={{14,0},{15,1},{0,2},{1,3},{2,4},{3,5},{4,6},{5,7},{6,8},{7,9},{8,1... | collective-permute-start | bytes 1179656 | tf_op jit(solution)/shard_map/ppermute | solution.py:268
  77.2 3.7 %collective-permute-start.14 = (bf16[768,256]{1,0:T(8,128)(2,1)}, bf16[768,256]{1,0:T(8,128)(2,1)}, u32[]{:S(2)}, u32[]{:S(2)}) collective-permute-start(bf16[768,256]{1,0:T(8,128)(2,1)} %get-tuple-element.142), channel_id=1, source_target_pairs={{2,0},{3,1},{4,2},{5,3},{6,4},{7,5},{8,6},{9,7},{10,8},{11,9},{12,... | collective-permute-start | bytes 1179656 | tf_op jit(solution)/shard_map/ppermute | solution.py:268
  80.9 3.8 %collective-permute-done.8 = bf16[512,256]{1,0:T(8,128)(2,1)} collective-permute-done((bf16[512,256]{1,0:T(8,128)(2,1)}, bf16[512,256]{1,0:T(8,128)(2,1)}, u32[]{:S(2)}, u32[]{:S(2)}) %collective-permute-start.8) | collective-permute-done | bytes 262176 | tf_op jit(solution)/shard_map/ppermute | solution.py:273
  84.7 1.0 copy-done.20
  85.7 0.7 copy-done.34
  86.4 1.1 added_split.16
  87.5 11.3 %collective-permute-start.11 = (bf16[256,256]{1,0:T(8,128)(2,1)S(1)}, bf16[256,256]{1,0:T(8,128)(2,1)S(1)}, u32[]{:S(2)}, u32[]{:S(2)}) collective-permute-start(bf16[256,256]{1,0:T(8,128)(2,1)S(1)} %get-tuple-element.137), channel_id=1, source_target_pairs={{0,8},{1,9},{2,10},{3,11},{4,12},{5,13},{6,14},{7,15},{8,0},{9,1},... | collective-permute-start | bytes 393224 | tf_op jit(solution)/shard_map/ppermute | solution.py:273
  98.7 3.5 %collective-permute-done.11 = bf16[256,256]{1,0:T(8,128)(2,1)S(1)} collective-permute-done((bf16[256,256]{1,0:T(8,128)(2,1)S(1)}, bf16[256,256]{1,0:T(8,128)(2,1)S(1)}, u32[]{:S(2)}, u32[]{:S(2)}) %collective-permute-start.11) | collective-permute-done | bytes 131104 | tf_op jit(solution)/shard_map/ppermute | solution.py:273
  102.3 0.8 copy-done.27
  103.1 3.1 %coupled_rows.8 = (bf16[768,128]{1,0:T(8,128)(2,1)S(1)}, bf16[768,128]{1,0:T(8,128)(2,1)S(1)}, bf16[1024,128]{1,0:T(8,128)(2,1)S(1)}, f32[8,128]{1,0:T(8,128)S(1)}) custom-call(s32[1]{0:T(128)} %bitcast.refs_0_, s32[20,4]{1,0:T(8,128)S(1)} %copy.16.refs_1_, s32[20,4]{1,0:T(8,128)S(1)} %copy-done.27, bf16[512,2048]{1,0:T(8,128)(2,1)S(1)} %copy-done.1, ...), custom_call_target="tpu_custom_call" | custom-call | tf_op jit(solution)/shard_map/coupled_rows/pallas_call | solution.py:28
  106.2 1.3 copy-done.16
  107.5 1.1 added_split.18
  108.8 5.3 %panel_part.7 = (f32[1024,256]{1,0:T(8,128)S(1)}, bf16[1024,256]{1,0:T(8,128)(2,1)S(1)}, f32[8,128]{1,0:T(8,128)S(1)}) custom-call(s32[1]{0:T(128)} %bitcast.refs_0_, s32[12]{0:T(128)S(1)} %copy-done.29, s32[12]{0:T(128)S(1)} %copy-done.32, bf16[1024,768]{1,0:T(8,128)(2,1)S(1)} %copy-done.4, bf16[1024,768]{1,0:T(8,128)(2,1)S(1)} %copy-done.7, ...), custom_call_target="tpu_custom_call" | custom-call | tf_op jit(solution)/shard_map/panel_part/pallas_call | solution.py:28
  114.1 2.4 %collective-permute-start.19 = (bf16[512,256]{1,0:T(8,128)(2,1)S(1)}, bf16[512,256]{1,0:T(8,128)(2,1)S(1)}, u32[]{:S(2)}, u32[]{:S(2)}) collective-permute-start(bf16[512,256]{1,0:T(8,128)(2,1)S(1)} %get-tuple-element.159), channel_id=1, source_target_pairs={{0,2},{1,3},{2,0},{3,1},{4,6},{5,7},{6,4},{7,5},{8,10},{9,11},{10,... | collective-permute-start | bytes 786440 | tf_op jit(solution)/shard_map/ppermute | solution.py:273
  116.6 4.7 %collective-permute-start.22 = (bf16[768,128]{1,0:T(8,128)(2,1)S(1)}, bf16[768,128]{1,0:T(8,128)(2,1)S(1)}, u32[]{:S(2)}, u32[]{:S(2)}) collective-permute-start(bf16[768,128]{1,0:T(8,128)(2,1)S(1)} %get-tuple-element.164), channel_id=1, source_target_pairs={{2,0},{3,1},{4,2},{5,3},{6,4},{7,5},{8,6},{9,7},{10,8},{11,9},{12,... | collective-permute-start | bytes 589832 | tf_op jit(solution)/shard_map/ppermute | solution.py:268
  121.3 0.7 place.10
  121.9 0.7 place.11
  122.6 3.1 %coupled_rows.9 = (bf16[768,128]{1,0:T(8,128)(2,1)S(1)}, bf16[768,128]{1,0:T(8,128)(2,1)S(1)}, bf16[1024,128]{1,0:T(8,128)(2,1)S(1)}, f32[8,128]{1,0:T(8,128)S(1)}) custom-call(s32[1]{0:T(128)} %bitcast.refs_0_, s32[20,4]{1,0:T(8,128)S(1)} %copy.16.refs_1_, s32[20,4]{1,0:T(8,128)S(1)} %copy-done.28, bf16[512,2048]{1,0:T(8,128)(2,1)S(1)} %copy-done.1, ...), custom_call_target="tpu_custom_call" | custom-call | tf_op jit(solution)/shard_map/coupled_rows/pallas_call | solution.py:28
  125.7 1.8 %collective-permute-done.19 = bf16[512,256]{1,0:T(8,128)(2,1)S(1)} collective-permute-done((bf16[512,256]{1,0:T(8,128)(2,1)S(1)}, bf16[512,256]{1,0:T(8,128)(2,1)S(1)}, u32[]{:S(2)}, u32[]{:S(2)}) %collective-permute-start.19) | collective-permute-done | bytes 262176 | tf_op jit(solution)/shard_map/ppermute | solution.py:273
  127.5 1.7 %collective-permute-start.20 = (bf16[256,256]{1,0:T(8,128)(2,1)S(1)}, bf16[256,256]{1,0:T(8,128)(2,1)S(1)}, u32[]{:S(2)}, u32[]{:S(2)}) collective-permute-start(bf16[256,256]{1,0:T(8,128)(2,1)S(1)} %get-tuple-element.162), channel_id=1, source_target_pairs={{0,8},{1,9},{2,10},{3,11},{4,12},{5,13},{6,14},{7,15},{8,0},{9,1},... | collective-permute-start | bytes 393224 | tf_op jit(solution)/shard_map/ppermute | solution.py:273
  129.2 0.9 collective-permute-start.16
  130.1 3.7 %collective-permute-done.21.refs_7_ = bf16[768,128]{1,0:T(8,128)(2,1)S(1)} collective-permute-done((bf16[768,128]{1,0:T(8,128)(2,1)S(1)}, bf16[768,128]{1,0:T(8,128)(2,1)S(1)}, u32[]{:S(2)}, u32[]{:S(2)}) %collective-permute-start.21) | collective-permute-done | bytes 196640 | tf_op jit(solution)/shard_map/ppermute | solution.py:268
  134.0 4.3 %panel_part.8 = (f32[1024,128]{1,0:T(8,128)S(1)}, bf16[1024,128]{1,0:T(8,128)(2,1)S(1)}, f32[8,128]{1,0:T(8,128)S(1)}) custom-call(s32[1]{0:T(128)} %bitcast.refs_0_, s32[12]{0:T(128)S(1)} %copy-done.29, s32[12]{0:T(128)S(1)} %copy-done.32, bf16[1024,768]{1,0:T(8,128)(2,1)S(1)} %copy-done.4, bf16[1024,768]{1,0:T(8,128)(2,1)S(1)} %copy-done.7, ...), custom_call_target="tpu_custom_call" | custom-call | tf_op jit(solution)/shard_map/panel_part/pallas_call | solution.py:28
  138.3 1.7 collective-permute-start.24
  140.2 2.9 %collective-permute-start.27 = (bf16[512,256]{1,0:T(8,128)(2,1)S(1)}, bf16[512,256]{1,0:T(8,128)(2,1)S(1)}, u32[]{:S(2)}, u32[]{:S(2)}) collective-permute-start(bf16[512,256]{1,0:T(8,128)(2,1)S(1)} %get-tuple-element.184), channel_id=1, source_target_pairs={{0,2},{1,3},{2,0},{3,1},{4,6},{5,7},{6,4},{7,5},{8,10},{9,11},{10,... | collective-permute-start | bytes 786440 | tf_op jit(solution)/shard_map/ppermute | solution.py:273
  143.1 4.3 %panel_part.9 = (f32[1024,128]{1,0:T(8,128)S(1)}, bf16[1024,128]{1,0:T(8,128)(2,1)S(1)}, f32[8,128]{1,0:T(8,128)S(1)}) custom-call(s32[1]{0:T(128)} %bitcast.refs_0_, s32[12]{0:T(128)S(1)} %copy-done.29, s32[12]{0:T(128)S(1)} %copy-done.32, bf16[1024,768]{1,0:T(8,128)(2,1)S(1)} %copy-done.4, bf16[1024,768]{1,0:T(8,128)(2,1)S(1)} %copy-done.7, ...), custom_call_target="tpu_custom_call" | custom-call | tf_op jit(solution)/shard_map/panel_part/pallas_call | solution.py:28
  147.4 2.7 %collective-permute-start.23 = (bf16[1024,128]{1,0:T(8,128)(2,1)S(1)}, bf16[1024,128]{1,0:T(8,128)(2,1)S(1)}, u32[]{:S(2)}, u32[]{:S(2)}) collective-permute-start(bf16[1024,128]{1,0:T(8,128)(2,1)S(1)} %get-tuple-element.171), channel_id=1, source_target_pairs={{0,4},{1,5},{2,6},{3,7},{4,0},{5,1},{6,2},{7,3},{8,12},{9,13},{10,... | collective-permute-start | bytes 786440 | tf_op jit(solution)/shard_map/ppermute | solution.py:273
  150.1 0.7 place.12
  150.7 0.7 place.13
  151.9 4.6 %collective-permute-done.26 = bf16[512,128]{1,0:T(8,128)(2,1)S(1)} collective-permute-done((bf16[512,128]{1,0:T(8,128)(2,1)S(1)}, bf16[512,128]{1,0:T(8,128)(2,1)S(1)}, u32[]{:S(2)}, u32[]{:S(2)}) %collective-permute-start.26) | collective-permute-done | bytes 131104 | tf_op jit(solution)/shard_map/ppermute | solution.py:273
  156.6 1.0 collective-permute-done.23
  157.8 4.3 %collective-permute-done.30 = bf16[256,128]{1,0:T(8,128)(2,1)S(1)} collective-permute-done((bf16[256,128]{1,0:T(8,128)(2,1)S(1)}, bf16[256,128]{1,0:T(8,128)(2,1)S(1)}, u32[]{:S(2)}, u32[]{:S(2)}) %collective-permute-start.30) | collective-permute-done | bytes 65568 | tf_op jit(solution)/shard_map/ppermute | solution.py:273
  162.8 1.9 %collective-permute-start.31 = (bf16[256,128]{1,0:T(8,128)(2,1)S(1)}, bf16[256,128]{1,0:T(8,128)(2,1)S(1)}, u32[]{:S(2)}, u32[]{:S(2)}) collective-permute-start(bf16[256,128]{1,0:T(8,128)(2,1)S(1)} %get-tuple-element.198), channel_id=1, source_target_pairs={{0,8},{1,9},{2,10},{3,11},{4,12},{5,13},{6,14},{7,15},{8,0},{9,1},... | collective-permute-start | bytes 196616 | tf_op jit(solution)/shard_map/ppermute | solution.py:273
  165.4 0.6 place.15
  166.0 0.7 place.16
  166.7 0.7 place.17
  167.4 1.4 collective-permute-done.31
  168.8 0.6 place.18
  170.1 0.6 place.19
  (121 shorter events, 6.6 us)
Async XLA Ops:
  0.0 3.7 %copy-start.37 = (s32[20,4]{0,1:T(4,128)S(1)}, s32[20,4]{0,1:T(4,128)}, u32[]{:S(2)}) copy-start(s32[20,4]{0,1:T(4,128)} %param.9) | copy-start | bytes 964
  0.0 17.8 %collective-permute-start.1 = (bf16[768,2048]{1,0:T(8,128)(2,1)}, bf16[768,2048]{1,0:T(8,128)(2,1)}, u32[]{:S(2)}, u32[]{:S(2)}) collective-permute-start(bf16[768,2048]{1,0:T(8,128)(2,1)} %refs_2_.1), channel_id=1, source_target_pairs={{0,1},{1,0},{2,3},{3,2},{4,5},{5,4},{6,7},{7,6},{8,9},{9,8},{10,11... | collective-permute-start | bytes 9437192 | tf_op jit(solution)/shard_map/ppermute | solution.py:273
  0.5 1.6 copy-start
  3.1 5.3 %collective-permute-start.3 = (bf16[512,1024]{1,0:T(8,128)(2,1)}, bf16[512,1024]{1,0:T(8,128)(2,1)S(1)}, u32[]{:S(2)}, u32[]{:S(2)}) collective-permute-start(bf16[512,1024]{1,0:T(8,128)(2,1)} %get-tuple-element.115), channel_id=1, source_target_pairs={{0,1},{1,0},{2,3},{3,2},{4,5},{5,4},{6,7},{7,6},{8,9},{9,8},{10,11... | collective-permute-start | bytes 3145736 | tf_op jit(solution)/shard_map/ppermute | solution.py:273
  3.2 4.9 %collective-permute-start.4 = (bf16[20,64,256]{2,1,0:T(8,128)(2,1)}, bf16[20,64,256]{2,1,0:T(8,128)(2,1)}, u32[]{:S(2)}, u32[]{:S(2)}) collective-permute-start(bf16[20,64,256]{2,1,0:T(8,128)(2,1)} %refs_5_.9), channel_id=1, source_target_pairs={{0,1},{1,0},{2,3},{3,2},{4,5},{5,4},{6,7},{7,6},{8,9},{9,8},{10,11... | collective-permute-start | bytes 1966088 | tf_op jit(solution)/shard_map/ppermute | solution.py:273
  3.8 4.4 %collective-permute-start.2 = (s32[20,4]{1,0:T(8,128)S(1)}, s32[20,4]{1,0:T(8,128)S(1)}, u32[]{:S(2)}, u32[]{:S(2)}) collective-permute-start(s32[20,4]{1,0:T(8,128)S(1)} %copy.16.refs_1_), channel_id=1, source_target_pairs={{0,1},{1,0},{2,3},{3,2},{4,5},{5,4},{6,7},{7,6},{8,9},{9,8},{10,11... | collective-permute-start | bytes 968 | tf_op jit(solution)/shard_map/ppermute | solution.py:273
  3.8 1.9 %copy-start.14 = (bf16[768,2048]{1,0:T(8,128)(2,1)S(1)}, bf16[768,2048]{1,0:T(8,128)(2,1)}, u32[]{:S(2)}) copy-start(bf16[768,2048]{1,0:T(8,128)(2,1)} %refs_2_.1) | copy-start | bytes 9437188
  5.7 2.7 %copy-start.1 = (bf16[512,2048]{1,0:T(8,128)(2,1)S(1)}, bf16[512,2048]{1,0:T(8,128)(2,1)}, u32[]{:S(2)}) copy-start(bf16[512,2048]{1,0:T(8,128)(2,1)} %refs_3_.9) | copy-start | bytes 6291460
  8.1 25.9 %copy-start.2 = (bf16[1024,768]{1,0:T(8,128)(2,1)}, bf16[1024,768]{1,0:T(8,128)(2,1)S(1)}, u32[]{:S(2)}) copy-start(bf16[1024,768]{1,0:T(8,128)(2,1)S(1)} %get-tuple-element.113.refs_3_) | copy-start | bytes 4718596
  8.1 25.9 %copy-start.5 = (bf16[1024,768]{1,0:T(8,128)(2,1)}, bf16[1024,768]{1,0:T(8,128)(2,1)S(1)}, u32[]{:S(2)}) copy-start(bf16[1024,768]{1,0:T(8,128)(2,1)S(1)} %get-tuple-element.114.refs_4_) | copy-start | bytes 4718596
  8.1 14.9 %copy-start.25 = (s32[20,4]{1,0:T(8,128)}, s32[20,4]{1,0:T(8,128)S(1)}, u32[]{:S(2)}) copy-start(s32[20,4]{1,0:T(8,128)S(1)} %collective-permute-done.2.refs_2_) | copy-start | bytes 964
  8.4 9.4 %copy-start.29 = (s32[12]{0:T(128)S(1)}, s32[12]{0:T(128)}, u32[]{:S(2)}) copy-start(s32[12]{0:T(128)} %refs_1_.18) | copy-start | bytes 148
  11.8 20.0 %collective-permute-start.5 = (bf16[768,256]{1,0:T(8,128)(2,1)S(1)}, bf16[768,256]{1,0:T(8,128)(2,1)S(1)}, u32[]{:S(2)}, u32[]{:S(2)}) collective-permute-start(bf16[768,256]{1,0:T(8,128)(2,1)S(1)} %get-tuple-element.120), channel_id=1, source_target_pairs={{14,0},{15,1},{0,2},{1,3},{2,4},{3,5},{4,6},{5,7},{6,8},{7,9},{8,1... | collective-permute-start | bytes 1179656 | tf_op jit(solution)/shard_map/ppermute | solution.py:268
  14.7 19.3 %collective-permute-start.6 = (bf16[768,256]{1,0:T(8,128)(2,1)S(1)}, bf16[768,256]{1,0:T(8,128)(2,1)S(1)}, u32[]{:S(2)}, u32[]{:S(2)}) collective-permute-start(bf16[768,256]{1,0:T(8,128)(2,1)S(1)} %get-tuple-element.121), channel_id=1, source_target_pairs={{2,0},{3,1},{4,2},{5,3},{6,4},{7,5},{8,6},{9,7},{10,8},{11,9},{12,... | collective-permute-start | bytes 1179656 | tf_op jit(solution)/shard_map/ppermute | solution.py:268
  17.8 9.3 %collective-permute-start = (s32[12]{0:T(128)S(1)}, s32[12]{0:T(128)S(1)}, u32[]{:S(2)}, u32[]{:S(2)}) collective-permute-start(s32[12]{0:T(128)S(1)} %copy-done.29), channel_id=1, source_target_pairs={{0,1},{1,0},{2,3},{3,2},{4,5},{5,4},{6,7},{7,6},{8,9},{9,8},{10,11... | collective-permute-start | bytes 152 | tf_op jit(solution)/shard_map/ppermute | solution.py:273
  23.0 11.0 %copy-start.8 = (bf16[1024,768]{1,0:T(8,128)(2,1)}, bf16[1024,768]{1,0:T(8,128)(2,1)S(1)}, u32[]{:S(2)}) copy-start(bf16[1024,768]{1,0:T(8,128)(2,1)S(1)} %get-tuple-element.118.refs_5_) | copy-start | bytes 4718596
  23.0 11.0 %copy-start.11 = (bf16[1024,768]{1,0:T(8,128)(2,1)}, bf16[1024,768]{1,0:T(8,128)(2,1)S(1)}, u32[]{:S(2)}) copy-start(bf16[1024,768]{1,0:T(8,128)(2,1)S(1)} %get-tuple-element.119.refs_6_) | copy-start | bytes 4718596
  27.1 12.5 %copy-start.23 = (bf16[1024,256]{1,0:T(8,128)(2,1)}, bf16[1024,256]{1,0:T(8,128)(2,1)S(1)}, u32[]{:S(2)}) copy-start(bf16[1024,256]{1,0:T(8,128)(2,1)S(1)} %get-tuple-element.133.refs_9_) | copy-start | bytes 1572868
  27.1 12.5 %copy-start.30 = (s32[12]{0:T(128)}, s32[12]{0:T(128)S(1)}, u32[]{:S(2)}) copy-start(s32[12]{0:T(128)S(1)} %collective-permute-done.refs_2_) | copy-start | bytes 148
  41.1 15.2 %collective-permute-start.7 = (bf16[1024,256]{1,0:T(8,128)(2,1)}, bf16[1024,256]{1,0:T(8,128)(2,1)}, u32[]{:S(2)}, u32[]{:S(2)}) collective-permute-start(bf16[1024,256]{1,0:T(8,128)(2,1)} %get-tuple-element.126), channel_id=1, source_target_pairs={{0,4},{1,5},{2,6},{3,7},{4,0},{5,1},{6,2},{7,3},{8,12},{9,13},{10,... | collective-permute-start | bytes 1572872 | tf_op jit(solution)/shard_map/ppermute | solution.py:273
  42.4 22.3 %collective-permute-start.9 = (bf16[768,256]{1,0:T(8,128)(2,1)}, bf16[768,256]{1,0:T(8,128)(2,1)S(1)}, u32[]{:S(2)}, u32[]{:S(2)}) collective-permute-start(bf16[768,256]{1,0:T(8,128)(2,1)} %get-tuple-element.131), channel_id=1, source_target_pairs={{14,0},{15,1},{0,2},{1,3},{2,4},{3,5},{4,6},{5,7},{6,8},{7,9},{8,1... | collective-permute-start | bytes 1179656 | tf_op jit(solution)/shard_map/ppermute | solution.py:268
  43.0 21.7 %collective-permute-start.10 = (bf16[768,256]{1,0:T(8,128)(2,1)}, bf16[768,256]{1,0:T(8,128)(2,1)}, u32[]{:S(2)}, u32[]{:S(2)}) collective-permute-start(bf16[768,256]{1,0:T(8,128)(2,1)} %get-tuple-element.132), channel_id=1, source_target_pairs={{2,0},{3,1},{4,2},{5,3},{6,4},{7,5},{8,6},{9,7},{10,8},{11,9},{12,... | collective-permute-start | bytes 1179656 | tf_op jit(solution)/shard_map/ppermute | solution.py:268
  48.5 7.8 %copy-start.18 = (f32[1024,256]{1,0:T(8,128)S(1)}, f32[1024,256]{1,0:T(8,128)}, u32[]{:S(2)}) copy-start(f32[1024,256]{1,0:T(8,128)} %copy-done.17) | copy-start | bytes 3145732
  48.5 16.2 %copy-start.6 = (bf16[1024,768]{1,0:T(8,128)(2,1)S(1)}, bf16[1024,768]{1,0:T(8,128)(2,1)}, u32[]{:S(2)}) copy-start(bf16[1024,768]{1,0:T(8,128)(2,1)} %copy-done.5) | copy-start | bytes 4718596
  48.5 16.2 %copy-start.9 = (bf16[1024,768]{1,0:T(8,128)(2,1)S(1)}, bf16[1024,768]{1,0:T(8,128)(2,1)}, u32[]{:S(2)}) copy-start(bf16[1024,768]{1,0:T(8,128)(2,1)} %copy-done.8) | copy-start | bytes 4718596
  52.8 20.8 %copy-start.21 = (bf16[1024,256]{1,0:T(8,128)(2,1)}, bf16[1024,256]{1,0:T(8,128)(2,1)S(1)}, u32[]{:S(2)}) copy-start(bf16[1024,256]{1,0:T(8,128)(2,1)S(1)} %get-tuple-element.143.refs_9_) | copy-start | bytes 1572868
  52.8 11.9 %copy-start.3 = (bf16[1024,768]{1,0:T(8,128)(2,1)S(1)}, bf16[1024,768]{1,0:T(8,128)(2,1)}, u32[]{:S(2)}) copy-start(bf16[1024,768]{1,0:T(8,128)(2,1)} %copy-done.2) | copy-start | bytes 4718596
  52.8 11.9 %copy-start.31 = (s32[12]{0:T(128)S(1)}, s32[12]{0:T(128)}, u32[]{:S(2)}) copy-start(s32[12]{0:T(128)} %copy-done.30) | copy-start | bytes 148
  58.0 15.6 %copy-start.19 = (f32[512,256]{1,0:T(8,128)}, f32[512,256]{1,0:T(8,128)S(1)}, u32[]{:S(2)}) copy-start(f32[512,256]{1,0:T(8,128)S(1)} %get-tuple-element.129) | copy-start | bytes 1572868
  64.7 1.4 copy-start.12
  75.1 31.1 %collective-permute-start.15 = (bf16[1024,256]{1,0:T(8,128)(2,1)}, bf16[1024,256]{1,0:T(8,128)(2,1)}, u32[]{:S(2)}, u32[]{:S(2)}) collective-permute-start(bf16[1024,256]{1,0:T(8,128)(2,1)} %get-tuple-element.145), channel_id=1, source_target_pairs={{0,4},{1,5},{2,6},{3,7},{4,0},{5,1},{6,2},{7,3},{8,12},{9,13},{10,... | collective-permute-start | bytes 1572872 | tf_op jit(solution)/shard_map/ppermute | solution.py:273
  75.1 9.6 %collective-permute-start.8 = (bf16[512,256]{1,0:T(8,128)(2,1)}, bf16[512,256]{1,0:T(8,128)(2,1)}, u32[]{:S(2)}, u32[]{:S(2)}) collective-permute-start(bf16[512,256]{1,0:T(8,128)(2,1)} %get-tuple-element.130), channel_id=1, source_target_pairs={{0,2},{1,3},{2,0},{3,1},{4,6},{5,7},{6,4},{7,5},{8,10},{9,11},{10,... | collective-permute-start | bytes 786440 | tf_op jit(solution)/shard_map/ppermute | solution.py:273
  75.2 33.5 %collective-permute-start.13 = (bf16[768,256]{1,0:T(8,128)(2,1)}, bf16[768,256]{1,0:T(8,128)(2,1)S(1)}, u32[]{:S(2)}, u32[]{:S(2)}) collective-permute-start(bf16[768,256]{1,0:T(8,128)(2,1)} %get-tuple-element.141), channel_id=1, source_target_pairs={{14,0},{15,1},{0,2},{1,3},{2,4},{3,5},{4,6},{5,7},{6,8},{7,9},{8,1... | collective-permute-start | bytes 1179656 | tf_op jit(solution)/shard_map/ppermute | solution.py:268
  77.2 31.5 %collective-permute-start.14 = (bf16[768,256]{1,0:T(8,128)(2,1)}, bf16[768,256]{1,0:T(8,128)(2,1)}, u32[]{:S(2)}, u32[]{:S(2)}) collective-permute-start(bf16[768,256]{1,0:T(8,128)(2,1)} %get-tuple-element.142), channel_id=1, source_target_pairs={{2,0},{3,1},{4,2},{5,3},{6,4},{7,5},{8,6},{9,7},{10,8},{11,9},{12,... | collective-permute-start | bytes 1179656 | tf_op jit(solution)/shard_map/ppermute | solution.py:268
  84.7 1.0 copy-start.20
  86.4 22.3 %copy-start.22 = (bf16[1024,256]{1,0:T(8,128)(2,1)S(1)}, bf16[1024,256]{1,0:T(8,128)(2,1)}, u32[]{:S(2)}) copy-start(bf16[1024,256]{1,0:T(8,128)(2,1)} %copy-done.21) | copy-start | bytes 1572868
  87.5 14.8 %collective-permute-start.11 = (bf16[256,256]{1,0:T(8,128)(2,1)S(1)}, bf16[256,256]{1,0:T(8,128)(2,1)S(1)}, u32[]{:S(2)}, u32[]{:S(2)}) collective-permute-start(bf16[256,256]{1,0:T(8,128)(2,1)S(1)} %get-tuple-element.137), channel_id=1, source_target_pairs={{0,8},{1,9},{2,10},{3,11},{4,12},{5,13},{6,14},{7,15},{8,0},{9,1},... | collective-permute-start | bytes 393224 | tf_op jit(solution)/shard_map/ppermute | solution.py:273
  102.2 6.5 %copy-start.13 = (bf16[1024,768]{1,0:T(8,128)(2,1)S(1)}, bf16[1024,768]{1,0:T(8,128)(2,1)}, u32[]{:S(2)}) copy-start(bf16[1024,768]{1,0:T(8,128)(2,1)} %copy-done.11) | copy-start | bytes 4718596
  103.1 5.6 %copy-start.7 = (bf16[1024,768]{1,0:T(8,128)(2,1)S(1)}, bf16[1024,768]{1,0:T(8,128)(2,1)}, u32[]{:S(2)}) copy-start(bf16[1024,768]{1,0:T(8,128)(2,1)} %copy-done.5) | copy-start | bytes 4718596
  103.1 5.6 %copy-start.10 = (bf16[1024,768]{1,0:T(8,128)(2,1)S(1)}, bf16[1024,768]{1,0:T(8,128)(2,1)}, u32[]{:S(2)}) copy-start(bf16[1024,768]{1,0:T(8,128)(2,1)} %copy-done.8) | copy-start | bytes 4718596
  103.1 5.6 %copy-start.32 = (s32[12]{0:T(128)S(1)}, s32[12]{0:T(128)}, u32[]{:S(2)}) copy-start(s32[12]{0:T(128)} %copy-done.30) | copy-start | bytes 148
  106.2 2.6 %copy-start.4 = (bf16[1024,768]{1,0:T(8,128)(2,1)S(1)}, bf16[1024,768]{1,0:T(8,128)(2,1)}, u32[]{:S(2)}) copy-start(bf16[1024,768]{1,0:T(8,128)(2,1)} %copy-done.2) | copy-start | bytes 4718596
  106.2 1.3 copy-start.16
  108.7 13.9 %copy-start.28 = (s32[20,4]{1,0:T(8,128)S(1)}, s32[20,4]{1,0:T(8,128)}, u32[]{:S(2)}) copy-start(s32[20,4]{1,0:T(8,128)} %copy-done.25) | copy-start | bytes 964
  114.1 25.9 %collective-permute-start.18 = (bf16[1024,256]{1,0:T(8,128)(2,1)S(1)}, bf16[1024,256]{1,0:T(8,128)(2,1)S(1)}, u32[]{:S(2)}, u32[]{:S(2)}) collective-permute-start(bf16[1024,256]{1,0:T(8,128)(2,1)S(1)} %get-tuple-element.157), channel_id=1, source_target_pairs={{0,4},{1,5},{2,6},{3,7},{4,0},{5,1},{6,2},{7,3},{8,12},{9,13},{10,... | collective-permute-start | bytes 1572872 | tf_op jit(solution)/shard_map/ppermute | solution.py:273
  114.1 13.3 %collective-permute-start.19 = (bf16[512,256]{1,0:T(8,128)(2,1)S(1)}, bf16[512,256]{1,0:T(8,128)(2,1)S(1)}, u32[]{:S(2)}, u32[]{:S(2)}) collective-permute-start(bf16[512,256]{1,0:T(8,128)(2,1)S(1)} %get-tuple-element.159), channel_id=1, source_target_pairs={{0,2},{1,3},{2,0},{3,1},{4,6},{5,7},{6,4},{7,5},{8,10},{9,11},{10,... | collective-permute-start | bytes 786440 | tf_op jit(solution)/shard_map/ppermute | solution.py:273
  116.5 17.3 %collective-permute-start.21 = (bf16[768,128]{1,0:T(8,128)(2,1)S(1)}, bf16[768,128]{1,0:T(8,128)(2,1)S(1)}, u32[]{:S(2)}, u32[]{:S(2)}) collective-permute-start(bf16[768,128]{1,0:T(8,128)(2,1)S(1)} %get-tuple-element.163), channel_id=1, source_target_pairs={{14,0},{15,1},{0,2},{1,3},{2,4},{3,5},{4,6},{5,7},{6,8},{7,9},{8,1... | collective-permute-start | bytes 589832 | tf_op jit(solution)/shard_map/ppermute | solution.py:268
  116.6 5.3 %collective-permute-start.12 = (f32[128,256]{1,0:T(8,128)S(1)}, f32[128,256]{1,0:T(8,128)S(1)}, u32[]{:S(2)}, u32[]{:S(2)}) collective-permute-start(f32[128,256]{1,0:T(8,128)S(1)} %get-tuple-element.139), channel_id=1, source_target_pairs={{0,1},{1,0},{2,3},{3,2},{4,5},{5,4},{6,7},{7,6},{8,9},{9,8},{10,11... | collective-permute-start | bytes 393224 | tf_op jit(solution)/shard_map/ppermute | solution.py:273
  116.6 17.4 %collective-permute-start.22 = (bf16[768,128]{1,0:T(8,128)(2,1)S(1)}, bf16[768,128]{1,0:T(8,128)(2,1)S(1)}, u32[]{:S(2)}, u32[]{:S(2)}) collective-permute-start(bf16[768,128]{1,0:T(8,128)(2,1)S(1)} %get-tuple-element.164), channel_id=1, source_target_pairs={{2,0},{3,1},{4,2},{5,3},{6,4},{7,5},{8,6},{9,7},{10,8},{11,9},{12,... | collective-permute-start | bytes 589832 | tf_op jit(solution)/shard_map/ppermute | solution.py:268
  127.5 12.5 %collective-permute-start.20 = (bf16[256,256]{1,0:T(8,128)(2,1)S(1)}, bf16[256,256]{1,0:T(8,128)(2,1)S(1)}, u32[]{:S(2)}, u32[]{:S(2)}) collective-permute-start(bf16[256,256]{1,0:T(8,128)(2,1)S(1)} %get-tuple-element.162), channel_id=1, source_target_pairs={{0,8},{1,9},{2,10},{3,11},{4,12},{5,13},{6,14},{7,15},{8,0},{9,1},... | collective-permute-start | bytes 393224 | tf_op jit(solution)/shard_map/ppermute | solution.py:273
  129.2 13.8 %collective-permute-start.16 = (bf16[768,128]{1,0:T(8,128)(2,1)S(1)}, bf16[768,128]{1,0:T(8,128)(2,1)S(1)}, u32[]{:S(2)}, u32[]{:S(2)}) collective-permute-start(bf16[768,128]{1,0:T(8,128)(2,1)S(1)} %get-tuple-element.153), channel_id=1, source_target_pairs={{14,0},{15,1},{0,2},{1,3},{2,4},{3,5},{4,6},{5,7},{6,8},{7,9},{8,1... | collective-permute-start | bytes 589832 | tf_op jit(solution)/shard_map/ppermute | solution.py:268
  133.8 9.2 %collective-permute-start.17 = (bf16[768,128]{1,0:T(8,128)(2,1)S(1)}, bf16[768,128]{1,0:T(8,128)(2,1)S(1)}, u32[]{:S(2)}, u32[]{:S(2)}) collective-permute-start(bf16[768,128]{1,0:T(8,128)(2,1)S(1)} %get-tuple-element.154), channel_id=1, source_target_pairs={{2,0},{3,1},{4,2},{5,3},{6,4},{7,5},{8,6},{9,7},{10,8},{11,9},{12,... | collective-permute-start | bytes 589832 | tf_op jit(solution)/shard_map/ppermute | solution.py:268
  138.3 13.1 %collective-permute-start.24 = (bf16[1024,128]{1,0:T(8,128)(2,1)S(1)}, bf16[1024,128]{1,0:T(8,128)(2,1)S(1)}, u32[]{:S(2)}, u32[]{:S(2)}) collective-permute-start(bf16[1024,128]{1,0:T(8,128)(2,1)S(1)} %get-tuple-element.173), channel_id=1, source_target_pairs={{0,4},{1,5},{2,6},{3,7},{4,0},{5,1},{6,2},{7,3},{8,12},{9,13},{10,... | collective-permute-start | bytes 786440 | tf_op jit(solution)/shard_map/ppermute | solution.py:273
  140.2 11.4 %collective-permute-start.27 = (bf16[512,256]{1,0:T(8,128)(2,1)S(1)}, bf16[512,256]{1,0:T(8,128)(2,1)S(1)}, u32[]{:S(2)}, u32[]{:S(2)}) collective-permute-start(bf16[512,256]{1,0:T(8,128)(2,1)S(1)} %get-tuple-element.184), channel_id=1, source_target_pairs={{0,2},{1,3},{2,0},{3,1},{4,6},{5,7},{6,4},{7,5},{8,10},{9,11},{10,... | collective-permute-start | bytes 786440 | tf_op jit(solution)/shard_map/ppermute | solution.py:273
  143.1 7.7 %collective-permute-start.25 = (f32[128,256]{1,0:T(8,128)S(1)}, f32[128,256]{1,0:T(8,128)S(1)}, u32[]{:S(2)}, u32[]{:S(2)}) collective-permute-start(f32[128,256]{1,0:T(8,128)S(1)} %get-tuple-element.174), channel_id=1, source_target_pairs={{0,1},{1,0},{2,3},{3,2},{4,5},{5,4},{6,7},{7,6},{8,9},{9,8},{10,11... | collective-permute-start | bytes 393224 | tf_op jit(solution)/shard_map/ppermute | solution.py:273
  147.4 10.3 %collective-permute-start.23 = (bf16[1024,128]{1,0:T(8,128)(2,1)S(1)}, bf16[1024,128]{1,0:T(8,128)(2,1)S(1)}, u32[]{:S(2)}, u32[]{:S(2)}) collective-permute-start(bf16[1024,128]{1,0:T(8,128)(2,1)S(1)} %get-tuple-element.171), channel_id=1, source_target_pairs={{0,4},{1,5},{2,6},{3,7},{4,0},{5,1},{6,2},{7,3},{8,12},{9,13},{10,... | collective-permute-start | bytes 786440 | tf_op jit(solution)/shard_map/ppermute | solution.py:273
  151.5 5.0 %collective-permute-start.26 = (bf16[512,128]{1,0:T(8,128)(2,1)S(1)}, bf16[512,128]{1,0:T(8,128)(2,1)S(1)}, u32[]{:S(2)}, u32[]{:S(2)}) collective-permute-start(bf16[512,128]{1,0:T(8,128)(2,1)S(1)} %get-tuple-element.182), channel_id=1, source_target_pairs={{0,2},{1,3},{2,0},{3,1},{4,6},{5,7},{6,4},{7,5},{8,10},{9,11},{10,... | collective-permute-start | bytes 393224 | tf_op jit(solution)/shard_map/ppermute | solution.py:273
  151.6 10.5 %collective-permute-start.29 = (bf16[256,256]{1,0:T(8,128)(2,1)S(1)}, bf16[256,256]{1,0:T(8,128)(2,1)S(1)}, u32[]{:S(2)}, u32[]{:S(2)}) collective-permute-start(bf16[256,256]{1,0:T(8,128)(2,1)S(1)} %get-tuple-element.191), channel_id=1, source_target_pairs={{0,8},{1,9},{2,10},{3,11},{4,12},{5,13},{6,14},{7,15},{8,0},{9,1},... | collective-permute-start | bytes 393224 | tf_op jit(solution)/shard_map/ppermute | solution.py:273
  156.6 5.6 %collective-permute-start.30 = (bf16[256,128]{1,0:T(8,128)(2,1)S(1)}, bf16[256,128]{1,0:T(8,128)(2,1)S(1)}, u32[]{:S(2)}, u32[]{:S(2)}) collective-permute-start(bf16[256,128]{1,0:T(8,128)(2,1)S(1)} %get-tuple-element.193), channel_id=1, source_target_pairs={{0,8},{1,9},{2,10},{3,11},{4,12},{5,13},{6,14},{7,15},{8,0},{9,1},... | collective-permute-start | bytes 196616 | tf_op jit(solution)/shard_map/ppermute | solution.py:273
  157.7 5.0 %collective-permute-start.28 = (bf16[512,128]{1,0:T(8,128)(2,1)S(1)}, bf16[512,128]{1,0:T(8,128)(2,1)S(1)}, u32[]{:S(2)}, u32[]{:S(2)}) collective-permute-start(bf16[512,128]{1,0:T(8,128)(2,1)S(1)} %get-tuple-element.189), channel_id=1, source_target_pairs={{0,2},{1,3},{2,0},{3,1},{4,6},{5,7},{6,4},{7,5},{8,10},{9,11},{10,... | collective-permute-start | bytes 393224 | tf_op jit(solution)/shard_map/ppermute | solution.py:273
  162.2 4.5 %collective-permute-start.32 = (f32[128,256]{1,0:T(8,128)S(1)}, f32[128,256]{1,0:T(8,128)S(1)}, u32[]{:S(2)}, u32[]{:S(2)}) collective-permute-start(f32[128,256]{1,0:T(8,128)S(1)} %get-tuple-element.199), channel_id=1, source_target_pairs={{0,1},{1,0},{2,3},{3,2},{4,5},{5,4},{6,7},{7,6},{8,9},{9,8},{10,11... | collective-permute-start | bytes 393224 | tf_op jit(solution)/shard_map/ppermute | solution.py:273
  162.2 3.1 %collective-permute-start.33 = (f32[128,128]{1,0:T(8,128)S(1)}, f32[128,128]{1,0:T(8,128)S(1)}, u32[]{:S(2)}, u32[]{:S(2)}) collective-permute-start(f32[128,128]{1,0:T(8,128)S(1)} %get-tuple-element.201), channel_id=1, source_target_pairs={{0,1},{1,0},{2,3},{3,2},{4,5},{5,4},{6,7},{7,6},{8,9},{9,8},{10,11... | collective-permute-start | bytes 196616 | tf_op jit(solution)/shard_map/ppermute | solution.py:273
  162.8 5.9 %collective-permute-start.31 = (bf16[256,128]{1,0:T(8,128)(2,1)S(1)}, bf16[256,128]{1,0:T(8,128)(2,1)S(1)}, u32[]{:S(2)}, u32[]{:S(2)}) collective-permute-start(bf16[256,128]{1,0:T(8,128)(2,1)S(1)} %get-tuple-element.198), channel_id=1, source_target_pairs={{0,8},{1,9},{2,10},{3,11},{4,12},{5,13},{6,14},{7,15},{8,0},{9,1},... | collective-permute-start | bytes 196616 | tf_op jit(solution)/shard_map/ppermute | solution.py:273
  168.8 1.3 collective-permute-start.34
  (9 other events, 7.1 us)

commit v4 on v3

v4 whole, which is shorter than its diff:
```python
import jax
import jax.numpy as jnp
from jax import lax
from jax.experimental import pallas as pl
from jax.experimental.pallas import tpu as pltpu
from jax.sharding import PartitionSpec as P

CLASSES = 5
UNITS = (3, 3, 2)
LIMIT = 16 * 2**20
COVER = 10**11
ANY = pl.BlockSpec(memory_space=pl.ANY)
BF16, F32 = jnp.bfloat16, jnp.float32
NEXT = ((0, 0), (1, 0), (1, 1))
BEFORE = ((0, 3), (0, 4), (1, 4))
HERE = ((0, 1), (0, 2), (1, 2), (1, 3))
FOUND = ((0, 2, 7, 9, 4), (1, 6, 8, 3, 5))


def call(body, scalars, arrays, after, out_shape, scratch=(), flops=10**11):
    lead = len(scalars) + len(arrays)
    extra = len(after)
    outs = len(out_shape)

    def kernel(*refs):
        rest = refs[lead + extra :]
        body(*refs[:lead], *rest[:outs], *rest[outs + 1 :])

    kernel.__name__ = body.__name__
    vmem = pl.BlockSpec(memory_space=pltpu.VMEM)
    return pl.pallas_call(
        kernel,
        out_shape=[*out_shape, jax.ShapeDtypeStruct((8, 128), F32)],
        in_specs=[pl.BlockSpec(memory_space=pltpu.SMEM)] * len(scalars) + [vmem] * len(arrays) + [ANY] * extra,
        out_specs=[vmem] * outs + [ANY],
        scratch_shapes=scratch,
        compiler_params=pltpu.CompilerParams(vmem_limit_bytes=LIMIT),
        cost_estimate=pl.CostEstimate(flops=flops, bytes_accessed=1, transcendentals=0),
        name=body.__name__,
    )(*scalars, *arrays, *after)


def coupled(core, blocks, acoustic, coupling, at, width, after):
    slots, rows, depth = coupling[0].shape
    per = slots // CLASSES
    nodes, modes = acoustic[0].shape
    lists = (NEXT, BEFORE, HERE)

    def coupled_rows(core_ref, own_blocks, far_blocks, own_a, far_a, own_c, far_c, *refs):
        outs, both, picked = refs[:3], refs[3], refs[4]
        core = core_ref[0]
        columns = pl.ds(pl.multiple_of(core * (modes // 2) + at, 128), width)
        both[pl.ds(pl.multiple_of(core * nodes, nodes), nodes), :] = own_a[:, columns]
        both[pl.ds(pl.multiple_of((1 - core) * nodes, nodes), nodes), :] = far_a[:, columns]
        for out, pairs in zip(outs, lists):
            for place, (face, k) in enumerate(pairs):
                own = core == face
                for s in range(per):
                    slot = k * per + s
                    for n in range(depth // rows):
                        block = jnp.where(own, own_blocks[slot, n], far_blocks[slot, n])
                        first = pl.multiple_of(face * nodes + block * rows, rows)
                        picked[n * rows : (n + 1) * rows, :] = both[pl.ds(first, rows), :]
                    weights = jnp.where(own, own_c[slot], far_c[slot])
                    row = (place * per + s) * rows
                    out[row : row + rows, :] = jnp.dot(
                        weights, picked[...], preferred_element_type=F32
                    ).astype(BF16)

    shapes = [(len(pairs) * per * rows, width) for pairs in lists]
    return call(
        coupled_rows,
        [core, *blocks],
        [*acoustic, *coupling],
        after,
        [jax.ShapeDtypeStruct(shape, BF16) for shape in shapes],
        [pltpu.VMEM((2 * nodes, width), BF16), pltpu.VMEM((depth, width), BF16)],
    )


def turned(side, bit, struct_modes, share, after):
    depth, modes = struct_modes.shape
    half = modes // 2
    low = 2**bit

    def turn(side_ref, in_ref, kept_out, sent_out):
        for which, out in ((side_ref[0], kept_out), (1 - side_ref[0], sent_out)):
            for i in range(half // share):
                column = (i // low * 2 * low + i % low + which * low) * share
                block = in_ref[:, pl.ds(pl.multiple_of(column, share), share)]
                out[i * share : (i + 1) * share, :] = block.T

    if share % 128:
        sides = struct_modes.T.reshape(-1, 2, low * share, depth)
        pair = [
            lax.dynamic_index_in_dim(sides, one, 1, keepdims=False).reshape(half, depth)
            for one in (side[0], 1 - side[0])
        ]
        return [*pair, after[0]]
    return call(turn, [side], [struct_modes], after, [jax.ShapeDtypeStruct((half, depth), BF16)] * 2)


def rows_times(left_own, left_far, picked, out):
    tall, depth = left_own.shape
    tile = min(tall, 256)

    @pl.loop(0, tall // tile)
    def _(i):
        here = pl.ds(pl.multiple_of(i * tile, tile), tile)
        product = jnp.dot(left_own[here, :], picked[:depth, :], preferred_element_type=F32)
        product += jnp.dot(left_far[here, :], picked[depth:, :], preferred_element_type=F32)
        out[here, :] = product.astype(out.dtype)


def panel_sent(core, shifts, lefts, pieces, after):
    tall, depth = lefts[0].shape
    width = pieces[0].shape[1]
    count = shifts[0].shape[0]
    rows = depth // count
    per = pieces[0].shape[0] // len(NEXT) // rows

    def panel_away(core_ref, own_shift, far_shift, own, far, *refs):
        parts, sent, picked = refs[:3], refs[3], refs[4]
        for half, shift in enumerate((own_shift, far_shift)):
            first_core = core_ref[0] == half
            seen = [jnp.int32(0)] * CLASSES
            for b in range(count):
                kind = shift[b]
                slot = jnp.int32(0)
                for k in range(CLASSES):
                    group = jnp.where(first_core, FOUND[0][k], FOUND[1][k])
                    slot = jnp.where(kind == k, group * per + seen[k], slot)
                    seen[k] = seen[k] + (kind == k).astype(jnp.int32)
                row = (half * count + b) * rows
                base = 0
                for part in parts:
                    many = part.shape[0] // rows

                    @pl.when((slot >= base) & (slot < base + many))
                    def _(part=part, row=row, slot=slot, base=base):
                        first = pl.multiple_of((slot - base) * rows, rows)
                        picked[row : row + rows, :] = part[pl.ds(first, rows), :]

                    base += many
        rows_times(own, far, picked, sent)

    return call(
        panel_away,
        [core, *shifts],
        [*lefts, *pieces],
        after,
        [jax.ShapeDtypeStruct((tall, width), BF16), jax.ShapeDtypeStruct((2 * depth, width), BF16)],
        flops=COVER,
    )


def panel_kept(lefts, picked, after):
    def panel_own(own, far, picked_ref, kept):
        rows_times(own, far, picked_ref, kept)

    shape = (lefts[0].shape[0], picked.shape[1])
    return call(panel_own, [], [*lefts, picked], after, [jax.ShapeDtypeStruct(shape, F32)])


def added(held, got, here, before, wire, after):
    width = held.shape[1]
    shape = (before, 2, held.shape[0] // before // 2, width)
    tall = shape[2]

    def added_split(here_ref, held_ref, got_ref, kept_ref, away_ref):
        side = here_ref[0]
        for i in range(before):
            at = slice(i * tall, (i + 1) * tall)
            kept_ref[at, :] = held_ref[i, side] + got_ref[i, side].astype(F32)
            away_ref[at, :] = (held_ref[i, 1 - side] + got_ref[i, 1 - side].astype(F32)).astype(wire)

    out = (before * tall, width)
    return call(
        added_split,
        [here],
        [held.reshape(shape), got.reshape(shape)],
        after,
        [jax.ShapeDtypeStruct(out, F32), jax.ShapeDtypeStruct(out, wire)],
    )


def together(core, own, far, starts, modes):
    rows = own[0].shape[0]

    def put_together(core_ref, *refs):
        out = refs[-1]
        for half, blocks in enumerate((refs[: len(own)], refs[len(own) : -1])):
            side = core_ref[0] if half == 0 else 1 - core_ref[0]
            for at, block in zip(starts, blocks):
                first = pl.multiple_of(side * (modes // 2) + at, 128)
                out[:, pl.ds(first, block.shape[1])] = block[...]

    out, _ = call(put_together, [core], [*own, *far], [], [jax.ShapeDtypeStruct((rows, modes), F32)])
    return out


def passed_along(block, distance):
    size = lax.axis_size("mesh")
    return lax.ppermute(block, "mesh", [((i - distance) % size, i) for i in range(size)])


def swapped(block, bit):
    size = lax.axis_size("mesh")
    return lax.ppermute(block, "mesh", [(i, i ^ (1 << bit)) for i in range(size)])


def planned(levels):
    steps, arrived, issued = [], 10.0, [0.0, 0.0]
    for j, units in enumerate(UNITS):
        size = units / 2
        arrived += 20.0 * size
        steps.append((max(issued[j] - 4.0, 0.0), "coupled", j))
        steps.append((arrived, "panel", j))
        at = arrived + 4.0
        for level in range(1, levels + 1):
            at += (2.0 + 12.0 * size) if level == 1 else (2.0 + 7.0 * size)
            steps.append((at, level, j))
        issued.append(arrived)
    return [step[1:] for step in sorted(steps, key=lambda step: step[0])]


def per_device(struct_modes, acoustic_modes, coupling, face_shift, face_blocks):
    size = lax.axis_size("mesh")
    me = lax.axis_index("mesh")
    modes = acoustic_modes.shape[1]
    share = struct_modes.shape[1] // size
    bits = list(range(1, size.bit_length() - 1))
    order = [2, 1, *bits[2:]]
    levels = len(order)
    widths = [units * (modes // 2 // sum(UNITS)) for units in UNITS]
    starts = [sum(widths[:j]) for j in range(len(widths))]

    def bit_of(bit):
        return ((me >> bit) & 1).reshape(1)

    core = bit_of(0)
    token = []
    blocks = (face_blocks, swapped(face_blocks, 0))
    couplings = (coupling, swapped(coupling, 0))
    acoustics = (acoustic_modes, swapped(acoustic_modes, 0))
    far_struct = swapped(struct_modes, 0)
    shifts = (face_shift, swapped(face_shift, 0))
    lefts = []

    state = [dict(bits=sorted([0, *order[1:]], reverse=True)) for _ in widths]
    for stage, j in planned(levels):
        now = state[j]
        if stage == "coupled":
            ahead, behind, here, last = coupled(
                core, blocks, acoustics, couplings, starts[j], widths[j], token
            )
            now["pieces"] = [passed_along(ahead, 2), passed_along(behind, -2), here]
            token = [last]
            for one in (struct_modes, far_struct) if not lefts else ():
                *pair, last = turned(bit_of(order[0]), order[0], one, share, token)
                lefts.append(pair)
                token = [last]
        elif stage == "panel":
            kept, sent = zip(*lefts)
            away, picked, last = panel_sent(core, shifts, sent, now["pieces"], token)
            now["got"] = swapped(away, order[0])
            now["held"], last = panel_kept(kept, picked, [last])
            token = [last]
        else:
            bit = order[stage] if stage < levels else 0
            place = now["bits"].index(bit)
            now["bits"].remove(bit)
            wire = BF16 if stage < min(levels, 3) else F32
            now["held"], away, last = added(
                now["held"], now["got"], bit_of(bit), 2**place, wire, token
            )
            now["got"] = swapped(away, bit)
            token = [last]
    return together(
        core, [now["held"] for now in state], [now["got"] for now in state], starts, modes
    )


def solution(mesh):
    placed = (
        P(("member", "mesh"), None),
        P(("member", "mesh"), None),
        P("mesh", None, None),
        P("mesh"),
        P("mesh", None),
    )
    return jax.shard_map(
        per_device,
        mesh=mesh,
        in_specs=placed,
        out_specs=P(("member", "mesh"), None),
        check_vma=False,
    )
```

time: 172 us -> 162 us (0.942)
  waiting for transfers between devices: 42.1 us -> 100 us
  starting transfers between devices: 50.2 us -> 19.7 us
  Pallas kernels: 63.4 us -> 37.7 us
  local copies, waits for them, and re-layouts: 14.5 us -> 3.48 us
    ppermute x25 -> x17, waiting for transfers between devices: 24.9 us -> 63.1 us  [swapped(): return lax.ppermute(block, 'mesh', [(i, i ^ 1 << bit) for i in range(size)])]
    pallas_call x38 -> x21, Pallas kernels: 63.4 us -> 37.7 us  [call(): pl.pallas_call(kernel, out_shape=[*out_shape, jax.ShapeDtypeStruct((8, 12...]
    ppermute x25 -> x17, starting transfers between devices: 28.1 us -> 6.59 us  [swapped(): return lax.ppermute(block, 'mesh', [(i, i ^ 1 << bit) for i in range(size)])]
    ppermute x10 -> x6, waiting for transfers between devices: 17.3 us -> 37.2 us  [passed_along(): lax.ppermute(block, 'mesh', [((i - distance) % size, i) for i in range(si...]
    unnamed x77 -> x17, local copies, waits for them, and re-layouts: 14.5 us -> 3.48 us
    ppermute x10 -> x6, starting transfers between devices: 22.2 us -> 13.1 us  [passed_along(): lax.ppermute(block, 'mesh', [((i - distance) % size, i) for i in range(si...]
  transfers between devices with their start and end apart: 35 -> 23, of which waited for: 14 -> 18; matrix products, arithmetic and copies ran while one was open for 0% -> 0% of each run, Pallas kernels for 27% -> 18%
where the time goes in v4:
time: 162 us; the launch traced here: 161 us
  waiting for transfers between devices  100 us (62%)
  Pallas kernels  37.7 us (23%)
  starting transfers between devices  19.7 us (12%)
  local copies, waits for them, and re-layouts  3.48 us (2%)
    ppermute x17, waiting for transfers between devices, swapped(): return lax.ppermute(block, 'mesh', [(i, i ^ 1 << bit) for i in range(size)])  63.1 us
    pallas_call x21, Pallas kernels, call(): pl.pallas_call(kernel, out_shape=[*out_shape, jax.ShapeDtypeStruct((8, 12...  37.7 us
    ppermute x6, waiting for transfers between devices, passed_along(): lax.ppermute(block, 'mesh', [((i - distance) % size, i) for i in range(si...  37.2 us
    ppermute x6, starting transfers between devices, passed_along(): lax.ppermute(block, 'mesh', [((i - distance) % size, i) for i in range(si...  13.1 us
    ppermute x17, starting transfers between devices, swapped(): return lax.ppermute(block, 'mesh', [(i, i ^ 1 << bit) for i in range(size)])  6.59 us
    unnamed x17, local copies, waits for them, and re-layouts  3.48 us
  transfers between devices with their start and end apart: 23, of which 18 were waited for; matrix products, arithmetic and copies ran while one was open for 0% of the time, Pallas kernels for 18%

profile of v4, /device:TPU:0, one launch (start us, length us, event | category | flops | bytes accessed | tf_op | source)
XLA Modules:
  0.0 161.3 jit_solution(3713530043015538798)
XLA Ops:
  0.0 0.5 collective-permute-start.1
  0.5 0.1 collective-permute-start.2
  0.5 0.8 copy.7.refs_1_
  1.3 0.5 collective-permute-start
  1.7 0.1 collective-permute-start.3
  1.8 0.5 collective-permute-start.4
  2.2 2.0 %collective-permute-done.refs_2_ = s32[20,4]{1,0:T(8,128)S(1)} collective-permute-done((s32[20,4]{1,0:T(8,128)S(1)}, s32[20,4]{1,0:T(8,128)S(1)}, u32[]{:S(2)}, u32[]{:S(2)}) %collective-permute-start) | collective-permute-done | bytes 352 | tf_op jit(solution)/shard_map/ppermute | solution.py:209
  4.3 2.1 %collective-permute-done.2.refs_6_ = bf16[20,64,256]{2,1,0:T(8,128)(2,1)S(1)} collective-permute-done((bf16[20,64,256]{2,1,0:T(8,128)(2,1)}, bf16[20,64,256]{2,1,0:T(8,128)(2,1)S(1)}, u32[]{:S(2)}, u32[]{:S(2)}) %collective-permute-start.2) | collective-permute-done | bytes 655392 | tf_op jit(solution)/shard_map/ppermute | solution.py:209
  6.3 0.0 collective-permute-done.1.refs_4_
  6.3 1.6 copy-done.1
  7.9 1.1 copy-done.3
  9.0 3.6 %coupled_rows.3 = (bf16[768,384]{1,0:T(8,128)(2,1)}, bf16[768,384]{1,0:T(8,128)(2,1)}, bf16[1024,384]{1,0:T(8,128)(2,1)S(1)}, f32[8,128]{1,0:T(8,128)S(1)}) custom-call(s32[1]{0:T(128)} %bitcast.refs_0_, s32[20,4]{1,0:T(8,128)S(1)} %copy.7.refs_1_, s32[20,4]{1,0:T(8,128)S(1)} %collective-permute-done.refs_2_, bf16[512,2048]{1,0:T(8,128)(2,1)S(1)} %copy-done.1, ...), custom_call_target="tpu_custom_call" | custom-call | flops 99999997952 | bytes 1 | tf_op jit(solution)/shard_map/coupled_rows/pallas_call | solution.py:31
  12.6 2.9 %collective-permute-start.5 = (bf16[768,384]{1,0:T(8,128)(2,1)}, bf16[768,384]{1,0:T(8,128)(2,1)}, u32[]{:S(2)}, u32[]{:S(2)}) collective-permute-start(bf16[768,384]{1,0:T(8,128)(2,1)} %get-tuple-element.71), channel_id=1, source_target_pairs={{14,0},{15,1},{0,2},{1,3},{2,4},{3,5},{4,6},{5,7},{6,8},{7,9},{8,1... | collective-permute-start | bytes 1769480 | tf_op jit(solution)/shard_map/ppermute | solution.py:204
  15.5 3.0 %collective-permute-start.6 = (bf16[768,384]{1,0:T(8,128)(2,1)}, bf16[768,384]{1,0:T(8,128)(2,1)}, u32[]{:S(2)}, u32[]{:S(2)}) collective-permute-start(bf16[768,384]{1,0:T(8,128)(2,1)} %get-tuple-element.72), channel_id=1, source_target_pairs={{2,0},{3,1},{4,2},{5,3},{6,4},{7,5},{8,6},{9,7},{10,8},{11,9},{12,... | collective-permute-start | bytes 1769480 | tf_op jit(solution)/shard_map/ppermute | solution.py:204
  18.6 0.9 turn.2
  19.4 0.0 collective-permute-done.3.refs_1_
  19.4 0.0 copy-start.2
  19.5 0.0 copy-start.4
  19.5 2.9 %turn.3 = (bf16[1024,768]{1,0:T(8,128)(2,1)S(1)}, bf16[1024,768]{1,0:T(8,128)(2,1)S(1)}, f32[8,128]{1,0:T(8,128)S(1)}) custom-call(s32[1]{0:T(128)} %bitcast.3.refs_0_, bf16[768,2048]{1,0:T(8,128)(2,1)} %collective-permute-done.3.refs_1_, f32[8,128]{1,0:T(8,128)S(1)} %get-tuple-element.67.refs_2_), custom_call_target="tpu_custom_call" | custom-call | flops 99999997952 | bytes 1 | tf_op jit(solution)/shard_map/turn/pallas_call | solution.py:31
  22.4 3.7 %coupled_rows.4 = (bf16[768,384]{1,0:T(8,128)(2,1)}, bf16[768,384]{1,0:T(8,128)(2,1)}, bf16[1024,384]{1,0:T(8,128)(2,1)S(1)}, f32[8,128]{1,0:T(8,128)S(1)}) custom-call(s32[1]{0:T(128)} %bitcast.refs_0_, s32[20,4]{1,0:T(8,128)S(1)} %copy.7.refs_1_, s32[20,4]{1,0:T(8,128)S(1)} %collective-permute-done.refs_2_, bf16[512,2048]{1,0:T(8,128)(2,1)S(1)} %copy-done.2, ...), custom_call_target="tpu_custom_call" | custom-call | flops 99999997952 | bytes 1 | tf_op jit(solution)/shard_map/coupled_rows/pallas_call | solution.py:31
  26.1 2.1 %coupled_rows.5 = (bf16[768,256]{1,0:T(8,128)(2,1)S(1)}, bf16[768,256]{1,0:T(8,128)(2,1)S(1)}, bf16[1024,256]{1,0:T(8,128)(2,1)S(1)}, f32[8,128]{1,0:T(8,128)S(1)}) custom-call(s32[1]{0:T(128)} %bitcast.refs_0_, s32[20,4]{1,0:T(8,128)S(1)} %copy.7.refs_1_, s32[20,4]{1,0:T(8,128)S(1)} %collective-permute-done.refs_2_, bf16[512,2048]{1,0:T(8,128)(2,1)S(1)} %copy-done.2, ...), custom_call_target="tpu_custom_call" | custom-call | flops 99999997952 | bytes 1 | tf_op jit(solution)/shard_map/coupled_rows/pallas_call | solution.py:31
  28.2 0.0 collective-permute-done.4.refs_2_
  28.2 13.2 %collective-permute-done.5.refs_5_ = bf16[768,384]{1,0:T(8,128)(2,1)} collective-permute-done((bf16[768,384]{1,0:T(8,128)(2,1)}, bf16[768,384]{1,0:T(8,128)(2,1)}, u32[]{:S(2)}, u32[]{:S(2)}) %collective-permute-start.5) | collective-permute-done | bytes 589856 | tf_op jit(solution)/shard_map/ppermute | solution.py:204
  41.4 2.2 %collective-permute-done.6.refs_6_ = bf16[768,384]{1,0:T(8,128)(2,1)} collective-permute-done((bf16[768,384]{1,0:T(8,128)(2,1)}, bf16[768,384]{1,0:T(8,128)(2,1)}, u32[]{:S(2)}, u32[]{:S(2)}) %collective-permute-start.6) | collective-permute-done | bytes 589856 | tf_op jit(solution)/shard_map/ppermute | solution.py:204
  43.6 4.3 %panel_away.3 = (bf16[1024,384]{1,0:T(8,128)(2,1)S(1)}, bf16[1536,384]{1,0:T(8,128)(2,1)S(1)}, f32[8,128]{1,0:T(8,128)S(1)}) custom-call(s32[1]{0:T(128)} %bitcast.refs_0_, s32[12]{0:T(128)S(1)} %copy-done.5, s32[12]{0:T(128)} %collective-permute-done.4.refs_2_, bf16[1024,768]{1,0:T(8,128)(2,1)S(1)} %get-tuple-element.69.refs_3_, ...), custom_call_target="tpu_custom_call" | custom-call | flops 99999997952 | bytes 1 | tf_op jit(solution)/shard_map/panel_away/pallas_call | solution.py:31
  47.8 1.3 collective-permute-start.7
  49.1 2.5 %collective-permute-start.10 = (bf16[768,384]{1,0:T(8,128)(2,1)}, bf16[768,384]{1,0:T(8,128)(2,1)}, u32[]{:S(2)}, u32[]{:S(2)}) collective-permute-start(bf16[768,384]{1,0:T(8,128)(2,1)} %get-tuple-element.85), channel_id=1, source_target_pairs={{2,0},{3,1},{4,2},{5,3},{6,4},{7,5},{8,6},{9,7},{10,8},{11,9},{12,... | collective-permute-start | bytes 1769480 | tf_op jit(solution)/shard_map/ppermute | solution.py:204
  51.7 2.3 %panel_own.3 = (f32[1024,384]{1,0:T(8,128)S(1)}, f32[8,128]{1,0:T(8,128)S(1)}) custom-call(bf16[1024,768]{1,0:T(8,128)(2,1)S(1)} %get-tuple-element.66.refs_0_, bf16[1024,768]{1,0:T(8,128)(2,1)S(1)} %get-tuple-element.68.refs_1_, bf16[1536,384]{1,0:T(8,128)(2,1)S(1)} %get-tuple-element.77.refs_2_, f32[8,128]{1,0:T(8,128)S(1)} %get-tuple-element.78.refs_3_), custom_call_target="tpu_custom_call" | custom-call | flops 99999997952 | bytes 1 | tf_op jit(solution)/shard_map/panel_own/pallas_call | solution.py:31
  53.9 14.4 %collective-permute-done.7 = bf16[1024,384]{1,0:T(8,128)(2,1)S(1)} collective-permute-done((bf16[1024,384]{1,0:T(8,128)(2,1)S(1)}, bf16[1024,384]{1,0:T(8,128)(2,1)S(1)}, u32[]{:S(2)}, u32[]{:S(2)}) %collective-permute-start.7) | collective-permute-done | bytes 786464 | tf_op jit(solution)/shard_map/ppermute | solution.py:209
  68.4 0.9 added_split.9
  69.3 9.7 %collective-permute-done.10.refs_6_ = bf16[768,384]{1,0:T(8,128)(2,1)} collective-permute-done((bf16[768,384]{1,0:T(8,128)(2,1)}, bf16[768,384]{1,0:T(8,128)(2,1)}, u32[]{:S(2)}, u32[]{:S(2)}) %collective-permute-start.10) | collective-permute-done | bytes 589856 | tf_op jit(solution)/shard_map/ppermute | solution.py:204
  78.9 2.3 %collective-permute-done.9.refs_5_ = bf16[768,384]{1,0:T(8,128)(2,1)} collective-permute-done((bf16[768,384]{1,0:T(8,128)(2,1)}, bf16[768,384]{1,0:T(8,128)(2,1)}, u32[]{:S(2)}, u32[]{:S(2)}) %collective-permute-start.9) | collective-permute-done | bytes 589856 | tf_op jit(solution)/shard_map/ppermute | solution.py:204
  81.2 5.1 %panel_away.4 = (bf16[1024,384]{1,0:T(8,128)(2,1)}, bf16[1536,384]{1,0:T(8,128)(2,1)S(1)}, f32[8,128]{1,0:T(8,128)S(1)}) custom-call(s32[1]{0:T(128)} %bitcast.refs_0_, s32[12]{0:T(128)S(1)} %copy-done.6, s32[12]{0:T(128)} %collective-permute-done.4.refs_2_, bf16[1024,768]{1,0:T(8,128)(2,1)S(1)} %get-tuple-element.69.refs_3_, ...), custom_call_target="tpu_custom_call" | custom-call | flops 99999997952 | bytes 1 | tf_op jit(solution)/shard_map/panel_away/pallas_call | solution.py:31
  86.4 2.3 %panel_own.4 = (f32[1024,384]{1,0:T(8,128)S(1)}, f32[8,128]{1,0:T(8,128)S(1)}) custom-call(bf16[1024,768]{1,0:T(8,128)(2,1)S(1)} %get-tuple-element.66.refs_0_, bf16[1024,768]{1,0:T(8,128)(2,1)S(1)} %get-tuple-element.68.refs_1_, bf16[1536,384]{1,0:T(8,128)(2,1)S(1)} %get-tuple-element.88.refs_2_, f32[8,128]{1,0:T(8,128)S(1)} %get-tuple-element.89.refs_3_), custom_call_target="tpu_custom_call" | custom-call | flops 99999997952 | bytes 1 | tf_op jit(solution)/shard_map/panel_own/pallas_call | solution.py:31
  88.7 0.4 collective-permute-done.8
  89.1 1.1 added_split.10
  90.2 0.8 collective-permute-start.11
  90.9 2.5 %collective-permute-start.13 = (bf16[768,256]{1,0:T(8,128)(2,1)S(1)}, bf16[768,256]{1,0:T(8,128)(2,1)S(1)}, u32[]{:S(2)}, u32[]{:S(2)}) collective-permute-start(bf16[768,256]{1,0:T(8,128)(2,1)S(1)} %get-tuple-element.97), channel_id=1, source_target_pairs={{14,0},{15,1},{0,2},{1,3},{2,4},{3,5},{4,6},{5,7},{6,8},{7,9},{8,1... | collective-permute-start | bytes 1179656 | tf_op jit(solution)/shard_map/ppermute | solution.py:204
  93.4 2.2 %collective-permute-start.14 = (bf16[768,256]{1,0:T(8,128)(2,1)S(1)}, bf16[768,256]{1,0:T(8,128)(2,1)S(1)}, u32[]{:S(2)}, u32[]{:S(2)}) collective-permute-start(bf16[768,256]{1,0:T(8,128)(2,1)S(1)} %get-tuple-element.98), channel_id=1, source_target_pairs={{2,0},{3,1},{4,2},{5,3},{6,4},{7,5},{8,6},{9,7},{10,8},{11,9},{12,... | collective-permute-start | bytes 1179656 | tf_op jit(solution)/shard_map/ppermute | solution.py:204
  95.7 1.3 collective-permute-start.12
  96.9 4.9 %collective-permute-done.11 = bf16[256,384]{1,0:T(8,128)(2,1)S(1)} collective-permute-done((bf16[256,384]{1,0:T(8,128)(2,1)S(1)}, bf16[256,384]{1,0:T(8,128)(2,1)S(1)}, u32[]{:S(2)}, u32[]{:S(2)}) %collective-permute-start.11) | collective-permute-done | bytes 196640 | tf_op jit(solution)/shard_map/ppermute | solution.py:209
  101.8 0.7 added_split.11
  102.5 7.6 %collective-permute-done.13.refs_5_ = bf16[768,256]{1,0:T(8,128)(2,1)S(1)} collective-permute-done((bf16[768,256]{1,0:T(8,128)(2,1)S(1)}, bf16[768,256]{1,0:T(8,128)(2,1)S(1)}, u32[]{:S(2)}, u32[]{:S(2)}) %collective-permute-start.13) | collective-permute-done | bytes 393248 | tf_op jit(solution)/shard_map/ppermute | solution.py:204
  110.1 2.2 %collective-permute-done.14.refs_6_ = bf16[768,256]{1,0:T(8,128)(2,1)S(1)} collective-permute-done((bf16[768,256]{1,0:T(8,128)(2,1)S(1)}, bf16[768,256]{1,0:T(8,128)(2,1)S(1)}, u32[]{:S(2)}, u32[]{:S(2)}) %collective-permute-start.14) | collective-permute-done | bytes 393248 | tf_op jit(solution)/shard_map/ppermute | solution.py:204
  112.3 2.8 %panel_away.5 = (bf16[1024,256]{1,0:T(8,128)(2,1)S(1)}, bf16[1536,256]{1,0:T(8,128)(2,1)S(1)}, f32[8,128]{1,0:T(8,128)S(1)}) custom-call(s32[1]{0:T(128)} %bitcast.refs_0_, s32[12]{0:T(128)S(1)} %copy-done.7, s32[12]{0:T(128)} %collective-permute-done.4.refs_2_, bf16[1024,768]{1,0:T(8,128)(2,1)S(1)} %get-tuple-element.69.refs_3_, ...), custom_call_target="tpu_custom_call" | custom-call | flops 99999997952 | bytes 1 | tf_op jit(solution)/shard_map/panel_away/pallas_call | solution.py:31
  115.1 1.5 panel_own.5
  116.6 8.1 %collective-permute-done.12 = bf16[1024,384]{1,0:T(8,128)(2,1)} collective-permute-done((bf16[1024,384]{1,0:T(8,128)(2,1)}, bf16[1024,384]{1,0:T(8,128)(2,1)}, u32[]{:S(2)}, u32[]{:S(2)}) %collective-permute-start.12) | collective-permute-done | bytes 786464 | tf_op jit(solution)/shard_map/ppermute | solution.py:209
  124.7 1.3 added_split.12
  126.0 0.9 collective-permute-start.15
  126.9 0.2 collective-permute-start.17
  127.1 8.3 %collective-permute-done.15 = bf16[512,384]{1,0:T(8,128)(2,1)S(1)} collective-permute-done((bf16[512,384]{1,0:T(8,128)(2,1)S(1)}, bf16[512,384]{1,0:T(8,128)(2,1)S(1)}, u32[]{:S(2)}, u32[]{:S(2)}) %collective-permute-start.15) | collective-permute-done | bytes 393248 | tf_op jit(solution)/shard_map/ppermute | solution.py:209
  135.3 0.1 added_split.13
  135.4 4.2 %collective-permute-done.17 = bf16[1024,256]{1,0:T(8,128)(2,1)S(1)} collective-permute-done((bf16[1024,256]{1,0:T(8,128)(2,1)S(1)}, bf16[1024,256]{1,0:T(8,128)(2,1)S(1)}, u32[]{:S(2)}, u32[]{:S(2)}) %collective-permute-start.17) | collective-permute-done | bytes 524320 | tf_op jit(solution)/shard_map/ppermute | solution.py:209
  139.6 0.1 added_split.14
  139.7 0.4 collective-permute-start.18
  140.2 6.0 %collective-permute-done.18 = bf16[512,256]{1,0:T(8,128)(2,1)S(1)} collective-permute-done((bf16[512,256]{1,0:T(8,128)(2,1)S(1)}, bf16[512,256]{1,0:T(8,128)(2,1)S(1)}, u32[]{:S(2)}, u32[]{:S(2)}) %collective-permute-start.18) | collective-permute-done | bytes 262176 | tf_op jit(solution)/shard_map/ppermute | solution.py:209
  146.2 0.1 added_split.15
  146.2 0.1 collective-permute-start.19
  146.3 8.8 %collective-permute-done.16 = bf16[256,384]{1,0:T(8,128)(2,1)S(1)} collective-permute-done((bf16[256,384]{1,0:T(8,128)(2,1)S(1)}, bf16[256,384]{1,0:T(8,128)(2,1)S(1)}, u32[]{:S(2)}, u32[]{:S(2)}) %collective-permute-start.16) | collective-permute-done | bytes 196640 | tf_op jit(solution)/shard_map/ppermute | solution.py:209
  155.2 0.1 collective-permute-start.21
  155.3 2.6 %collective-permute-done.19 = bf16[256,256]{1,0:T(8,128)(2,1)S(1)} collective-permute-done((bf16[256,256]{1,0:T(8,128)(2,1)S(1)}, bf16[256,256]{1,0:T(8,128)(2,1)S(1)}, u32[]{:S(2)}, u32[]{:S(2)}) %collective-permute-start.19) | collective-permute-done | bytes 131104 | tf_op jit(solution)/shard_map/ppermute | solution.py:209
  158.0 0.1 collective-permute-start.22
  158.1 1.3 collective-permute-done.22.refs_6_
  159.4 2.0 %put_together.1 = (f32[128,2048]{1,0:T(8,128)}, f32[8,128]{1,0:T(8,128)}) custom-call(s32[1]{0:T(128)} %bitcast.refs_0_, f32[128,384]{1,0:T(8,128)S(1)} %get-tuple-element.94.refs_1_, f32[128,384]{1,0:T(8,128)S(1)} %get-tuple-element.116.refs_2_, f32[128,256]{1,0:T(8,128)S(1)} %get-tuple-element.120.refs_3_, f32[128,384]{1,0:T(8,128)} %collective-permute-done.20.refs_4_, ...), custom_call_target="tpu_custom_call" | custom-call | flops 99999997952 | bytes 1 | tf_op jit(solution)/shard_map/put_together/pallas_call | solution.py:31
  (20 shorter events, 0.1 us)
Async XLA Ops:
  0.0 6.3 %collective-permute-start.1 = (bf16[512,2048]{1,0:T(8,128)(2,1)}, bf16[512,2048]{1,0:T(8,128)(2,1)S(1)}, u32[]{:S(2)}, u32[]{:S(2)}) collective-permute-start(bf16[512,2048]{1,0:T(8,128)(2,1)} %refs_3_.5), channel_id=1, source_target_pairs={{0,1},{1,0},{2,3},{3,2},{4,5},{5,4},{6,7},{7,6},{8,9},{9,8},{10,11... | collective-permute-start | bytes 6291464 | tf_op jit(solution)/shard_map/ppermute | solution.py:209
  0.5 5.9 %collective-permute-start.2 = (bf16[20,64,256]{2,1,0:T(8,128)(2,1)}, bf16[20,64,256]{2,1,0:T(8,128)(2,1)S(1)}, u32[]{:S(2)}, u32[]{:S(2)}) collective-permute-start(bf16[20,64,256]{2,1,0:T(8,128)(2,1)} %refs_5_.5), channel_id=1, source_target_pairs={{0,1},{1,0},{2,3},{3,2},{4,5},{5,4},{6,7},{7,6},{8,9},{9,8},{10,11... | collective-permute-start | bytes 1966088 | tf_op jit(solution)/shard_map/ppermute | solution.py:209
  1.3 3.0 %collective-permute-start = (s32[20,4]{1,0:T(8,128)S(1)}, s32[20,4]{1,0:T(8,128)S(1)}, u32[]{:S(2)}, u32[]{:S(2)}) collective-permute-start(s32[20,4]{1,0:T(8,128)S(1)} %copy.7.refs_1_), channel_id=1, source_target_pairs={{0,1},{1,0},{2,3},{3,2},{4,5},{5,4},{6,7},{7,6},{8,9},{9,8},{10,11... | collective-permute-start | bytes 968 | tf_op jit(solution)/shard_map/ppermute | solution.py:209
  1.7 17.7 %collective-permute-start.3 = (bf16[768,2048]{1,0:T(8,128)(2,1)}, bf16[768,2048]{1,0:T(8,128)(2,1)}, u32[]{:S(2)}, u32[]{:S(2)}) collective-permute-start(bf16[768,2048]{1,0:T(8,128)(2,1)} %refs_1_.7), channel_id=1, source_target_pairs={{0,1},{1,0},{2,3},{3,2},{4,5},{5,4},{6,7},{7,6},{8,9},{9,8},{10,11... | collective-permute-start | bytes 9437192 | tf_op jit(solution)/shard_map/ppermute | solution.py:209
  1.8 26.4 %collective-permute-start.4 = (s32[12]{0:T(128)}, s32[12]{0:T(128)}, u32[]{:S(2)}, u32[]{:S(2)}) collective-permute-start(s32[12]{0:T(128)} %refs_1_.10), channel_id=1, source_target_pairs={{0,1},{1,0},{2,3},{3,2},{4,5},{5,4},{6,7},{7,6},{8,9},{9,8},{10,11... | collective-permute-start | bytes 152 | tf_op jit(solution)/shard_map/ppermute | solution.py:209
  6.3 1.6 copy-start.1
  7.9 1.1 copy-start.3
  9.0 9.5 %copy-start = (bf16[768,2048]{1,0:T(8,128)(2,1)S(1)}, bf16[768,2048]{1,0:T(8,128)(2,1)}, u32[]{:S(2)}) copy-start(bf16[768,2048]{1,0:T(8,128)(2,1)} %refs_1_.7) | copy-start | bytes 9437188
  12.6 28.7 %collective-permute-start.5 = (bf16[768,384]{1,0:T(8,128)(2,1)}, bf16[768,384]{1,0:T(8,128)(2,1)}, u32[]{:S(2)}, u32[]{:S(2)}) collective-permute-start(bf16[768,384]{1,0:T(8,128)(2,1)} %get-tuple-element.71), channel_id=1, source_target_pairs={{14,0},{15,1},{0,2},{1,3},{2,4},{3,5},{4,6},{5,7},{6,8},{7,9},{8,1... | collective-permute-start | bytes 1769480 | tf_op jit(solution)/shard_map/ppermute | solution.py:204
  15.5 28.0 %collective-permute-start.6 = (bf16[768,384]{1,0:T(8,128)(2,1)}, bf16[768,384]{1,0:T(8,128)(2,1)}, u32[]{:S(2)}, u32[]{:S(2)}) collective-permute-start(bf16[768,384]{1,0:T(8,128)(2,1)} %get-tuple-element.72), channel_id=1, source_target_pairs={{2,0},{3,1},{4,2},{5,3},{6,4},{7,5},{8,6},{9,7},{10,8},{11,9},{12,... | collective-permute-start | bytes 1769480 | tf_op jit(solution)/shard_map/ppermute | solution.py:204
  19.4 3.0 %copy-start.2 = (bf16[512,2048]{1,0:T(8,128)(2,1)S(1)}, bf16[512,2048]{1,0:T(8,128)(2,1)}, u32[]{:S(2)}) copy-start(bf16[512,2048]{1,0:T(8,128)(2,1)} %refs_3_.5) | copy-start | bytes 6291460
  19.5 3.0 %copy-start.4 = (bf16[20,64,256]{2,1,0:T(8,128)(2,1)S(1)}, bf16[20,64,256]{2,1,0:T(8,128)(2,1)}, u32[]{:S(2)}) copy-start(bf16[20,64,256]{2,1,0:T(8,128)(2,1)} %refs_5_.5) | copy-start | bytes 1966084
  26.1 17.5 %copy-start.5 = (s32[12]{0:T(128)S(1)}, s32[12]{0:T(128)}, u32[]{:S(2)}) copy-start(s32[12]{0:T(128)} %refs_1_.10) | copy-start | bytes 148
  47.8 20.5 %collective-permute-start.7 = (bf16[1024,384]{1,0:T(8,128)(2,1)S(1)}, bf16[1024,384]{1,0:T(8,128)(2,1)S(1)}, u32[]{:S(2)}, u32[]{:S(2)}) collective-permute-start(bf16[1024,384]{1,0:T(8,128)(2,1)S(1)} %get-tuple-element.80), channel_id=1, source_target_pairs={{0,4},{1,5},{2,6},{3,7},{4,0},{5,1},{6,2},{7,3},{8,12},{9,13},{10,... | collective-permute-start | bytes 2359304 | tf_op jit(solution)/shard_map/ppermute | solution.py:209
  49.1 29.8 %collective-permute-start.10 = (bf16[768,384]{1,0:T(8,128)(2,1)}, bf16[768,384]{1,0:T(8,128)(2,1)}, u32[]{:S(2)}, u32[]{:S(2)}) collective-permute-start(bf16[768,384]{1,0:T(8,128)(2,1)} %get-tuple-element.85), channel_id=1, source_target_pairs={{2,0},{3,1},{4,2},{5,3},{6,4},{7,5},{8,6},{9,7},{10,8},{11,9},{12,... | collective-permute-start | bytes 1769480 | tf_op jit(solution)/shard_map/ppermute | solution.py:204
  51.7 29.6 %collective-permute-start.9 = (bf16[768,384]{1,0:T(8,128)(2,1)}, bf16[768,384]{1,0:T(8,128)(2,1)}, u32[]{:S(2)}, u32[]{:S(2)}) collective-permute-start(bf16[768,384]{1,0:T(8,128)(2,1)} %get-tuple-element.84), channel_id=1, source_target_pairs={{14,0},{15,1},{0,2},{1,3},{2,4},{3,5},{4,6},{5,7},{6,8},{7,9},{8,1... | collective-permute-start | bytes 1769480 | tf_op jit(solution)/shard_map/ppermute | solution.py:204
  68.4 12.9 %copy-start.6 = (s32[12]{0:T(128)S(1)}, s32[12]{0:T(128)}, u32[]{:S(2)}) copy-start(s32[12]{0:T(128)} %refs_1_.10) | copy-start | bytes 148
  69.2 19.8 %collective-permute-start.8 = (bf16[512,384]{1,0:T(8,128)(2,1)}, bf16[512,384]{1,0:T(8,128)(2,1)}, u32[]{:S(2)}, u32[]{:S(2)}) collective-permute-start(bf16[512,384]{1,0:T(8,128)(2,1)} %get-tuple-element.83), channel_id=1, source_target_pairs={{0,2},{1,3},{2,0},{3,1},{4,6},{5,7},{6,4},{7,5},{8,10},{9,11},{10,... | collective-permute-start | bytes 1179656 | tf_op jit(solution)/shard_map/ppermute | solution.py:209
  90.2 11.6 %collective-permute-start.11 = (bf16[256,384]{1,0:T(8,128)(2,1)S(1)}, bf16[256,384]{1,0:T(8,128)(2,1)S(1)}, u32[]{:S(2)}, u32[]{:S(2)}) collective-permute-start(bf16[256,384]{1,0:T(8,128)(2,1)S(1)} %get-tuple-element.92), channel_id=1, source_target_pairs={{0,8},{1,9},{2,10},{3,11},{4,12},{5,13},{6,14},{7,15},{8,0},{9,1},... | collective-permute-start | bytes 589832 | tf_op jit(solution)/shard_map/ppermute | solution.py:209
  90.9 19.2 %collective-permute-start.13 = (bf16[768,256]{1,0:T(8,128)(2,1)S(1)}, bf16[768,256]{1,0:T(8,128)(2,1)S(1)}, u32[]{:S(2)}, u32[]{:S(2)}) collective-permute-start(bf16[768,256]{1,0:T(8,128)(2,1)S(1)} %get-tuple-element.97), channel_id=1, source_target_pairs={{14,0},{15,1},{0,2},{1,3},{2,4},{3,5},{4,6},{5,7},{6,8},{7,9},{8,1... | collective-permute-start | bytes 1179656 | tf_op jit(solution)/shard_map/ppermute | solution.py:204
  93.4 18.9 %collective-permute-start.14 = (bf16[768,256]{1,0:T(8,128)(2,1)S(1)}, bf16[768,256]{1,0:T(8,128)(2,1)S(1)}, u32[]{:S(2)}, u32[]{:S(2)}) collective-permute-start(bf16[768,256]{1,0:T(8,128)(2,1)S(1)} %get-tuple-element.98), channel_id=1, source_target_pairs={{2,0},{3,1},{4,2},{5,3},{6,4},{7,5},{8,6},{9,7},{10,8},{11,9},{12,... | collective-permute-start | bytes 1179656 | tf_op jit(solution)/shard_map/ppermute | solution.py:204
  95.7 29.1 %collective-permute-start.12 = (bf16[1024,384]{1,0:T(8,128)(2,1)}, bf16[1024,384]{1,0:T(8,128)(2,1)}, u32[]{:S(2)}, u32[]{:S(2)}) collective-permute-start(bf16[1024,384]{1,0:T(8,128)(2,1)} %get-tuple-element.96), channel_id=1, source_target_pairs={{0,4},{1,5},{2,6},{3,7},{4,0},{5,1},{6,2},{7,3},{8,12},{9,13},{10,... | collective-permute-start | bytes 2359304 | tf_op jit(solution)/shard_map/ppermute | solution.py:209
  101.8 10.5 %copy-start.7 = (s32[12]{0:T(128)S(1)}, s32[12]{0:T(128)}, u32[]{:S(2)}) copy-start(s32[12]{0:T(128)} %refs_1_.10) | copy-start | bytes 148
  126.0 9.3 %collective-permute-start.15 = (bf16[512,384]{1,0:T(8,128)(2,1)S(1)}, bf16[512,384]{1,0:T(8,128)(2,1)S(1)}, u32[]{:S(2)}, u32[]{:S(2)}) collective-permute-start(bf16[512,384]{1,0:T(8,128)(2,1)S(1)} %get-tuple-element.105), channel_id=1, source_target_pairs={{0,2},{1,3},{2,0},{3,1},{4,6},{5,7},{6,4},{7,5},{8,10},{9,11},{10,... | collective-permute-start | bytes 1179656 | tf_op jit(solution)/shard_map/ppermute | solution.py:209
  126.9 12.7 %collective-permute-start.17 = (bf16[1024,256]{1,0:T(8,128)(2,1)S(1)}, bf16[1024,256]{1,0:T(8,128)(2,1)S(1)}, u32[]{:S(2)}, u32[]{:S(2)}) collective-permute-start(bf16[1024,256]{1,0:T(8,128)(2,1)S(1)} %get-tuple-element.110), channel_id=1, source_target_pairs={{0,4},{1,5},{2,6},{3,7},{4,0},{5,1},{6,2},{7,3},{8,12},{9,13},{10,... | collective-permute-start | bytes 1572872 | tf_op jit(solution)/shard_map/ppermute | solution.py:209
  139.7 6.4 %collective-permute-start.18 = (bf16[512,256]{1,0:T(8,128)(2,1)S(1)}, bf16[512,256]{1,0:T(8,128)(2,1)S(1)}, u32[]{:S(2)}, u32[]{:S(2)}) collective-permute-start(bf16[512,256]{1,0:T(8,128)(2,1)S(1)} %get-tuple-element.113), channel_id=1, source_target_pairs={{0,2},{1,3},{2,0},{3,1},{4,6},{5,7},{6,4},{7,5},{8,10},{9,11},{10,... | collective-permute-start | bytes 786440 | tf_op jit(solution)/shard_map/ppermute | solution.py:209
  140.2 17.9 %collective-permute-start.20 = (f32[128,384]{1,0:T(8,128)}, f32[128,384]{1,0:T(8,128)}, u32[]{:S(2)}, u32[]{:S(2)}) collective-permute-start(f32[128,384]{1,0:T(8,128)} %get-tuple-element.121), channel_id=1, source_target_pairs={{0,1},{1,0},{2,3},{3,2},{4,5},{5,4},{6,7},{7,6},{8,9},{9,8},{10,11... | collective-permute-start | bytes 589832 | tf_op jit(solution)/shard_map/ppermute | solution.py:209
  140.2 15.0 %collective-permute-start.16 = (bf16[256,384]{1,0:T(8,128)(2,1)S(1)}, bf16[256,384]{1,0:T(8,128)(2,1)S(1)}, u32[]{:S(2)}, u32[]{:S(2)}) collective-permute-start(bf16[256,384]{1,0:T(8,128)(2,1)S(1)} %get-tuple-element.108), channel_id=1, source_target_pairs={{0,8},{1,9},{2,10},{3,11},{4,12},{5,13},{6,14},{7,15},{8,0},{9,1},... | collective-permute-start | bytes 589832 | tf_op jit(solution)/shard_map/ppermute | solution.py:209
  146.2 11.7 %collective-permute-start.19 = (bf16[256,256]{1,0:T(8,128)(2,1)S(1)}, bf16[256,256]{1,0:T(8,128)(2,1)S(1)}, u32[]{:S(2)}, u32[]{:S(2)}) collective-permute-start(bf16[256,256]{1,0:T(8,128)(2,1)S(1)} %get-tuple-element.118), channel_id=1, source_target_pairs={{0,8},{1,9},{2,10},{3,11},{4,12},{5,13},{6,14},{7,15},{8,0},{9,1},... | collective-permute-start | bytes 393224 | tf_op jit(solution)/shard_map/ppermute | solution.py:209
  155.2 2.9 %collective-permute-start.21 = (f32[128,384]{1,0:T(8,128)S(1)}, f32[128,384]{1,0:T(8,128)S(1)}, u32[]{:S(2)}, u32[]{:S(2)}) collective-permute-start(f32[128,384]{1,0:T(8,128)S(1)} %get-tuple-element.122), channel_id=1, source_target_pairs={{0,1},{1,0},{2,3},{3,2},{4,5},{5,4},{6,7},{7,6},{8,9},{9,8},{10,11... | collective-permute-start | bytes 589832 | tf_op jit(solution)/shard_map/ppermute | solution.py:209
  158.0 1.4 collective-permute-start.22

commit v5 on v4

v5 whole, which is shorter than its diff:
```python
import jax
import jax.numpy as jnp
from jax import lax
from jax.experimental import pallas as pl
from jax.experimental.pallas import tpu as pltpu
from jax.sharding import PartitionSpec as P

CLASSES = 5
UNITS = (2, 2, 2, 2)
PARTS = 2
EARLY = 4
LIMIT = 16 * 2**20
ANY = pl.BlockSpec(memory_space=pl.ANY)
BF16, F32 = jnp.bfloat16, jnp.float32
NEXT = ((0, 0), (1, 0), (1, 1))
BEFORE = ((0, 3), (0, 4), (1, 4))
HERE = ((0, 1), (0, 2), (1, 2), (1, 3))
FOUND = ((0, 2, 7, 9, 4), (1, 6, 8, 3, 5))


def call(body, scalars, arrays, after, out_shape, scratch=(), fetched=0, scalar_out=False):
    lead = len(scalars) + len(arrays)
    extra = len(after)
    outs = len(out_shape)

    def kernel(*refs):
        rest = refs[lead + extra :]
        body(*refs[:lead], *rest[:outs], *rest[outs + 1 :])

    kernel.__name__ = body.__name__
    vmem, smem = (pl.BlockSpec(memory_space=space) for space in (pltpu.VMEM, pltpu.SMEM))
    return pl.pallas_call(
        kernel,
        out_shape=[*out_shape, jax.ShapeDtypeStruct((8, 128), F32)],
        in_specs=[smem] * len(scalars)
        + ([ANY] * fetched or [vmem] * len(arrays))
        + [ANY] * extra,
        out_specs=[smem if scalar_out else vmem] * outs + [ANY],
        scratch_shapes=scratch,
        compiler_params=pltpu.CompilerParams(vmem_limit_bytes=LIMIT),
        cost_estimate=pl.CostEstimate(flops=1, bytes_accessed=1, transcendentals=0),
        name=body.__name__,
    )(*scalars, *arrays, *after)


def coupled(core, blocks, acoustic, coupling, at, width, after):
    slots, rows, depth = coupling[0].shape
    per = slots // CLASSES
    nodes, modes = acoustic[0].shape
    lists = (NEXT, BEFORE, HERE)

    def coupled_rows(core_ref, own_blocks, far_blocks, own_a, far_a, own_c, far_c, *refs):
        outs, both, weights, picked, sems = refs[:3], *refs[3:]
        core = core_ref[0]
        columns = pl.ds(pl.multiple_of(core * (modes // 2) + at, 128), width)
        copies = []
        for i, (a, c) in enumerate(((own_a, own_c), (far_a, far_c))):
            side = core if i == 0 else 1 - core
            nodes_here = pl.ds(pl.multiple_of(side * nodes, nodes), nodes)
            copies.append(pltpu.make_async_copy(a.at[:, columns], both.at[nodes_here, :], sems.at[2 * i]))
            copies.append(pltpu.make_async_copy(c, weights.at[side], sems.at[2 * i + 1]))
        for copy in copies:
            copy.start()
        for copy in copies:
            copy.wait()
        for out, pairs in zip(outs, lists):
            for place, (face, k) in enumerate(pairs):
                own = core == face
                for s in range(per):
                    slot = k * per + s
                    for n in range(depth // rows):
                        block = jnp.where(own, own_blocks[slot, n], far_blocks[slot, n])
                        first = pl.multiple_of(face * nodes + block * rows, rows)
                        picked[n * rows : (n + 1) * rows, :] = both[pl.ds(first, rows), :]
                    row = (place * per + s) * rows
                    out[row : row + rows, :] = jnp.dot(
                        weights[face, slot], picked[...], preferred_element_type=F32
                    ).astype(BF16)

    shapes = [(len(pairs) * per * rows, width) for pairs in lists]
    return call(
        coupled_rows,
        [core, *blocks],
        [*acoustic, *coupling],
        after,
        [jax.ShapeDtypeStruct(shape, BF16) for shape in shapes],
        [
            pltpu.VMEM((2 * nodes, width), BF16),
            pltpu.VMEM((2, *coupling[0].shape), BF16),
            pltpu.VMEM((depth, width), BF16),
            pltpu.SemaphoreType.DMA((4,)),
        ],
        fetched=4,
    )


def turned(side, bit, struct_modes, share, after):
    depth, modes = struct_modes.shape
    half = modes // 2
    low = 2**bit

    def turn(side_ref, in_ref, kept_out, sent_out):
        for which, out in ((side_ref[0], kept_out), (1 - side_ref[0], sent_out)):
            for i in range(half // share):
                column = (i // low * 2 * low + i % low + which * low) * share
                block = in_ref[:, pl.ds(pl.multiple_of(column, share), share)]
                out[i * share : (i + 1) * share, :] = block.T

    if share % 128:
        sides = struct_modes.T.reshape(-1, 2, low * share, depth)
        pair = [
            lax.dynamic_index_in_dim(sides, one, 1, keepdims=False).reshape(half, depth)
            for one in (side[0], 1 - side[0])
        ]
        return [*pair, after[0]]
    return call(turn, [side], [struct_modes], after, [jax.ShapeDtypeStruct((half, depth), BF16)] * 2)


def rows_times(left_own, left_far, picked, out):
    tall, depth = left_own.shape
    tile = min(tall, 256)

    @pl.loop(0, tall // tile)
    def _(i):
        here = pl.ds(pl.multiple_of(i * tile, tile), tile)
        product = jnp.dot(left_own[here, :], picked[:depth, :], preferred_element_type=F32)
        product += jnp.dot(left_far[here, :], picked[depth:, :], preferred_element_type=F32)
        out[here, :] = product.astype(out.dtype)


def slots_of(core, shifts, per, after):
    count = shifts[0].shape[0]

    def slots(core_ref, own_shift, far_shift, out):
        for half, shift in enumerate((own_shift, far_shift)):
            first_core = core_ref[0] == half
            bases = [jnp.where(first_core, FOUND[0][k], FOUND[1][k]) * per for k in range(CLASSES)]
            for b in range(count):
                kind = shift[b]
                slot = jnp.int32(0)
                for k in range(CLASSES):
                    slot = jnp.where(kind == k, bases[k], slot)
                    bases[k] = bases[k] + (kind == k).astype(jnp.int32)
                out[half * count + b] = slot

    shape = jax.ShapeDtypeStruct((2 * count,), jnp.int32)
    return call(slots, [core, *shifts], [], after, [shape], scalar_out=True)


def panel(slots, lefts, pieces, after):
    tall, depth = lefts[0].shape
    width = pieces[0].shape[1]
    count = slots.shape[0]
    rows = 2 * depth // count

    def panel_part(slot_ref, own_kept, far_kept, own_sent, far_sent, *refs):
        parts, away, kept, picked = refs[:3], refs[3 : 3 + PARTS], refs[3 + PARTS], refs[4 + PARTS]
        for b in range(count):
            slot = slot_ref[b]
            base = 0
            for part in parts:
                many = part.shape[0] // rows

                @pl.when((slot >= base) & (slot < base + many))
                def _(part=part, b=b, slot=slot, base=base):
                    first = pl.multiple_of((slot - base) * rows, rows)
                    picked[b * rows : (b + 1) * rows, :] = part[pl.ds(first, rows), :]

                base += many
        for i in range(PARTS):
            side = pl.ds(i * (tall // PARTS), tall // PARTS)
            rows_times(own_sent.at[side, :], far_sent.at[side, :], picked, away[i])
        rows_times(own_kept, far_kept, picked, kept)

    return call(
        panel_part,
        [slots],
        [*lefts, *pieces],
        after,
        [jax.ShapeDtypeStruct((tall // PARTS, width), BF16)] * PARTS
        + [jax.ShapeDtypeStruct((tall, width), F32)],
        [pltpu.VMEM((2 * depth, width), BF16)],
    )


def added(held, got, here, before, wire, after):
    width = held.shape[1]
    shape = (before, 2, held.shape[0] // before // 2, width)
    tall = shape[2]
    each = before // len(got)

    def added_split(here_ref, held_ref, *refs):
        kept_ref, away_ref = refs[-2:]
        side = here_ref[0]
        for i in range(before):
            at = slice(i * tall, (i + 1) * tall)
            arrived = refs[i // each]
            kept_ref[at, :] = held_ref[i, side] + arrived[i % each, side].astype(F32)
            away = held_ref[i, 1 - side] + arrived[i % each, 1 - side].astype(F32)
            away_ref[at, :] = away.astype(wire)

    out = (before * tall, width)
    return call(
        added_split,
        [here],
        [held.reshape(shape), *[block.reshape(each, *shape[1:]) for block in got]],
        after,
        [jax.ShapeDtypeStruct(out, F32), jax.ShapeDtypeStruct(out, wire)],
    )


def together(core, own, far, starts, modes):
    rows = own[0].shape[0]

    def put_together(core_ref, *refs):
        out = refs[-1]
        for half, blocks in enumerate((refs[: len(own)], refs[len(own) : -1])):
            side = core_ref[0] if half == 0 else 1 - core_ref[0]
            for at, block in zip(starts, blocks):
                first = pl.multiple_of(side * (modes // 2) + at, 128)
                out[:, pl.ds(first, block.shape[1])] = block[...]

    out, _ = call(put_together, [core], [*own, *far], [], [jax.ShapeDtypeStruct((rows, modes), F32)])
    return out


def passed_along(block, distance):
    size = lax.axis_size("mesh")
    return lax.ppermute(block, "mesh", [((i - distance) % size, i) for i in range(size)])


def swapped(block, bit):
    size = lax.axis_size("mesh")
    return lax.ppermute(block, "mesh", [(i, i ^ (1 << bit)) for i in range(size)])


def planned(levels):
    chunks = len(UNITS)
    steps = [("coupled", 0), ("turned", 0), *(("coupled", j) for j in range(1, EARLY))]
    for now in range(chunks + levels):
        steps.append(("panel", now))
        steps.extend((level, now - level) for level in range(1, levels + 1))
        steps.append(("coupled", now + EARLY))
    return [step for step in steps if 0 <= step[1] < chunks]


def per_device(struct_modes, acoustic_modes, coupling, face_shift, face_blocks):
    size = lax.axis_size("mesh")
    me = lax.axis_index("mesh")
    modes = acoustic_modes.shape[1]
    share = struct_modes.shape[1] // size
    bits = list(range(1, size.bit_length() - 1))
    order = [2, 1, *bits[2:]]
    levels = len(order)
    widths = [units * (modes // 2 // sum(UNITS)) for units in UNITS]
    starts = [sum(widths[:j]) for j in range(len(widths))]

    def bit_of(bit):
        return ((me >> bit) & 1).reshape(1)

    core = bit_of(0)
    token = []
    blocks = (face_blocks, swapped(face_blocks, 0))
    couplings = (coupling, swapped(coupling, 0))
    acoustics = (acoustic_modes, swapped(acoustic_modes, 0))
    far_struct = swapped(struct_modes, 0)
    shifts = (face_shift, swapped(face_shift, 0))
    per = coupling.shape[0] // CLASSES
    state = [dict(bits=sorted([0, *order[1:]], reverse=True)) for _ in widths]
    finished = []
    for stage, j in planned(levels):
        now = state[j]
        if stage == "coupled":
            ahead, behind, here, last = coupled(
                core, blocks, acoustics, couplings, starts[j], widths[j], token
            )
            now["pieces"] = [passed_along(ahead, 2), passed_along(behind, -2), here]
        elif stage == "turned":
            side = bit_of(order[0])
            *own, last = turned(side, order[0], struct_modes, share, token)
            slots, last = slots_of(core, shifts, per, [last])
            *far, last = turned(side, order[0], far_struct, share, [last])
            kept, sent = zip(own, far)
        elif stage == "panel":
            *away, now["held"], last = panel(slots, (*kept, *sent), now["pieces"], token)
            now["got"] = [swapped(one, order[0]) for one in away]
        else:
            bit = order[stage] if stage < levels else 0
            place = now["bits"].index(bit)
            now["bits"].remove(bit)
            wire = BF16 if stage < min(levels, 3) else F32
            now["held"], away, last = added(
                now["held"], now["got"], bit_of(bit), 2**place, wire, token
            )
            now["got"] = [swapped(away, bit)]
        token = [last]
    return together(
        core, [now["held"] for now in state], [now["got"][0] for now in state], starts, modes
    )


def solution(mesh):
    placed = (
        P(("member", "mesh"), None),
        P(("member", "mesh"), None),
        P("mesh", None, None),
        P("mesh"),
        P("mesh", None),
    )
    return jax.shard_map(
        per_device,
        mesh=mesh,
        in_specs=placed,
        out_specs=P(("member", "mesh"), None),
        check_vma=False,
    )
```

time: 162 us -> 146 us (0.901)
  waiting for transfers between devices: 100 us -> 48.3 us
  local copies, waits for them, and re-layouts: 3.48 us -> 22.1 us
  starting transfers between devices: 19.7 us -> 35.4 us
    ppermute x17 -> x25, waiting for transfers between devices: 63.1 us -> 33.3 us  [swapped(): return lax.ppermute(block, 'mesh', [(i, i ^ 1 << bit) for i in range(size)])]
    ppermute x6 -> x8, waiting for transfers between devices: 37.2 us -> 15.1 us  [passed_along(): lax.ppermute(block, 'mesh', [((i - distance) % size, i) for i in range(si...]
    unnamed x17 -> x67, local copies, waits for them, and re-layouts: 3.48 us -> 22.1 us
    ppermute x17 -> x25, starting transfers between devices: 6.59 us -> 17.7 us  [swapped(): return lax.ppermute(block, 'mesh', [(i, i ^ 1 << bit) for i in range(size)])]
    ppermute x6 -> x8, starting transfers between devices: 13.1 us -> 17.7 us  [passed_along(): lax.ppermute(block, 'mesh', [((i - distance) % size, i) for i in range(si...]
    pallas_call x21 -> x24, Pallas kernels: 37.7 us -> 39.3 us  [call(): pl.pallas_call(kernel, out_shape=[*out_shape, jax.ShapeDtypeStruct((8, 12...]
  transfers between devices with their start and end apart: 23 -> 33, of which waited for: 18 -> 12; matrix products, arithmetic and copies ran while one was open for 0% -> 1% of each run, Pallas kernels for 18% -> 26%
where the time goes in v5:
time: 146 us; the launch traced here: 145 us
  waiting for transfers between devices  48.3 us (33%)
  Pallas kernels  39.3 us (27%)
  starting transfers between devices  35.4 us (24%)
  local copies, waits for them, and re-layouts  22.1 us (15%)
    pallas_call x24, Pallas kernels, call(): pl.pallas_call(kernel, out_shape=[*out_shape, jax.ShapeDtypeStruct((8, 12...  39.3 us
    ppermute x25, waiting for transfers between devices, swapped(): return lax.ppermute(block, 'mesh', [(i, i ^ 1 << bit) for i in range(size)])  33.3 us
    unnamed x67, local copies, waits for them, and re-layouts  22.1 us
    ppermute x8, starting transfers between devices, passed_along(): lax.ppermute(block, 'mesh', [((i - distance) % size, i) for i in range(si...  17.7 us
    ppermute x25, starting transfers between devices, swapped(): return lax.ppermute(block, 'mesh', [(i, i ^ 1 << bit) for i in range(size)])  17.7 us
    ppermute x8, waiting for transfers between devices, passed_along(): lax.ppermute(block, 'mesh', [((i - distance) % size, i) for i in range(si...  15.1 us
  transfers between devices with their start and end apart: 33, of which 12 were waited for; matrix products, arithmetic and copies ran while one was open for 1% of the time, Pallas kernels for 26%

profile of v5, /device:TPU:0, one launch (start us, length us, event | category | flops | bytes accessed | tf_op | source)
XLA Modules:
  0.0 145.5 jit_solution(5700214609347899415)
XLA Ops:
  0.0 0.5 collective-permute-start.4
  1.0 0.8 copy.7.refs_1_
  2.2 5.6 %collective-permute-done.1.refs_2_ = s32[20,4]{1,0:T(8,128)S(1)} collective-permute-done((s32[20,4]{1,0:T(8,128)S(1)}, s32[20,4]{1,0:T(8,128)S(1)}, u32[]{:S(2)}, u32[]{:S(2)}) %collective-permute-start.1) | collective-permute-done | bytes 352 | tf_op jit(solution)/shard_map/ppermute | solution.py:234
  7.9 2.0 %collective-permute-done.3.refs_6_ = bf16[20,64,256]{2,1,0:T(8,128)(2,1)S(1)} collective-permute-done((bf16[20,64,256]{2,1,0:T(8,128)(2,1)}, bf16[20,64,256]{2,1,0:T(8,128)(2,1)S(1)}, u32[]{:S(2)}, u32[]{:S(2)}) %collective-permute-start.3) | collective-permute-done | bytes 655392 | tf_op jit(solution)/shard_map/ppermute | solution.py:234
  9.9 1.6 %copy-done = bf16[512,2048]{1,0:T(8,128)(2,1)S(1)} copy-done((bf16[512,2048]{1,0:T(8,128)(2,1)S(1)}, bf16[512,2048]{1,0:T(8,128)(2,1)}, u32[]{:S(2)}) %copy-start) | copy-done | bytes 2097176
  11.5 1.1 copy-done.13
  12.6 2.5 %coupled_rows.4 = (bf16[768,256]{1,0:T(8,128)(2,1)S(1)}, bf16[768,256]{1,0:T(8,128)(2,1)S(1)}, bf16[1024,256]{1,0:T(8,128)(2,1)S(1)}, f32[8,128]{1,0:T(8,128)S(1)}) custom-call(s32[1]{0:T(128)} %bitcast.refs_0_, s32[20,4]{1,0:T(8,128)S(1)} %copy.7.refs_1_, s32[20,4]{1,0:T(8,128)S(1)} %collective-permute-done.1.refs_2_, bf16[512,2048]{1,0:T(8,128)(2,1)S(1)} %copy-done, ...), custom_call_target="tpu_custom_call" | custom-call | flops 1 | bytes 1 | tf_op jit(solution)/shard_map/coupled_rows/pallas_call | solution.py:32
  15.1 2.6 %collective-permute-start.5 = (bf16[768,256]{1,0:T(8,128)(2,1)S(1)}, bf16[768,256]{1,0:T(8,128)(2,1)S(1)}, u32[]{:S(2)}, u32[]{:S(2)}) collective-permute-start(bf16[768,256]{1,0:T(8,128)(2,1)S(1)} %get-tuple-element.89), channel_id=1, source_target_pairs={{14,0},{15,1},{0,2},{1,3},{2,4},{3,5},{4,6},{5,7},{6,8},{7,9},{8,1... | collective-permute-start | bytes 1179656 | tf_op jit(solution)/shard_map/ppermute | solution.py:229
  17.6 3.1 %collective-permute-start.6 = (bf16[768,256]{1,0:T(8,128)(2,1)S(1)}, bf16[768,256]{1,0:T(8,128)(2,1)S(1)}, u32[]{:S(2)}, u32[]{:S(2)}) collective-permute-start(bf16[768,256]{1,0:T(8,128)(2,1)S(1)} %get-tuple-element.90), channel_id=1, source_target_pairs={{2,0},{3,1},{4,2},{5,3},{6,4},{7,5},{8,6},{9,7},{10,8},{11,9},{12,... | collective-permute-start | bytes 1179656 | tf_op jit(solution)/shard_map/ppermute | solution.py:229
  20.8 0.9 turn.2
  21.7 1.3 slots.1
  23.1 3.3 %turn.3 = (bf16[1024,768]{1,0:T(8,128)(2,1)S(1)}, bf16[1024,768]{1,0:T(8,128)(2,1)S(1)}, f32[8,128]{1,0:T(8,128)S(1)}) custom-call(s32[1]{0:T(128)} %bitcast.3.refs_0_, bf16[768,2048]{1,0:T(8,128)(2,1)} %collective-permute-done.4.refs_1_, f32[8,128]{1,0:T(8,128)S(1)} %get-tuple-element.85.refs_2_), custom_call_target="tpu_custom_call" | custom-call | flops 1 | bytes 1 | tf_op jit(solution)/shard_map/turn/pallas_call | solution.py:32
  26.4 2.5 %coupled_rows.5 = (bf16[768,256]{1,0:T(8,128)(2,1)S(1)}, bf16[768,256]{1,0:T(8,128)(2,1)S(1)}, bf16[1024,256]{1,0:T(8,128)(2,1)S(1)}, f32[8,128]{1,0:T(8,128)S(1)}) custom-call(s32[1]{0:T(128)} %bitcast.refs_0_, s32[20,4]{1,0:T(8,128)S(1)} %copy.7.refs_1_, s32[20,4]{1,0:T(8,128)S(1)} %collective-permute-done.1.refs_2_, bf16[512,2048]{1,0:T(8,128)(2,1)S(1)} %copy-done.1, ...), custom_call_target="tpu_custom_call" | custom-call | flops 1 | bytes 1 | tf_op jit(solution)/shard_map/coupled_rows/pallas_call | solution.py:32
  28.9 2.0 %collective-permute-start.10 = (bf16[768,256]{1,0:T(8,128)(2,1)S(1)}, bf16[768,256]{1,0:T(8,128)(2,1)S(1)}, u32[]{:S(2)}, u32[]{:S(2)}) collective-permute-start(bf16[768,256]{1,0:T(8,128)(2,1)S(1)} %get-tuple-element.100), channel_id=1, source_target_pairs={{2,0},{3,1},{4,2},{5,3},{6,4},{7,5},{8,6},{9,7},{10,8},{11,9},{12,... | collective-permute-start | bytes 1179656 | tf_op jit(solution)/shard_map/ppermute | solution.py:229
  31.0 3.2 %coupled_rows.6 = (bf16[768,256]{1,0:T(8,128)(2,1)}, bf16[768,256]{1,0:T(8,128)(2,1)}, bf16[1024,256]{1,0:T(8,128)(2,1)S(1)}, f32[8,128]{1,0:T(8,128)S(1)}) custom-call(s32[1]{0:T(128)} %bitcast.refs_0_, s32[20,4]{1,0:T(8,128)S(1)} %copy.7.refs_1_, s32[20,4]{1,0:T(8,128)S(1)} %collective-permute-done.1.refs_2_, bf16[512,2048]{1,0:T(8,128)(2,1)S(1)} %copy-done.1, ...), custom_call_target="tpu_custom_call" | custom-call | flops 1 | bytes 1 | tf_op jit(solution)/shard_map/coupled_rows/pallas_call | solution.py:32
  34.3 3.1 %coupled_rows.7 = (bf16[768,256]{1,0:T(8,128)(2,1)}, bf16[768,256]{1,0:T(8,128)(2,1)}, bf16[1024,256]{1,0:T(8,128)(2,1)S(1)}, f32[8,128]{1,0:T(8,128)S(1)}) custom-call(s32[1]{0:T(128)} %bitcast.refs_0_, s32[20,4]{1,0:T(8,128)S(1)} %copy.7.refs_1_, s32[20,4]{1,0:T(8,128)S(1)} %collective-permute-done.1.refs_2_, bf16[512,2048]{1,0:T(8,128)(2,1)S(1)} %copy-done.1, ...), custom_call_target="tpu_custom_call" | custom-call | flops 1 | bytes 1 | tf_op jit(solution)/shard_map/coupled_rows/pallas_call | solution.py:32
  37.4 0.8 copy-done.20
  38.2 5.8 %collective-permute-done.5.refs_5_ = bf16[768,256]{1,0:T(8,128)(2,1)S(1)} collective-permute-done((bf16[768,256]{1,0:T(8,128)(2,1)S(1)}, bf16[768,256]{1,0:T(8,128)(2,1)S(1)}, u32[]{:S(2)}, u32[]{:S(2)}) %collective-permute-start.5) | collective-permute-done | bytes 393248 | tf_op jit(solution)/shard_map/ppermute | solution.py:229
  44.0 5.5 %collective-permute-start.15 = (bf16[768,256]{1,0:T(8,128)(2,1)}, bf16[768,256]{1,0:T(8,128)(2,1)}, u32[]{:S(2)}, u32[]{:S(2)}) collective-permute-start(bf16[768,256]{1,0:T(8,128)(2,1)} %get-tuple-element.110), channel_id=1, source_target_pairs={{2,0},{3,1},{4,2},{5,3},{6,4},{7,5},{8,6},{9,7},{10,8},{11,9},{12,... | collective-permute-start | bytes 1179656 | tf_op jit(solution)/shard_map/ppermute | solution.py:229
  49.5 5.4 %collective-permute-done.6.refs_6_ = bf16[768,256]{1,0:T(8,128)(2,1)S(1)} collective-permute-done((bf16[768,256]{1,0:T(8,128)(2,1)S(1)}, bf16[768,256]{1,0:T(8,128)(2,1)S(1)}, u32[]{:S(2)}, u32[]{:S(2)}) %collective-permute-start.6) | collective-permute-done | bytes 393248 | tf_op jit(solution)/shard_map/ppermute | solution.py:229
  54.9 4.0 %panel_part.4 = (bf16[512,256]{1,0:T(8,128)(2,1)S(1)}, bf16[512,256]{1,0:T(8,128)(2,1)S(1)}, f32[1024,256]{1,0:T(8,128)S(1)}, f32[8,128]{1,0:T(8,128)S(1)}) custom-call(s32[24]{0:T(128)S(1)} %get-tuple-element.83.refs_0_, bf16[1024,768]{1,0:T(8,128)(2,1)S(1)} %get-tuple-element.84.refs_1_, bf16[1024,768]{1,0:T(8,128)(2,1)S(1)} %get-tuple-element.86.refs_2_, ...), custom_call_target="tpu_custom_call" | custom-call | flops 1 | bytes 1 | tf_op jit(solution)/shard_map/panel_part/pallas_call | solution.py:32
  58.9 0.5 collective-permute-start.7
  59.5 3.9 %collective-permute-done.10.refs_6_ = bf16[768,256]{1,0:T(8,128)(2,1)S(1)} collective-permute-done((bf16[768,256]{1,0:T(8,128)(2,1)S(1)}, bf16[768,256]{1,0:T(8,128)(2,1)S(1)}, u32[]{:S(2)}, u32[]{:S(2)}) %collective-permute-start.10) | collective-permute-done | bytes 393248 | tf_op jit(solution)/shard_map/ppermute | solution.py:229
  63.3 0.5 collective-permute-start.8
  63.8 4.4 %panel_part.5 = (bf16[512,256]{1,0:T(8,128)(2,1)}, bf16[512,256]{1,0:T(8,128)(2,1)S(1)}, f32[1024,256]{1,0:T(8,128)S(1)}, f32[8,128]{1,0:T(8,128)S(1)}) custom-call(s32[24]{0:T(128)S(1)} %get-tuple-element.83.refs_0_, bf16[1024,768]{1,0:T(8,128)(2,1)S(1)} %get-tuple-element.84.refs_1_, bf16[1024,768]{1,0:T(8,128)(2,1)S(1)} %get-tuple-element.86.refs_2_, ...), custom_call_target="tpu_custom_call" | custom-call | flops 1 | bytes 1 | tf_op jit(solution)/shard_map/panel_part/pallas_call | solution.py:32
  68.2 1.0 copy-done.18
  69.2 1.5 %collective-permute-start.12 = (bf16[512,256]{1,0:T(8,128)(2,1)}, bf16[512,256]{1,0:T(8,128)(2,1)S(1)}, u32[]{:S(2)}, u32[]{:S(2)}) collective-permute-start(bf16[512,256]{1,0:T(8,128)(2,1)} %get-tuple-element.107), channel_id=1, source_target_pairs={{0,4},{1,5},{2,6},{3,7},{4,0},{5,1},{6,2},{7,3},{8,12},{9,13},{10,... | collective-permute-start | bytes 786440 | tf_op jit(solution)/shard_map/ppermute | solution.py:234
  70.7 0.7 copy-done.26
  71.8 0.7 copy-done.28
  72.5 4.4 %collective-permute-start.21 = (bf16[768,256]{1,0:T(8,128)(2,1)}, bf16[768,256]{1,0:T(8,128)(2,1)}, u32[]{:S(2)}, u32[]{:S(2)}) collective-permute-start(bf16[768,256]{1,0:T(8,128)(2,1)} %get-tuple-element.123), channel_id=1, source_target_pairs={{2,0},{3,1},{4,2},{5,3},{6,4},{7,5},{8,6},{9,7},{10,8},{11,9},{12,... | collective-permute-start | bytes 1179656 | tf_op jit(solution)/shard_map/ppermute | solution.py:229
  76.9 0.9 copy-done.27
  77.8 0.9 copy-done.29
  78.8 0.8 added_split.12
  79.6 0.8 copy-done.22
  80.5 1.4 copy-done.5
  81.9 1.4 copy-done.8
  83.3 1.4 copy-done.11
  84.7 5.0 %panel_part.6 = (bf16[512,256]{1,0:T(8,128)(2,1)}, bf16[512,256]{1,0:T(8,128)(2,1)S(1)}, f32[1024,256]{1,0:T(8,128)S(1)}, f32[8,128]{1,0:T(8,128)S(1)}) custom-call(s32[24]{0:T(128)S(1)} %get-tuple-element.83.refs_0_, bf16[1024,768]{1,0:T(8,128)(2,1)S(1)} %copy-done.3, bf16[1024,768]{1,0:T(8,128)(2,1)S(1)} %copy-done.8, bf16[1024,768]{1,0:T(8,128)(2,1)S(1)} %copy-done.5, ...), custom_call_target="tpu_custom_call" | custom-call | flops 1 | bytes 1 | tf_op jit(solution)/shard_map/panel_part/pallas_call | solution.py:32
  89.7 1.1 copy-done.16
  90.7 0.7 copy-done.31
  91.4 0.7 copy-done.24
  92.1 1.9 %collective-permute-start.18 = (bf16[512,256]{1,0:T(8,128)(2,1)}, bf16[512,256]{1,0:T(8,128)(2,1)S(1)}, u32[]{:S(2)}, u32[]{:S(2)}) collective-permute-start(bf16[512,256]{1,0:T(8,128)(2,1)} %get-tuple-element.120), channel_id=1, source_target_pairs={{0,4},{1,5},{2,6},{3,7},{4,0},{5,1},{6,2},{7,3},{8,12},{9,13},{10,... | collective-permute-start | bytes 786440 | tf_op jit(solution)/shard_map/ppermute | solution.py:234
  94.2 1.2 copy-done.19
  95.4 0.9 copy-done.25
  96.3 1.1 added_split.13
  97.5 2.0 %collective-permute-start.17 = (bf16[512,256]{1,0:T(8,128)(2,1)S(1)}, bf16[512,256]{1,0:T(8,128)(2,1)S(1)}, u32[]{:S(2)}, u32[]{:S(2)}) collective-permute-start(bf16[512,256]{1,0:T(8,128)(2,1)S(1)} %get-tuple-element.118), channel_id=1, source_target_pairs={{0,2},{1,3},{2,0},{3,1},{4,6},{5,7},{6,4},{7,5},{8,10},{9,11},{10,... | collective-permute-start | bytes 786440 | tf_op jit(solution)/shard_map/ppermute | solution.py:234
  99.5 1.0 copy-done.23
  100.5 1.0 added_split.14
  101.6 1.4 copy-done.9
  103.0 1.4 copy-done.12
  104.4 4.7 %panel_part.7 = (bf16[512,256]{1,0:T(8,128)(2,1)S(1)}, bf16[512,256]{1,0:T(8,128)(2,1)S(1)}, f32[1024,256]{1,0:T(8,128)S(1)}, f32[8,128]{1,0:T(8,128)S(1)}) custom-call(s32[24]{0:T(128)S(1)} %get-tuple-element.83.refs_0_, bf16[1024,768]{1,0:T(8,128)(2,1)S(1)} %copy-done.3, bf16[1024,768]{1,0:T(8,128)(2,1)S(1)} %copy-done.9, bf16[1024,768]{1,0:T(8,128)(2,1)S(1)} %copy-done.6, ...), custom_call_target="tpu_custom_call" | custom-call | flops 1 | bytes 1 | tf_op jit(solution)/shard_map/panel_part/pallas_call | solution.py:32
  109.1 2.1 %collective-permute-start.24 = (bf16[512,256]{1,0:T(8,128)(2,1)S(1)}, bf16[512,256]{1,0:T(8,128)(2,1)S(1)}, u32[]{:S(2)}, u32[]{:S(2)}) collective-permute-start(bf16[512,256]{1,0:T(8,128)(2,1)S(1)} %get-tuple-element.135), channel_id=1, source_target_pairs={{0,4},{1,5},{2,6},{3,7},{4,0},{5,1},{6,2},{7,3},{8,12},{9,13},{10,... | collective-permute-start | bytes 786440 | tf_op jit(solution)/shard_map/ppermute | solution.py:234
  111.2 1.2 collective-permute-start.16
  112.5 1.5 %collective-permute-start.23 = (bf16[512,256]{1,0:T(8,128)(2,1)S(1)}, bf16[512,256]{1,0:T(8,128)(2,1)S(1)}, u32[]{:S(2)}, u32[]{:S(2)}) collective-permute-start(bf16[512,256]{1,0:T(8,128)(2,1)S(1)} %get-tuple-element.133), channel_id=1, source_target_pairs={{0,2},{1,3},{2,0},{3,1},{4,6},{5,7},{6,4},{7,5},{8,10},{9,11},{10,... | collective-permute-start | bytes 786440 | tf_op jit(solution)/shard_map/ppermute | solution.py:234
  114.1 7.4 %collective-permute-done.16 = bf16[256,256]{1,0:T(8,128)(2,1)S(1)} collective-permute-done((bf16[256,256]{1,0:T(8,128)(2,1)S(1)}, bf16[256,256]{1,0:T(8,128)(2,1)S(1)}, u32[]{:S(2)}, u32[]{:S(2)}) %collective-permute-start.16) | collective-permute-done | bytes 131104 | tf_op jit(solution)/shard_map/ppermute | solution.py:234
  121.5 0.7 collective-permute-done.25
  122.3 0.9 collective-permute-start.27
  123.2 2.7 %collective-permute-start.22 = (bf16[256,256]{1,0:T(8,128)(2,1)S(1)}, bf16[256,256]{1,0:T(8,128)(2,1)S(1)}, u32[]{:S(2)}, u32[]{:S(2)}) collective-permute-start(bf16[256,256]{1,0:T(8,128)(2,1)S(1)} %get-tuple-element.131), channel_id=1, source_target_pairs={{0,8},{1,9},{2,10},{3,11},{4,12},{5,13},{6,14},{7,15},{8,0},{9,1},... | collective-permute-start | bytes 393224 | tf_op jit(solution)/shard_map/ppermute | solution.py:234
  126.3 10.2 %collective-permute-done.22 = bf16[256,256]{1,0:T(8,128)(2,1)S(1)} collective-permute-done((bf16[256,256]{1,0:T(8,128)(2,1)S(1)}, bf16[256,256]{1,0:T(8,128)(2,1)S(1)}, u32[]{:S(2)}, u32[]{:S(2)}) %collective-permute-start.22) | collective-permute-done | bytes 131104 | tf_op jit(solution)/shard_map/ppermute | solution.py:234
  136.7 0.5 collective-permute-start.30
  137.2 1.1 collective-permute-done.26
  138.5 4.5 %collective-permute-done.28 = bf16[256,256]{1,0:T(8,128)(2,1)S(1)} collective-permute-done((bf16[256,256]{1,0:T(8,128)(2,1)S(1)}, bf16[256,256]{1,0:T(8,128)(2,1)S(1)}, u32[]{:S(2)}, u32[]{:S(2)}) %collective-permute-start.28) | collective-permute-done | bytes 131104 | tf_op jit(solution)/shard_map/ppermute | solution.py:234
  143.1 1.3 collective-permute-done.32.refs_8_
  144.4 1.0 put_together.1
  (93 shorter events, 3.0 us)
Async XLA Ops:
  0.0 23.1 %collective-permute-start.4 = (bf16[768,2048]{1,0:T(8,128)(2,1)}, bf16[768,2048]{1,0:T(8,128)(2,1)}, u32[]{:S(2)}, u32[]{:S(2)}) collective-permute-start(bf16[768,2048]{1,0:T(8,128)(2,1)} %refs_1_.6), channel_id=1, source_target_pairs={{0,1},{1,0},{2,3},{3,2},{4,5},{5,4},{6,7},{7,6},{8,9},{9,8},{10,11... | collective-permute-start | bytes 9437192 | tf_op jit(solution)/shard_map/ppermute | solution.py:234
  0.5 9.5 %collective-permute-start.2 = (bf16[512,2048]{1,0:T(8,128)(2,1)}, bf16[512,2048]{1,0:T(8,128)(2,1)S(1)}, u32[]{:S(2)}, u32[]{:S(2)}) collective-permute-start(bf16[512,2048]{1,0:T(8,128)(2,1)} %refs_3_.7), channel_id=1, source_target_pairs={{0,1},{1,0},{2,3},{3,2},{4,5},{5,4},{6,7},{7,6},{8,9},{9,8},{10,11... | collective-permute-start | bytes 6291464 | tf_op jit(solution)/shard_map/ppermute | solution.py:234
  0.5 9.4 %collective-permute-start.3 = (bf16[20,64,256]{2,1,0:T(8,128)(2,1)}, bf16[20,64,256]{2,1,0:T(8,128)(2,1)S(1)}, u32[]{:S(2)}, u32[]{:S(2)}) collective-permute-start(bf16[20,64,256]{2,1,0:T(8,128)(2,1)} %refs_5_.7), channel_id=1, source_target_pairs={{0,1},{1,0},{2,3},{3,2},{4,5},{5,4},{6,7},{7,6},{8,9},{9,8},{10,11... | collective-permute-start | bytes 1966088 | tf_op jit(solution)/shard_map/ppermute | solution.py:234
  1.7 6.1 %collective-permute-start.1 = (s32[20,4]{1,0:T(8,128)S(1)}, s32[20,4]{1,0:T(8,128)S(1)}, u32[]{:S(2)}, u32[]{:S(2)}) collective-permute-start(s32[20,4]{1,0:T(8,128)S(1)} %copy.7.refs_1_), channel_id=1, source_target_pairs={{0,1},{1,0},{2,3},{3,2},{4,5},{5,4},{6,7},{7,6},{8,9},{9,8},{10,11... | collective-permute-start | bytes 968 | tf_op jit(solution)/shard_map/ppermute | solution.py:234
  1.8 19.9 %collective-permute-start = (s32[12]{0:T(128)}, s32[12]{0:T(128)S(1)}, u32[]{:S(2)}, u32[]{:S(2)}) collective-permute-start(s32[12]{0:T(128)} %refs_1_.7), channel_id=1, source_target_pairs={{0,1},{1,0},{2,3},{3,2},{4,5},{5,4},{6,7},{7,6},{8,9},{9,8},{10,11... | collective-permute-start | bytes 152 | tf_op jit(solution)/shard_map/ppermute | solution.py:234
  9.9 1.6 %copy-start = (bf16[512,2048]{1,0:T(8,128)(2,1)S(1)}, bf16[512,2048]{1,0:T(8,128)(2,1)}, u32[]{:S(2)}) copy-start(bf16[512,2048]{1,0:T(8,128)(2,1)} %refs_3_.7) | copy-start | bytes 6291460
  11.5 1.1 copy-start.13
  12.6 8.2 %copy-start.15 = (bf16[768,2048]{1,0:T(8,128)(2,1)S(1)}, bf16[768,2048]{1,0:T(8,128)(2,1)}, u32[]{:S(2)}) copy-start(bf16[768,2048]{1,0:T(8,128)(2,1)} %refs_1_.6) | copy-start | bytes 9437188
  15.1 6.6 %copy-start.30 = (s32[12]{0:T(128)S(1)}, s32[12]{0:T(128)}, u32[]{:S(2)}) copy-start(s32[12]{0:T(128)} %refs_1_.7) | copy-start | bytes 148
  15.1 28.9 %collective-permute-start.5 = (bf16[768,256]{1,0:T(8,128)(2,1)S(1)}, bf16[768,256]{1,0:T(8,128)(2,1)S(1)}, u32[]{:S(2)}, u32[]{:S(2)}) collective-permute-start(bf16[768,256]{1,0:T(8,128)(2,1)S(1)} %get-tuple-element.89), channel_id=1, source_target_pairs={{14,0},{15,1},{0,2},{1,3},{2,4},{3,5},{4,6},{5,7},{6,8},{7,9},{8,1... | collective-permute-start | bytes 1179656 | tf_op jit(solution)/shard_map/ppermute | solution.py:229
  17.6 37.3 %collective-permute-start.6 = (bf16[768,256]{1,0:T(8,128)(2,1)S(1)}, bf16[768,256]{1,0:T(8,128)(2,1)S(1)}, u32[]{:S(2)}, u32[]{:S(2)}) collective-permute-start(bf16[768,256]{1,0:T(8,128)(2,1)S(1)} %get-tuple-element.90), channel_id=1, source_target_pairs={{2,0},{3,1},{4,2},{5,3},{6,4},{7,5},{8,6},{9,7},{10,8},{11,9},{12,... | collective-permute-start | bytes 1179656 | tf_op jit(solution)/shard_map/ppermute | solution.py:229
  21.6 42.2 %copy-start.2 = (bf16[1024,768]{1,0:T(8,128)(2,1)}, bf16[1024,768]{1,0:T(8,128)(2,1)S(1)}, u32[]{:S(2)}) copy-start(bf16[1024,768]{1,0:T(8,128)(2,1)S(1)} %get-tuple-element.84.refs_1_) | copy-start | bytes 4718596
  21.7 42.2 %copy-start.4 = (bf16[1024,768]{1,0:T(8,128)(2,1)}, bf16[1024,768]{1,0:T(8,128)(2,1)S(1)}, u32[]{:S(2)}) copy-start(bf16[1024,768]{1,0:T(8,128)(2,1)S(1)} %get-tuple-element.87.refs_3_) | copy-start | bytes 4718596
  21.7 4.8 %copy-start.1 = (bf16[512,2048]{1,0:T(8,128)(2,1)S(1)}, bf16[512,2048]{1,0:T(8,128)(2,1)}, u32[]{:S(2)}) copy-start(bf16[512,2048]{1,0:T(8,128)(2,1)} %refs_3_.7) | copy-start | bytes 6291460
  21.7 4.8 %copy-start.14 = (bf16[20,64,256]{2,1,0:T(8,128)(2,1)S(1)}, bf16[20,64,256]{2,1,0:T(8,128)(2,1)}, u32[]{:S(2)}) copy-start(bf16[20,64,256]{2,1,0:T(8,128)(2,1)} %refs_5_.7) | copy-start | bytes 1966084
  26.4 37.4 %copy-start.7 = (bf16[1024,768]{1,0:T(8,128)(2,1)}, bf16[1024,768]{1,0:T(8,128)(2,1)S(1)}, u32[]{:S(2)}) copy-start(bf16[1024,768]{1,0:T(8,128)(2,1)S(1)} %get-tuple-element.86.refs_2_) | copy-start | bytes 4718596
  26.4 37.4 %copy-start.10 = (bf16[1024,768]{1,0:T(8,128)(2,1)}, bf16[1024,768]{1,0:T(8,128)(2,1)S(1)}, u32[]{:S(2)}) copy-start(bf16[1024,768]{1,0:T(8,128)(2,1)S(1)} %get-tuple-element.88.refs_4_) | copy-start | bytes 4718596
  28.9 34.4 %collective-permute-start.10 = (bf16[768,256]{1,0:T(8,128)(2,1)S(1)}, bf16[768,256]{1,0:T(8,128)(2,1)S(1)}, u32[]{:S(2)}, u32[]{:S(2)}) collective-permute-start(bf16[768,256]{1,0:T(8,128)(2,1)S(1)} %get-tuple-element.100), channel_id=1, source_target_pairs={{2,0},{3,1},{4,2},{5,3},{6,4},{7,5},{8,6},{9,7},{10,8},{11,9},{12,... | collective-permute-start | bytes 1179656 | tf_op jit(solution)/shard_map/ppermute | solution.py:229
  31.0 32.9 %collective-permute-start.9 = (bf16[768,256]{1,0:T(8,128)(2,1)S(1)}, bf16[768,256]{1,0:T(8,128)(2,1)S(1)}, u32[]{:S(2)}, u32[]{:S(2)}) collective-permute-start(bf16[768,256]{1,0:T(8,128)(2,1)S(1)} %get-tuple-element.99), channel_id=1, source_target_pairs={{14,0},{15,1},{0,2},{1,3},{2,4},{3,5},{4,6},{5,7},{6,8},{7,9},{8,1... | collective-permute-start | bytes 1179656 | tf_op jit(solution)/shard_map/ppermute | solution.py:229
  34.2 42.7 %collective-permute-start.14 = (bf16[768,256]{1,0:T(8,128)(2,1)}, bf16[768,256]{1,0:T(8,128)(2,1)}, u32[]{:S(2)}, u32[]{:S(2)}) collective-permute-start(bf16[768,256]{1,0:T(8,128)(2,1)} %get-tuple-element.109), channel_id=1, source_target_pairs={{14,0},{15,1},{0,2},{1,3},{2,4},{3,5},{4,6},{5,7},{6,8},{7,9},{8,1... | collective-permute-start | bytes 1179656 | tf_op jit(solution)/shard_map/ppermute | solution.py:229
  37.4 0.8 copy-start.20
  44.0 36.4 %collective-permute-start.15 = (bf16[768,256]{1,0:T(8,128)(2,1)}, bf16[768,256]{1,0:T(8,128)(2,1)}, u32[]{:S(2)}, u32[]{:S(2)}) collective-permute-start(bf16[768,256]{1,0:T(8,128)(2,1)} %get-tuple-element.110), channel_id=1, source_target_pairs={{2,0},{3,1},{4,2},{5,3},{6,4},{7,5},{8,6},{9,7},{10,8},{11,9},{12,... | collective-permute-start | bytes 1179656 | tf_op jit(solution)/shard_map/ppermute | solution.py:229
  58.9 11.8 %collective-permute-start.7 = (bf16[512,256]{1,0:T(8,128)(2,1)S(1)}, bf16[512,256]{1,0:T(8,128)(2,1)S(1)}, u32[]{:S(2)}, u32[]{:S(2)}) collective-permute-start(bf16[512,256]{1,0:T(8,128)(2,1)S(1)} %get-tuple-element.97), channel_id=1, source_target_pairs={{0,4},{1,5},{2,6},{3,7},{4,0},{5,1},{6,2},{7,3},{8,12},{9,13},{10,... | collective-permute-start | bytes 786440 | tf_op jit(solution)/shard_map/ppermute | solution.py:234
  63.3 8.4 %collective-permute-start.8 = (bf16[512,256]{1,0:T(8,128)(2,1)S(1)}, bf16[512,256]{1,0:T(8,128)(2,1)S(1)}, u32[]{:S(2)}, u32[]{:S(2)}) collective-permute-start(bf16[512,256]{1,0:T(8,128)(2,1)S(1)} %get-tuple-element.98), channel_id=1, source_target_pairs={{0,4},{1,5},{2,6},{3,7},{4,0},{5,1},{6,2},{7,3},{8,12},{9,13},{10,... | collective-permute-start | bytes 786440 | tf_op jit(solution)/shard_map/ppermute | solution.py:234
  68.2 1.0 copy-start.18
  69.2 2.6 %copy-start.32 = (bf16[512,256]{1,0:T(8,128)(2,1)}, bf16[512,256]{1,0:T(8,128)(2,1)S(1)}, u32[]{:S(2)}) copy-start(bf16[512,256]{1,0:T(8,128)(2,1)S(1)} %get-tuple-element.108) | copy-start | bytes 786436
  69.2 11.3 %copy-start.3 = (bf16[1024,768]{1,0:T(8,128)(2,1)S(1)}, bf16[1024,768]{1,0:T(8,128)(2,1)}, u32[]{:S(2)}) copy-start(bf16[1024,768]{1,0:T(8,128)(2,1)} %copy-done.2) | copy-start | bytes 4718596
  69.2 21.6 %collective-permute-start.12 = (bf16[512,256]{1,0:T(8,128)(2,1)}, bf16[512,256]{1,0:T(8,128)(2,1)S(1)}, u32[]{:S(2)}, u32[]{:S(2)}) collective-permute-start(bf16[512,256]{1,0:T(8,128)(2,1)} %get-tuple-element.107), channel_id=1, source_target_pairs={{0,4},{1,5},{2,6},{3,7},{4,0},{5,1},{6,2},{7,3},{8,12},{9,13},{10,... | collective-permute-start | bytes 786440 | tf_op jit(solution)/shard_map/ppermute | solution.py:234
  70.7 0.7 copy-start.26
  71.4 30.1 %collective-permute-start.20 = (bf16[768,256]{1,0:T(8,128)(2,1)}, bf16[768,256]{1,0:T(8,128)(2,1)}, u32[]{:S(2)}, u32[]{:S(2)}) collective-permute-start(bf16[768,256]{1,0:T(8,128)(2,1)} %get-tuple-element.122), channel_id=1, source_target_pairs={{14,0},{15,1},{0,2},{1,3},{2,4},{3,5},{4,6},{5,7},{6,8},{7,9},{8,1... | collective-permute-start | bytes 1179656 | tf_op jit(solution)/shard_map/ppermute | solution.py:229
  72.5 29.1 %collective-permute-start.21 = (bf16[768,256]{1,0:T(8,128)(2,1)}, bf16[768,256]{1,0:T(8,128)(2,1)}, u32[]{:S(2)}, u32[]{:S(2)}) collective-permute-start(bf16[768,256]{1,0:T(8,128)(2,1)} %get-tuple-element.123), channel_id=1, source_target_pairs={{2,0},{3,1},{4,2},{5,3},{6,4},{7,5},{8,6},{9,7},{10,8},{11,9},{12,... | collective-permute-start | bytes 1179656 | tf_op jit(solution)/shard_map/ppermute | solution.py:229
  76.9 17.2 %collective-permute-start.13 = (bf16[512,256]{1,0:T(8,128)(2,1)}, bf16[512,256]{1,0:T(8,128)(2,1)}, u32[]{:S(2)}, u32[]{:S(2)}) collective-permute-start(bf16[512,256]{1,0:T(8,128)(2,1)} %copy-done.32), channel_id=1, source_target_pairs={{0,4},{1,5},{2,6},{3,7},{4,0},{5,1},{6,2},{7,3},{8,12},{9,13},{10,... | collective-permute-start | bytes 786440 | tf_op jit(solution)/shard_map/ppermute | solution.py:234
  76.9 1.0 copy-start.27
  77.8 0.9 copy-start.29
  79.6 0.8 copy-start.22
  80.4 17.1 %collective-permute-start.11 = (bf16[512,256]{1,0:T(8,128)(2,1)}, bf16[512,256]{1,0:T(8,128)(2,1)}, u32[]{:S(2)}, u32[]{:S(2)}) collective-permute-start(bf16[512,256]{1,0:T(8,128)(2,1)} %get-tuple-element.105), channel_id=1, source_target_pairs={{0,2},{1,3},{2,0},{3,1},{4,6},{5,7},{6,4},{7,5},{8,10},{9,11},{10,... | collective-permute-start | bytes 786440 | tf_op jit(solution)/shard_map/ppermute | solution.py:234
  80.5 1.4 copy-start.5
  81.9 1.4 copy-start.8
  83.3 1.4 copy-start.11
  89.7 1.1 copy-start.16
  90.7 10.8 %copy-start.6 = (bf16[1024,768]{1,0:T(8,128)(2,1)S(1)}, bf16[1024,768]{1,0:T(8,128)(2,1)}, u32[]{:S(2)}) copy-start(bf16[1024,768]{1,0:T(8,128)(2,1)} %copy-done.4) | copy-start | bytes 4718596
  91.4 0.7 copy-start.24
  92.1 19.1 %collective-permute-start.18 = (bf16[512,256]{1,0:T(8,128)(2,1)}, bf16[512,256]{1,0:T(8,128)(2,1)S(1)}, u32[]{:S(2)}, u32[]{:S(2)}) collective-permute-start(bf16[512,256]{1,0:T(8,128)(2,1)} %get-tuple-element.120), channel_id=1, source_target_pairs={{0,4},{1,5},{2,6},{3,7},{4,0},{5,1},{6,2},{7,3},{8,12},{9,13},{10,... | collective-permute-start | bytes 786440 | tf_op jit(solution)/shard_map/ppermute | solution.py:234
  94.1 18.4 %collective-permute-start.19 = (bf16[512,256]{1,0:T(8,128)(2,1)}, bf16[512,256]{1,0:T(8,128)(2,1)S(1)}, u32[]{:S(2)}, u32[]{:S(2)}) collective-permute-start(bf16[512,256]{1,0:T(8,128)(2,1)} %copy-done.31), channel_id=1, source_target_pairs={{0,4},{1,5},{2,6},{3,7},{4,0},{5,1},{6,2},{7,3},{8,12},{9,13},{10,... | collective-permute-start | bytes 786440 | tf_op jit(solution)/shard_map/ppermute | solution.py:234
  94.2 1.2 copy-start.19
  95.4 0.9 copy-start.25
  96.3 5.2 %copy-start.21 = (bf16[1024,256]{1,0:T(8,128)(2,1)S(1)}, bf16[1024,256]{1,0:T(8,128)(2,1)}, u32[]{:S(2)}) copy-start(bf16[1024,256]{1,0:T(8,128)(2,1)} %copy-done.20) | copy-start | bytes 1572868
  97.5 16.5 %collective-permute-start.17 = (bf16[512,256]{1,0:T(8,128)(2,1)S(1)}, bf16[512,256]{1,0:T(8,128)(2,1)S(1)}, u32[]{:S(2)}, u32[]{:S(2)}) collective-permute-start(bf16[512,256]{1,0:T(8,128)(2,1)S(1)} %get-tuple-element.118), channel_id=1, source_target_pairs={{0,2},{1,3},{2,0},{3,1},{4,6},{5,7},{6,4},{7,5},{8,10},{9,11},{10,... | collective-permute-start | bytes 786440 | tf_op jit(solution)/shard_map/ppermute | solution.py:234
  99.5 1.0 copy-start.23
  101.6 1.4 copy-start.9
  103.0 1.4 copy-start.12
  104.4 8.0 %copy-start.17 = (f32[1024,256]{1,0:T(8,128)S(1)}, f32[1024,256]{1,0:T(8,128)}, u32[]{:S(2)}) copy-start(f32[1024,256]{1,0:T(8,128)} %copy-done.16) | copy-start | bytes 3145732
  109.1 12.4 %collective-permute-start.24 = (bf16[512,256]{1,0:T(8,128)(2,1)S(1)}, bf16[512,256]{1,0:T(8,128)(2,1)S(1)}, u32[]{:S(2)}, u32[]{:S(2)}) collective-permute-start(bf16[512,256]{1,0:T(8,128)(2,1)S(1)} %get-tuple-element.135), channel_id=1, source_target_pairs={{0,4},{1,5},{2,6},{3,7},{4,0},{5,1},{6,2},{7,3},{8,12},{9,13},{10,... | collective-permute-start | bytes 786440 | tf_op jit(solution)/shard_map/ppermute | solution.py:234
  111.1 11.1 %collective-permute-start.25 = (bf16[512,256]{1,0:T(8,128)(2,1)S(1)}, bf16[512,256]{1,0:T(8,128)(2,1)S(1)}, u32[]{:S(2)}, u32[]{:S(2)}) collective-permute-start(bf16[512,256]{1,0:T(8,128)(2,1)S(1)} %get-tuple-element.136), channel_id=1, source_target_pairs={{0,4},{1,5},{2,6},{3,7},{4,0},{5,1},{6,2},{7,3},{8,12},{9,13},{10,... | collective-permute-start | bytes 786440 | tf_op jit(solution)/shard_map/ppermute | solution.py:234
  111.2 10.2 %collective-permute-start.16 = (bf16[256,256]{1,0:T(8,128)(2,1)S(1)}, bf16[256,256]{1,0:T(8,128)(2,1)S(1)}, u32[]{:S(2)}, u32[]{:S(2)}) collective-permute-start(bf16[256,256]{1,0:T(8,128)(2,1)S(1)} %get-tuple-element.116), channel_id=1, source_target_pairs={{0,8},{1,9},{2,10},{3,11},{4,12},{5,13},{6,14},{7,15},{8,0},{9,1},... | collective-permute-start | bytes 393224 | tf_op jit(solution)/shard_map/ppermute | solution.py:234
  112.5 13.4 %collective-permute-start.23 = (bf16[512,256]{1,0:T(8,128)(2,1)S(1)}, bf16[512,256]{1,0:T(8,128)(2,1)S(1)}, u32[]{:S(2)}, u32[]{:S(2)}) collective-permute-start(bf16[512,256]{1,0:T(8,128)(2,1)S(1)} %get-tuple-element.133), channel_id=1, source_target_pairs={{0,2},{1,3},{2,0},{3,1},{4,6},{5,7},{6,4},{7,5},{8,10},{9,11},{10,... | collective-permute-start | bytes 786440 | tf_op jit(solution)/shard_map/ppermute | solution.py:234
  122.3 14.2 %collective-permute-start.27 = (bf16[512,256]{1,0:T(8,128)(2,1)S(1)}, bf16[512,256]{1,0:T(8,128)(2,1)S(1)}, u32[]{:S(2)}, u32[]{:S(2)}) collective-permute-start(bf16[512,256]{1,0:T(8,128)(2,1)S(1)} %get-tuple-element.144), channel_id=1, source_target_pairs={{0,2},{1,3},{2,0},{3,1},{4,6},{5,7},{6,4},{7,5},{8,10},{9,11},{10,... | collective-permute-start | bytes 786440 | tf_op jit(solution)/shard_map/ppermute | solution.py:234
  123.2 13.3 %collective-permute-start.22 = (bf16[256,256]{1,0:T(8,128)(2,1)S(1)}, bf16[256,256]{1,0:T(8,128)(2,1)S(1)}, u32[]{:S(2)}, u32[]{:S(2)}) collective-permute-start(bf16[256,256]{1,0:T(8,128)(2,1)S(1)} %get-tuple-element.131), channel_id=1, source_target_pairs={{0,8},{1,9},{2,10},{3,11},{4,12},{5,13},{6,14},{7,15},{8,0},{9,1},... | collective-permute-start | bytes 393224 | tf_op jit(solution)/shard_map/ppermute | solution.py:234
  126.0 12.4 %collective-permute-start.26 = (bf16[256,256]{1,0:T(8,128)(2,1)S(1)}, bf16[256,256]{1,0:T(8,128)(2,1)S(1)}, u32[]{:S(2)}, u32[]{:S(2)}) collective-permute-start(bf16[256,256]{1,0:T(8,128)(2,1)S(1)} %get-tuple-element.142), channel_id=1, source_target_pairs={{0,8},{1,9},{2,10},{3,11},{4,12},{5,13},{6,14},{7,15},{8,0},{9,1},... | collective-permute-start | bytes 393224 | tf_op jit(solution)/shard_map/ppermute | solution.py:234
  136.6 6.4 %collective-permute-start.28 = (bf16[256,256]{1,0:T(8,128)(2,1)S(1)}, bf16[256,256]{1,0:T(8,128)(2,1)S(1)}, u32[]{:S(2)}, u32[]{:S(2)}) collective-permute-start(bf16[256,256]{1,0:T(8,128)(2,1)S(1)} %get-tuple-element.149), channel_id=1, source_target_pairs={{0,8},{1,9},{2,10},{3,11},{4,12},{5,13},{6,14},{7,15},{8,0},{9,1},... | collective-permute-start | bytes 393224 | tf_op jit(solution)/shard_map/ppermute | solution.py:234
  136.7 6.4 %collective-permute-start.29 = (f32[128,256]{1,0:T(8,128)S(1)}, f32[128,256]{1,0:T(8,128)S(1)}, u32[]{:S(2)}, u32[]{:S(2)}) collective-permute-start(f32[128,256]{1,0:T(8,128)S(1)} %get-tuple-element.152), channel_id=1, source_target_pairs={{0,1},{1,0},{2,3},{3,2},{4,5},{5,4},{6,7},{7,6},{8,9},{9,8},{10,11... | collective-permute-start | bytes 393224 | tf_op jit(solution)/shard_map/ppermute | solution.py:234
  136.7 6.4 %collective-permute-start.30 = (f32[128,256]{1,0:T(8,128)S(1)}, f32[128,256]{1,0:T(8,128)S(1)}, u32[]{:S(2)}, u32[]{:S(2)}) collective-permute-start(f32[128,256]{1,0:T(8,128)S(1)} %get-tuple-element.153), channel_id=1, source_target_pairs={{0,1},{1,0},{2,3},{3,2},{4,5},{5,4},{6,7},{7,6},{8,9},{9,8},{10,11... | collective-permute-start | bytes 393224 | tf_op jit(solution)/shard_map/ppermute | solution.py:234
  138.4 4.7 %collective-permute-start.31 = (f32[128,256]{1,0:T(8,128)S(1)}, f32[128,256]{1,0:T(8,128)S(1)}, u32[]{:S(2)}, u32[]{:S(2)}) collective-permute-start(f32[128,256]{1,0:T(8,128)S(1)} %get-tuple-element.154), channel_id=1, source_target_pairs={{0,1},{1,0},{2,3},{3,2},{4,5},{5,4},{6,7},{7,6},{8,9},{9,8},{10,11... | collective-permute-start | bytes 393224 | tf_op jit(solution)/shard_map/ppermute | solution.py:234
  143.0 1.4 collective-permute-start.32
  (2 other events, 1.4 us)

commit v6 on v5

--- a/solution.py
+++ b/solution.py
@@ -9,6 +9,7 @@
 UNITS = (2, 2, 2, 2)
 PARTS = 2
 EARLY = 4
+PACE = 4 * 10**9
 LIMIT = 16 * 2**20
 ANY = pl.BlockSpec(memory_space=pl.ANY)
 BF16, F32 = jnp.bfloat16, jnp.float32
@@ -18,7 +19,7 @@
 FOUND = ((0, 2, 7, 9, 4), (1, 6, 8, 3, 5))
 
 
-def call(body, scalars, arrays, after, out_shape, scratch=(), fetched=0, scalar_out=False):
+def call(body, scalars, arrays, after, out_shape, scratch=(), fetched=0, scalar_out=False, time=1.0):
     lead = len(scalars) + len(arrays)
     extra = len(after)
     outs = len(out_shape)
@@ -38,9 +39,13 @@
         out_specs=[smem if scalar_out else vmem] * outs + [ANY],
         scratch_shapes=scratch,
         compiler_params=pltpu.CompilerParams(vmem_limit_bytes=LIMIT),
-        cost_estimate=pl.CostEstimate(flops=1, bytes_accessed=1, transcendentals=0),
+        cost_estimate=pl.CostEstimate(flops=int(time * PACE), bytes_accessed=1, transcendentals=0),
         name=body.__name__,
     )(*scalars, *arrays, *after)
+
+
+def in_hbm(array):
+    return pltpu.with_memory_space_constraint(array, pltpu.HBM)
 
 
 def coupled(core, blocks, acoustic, coupling, at, width, after):
@@ -81,7 +86,7 @@
     return call(
         coupled_rows,
         [core, *blocks],
-        [*acoustic, *coupling],
+        [in_hbm(acoustic[0]), acoustic[1], in_hbm(coupling[0]), coupling[1]],
         after,
         [jax.ShapeDtypeStruct(shape, BF16) for shape in shapes],
         [
@@ -91,6 +96,7 @@
             pltpu.SemaphoreType.DMA((4,)),
         ],
         fetched=4,
+        time=2.5,
     )
 
 
@@ -113,7 +119,7 @@
             for one in (side[0], 1 - side[0])
         ]
         return [*pair, after[0]]
-    return call(turn, [side], [struct_modes], after, [jax.ShapeDtypeStruct((half, depth), BF16)] * 2)
+    return call(turn, [side], [struct_modes], after, [jax.ShapeDtypeStruct((half, depth), BF16)] * 2, time=2.5)
 
 
 def rows_times(left_own, left_far, picked, out):
@@ -180,6 +186,7 @@
         [jax.ShapeDtypeStruct((tall // PARTS, width), BF16)] * PARTS
         + [jax.ShapeDtypeStruct((tall, width), F32)],
         [pltpu.VMEM((2 * depth, width), BF16)],
+        time=4.0,
     )
 
 
@@ -263,7 +270,6 @@
     blocks = (face_blocks, swapped(face_blocks, 0))
     couplings = (coupling, swapped(coupling, 0))
     acoustics = (acoustic_modes, swapped(acoustic_modes, 0))
-    far_struct = swapped(struct_modes, 0)
     shifts = (face_shift, swapped(face_shift, 0))
     per = coupling.shape[0] // CLASSES
     state = [dict(bits=sorted([0, *order[1:]], reverse=True)) for _ in widths]
@@ -275,11 +281,14 @@
                 core, blocks, acoustics, couplings, starts[j], widths[j], token
             )
             now["pieces"] = [passed_along(ahead, 2), passed_along(behind, -2), here]
+            if j == 0:
+                later, _ = lax.optimization_barrier((struct_modes, last))
+                now["far"] = swapped(later, 0)
         elif stage == "turned":
             side = bit_of(order[0])
             *own, last = turned(side, order[0], struct_modes, share, token)
             slots, last = slots_of(core, shifts, per, [last])
-            *far, last = turned(side, order[0], far_struct, share, [last])
+            *far, last = turned(side, order[0], now["far"], share, [last])
             kept, sent = zip(own, far)
         elif stage == "panel":
             *away, now["held"], last = panel(slots, (*kept, *sent), now["pieces"], token)

time: 146 us -> 139 us (0.952)
  starting transfers between devices: 35.4 us -> 49.5 us
  local copies, waits for them, and re-layouts: 22.1 us -> 9.77 us
  waiting for transfers between devices: 48.3 us -> 43.2 us
  Pallas kernels: 39.3 us -> 35.7 us
    ppermute x25, starting transfers between devices: 17.7 us -> 31 us  [swapped(): return lax.ppermute(block, 'mesh', [(i, i ^ 1 << bit) for i in range(size)])]
    unnamed x67 -> x33, local copies, waits for them, and re-layouts: 22.1 us -> 9.77 us
    ppermute x25, waiting for transfers between devices: 33.3 us -> 28.1 us  [swapped(): return lax.ppermute(block, 'mesh', [(i, i ^ 1 << bit) for i in range(size)])]
    pallas_call x24, Pallas kernels: 39.3 us -> 35.7 us  [call(): pl.pallas_call(kernel, out_shape=[*out_shape, jax.ShapeDtypeStruct((8, 12...]
  transfers between devices with their start and end apart: 33 -> 33, of which waited for: 12 -> 13; matrix products, arithmetic and copies ran while one was open for 1% -> 1% of each run, Pallas kernels for 26% -> 23%
where the time goes in v6:
time: 139 us; the launch traced here: 138 us
  starting transfers between devices  49.5 us (36%)
  waiting for transfers between devices  43.2 us (31%)
  Pallas kernels  35.7 us (26%)
  local copies, waits for them, and re-layouts  9.77 us (7%)
    pallas_call x24, Pallas kernels, call(): pl.pallas_call(kernel, out_shape=[*out_shape, jax.ShapeDtypeStruct((8, 12...  35.7 us
    ppermute x25, starting transfers between devices, swapped(): return lax.ppermute(block, 'mesh', [(i, i ^ 1 << bit) for i in range(size)])  31 us
    ppermute x25, waiting for transfers between devices, swapped(): return lax.ppermute(block, 'mesh', [(i, i ^ 1 << bit) for i in range(size)])  28.1 us
    ppermute x8, starting transfers between devices, passed_along(): lax.ppermute(block, 'mesh', [((i - distance) % size, i) for i in range(si...  18.6 us
    ppermute x8, waiting for transfers between devices, passed_along(): lax.ppermute(block, 'mesh', [((i - distance) % size, i) for i in range(si...  15 us
    unnamed x33, local copies, waits for them, and re-layouts  9.77 us
  transfers between devices with their start and end apart: 33, of which 13 were waited for; matrix products, arithmetic and copies ran while one was open for 1% of the time, Pallas kernels for 23%

profile of v6, /device:TPU:0, one launch (start us, length us, event | category | flops | bytes accessed | tf_op | source)
XLA Modules:
  0.0 138.5 jit_solution(14263370068149601843)
XLA Ops:
  0.0 0.5 collective-permute-start.2
  0.5 0.8 copy.7.refs_1_
  1.3 0.5 collective-permute-start.1
  1.7 2.5 %collective-permute-done.1.refs_2_ = s32[20,4]{1,0:T(8,128)S(1)} collective-permute-done((s32[20,4]{1,0:T(8,128)S(1)}, s32[20,4]{1,0:T(8,128)S(1)}, u32[]{:S(2)}, u32[]{:S(2)}) %collective-permute-start.1) | collective-permute-done | bytes 352 | tf_op jit(solution)/shard_map/ppermute | solution.py:241
  4.3 0.6 copy-done.8
  4.9 0.5 collective-permute-done.3.refs_6_
  5.4 0.8 copy-done.4
  6.2 1.3 copy-done.1
  7.6 1.6 %copy-done.2 = bf16[512,2048]{1,0:T(8,128)(2,1)S(1)} copy-done((bf16[512,2048]{1,0:T(8,128)(2,1)S(1)}, bf16[512,2048]{1,0:T(8,128)(2,1)}, u32[]{:S(2)}) %copy-start.2) | copy-done | bytes 2097176
  9.2 1.1 copy-done.5
  10.3 0.7 copy-done.9
  11.0 3.2 %coupled_rows.4 = (bf16[768,256]{1,0:T(8,128)(2,1)S(1)}, bf16[768,256]{1,0:T(8,128)(2,1)S(1)}, bf16[1024,256]{1,0:T(8,128)(2,1)S(1)}, f32[8,128]{1,0:T(8,128)S(1)}) custom-call(s32[1]{0:T(128)} %bitcast.refs_0_, s32[20,4]{1,0:T(8,128)S(1)} %copy.7.refs_1_, s32[20,4]{1,0:T(8,128)S(1)} %copy-done.9, bf16[512,2048]{1,0:T(8,128)(2,1)} %refs_3_.7, ...), custom_call_target="tpu_custom_call" | custom-call | flops 10000000000 | bytes 1 | tf_op jit(solution)/shard_map/coupled_rows/pallas_call | solution.py:33
  14.2 0.8 copy-done.7
  14.9 0.8 copy-done.12
  15.7 0.6 copy-done.14
  16.3 0.4 collective-permute-start.4
  16.7 0.1 collective-permute-start
  16.8 2.9 %collective-permute-start.5 = (bf16[768,256]{1,0:T(8,128)(2,1)}, bf16[768,256]{1,0:T(8,128)(2,1)S(1)}, u32[]{:S(2)}, u32[]{:S(2)}) collective-permute-start(bf16[768,256]{1,0:T(8,128)(2,1)} %copy-done.7), channel_id=1, source_target_pairs={{14,0},{15,1},{0,2},{1,3},{2,4},{3,5},{4,6},{5,7},{6,8},{7,9},{8,1... | collective-permute-start | bytes 1179656 | tf_op jit(solution)/shard_map/ppermute | solution.py:236
  19.7 3.0 %collective-permute-start.6 = (bf16[768,256]{1,0:T(8,128)(2,1)S(1)}, bf16[768,256]{1,0:T(8,128)(2,1)S(1)}, u32[]{:S(2)}, u32[]{:S(2)}) collective-permute-start(bf16[768,256]{1,0:T(8,128)(2,1)S(1)} %get-tuple-element.92), channel_id=1, source_target_pairs={{2,0},{3,1},{4,2},{5,3},{6,4},{7,5},{8,6},{9,7},{10,8},{11,9},{12,... | collective-permute-start | bytes 1179656 | tf_op jit(solution)/shard_map/ppermute | solution.py:236
  22.7 0.7 copy-done.15
  23.4 0.9 turn.2
  24.3 1.5 %slots.1 = (s32[24]{0:T(128)S(1)}, f32[8,128]{1,0:T(8,128)S(1)}) custom-call(s32[1]{0:T(128)} %bitcast.refs_0_, s32[12]{0:T(128)S(1)} %copy-done.11, s32[12]{0:T(128)} %collective-permute-done.refs_2_, f32[8,128]{1,0:T(8,128)S(1)} %get-tuple-element.83.refs_3_), custom_call_target="tpu_custom_call" | custom-call | flops 4000000000 | bytes 1 | tf_op jit(solution)/shard_map/slots/pallas_call | solution.py:33
  25.8 2.9 %turn.3 = (bf16[1024,768]{1,0:T(8,128)(2,1)S(1)}, bf16[1024,768]{1,0:T(8,128)(2,1)S(1)}, f32[8,128]{1,0:T(8,128)S(1)}) custom-call(s32[1]{0:T(128)} %bitcast.3.refs_0_, bf16[768,2048]{1,0:T(8,128)(2,1)} %collective-permute-done.4.refs_1_, f32[8,128]{1,0:T(8,128)S(1)} %get-tuple-element.87.refs_2_), custom_call_target="tpu_custom_call" | custom-call | flops 10000000000 | bytes 1 | tf_op jit(solution)/shard_map/turn/pallas_call | solution.py:33
  28.8 3.2 %coupled_rows.5 = (bf16[768,256]{1,0:T(8,128)(2,1)S(1)}, bf16[768,256]{1,0:T(8,128)(2,1)S(1)}, bf16[1024,256]{1,0:T(8,128)(2,1)S(1)}, f32[8,128]{1,0:T(8,128)S(1)}) custom-call(s32[1]{0:T(128)} %bitcast.refs_0_, s32[20,4]{1,0:T(8,128)S(1)} %copy.7.refs_1_, s32[20,4]{1,0:T(8,128)S(1)} %copy-done.10, bf16[512,2048]{1,0:T(8,128)(2,1)} %refs_3_.7, ...), custom_call_target="tpu_custom_call" | custom-call | flops 10000000000 | bytes 1 | tf_op jit(solution)/shard_map/coupled_rows/pallas_call | solution.py:33
  32.0 3.7 %collective-permute-start.10 = (bf16[768,256]{1,0:T(8,128)(2,1)S(1)}, bf16[768,256]{1,0:T(8,128)(2,1)S(1)}, u32[]{:S(2)}, u32[]{:S(2)}) collective-permute-start(bf16[768,256]{1,0:T(8,128)(2,1)S(1)} %get-tuple-element.102), channel_id=1, source_target_pairs={{2,0},{3,1},{4,2},{5,3},{6,4},{7,5},{8,6},{9,7},{10,8},{11,9},{12,... | collective-permute-start | bytes 1179656 | tf_op jit(solution)/shard_map/ppermute | solution.py:236
  35.7 3.2 %coupled_rows.6 = (bf16[768,256]{1,0:T(8,128)(2,1)S(1)}, bf16[768,256]{1,0:T(8,128)(2,1)S(1)}, bf16[1024,256]{1,0:T(8,128)(2,1)S(1)}, f32[8,128]{1,0:T(8,128)S(1)}) custom-call(s32[1]{0:T(128)} %bitcast.refs_0_, s32[20,4]{1,0:T(8,128)S(1)} %copy.7.refs_1_, s32[20,4]{1,0:T(8,128)S(1)} %copy-done.10, bf16[512,2048]{1,0:T(8,128)(2,1)} %refs_3_.7, ...), custom_call_target="tpu_custom_call" | custom-call | flops 10000000000 | bytes 1 | tf_op jit(solution)/shard_map/coupled_rows/pallas_call | solution.py:33
  38.9 3.2 %coupled_rows.7 = (bf16[768,256]{1,0:T(8,128)(2,1)S(1)}, bf16[768,256]{1,0:T(8,128)(2,1)S(1)}, bf16[1024,256]{1,0:T(8,128)(2,1)S(1)}, f32[8,128]{1,0:T(8,128)S(1)}) custom-call(s32[1]{0:T(128)} %bitcast.refs_0_, s32[20,4]{1,0:T(8,128)S(1)} %copy.7.refs_1_, s32[20,4]{1,0:T(8,128)S(1)} %copy-done.10, bf16[512,2048]{1,0:T(8,128)(2,1)} %refs_3_.7, ...), custom_call_target="tpu_custom_call" | custom-call | flops 10000000000 | bytes 1 | tf_op jit(solution)/shard_map/coupled_rows/pallas_call | solution.py:33
  42.1 4.2 %collective-permute-done.5.refs_5_ = bf16[768,256]{1,0:T(8,128)(2,1)S(1)} collective-permute-done((bf16[768,256]{1,0:T(8,128)(2,1)}, bf16[768,256]{1,0:T(8,128)(2,1)S(1)}, u32[]{:S(2)}, u32[]{:S(2)}) %collective-permute-start.5) | collective-permute-done | bytes 393248 | tf_op jit(solution)/shard_map/ppermute | solution.py:236
  46.4 4.0 %panel_part.4 = (bf16[512,256]{1,0:T(8,128)(2,1)S(1)}, bf16[512,256]{1,0:T(8,128)(2,1)S(1)}, f32[1024,256]{1,0:T(8,128)S(1)}, f32[8,128]{1,0:T(8,128)S(1)}) custom-call(s32[24]{0:T(128)S(1)} %get-tuple-element.84.refs_0_, bf16[1024,768]{1,0:T(8,128)(2,1)S(1)} %get-tuple-element.85.refs_1_, bf16[1024,768]{1,0:T(8,128)(2,1)S(1)} %get-tuple-element.88.refs_2_, ...), custom_call_target="tpu_custom_call" | custom-call | flops 16000000000 | bytes 1 | tf_op jit(solution)/shard_map/panel_part/pallas_call | solution.py:33
  50.4 2.7 %collective-permute-start.7 = (bf16[512,256]{1,0:T(8,128)(2,1)S(1)}, bf16[512,256]{1,0:T(8,128)(2,1)S(1)}, u32[]{:S(2)}, u32[]{:S(2)}) collective-permute-start(bf16[512,256]{1,0:T(8,128)(2,1)S(1)} %get-tuple-element.99), channel_id=1, source_target_pairs={{0,4},{1,5},{2,6},{3,7},{4,0},{5,1},{6,2},{7,3},{8,12},{9,13},{10,... | collective-permute-start | bytes 786440 | tf_op jit(solution)/shard_map/ppermute | solution.py:241
  53.2 1.7 %collective-permute-start.14 = (bf16[768,256]{1,0:T(8,128)(2,1)S(1)}, bf16[768,256]{1,0:T(8,128)(2,1)S(1)}, u32[]{:S(2)}, u32[]{:S(2)}) collective-permute-start(bf16[768,256]{1,0:T(8,128)(2,1)S(1)} %get-tuple-element.111), channel_id=1, source_target_pairs={{14,0},{15,1},{0,2},{1,3},{2,4},{3,5},{4,6},{5,7},{6,8},{7,9},{8,1... | collective-permute-start | bytes 1179656 | tf_op jit(solution)/shard_map/ppermute | solution.py:236
  54.8 1.0 collective-permute-done.10.refs_6_
  55.9 2.5 %collective-permute-start.15 = (bf16[768,256]{1,0:T(8,128)(2,1)S(1)}, bf16[768,256]{1,0:T(8,128)(2,1)S(1)}, u32[]{:S(2)}, u32[]{:S(2)}) collective-permute-start(bf16[768,256]{1,0:T(8,128)(2,1)S(1)} %get-tuple-element.112), channel_id=1, source_target_pairs={{2,0},{3,1},{4,2},{5,3},{6,4},{7,5},{8,6},{9,7},{10,8},{11,9},{12,... | collective-permute-start | bytes 1179656 | tf_op jit(solution)/shard_map/ppermute | solution.py:236
  58.3 4.0 %panel_part.5 = (bf16[512,256]{1,0:T(8,128)(2,1)S(1)}, bf16[512,256]{1,0:T(8,128)(2,1)S(1)}, f32[1024,256]{1,0:T(8,128)S(1)}, f32[8,128]{1,0:T(8,128)S(1)}) custom-call(s32[24]{0:T(128)S(1)} %get-tuple-element.84.refs_0_, bf16[1024,768]{1,0:T(8,128)(2,1)S(1)} %get-tuple-element.85.refs_1_, bf16[1024,768]{1,0:T(8,128)(2,1)S(1)} %get-tuple-element.88.refs_2_, ...), custom_call_target="tpu_custom_call" | custom-call | flops 16000000000 | bytes 1 | tf_op jit(solution)/shard_map/panel_part/pallas_call | solution.py:33
  62.4 4.8 %collective-permute-start.21 = (bf16[768,256]{1,0:T(8,128)(2,1)S(1)}, bf16[768,256]{1,0:T(8,128)(2,1)S(1)}, u32[]{:S(2)}, u32[]{:S(2)}) collective-permute-start(bf16[768,256]{1,0:T(8,128)(2,1)S(1)} %get-tuple-element.125), channel_id=1, source_target_pairs={{2,0},{3,1},{4,2},{5,3},{6,4},{7,5},{8,6},{9,7},{10,8},{11,9},{12,... | collective-permute-start | bytes 1179656 | tf_op jit(solution)/shard_map/ppermute | solution.py:236
  67.1 0.7 collective-permute-start.12
  67.9 0.1 added_split.12
  68.0 9.7 %collective-permute-done.14.refs_5_ = bf16[768,256]{1,0:T(8,128)(2,1)S(1)} collective-permute-done((bf16[768,256]{1,0:T(8,128)(2,1)S(1)}, bf16[768,256]{1,0:T(8,128)(2,1)S(1)}, u32[]{:S(2)}, u32[]{:S(2)}) %collective-permute-start.14) | collective-permute-done | bytes 393248 | tf_op jit(solution)/shard_map/ppermute | solution.py:236
  77.7 5.1 %collective-permute-start.13 = (bf16[512,256]{1,0:T(8,128)(2,1)S(1)}, bf16[512,256]{1,0:T(8,128)(2,1)S(1)}, u32[]{:S(2)}, u32[]{:S(2)}) collective-permute-start(bf16[512,256]{1,0:T(8,128)(2,1)S(1)} %get-tuple-element.110), channel_id=1, source_target_pairs={{0,4},{1,5},{2,6},{3,7},{4,0},{5,1},{6,2},{7,3},{8,12},{9,13},{10,... | collective-permute-start | bytes 786440 | tf_op jit(solution)/shard_map/ppermute | solution.py:241
  82.8 2.5 %collective-permute-start.11 = (bf16[512,256]{1,0:T(8,128)(2,1)S(1)}, bf16[512,256]{1,0:T(8,128)(2,1)S(1)}, u32[]{:S(2)}, u32[]{:S(2)}) collective-permute-start(bf16[512,256]{1,0:T(8,128)(2,1)S(1)} %get-tuple-element.107), channel_id=1, source_target_pairs={{0,2},{1,3},{2,0},{3,1},{4,6},{5,7},{6,4},{7,5},{8,10},{9,11},{10,... | collective-permute-start | bytes 786440 | tf_op jit(solution)/shard_map/ppermute | solution.py:241
  85.3 4.0 %panel_part.6 = (bf16[512,256]{1,0:T(8,128)(2,1)S(1)}, bf16[512,256]{1,0:T(8,128)(2,1)S(1)}, f32[1024,256]{1,0:T(8,128)S(1)}, f32[8,128]{1,0:T(8,128)S(1)}) custom-call(s32[24]{0:T(128)S(1)} %get-tuple-element.84.refs_0_, bf16[1024,768]{1,0:T(8,128)(2,1)S(1)} %get-tuple-element.85.refs_1_, bf16[1024,768]{1,0:T(8,128)(2,1)S(1)} %get-tuple-element.88.refs_2_, ...), custom_call_target="tpu_custom_call" | custom-call | flops 16000000000 | bytes 1 | tf_op jit(solution)/shard_map/panel_part/pallas_call | solution.py:33
  89.3 1.0 collective-permute-start.18
  90.4 3.6 %collective-permute-done.13 = bf16[512,256]{1,0:T(8,128)(2,1)S(1)} collective-permute-done((bf16[512,256]{1,0:T(8,128)(2,1)S(1)}, bf16[512,256]{1,0:T(8,128)(2,1)S(1)}, u32[]{:S(2)}, u32[]{:S(2)}) %collective-permute-start.13) | collective-permute-done | bytes 262176 | tf_op jit(solution)/shard_map/ppermute | solution.py:241
  94.0 2.0 %collective-permute-start.19 = (bf16[512,256]{1,0:T(8,128)(2,1)S(1)}, bf16[512,256]{1,0:T(8,128)(2,1)S(1)}, u32[]{:S(2)}, u32[]{:S(2)}) collective-permute-start(bf16[512,256]{1,0:T(8,128)(2,1)S(1)} %get-tuple-element.123), channel_id=1, source_target_pairs={{0,4},{1,5},{2,6},{3,7},{4,0},{5,1},{6,2},{7,3},{8,12},{9,13},{10,... | collective-permute-start | bytes 786440 | tf_op jit(solution)/shard_map/ppermute | solution.py:241
  96.0 0.1 added_split.13
  96.1 0.7 collective-permute-done.11
  96.8 0.8 collective-permute-start.17
  97.6 3.1 %collective-permute-start.16 = (bf16[256,256]{1,0:T(8,128)(2,1)S(1)}, bf16[256,256]{1,0:T(8,128)(2,1)S(1)}, u32[]{:S(2)}, u32[]{:S(2)}) collective-permute-start(bf16[256,256]{1,0:T(8,128)(2,1)S(1)} %get-tuple-element.118), channel_id=1, source_target_pairs={{0,8},{1,9},{2,10},{3,11},{4,12},{5,13},{6,14},{7,15},{8,0},{9,1},... | collective-permute-start | bytes 393224 | tf_op jit(solution)/shard_map/ppermute | solution.py:241
  100.7 4.0 %panel_part.7 = (bf16[512,256]{1,0:T(8,128)(2,1)S(1)}, bf16[512,256]{1,0:T(8,128)(2,1)S(1)}, f32[1024,256]{1,0:T(8,128)S(1)}, f32[8,128]{1,0:T(8,128)S(1)}) custom-call(s32[24]{0:T(128)S(1)} %get-tuple-element.84.refs_0_, bf16[1024,768]{1,0:T(8,128)(2,1)S(1)} %get-tuple-element.85.refs_1_, bf16[1024,768]{1,0:T(8,128)(2,1)S(1)} %get-tuple-element.88.refs_2_, ...), custom_call_target="tpu_custom_call" | custom-call | flops 16000000000 | bytes 1 | tf_op jit(solution)/shard_map/panel_part/pallas_call | solution.py:33
  104.8 1.3 collective-permute-start.24
  106.1 0.8 collective-permute-start.25
  106.9 1.1 collective-permute-done.19
  108.1 0.9 collective-permute-start.23
  109.1 4.6 %collective-permute-start.22 = (bf16[256,256]{1,0:T(8,128)(2,1)S(1)}, bf16[256,256]{1,0:T(8,128)(2,1)S(1)}, u32[]{:S(2)}, u32[]{:S(2)}) collective-permute-start(bf16[256,256]{1,0:T(8,128)(2,1)S(1)} %get-tuple-element.133), channel_id=1, source_target_pairs={{0,8},{1,9},{2,10},{3,11},{4,12},{5,13},{6,14},{7,15},{8,0},{9,1},... | collective-permute-start | bytes 393224 | tf_op jit(solution)/shard_map/ppermute | solution.py:241
  113.7 3.2 %collective-permute-done.24 = bf16[512,256]{1,0:T(8,128)(2,1)S(1)} collective-permute-done((bf16[512,256]{1,0:T(8,128)(2,1)S(1)}, bf16[512,256]{1,0:T(8,128)(2,1)S(1)}, u32[]{:S(2)}, u32[]{:S(2)}) %collective-permute-start.24) | collective-permute-done | bytes 262176 | tf_op jit(solution)/shard_map/ppermute | solution.py:241
  116.9 4.4 %collective-permute-done.25 = bf16[512,256]{1,0:T(8,128)(2,1)S(1)} collective-permute-done((bf16[512,256]{1,0:T(8,128)(2,1)S(1)}, bf16[512,256]{1,0:T(8,128)(2,1)S(1)}, u32[]{:S(2)}, u32[]{:S(2)}) %collective-permute-start.25) | collective-permute-done | bytes 262176 | tf_op jit(solution)/shard_map/ppermute | solution.py:241
  121.4 0.5 collective-permute-start.27
  122.0 1.5 %collective-permute-start.26 = (bf16[256,256]{1,0:T(8,128)(2,1)S(1)}, bf16[256,256]{1,0:T(8,128)(2,1)S(1)}, u32[]{:S(2)}, u32[]{:S(2)}) collective-permute-start(bf16[256,256]{1,0:T(8,128)(2,1)S(1)} %get-tuple-element.144), channel_id=1, source_target_pairs={{0,8},{1,9},{2,10},{3,11},{4,12},{5,13},{6,14},{7,15},{8,0},{9,1},... | collective-permute-start | bytes 393224 | tf_op jit(solution)/shard_map/ppermute | solution.py:241
  123.5 0.6 collective-permute-start.30
  124.0 4.6 %collective-permute-done.27 = bf16[512,256]{1,0:T(8,128)(2,1)S(1)} collective-permute-done((bf16[512,256]{1,0:T(8,128)(2,1)S(1)}, bf16[512,256]{1,0:T(8,128)(2,1)S(1)}, u32[]{:S(2)}, u32[]{:S(2)}) %collective-permute-start.27) | collective-permute-done | bytes 262176 | tf_op jit(solution)/shard_map/ppermute | solution.py:241
  128.7 1.1 collective-permute-start.28
  129.9 6.1 %collective-permute-done.28 = bf16[256,256]{1,0:T(8,128)(2,1)S(1)} collective-permute-done((bf16[256,256]{1,0:T(8,128)(2,1)S(1)}, bf16[256,256]{1,0:T(8,128)(2,1)S(1)}, u32[]{:S(2)}, u32[]{:S(2)}) %collective-permute-start.28) | collective-permute-done | bytes 131104 | tf_op jit(solution)/shard_map/ppermute | solution.py:241
  136.1 1.3 collective-permute-done.32.refs_8_
  137.4 1.0 put_together.1
  (59 shorter events, 0.9 us)
Async XLA Ops:
  0.0 6.2 %collective-permute-start.2 = (bf16[512,2048]{1,0:T(8,128)(2,1)}, bf16[512,2048]{1,0:T(8,128)(2,1)S(1)}, u32[]{:S(2)}, u32[]{:S(2)}) collective-permute-start(bf16[512,2048]{1,0:T(8,128)(2,1)} %refs_3_.7), channel_id=1, source_target_pairs={{0,1},{1,0},{2,3},{3,2},{4,5},{5,4},{6,7},{7,6},{8,9},{9,8},{10,11... | collective-permute-start | bytes 6291464 | tf_op jit(solution)/shard_map/ppermute | solution.py:241
  0.5 5.0 %collective-permute-start.3 = (bf16[20,64,256]{2,1,0:T(8,128)(2,1)}, bf16[20,64,256]{2,1,0:T(8,128)(2,1)S(1)}, u32[]{:S(2)}, u32[]{:S(2)}) collective-permute-start(bf16[20,64,256]{2,1,0:T(8,128)(2,1)} %refs_5_.7), channel_id=1, source_target_pairs={{0,1},{1,0},{2,3},{3,2},{4,5},{5,4},{6,7},{7,6},{8,9},{9,8},{10,11... | collective-permute-start | bytes 1966088 | tf_op jit(solution)/shard_map/ppermute | solution.py:241
  1.3 3.0 %collective-permute-start.1 = (s32[20,4]{1,0:T(8,128)S(1)}, s32[20,4]{1,0:T(8,128)S(1)}, u32[]{:S(2)}, u32[]{:S(2)}) collective-permute-start(s32[20,4]{1,0:T(8,128)S(1)} %copy.7.refs_1_), channel_id=1, source_target_pairs={{0,1},{1,0},{2,3},{3,2},{4,5},{5,4},{6,7},{7,6},{8,9},{9,8},{10,11... | collective-permute-start | bytes 968 | tf_op jit(solution)/shard_map/ppermute | solution.py:241
  4.3 0.6 copy-start.8
  5.4 0.8 copy-start.4
  6.2 1.3 copy-start.1
  7.6 1.6 %copy-start.2 = (bf16[512,2048]{1,0:T(8,128)(2,1)S(1)}, bf16[512,2048]{1,0:T(8,128)(2,1)}, u32[]{:S(2)}) copy-start(bf16[512,2048]{1,0:T(8,128)(2,1)} %copy-done.1) | copy-start | bytes 6291460
  9.2 1.1 copy-start.5
  10.2 0.7 copy-start.9
  11.0 5.4 %copy-start = (bf16[768,2048]{1,0:T(8,128)(2,1)S(1)}, bf16[768,2048]{1,0:T(8,128)(2,1)}, u32[]{:S(2)}) copy-start(bf16[768,2048]{1,0:T(8,128)(2,1)} %refs_1_.6) | copy-start | bytes 9437188
  11.0 5.7 %copy-start.11 = (s32[12]{0:T(128)S(1)}, s32[12]{0:T(128)}, u32[]{:S(2)}) copy-start(s32[12]{0:T(128)} %refs_1_.7) | copy-start | bytes 148
  14.2 0.8 copy-start.7
  14.9 0.8 copy-start.12
  15.7 0.6 copy-start.14
  16.3 9.5 %collective-permute-start.4 = (bf16[768,2048]{1,0:T(8,128)(2,1)S(1)}, bf16[768,2048]{1,0:T(8,128)(2,1)}, u32[]{:S(2)}, u32[]{:S(2)}) collective-permute-start(bf16[768,2048]{1,0:T(8,128)(2,1)S(1)} %copy-done), channel_id=1, source_target_pairs={{0,1},{1,0},{2,3},{3,2},{4,5},{5,4},{6,7},{7,6},{8,9},{9,8},{10,11... | collective-permute-start | bytes 9437192 | tf_op jit(solution)/shard_map/ppermute | solution.py:241
  16.7 7.6 %collective-permute-start = (s32[12]{0:T(128)S(1)}, s32[12]{0:T(128)}, u32[]{:S(2)}, u32[]{:S(2)}) collective-permute-start(s32[12]{0:T(128)S(1)} %copy-done.11), channel_id=1, source_target_pairs={{0,1},{1,0},{2,3},{3,2},{4,5},{5,4},{6,7},{7,6},{8,9},{9,8},{10,11... | collective-permute-start | bytes 152 | tf_op jit(solution)/shard_map/ppermute | solution.py:241
  16.8 29.5 %collective-permute-start.5 = (bf16[768,256]{1,0:T(8,128)(2,1)}, bf16[768,256]{1,0:T(8,128)(2,1)S(1)}, u32[]{:S(2)}, u32[]{:S(2)}) collective-permute-start(bf16[768,256]{1,0:T(8,128)(2,1)} %copy-done.7), channel_id=1, source_target_pairs={{14,0},{15,1},{0,2},{1,3},{2,4},{3,5},{4,6},{5,7},{6,8},{7,9},{8,1... | collective-permute-start | bytes 1179656 | tf_op jit(solution)/shard_map/ppermute | solution.py:236
  19.7 26.6 %collective-permute-start.6 = (bf16[768,256]{1,0:T(8,128)(2,1)S(1)}, bf16[768,256]{1,0:T(8,128)(2,1)S(1)}, u32[]{:S(2)}, u32[]{:S(2)}) collective-permute-start(bf16[768,256]{1,0:T(8,128)(2,1)S(1)} %get-tuple-element.92), channel_id=1, source_target_pairs={{2,0},{3,1},{4,2},{5,3},{6,4},{7,5},{8,6},{9,7},{10,8},{11,9},{12,... | collective-permute-start | bytes 1179656 | tf_op jit(solution)/shard_map/ppermute | solution.py:236
  22.7 0.7 copy-start.15
  25.8 3.0 %copy-start.3 = (bf16[512,2048]{1,0:T(8,128)(2,1)S(1)}, bf16[512,2048]{1,0:T(8,128)(2,1)}, u32[]{:S(2)}) copy-start(bf16[512,2048]{1,0:T(8,128)(2,1)} %copy-done.1) | copy-start | bytes 6291460
  25.8 3.0 %copy-start.6 = (bf16[20,64,256]{2,1,0:T(8,128)(2,1)S(1)}, bf16[20,64,256]{2,1,0:T(8,128)(2,1)}, u32[]{:S(2)}) copy-start(bf16[20,64,256]{2,1,0:T(8,128)(2,1)} %copy-done.4) | copy-start | bytes 1966084
  25.8 3.0 %copy-start.10 = (s32[20,4]{1,0:T(8,128)S(1)}, s32[20,4]{1,0:T(8,128)}, u32[]{:S(2)}) copy-start(s32[20,4]{1,0:T(8,128)} %copy-done.8) | copy-start | bytes 964
  32.0 23.9 %collective-permute-start.10 = (bf16[768,256]{1,0:T(8,128)(2,1)S(1)}, bf16[768,256]{1,0:T(8,128)(2,1)S(1)}, u32[]{:S(2)}, u32[]{:S(2)}) collective-permute-start(bf16[768,256]{1,0:T(8,128)(2,1)S(1)} %get-tuple-element.102), channel_id=1, source_target_pairs={{2,0},{3,1},{4,2},{5,3},{6,4},{7,5},{8,6},{9,7},{10,8},{11,9},{12,... | collective-permute-start | bytes 1179656 | tf_op jit(solution)/shard_map/ppermute | solution.py:236
  35.7 22.6 %collective-permute-start.9 = (bf16[768,256]{1,0:T(8,128)(2,1)S(1)}, bf16[768,256]{1,0:T(8,128)(2,1)S(1)}, u32[]{:S(2)}, u32[]{:S(2)}) collective-permute-start(bf16[768,256]{1,0:T(8,128)(2,1)S(1)} %get-tuple-element.101), channel_id=1, source_target_pairs={{14,0},{15,1},{0,2},{1,3},{2,4},{3,5},{4,6},{5,7},{6,8},{7,9},{8,1... | collective-permute-start | bytes 1179656 | tf_op jit(solution)/shard_map/ppermute | solution.py:236
  38.9 7.4 %copy-start.13 = (bf16[1024,256]{1,0:T(8,128)(2,1)S(1)}, bf16[1024,256]{1,0:T(8,128)(2,1)}, u32[]{:S(2)}) copy-start(bf16[1024,256]{1,0:T(8,128)(2,1)} %copy-done.12) | copy-start | bytes 1572868
  50.4 12.0 %collective-permute-start.7 = (bf16[512,256]{1,0:T(8,128)(2,1)S(1)}, bf16[512,256]{1,0:T(8,128)(2,1)S(1)}, u32[]{:S(2)}, u32[]{:S(2)}) collective-permute-start(bf16[512,256]{1,0:T(8,128)(2,1)S(1)} %get-tuple-element.99), channel_id=1, source_target_pairs={{0,4},{1,5},{2,6},{3,7},{4,0},{5,1},{6,2},{7,3},{8,12},{9,13},{10,... | collective-permute-start | bytes 786440 | tf_op jit(solution)/shard_map/ppermute | solution.py:241
  53.1 14.1 %collective-permute-start.8 = (bf16[512,256]{1,0:T(8,128)(2,1)S(1)}, bf16[512,256]{1,0:T(8,128)(2,1)S(1)}, u32[]{:S(2)}, u32[]{:S(2)}) collective-permute-start(bf16[512,256]{1,0:T(8,128)(2,1)S(1)} %get-tuple-element.100), channel_id=1, source_target_pairs={{0,4},{1,5},{2,6},{3,7},{4,0},{5,1},{6,2},{7,3},{8,12},{9,13},{10,... | collective-permute-start | bytes 786440 | tf_op jit(solution)/shard_map/ppermute | solution.py:241
  53.2 24.5 %collective-permute-start.14 = (bf16[768,256]{1,0:T(8,128)(2,1)S(1)}, bf16[768,256]{1,0:T(8,128)(2,1)S(1)}, u32[]{:S(2)}, u32[]{:S(2)}) collective-permute-start(bf16[768,256]{1,0:T(8,128)(2,1)S(1)} %get-tuple-element.111), channel_id=1, source_target_pairs={{14,0},{15,1},{0,2},{1,3},{2,4},{3,5},{4,6},{5,7},{6,8},{7,9},{8,1... | collective-permute-start | bytes 1179656 | tf_op jit(solution)/shard_map/ppermute | solution.py:236
  55.9 27.0 %collective-permute-start.15 = (bf16[768,256]{1,0:T(8,128)(2,1)S(1)}, bf16[768,256]{1,0:T(8,128)(2,1)S(1)}, u32[]{:S(2)}, u32[]{:S(2)}) collective-permute-start(bf16[768,256]{1,0:T(8,128)(2,1)S(1)} %get-tuple-element.112), channel_id=1, source_target_pairs={{2,0},{3,1},{4,2},{5,3},{6,4},{7,5},{8,6},{9,7},{10,8},{11,9},{12,... | collective-permute-start | bytes 1179656 | tf_op jit(solution)/shard_map/ppermute | solution.py:236
  58.3 39.3 %collective-permute-start.20 = (bf16[768,256]{1,0:T(8,128)(2,1)S(1)}, bf16[768,256]{1,0:T(8,128)(2,1)S(1)}, u32[]{:S(2)}, u32[]{:S(2)}) collective-permute-start(bf16[768,256]{1,0:T(8,128)(2,1)S(1)} %get-tuple-element.124), channel_id=1, source_target_pairs={{14,0},{15,1},{0,2},{1,3},{2,4},{3,5},{4,6},{5,7},{6,8},{7,9},{8,1... | collective-permute-start | bytes 1179656 | tf_op jit(solution)/shard_map/ppermute | solution.py:236
  62.4 38.4 %collective-permute-start.21 = (bf16[768,256]{1,0:T(8,128)(2,1)S(1)}, bf16[768,256]{1,0:T(8,128)(2,1)S(1)}, u32[]{:S(2)}, u32[]{:S(2)}) collective-permute-start(bf16[768,256]{1,0:T(8,128)(2,1)S(1)} %get-tuple-element.125), channel_id=1, source_target_pairs={{2,0},{3,1},{4,2},{5,3},{6,4},{7,5},{8,6},{9,7},{10,8},{11,9},{12,... | collective-permute-start | bytes 1179656 | tf_op jit(solution)/shard_map/ppermute | solution.py:236
  67.1 22.2 %collective-permute-start.12 = (bf16[512,256]{1,0:T(8,128)(2,1)S(1)}, bf16[512,256]{1,0:T(8,128)(2,1)S(1)}, u32[]{:S(2)}, u32[]{:S(2)}) collective-permute-start(bf16[512,256]{1,0:T(8,128)(2,1)S(1)} %get-tuple-element.109), channel_id=1, source_target_pairs={{0,4},{1,5},{2,6},{3,7},{4,0},{5,1},{6,2},{7,3},{8,12},{9,13},{10,... | collective-permute-start | bytes 786440 | tf_op jit(solution)/shard_map/ppermute | solution.py:241
  77.7 16.3 %collective-permute-start.13 = (bf16[512,256]{1,0:T(8,128)(2,1)S(1)}, bf16[512,256]{1,0:T(8,128)(2,1)S(1)}, u32[]{:S(2)}, u32[]{:S(2)}) collective-permute-start(bf16[512,256]{1,0:T(8,128)(2,1)S(1)} %get-tuple-element.110), channel_id=1, source_target_pairs={{0,4},{1,5},{2,6},{3,7},{4,0},{5,1},{6,2},{7,3},{8,12},{9,13},{10,... | collective-permute-start | bytes 786440 | tf_op jit(solution)/shard_map/ppermute | solution.py:241
  82.8 13.9 %collective-permute-start.11 = (bf16[512,256]{1,0:T(8,128)(2,1)S(1)}, bf16[512,256]{1,0:T(8,128)(2,1)S(1)}, u32[]{:S(2)}, u32[]{:S(2)}) collective-permute-start(bf16[512,256]{1,0:T(8,128)(2,1)S(1)} %get-tuple-element.107), channel_id=1, source_target_pairs={{0,2},{1,3},{2,0},{3,1},{4,6},{5,7},{6,4},{7,5},{8,10},{9,11},{10,... | collective-permute-start | bytes 786440 | tf_op jit(solution)/shard_map/ppermute | solution.py:241
  89.3 16.7 %collective-permute-start.18 = (bf16[512,256]{1,0:T(8,128)(2,1)S(1)}, bf16[512,256]{1,0:T(8,128)(2,1)S(1)}, u32[]{:S(2)}, u32[]{:S(2)}) collective-permute-start(bf16[512,256]{1,0:T(8,128)(2,1)S(1)} %get-tuple-element.122), channel_id=1, source_target_pairs={{0,4},{1,5},{2,6},{3,7},{4,0},{5,1},{6,2},{7,3},{8,12},{9,13},{10,... | collective-permute-start | bytes 786440 | tf_op jit(solution)/shard_map/ppermute | solution.py:241
  94.0 14.0 %collective-permute-start.19 = (bf16[512,256]{1,0:T(8,128)(2,1)S(1)}, bf16[512,256]{1,0:T(8,128)(2,1)S(1)}, u32[]{:S(2)}, u32[]{:S(2)}) collective-permute-start(bf16[512,256]{1,0:T(8,128)(2,1)S(1)} %get-tuple-element.123), channel_id=1, source_target_pairs={{0,4},{1,5},{2,6},{3,7},{4,0},{5,1},{6,2},{7,3},{8,12},{9,13},{10,... | collective-permute-start | bytes 786440 | tf_op jit(solution)/shard_map/ppermute | solution.py:241
  96.8 12.3 %collective-permute-start.17 = (bf16[512,256]{1,0:T(8,128)(2,1)S(1)}, bf16[512,256]{1,0:T(8,128)(2,1)S(1)}, u32[]{:S(2)}, u32[]{:S(2)}) collective-permute-start(bf16[512,256]{1,0:T(8,128)(2,1)S(1)} %get-tuple-element.120), channel_id=1, source_target_pairs={{0,2},{1,3},{2,0},{3,1},{4,6},{5,7},{6,4},{7,5},{8,10},{9,11},{10,... | collective-permute-start | bytes 786440 | tf_op jit(solution)/shard_map/ppermute | solution.py:241
  97.6 16.1 %collective-permute-start.16 = (bf16[256,256]{1,0:T(8,128)(2,1)S(1)}, bf16[256,256]{1,0:T(8,128)(2,1)S(1)}, u32[]{:S(2)}, u32[]{:S(2)}) collective-permute-start(bf16[256,256]{1,0:T(8,128)(2,1)S(1)} %get-tuple-element.118), channel_id=1, source_target_pairs={{0,8},{1,9},{2,10},{3,11},{4,12},{5,13},{6,14},{7,15},{8,0},{9,1},... | collective-permute-start | bytes 393224 | tf_op jit(solution)/shard_map/ppermute | solution.py:241
  104.8 12.1 %collective-permute-start.24 = (bf16[512,256]{1,0:T(8,128)(2,1)S(1)}, bf16[512,256]{1,0:T(8,128)(2,1)S(1)}, u32[]{:S(2)}, u32[]{:S(2)}) collective-permute-start(bf16[512,256]{1,0:T(8,128)(2,1)S(1)} %get-tuple-element.137), channel_id=1, source_target_pairs={{0,4},{1,5},{2,6},{3,7},{4,0},{5,1},{6,2},{7,3},{8,12},{9,13},{10,... | collective-permute-start | bytes 786440 | tf_op jit(solution)/shard_map/ppermute | solution.py:241
  106.1 15.2 %collective-permute-start.25 = (bf16[512,256]{1,0:T(8,128)(2,1)S(1)}, bf16[512,256]{1,0:T(8,128)(2,1)S(1)}, u32[]{:S(2)}, u32[]{:S(2)}) collective-permute-start(bf16[512,256]{1,0:T(8,128)(2,1)S(1)} %get-tuple-element.138), channel_id=1, source_target_pairs={{0,4},{1,5},{2,6},{3,7},{4,0},{5,1},{6,2},{7,3},{8,12},{9,13},{10,... | collective-permute-start | bytes 786440 | tf_op jit(solution)/shard_map/ppermute | solution.py:241
  108.1 13.8 %collective-permute-start.23 = (bf16[512,256]{1,0:T(8,128)(2,1)S(1)}, bf16[512,256]{1,0:T(8,128)(2,1)S(1)}, u32[]{:S(2)}, u32[]{:S(2)}) collective-permute-start(bf16[512,256]{1,0:T(8,128)(2,1)S(1)} %get-tuple-element.135), channel_id=1, source_target_pairs={{0,2},{1,3},{2,0},{3,1},{4,6},{5,7},{6,4},{7,5},{8,10},{9,11},{10,... | collective-permute-start | bytes 786440 | tf_op jit(solution)/shard_map/ppermute | solution.py:241
  109.1 14.4 %collective-permute-start.22 = (bf16[256,256]{1,0:T(8,128)(2,1)S(1)}, bf16[256,256]{1,0:T(8,128)(2,1)S(1)}, u32[]{:S(2)}, u32[]{:S(2)}) collective-permute-start(bf16[256,256]{1,0:T(8,128)(2,1)S(1)} %get-tuple-element.133), channel_id=1, source_target_pairs={{0,8},{1,9},{2,10},{3,11},{4,12},{5,13},{6,14},{7,15},{8,0},{9,1},... | collective-permute-start | bytes 393224 | tf_op jit(solution)/shard_map/ppermute | solution.py:241
  121.4 7.2 %collective-permute-start.27 = (bf16[512,256]{1,0:T(8,128)(2,1)S(1)}, bf16[512,256]{1,0:T(8,128)(2,1)S(1)}, u32[]{:S(2)}, u32[]{:S(2)}) collective-permute-start(bf16[512,256]{1,0:T(8,128)(2,1)S(1)} %get-tuple-element.146), channel_id=1, source_target_pairs={{0,2},{1,3},{2,0},{3,1},{4,6},{5,7},{6,4},{7,5},{8,10},{9,11},{10,... | collective-permute-start | bytes 786440 | tf_op jit(solution)/shard_map/ppermute | solution.py:241
  122.0 7.8 %collective-permute-start.26 = (bf16[256,256]{1,0:T(8,128)(2,1)S(1)}, bf16[256,256]{1,0:T(8,128)(2,1)S(1)}, u32[]{:S(2)}, u32[]{:S(2)}) collective-permute-start(bf16[256,256]{1,0:T(8,128)(2,1)S(1)} %get-tuple-element.144), channel_id=1, source_target_pairs={{0,8},{1,9},{2,10},{3,11},{4,12},{5,13},{6,14},{7,15},{8,0},{9,1},... | collective-permute-start | bytes 393224 | tf_op jit(solution)/shard_map/ppermute | solution.py:241
  123.4 12.7 %collective-permute-start.29 = (f32[128,256]{1,0:T(8,128)S(1)}, f32[128,256]{1,0:T(8,128)S(1)}, u32[]{:S(2)}, u32[]{:S(2)}) collective-permute-start(f32[128,256]{1,0:T(8,128)S(1)} %get-tuple-element.154), channel_id=1, source_target_pairs={{0,1},{1,0},{2,3},{3,2},{4,5},{5,4},{6,7},{7,6},{8,9},{9,8},{10,11... | collective-permute-start | bytes 393224 | tf_op jit(solution)/shard_map/ppermute | solution.py:241
  123.5 12.7 %collective-permute-start.30 = (f32[128,256]{1,0:T(8,128)S(1)}, f32[128,256]{1,0:T(8,128)S(1)}, u32[]{:S(2)}, u32[]{:S(2)}) collective-permute-start(f32[128,256]{1,0:T(8,128)S(1)} %get-tuple-element.155), channel_id=1, source_target_pairs={{0,1},{1,0},{2,3},{3,2},{4,5},{5,4},{6,7},{7,6},{8,9},{9,8},{10,11... | collective-permute-start | bytes 393224 | tf_op jit(solution)/shard_map/ppermute | solution.py:241
  128.7 7.3 %collective-permute-start.28 = (bf16[256,256]{1,0:T(8,128)(2,1)S(1)}, bf16[256,256]{1,0:T(8,128)(2,1)S(1)}, u32[]{:S(2)}, u32[]{:S(2)}) collective-permute-start(bf16[256,256]{1,0:T(8,128)(2,1)S(1)} %get-tuple-element.151), channel_id=1, source_target_pairs={{0,8},{1,9},{2,10},{3,11},{4,12},{5,13},{6,14},{7,15},{8,0},{9,1},... | collective-permute-start | bytes 393224 | tf_op jit(solution)/shard_map/ppermute | solution.py:241
  129.8 6.3 %collective-permute-start.31 = (f32[128,256]{1,0:T(8,128)S(1)}, f32[128,256]{1,0:T(8,128)S(1)}, u32[]{:S(2)}, u32[]{:S(2)}) collective-permute-start(f32[128,256]{1,0:T(8,128)S(1)} %get-tuple-element.156), channel_id=1, source_target_pairs={{0,1},{1,0},{2,3},{3,2},{4,5},{5,4},{6,7},{7,6},{8,9},{9,8},{10,11... | collective-permute-start | bytes 393224 | tf_op jit(solution)/shard_map/ppermute | solution.py:241
  136.0 1.4 %collective-permute-start.32 = (f32[128,256]{1,0:T(8,128)S(1)}, f32[128,256]{1,0:T(8,128)S(1)}, u32[]{:S(2)}, u32[]{:S(2)}) collective-permute-start(f32[128,256]{1,0:T(8,128)S(1)} %get-tuple-element.157), channel_id=1, source_target_pairs={{0,1},{1,0},{2,3},{3,2},{4,5},{5,4},{6,7},{7,6},{8,9},{9,8},{10,11... | collective-permute-start | bytes 393224 | tf_op jit(solution)/shard_map/ppermute | solution.py:241

commit v7 on v6

--- a/solution.py
+++ b/solution.py
@@ -9,7 +9,7 @@
 UNITS = (2, 2, 2, 2)
 PARTS = 2
 EARLY = 4
-PACE = 4 * 10**9
+PACE = 10**10
 LIMIT = 16 * 2**20
 ANY = pl.BlockSpec(memory_space=pl.ANY)
 BF16, F32 = jnp.bfloat16, jnp.float32

time: 139 us -> 131 us (0.942)
  waiting for transfers between devices: 43.2 us -> 53.3 us
  local copies, waits for them, and re-layouts: 9.77 us -> 0.78 us
  starting transfers between devices: 49.5 us -> 42.5 us
  Pallas kernels: 35.7 us -> 33.6 us
    unnamed x33 -> x5, local copies, waits for them, and re-layouts: 9.77 us -> 0.78 us
    ppermute x8, waiting for transfers between devices: 15 us -> 21.5 us  [passed_along(): lax.ppermute(block, 'mesh', [((i - distance) % size, i) for i in range(si...]
    ppermute x25, starting transfers between devices: 31 us -> 25.5 us  [swapped(): return lax.ppermute(block, 'mesh', [(i, i ^ 1 << bit) for i in range(size)])]
    ppermute x25, waiting for transfers between devices: 28.1 us -> 31.8 us  [swapped(): return lax.ppermute(block, 'mesh', [(i, i ^ 1 << bit) for i in range(size)])]
    pallas_call x24, Pallas kernels: 35.7 us -> 33.6 us  [call(): pl.pallas_call(kernel, out_shape=[*out_shape, jax.ShapeDtypeStruct((8, 12...]
    ppermute x8, starting transfers between devices: 18.6 us -> 17 us  [passed_along(): lax.ppermute(block, 'mesh', [((i - distance) % size, i) for i in range(si...]
  transfers between devices with their start and end apart: 33 -> 33, of which waited for: 13 -> 16; matrix products, arithmetic and copies ran while one was open for 1% -> 1% of each run, Pallas kernels for 23% -> 25%
where the time goes in v7:
time: 131 us; the launch traced here: 130 us
  waiting for transfers between devices  53.3 us (41%)
  starting transfers between devices  42.5 us (32%)
  Pallas kernels  33.6 us (26%)
    pallas_call x24, Pallas kernels, call(): pl.pallas_call(kernel, out_shape=[*out_shape, jax.ShapeDtypeStruct((8, 12...  33.6 us
    ppermute x25, waiting for transfers between devices, swapped(): return lax.ppermute(block, 'mesh', [(i, i ^ 1 << bit) for i in range(size)])  31.8 us
    ppermute x25, starting transfers between devices, swapped(): return lax.ppermute(block, 'mesh', [(i, i ^ 1 << bit) for i in range(size)])  25.5 us
    ppermute x8, waiting for transfers between devices, passed_along(): lax.ppermute(block, 'mesh', [((i - distance) % size, i) for i in range(si...  21.5 us
    ppermute x8, starting transfers between devices, passed_along(): lax.ppermute(block, 'mesh', [((i - distance) % size, i) for i in range(si...  17 us
  transfers between devices with their start and end apart: 33, of which 16 were waited for; matrix products, arithmetic and copies ran while one was open for 1% of the time, Pallas kernels for 25%

profile of v7, /device:TPU:0, one launch (start us, length us, event | category | flops | bytes accessed | tf_op | source)
XLA Modules:
  0.0 130.3 jit_solution(6219176147881275214)
XLA Ops:
  0.0 0.5 collective-permute-start.2
  0.5 0.1 collective-permute-start.3
  0.5 0.8 copy.7.refs_1_
  1.3 0.5 collective-permute-start.1
  1.7 0.1 collective-permute-start
  1.8 2.5 %collective-permute-done.1.refs_2_ = s32[20,4]{1,0:T(8,128)S(1)} collective-permute-done((s32[20,4]{1,0:T(8,128)S(1)}, s32[20,4]{1,0:T(8,128)S(1)}, u32[]{:S(2)}, u32[]{:S(2)}) %collective-permute-start.1) | collective-permute-done | bytes 352 | tf_op jit(solution)/shard_map/ppermute | solution.py:241
  4.3 1.1 collective-permute-done.3.refs_6_
  5.4 0.0 collective-permute-done.2.refs_4_
  5.4 3.2 %coupled_rows.4 = (bf16[768,256]{1,0:T(8,128)(2,1)S(1)}, bf16[768,256]{1,0:T(8,128)(2,1)S(1)}, bf16[1024,256]{1,0:T(8,128)(2,1)S(1)}, f32[8,128]{1,0:T(8,128)S(1)}) custom-call(s32[1]{0:T(128)} %bitcast.refs_0_, s32[20,4]{1,0:T(8,128)S(1)} %copy.7.refs_1_, s32[20,4]{1,0:T(8,128)S(1)} %collective-permute-done.1.refs_2_, bf16[512,2048]{1,0:T(8,128)(2,1)} %refs_3_.7, ...), custom_call_target="tpu_custom_call" | custom-call | flops 24999999488 | bytes 1 | tf_op jit(solution)/shard_map/coupled_rows/pallas_call | solution.py:33
  8.6 0.4 collective-permute-start.4
  9.1 2.6 %collective-permute-start.5 = (bf16[768,256]{1,0:T(8,128)(2,1)S(1)}, bf16[768,256]{1,0:T(8,128)(2,1)S(1)}, u32[]{:S(2)}, u32[]{:S(2)}) collective-permute-start(bf16[768,256]{1,0:T(8,128)(2,1)S(1)} %get-tuple-element.91), channel_id=1, source_target_pairs={{14,0},{15,1},{0,2},{1,3},{2,4},{3,5},{4,6},{5,7},{6,8},{7,9},{8,1... | collective-permute-start | bytes 1179656 | tf_op jit(solution)/shard_map/ppermute | solution.py:236
  11.7 3.0 %collective-permute-start.6 = (bf16[768,256]{1,0:T(8,128)(2,1)S(1)}, bf16[768,256]{1,0:T(8,128)(2,1)S(1)}, u32[]{:S(2)}, u32[]{:S(2)}) collective-permute-start(bf16[768,256]{1,0:T(8,128)(2,1)S(1)} %get-tuple-element.92), channel_id=1, source_target_pairs={{2,0},{3,1},{4,2},{5,3},{6,4},{7,5},{8,6},{9,7},{10,8},{11,9},{12,... | collective-permute-start | bytes 1179656 | tf_op jit(solution)/shard_map/ppermute | solution.py:236
  14.7 0.9 turn.2
  15.7 1.3 %slots.1 = (s32[24]{0:T(128)S(1)}, f32[8,128]{1,0:T(8,128)S(1)}) custom-call(s32[1]{0:T(128)} %bitcast.refs_0_, s32[12]{0:T(128)S(1)} %copy-done.1, s32[12]{0:T(128)S(1)} %collective-permute-done.refs_2_, f32[8,128]{1,0:T(8,128)S(1)} %get-tuple-element.83.refs_3_), custom_call_target="tpu_custom_call" | custom-call | flops 10000000000 | bytes 1 | tf_op jit(solution)/shard_map/slots/pallas_call | solution.py:33
  17.0 0.9 turn.3
  17.9 3.2 %coupled_rows.5 = (bf16[768,256]{1,0:T(8,128)(2,1)S(1)}, bf16[768,256]{1,0:T(8,128)(2,1)S(1)}, bf16[1024,256]{1,0:T(8,128)(2,1)S(1)}, f32[8,128]{1,0:T(8,128)S(1)}) custom-call(s32[1]{0:T(128)} %bitcast.refs_0_, s32[20,4]{1,0:T(8,128)S(1)} %copy.7.refs_1_, s32[20,4]{1,0:T(8,128)S(1)} %collective-permute-done.1.refs_2_, bf16[512,2048]{1,0:T(8,128)(2,1)} %refs_3_.7, ...), custom_call_target="tpu_custom_call" | custom-call | flops 24999999488 | bytes 1 | tf_op jit(solution)/shard_map/coupled_rows/pallas_call | solution.py:33
  21.1 3.3 %collective-permute-start.10 = (bf16[768,256]{1,0:T(8,128)(2,1)S(1)}, bf16[768,256]{1,0:T(8,128)(2,1)S(1)}, u32[]{:S(2)}, u32[]{:S(2)}) collective-permute-start(bf16[768,256]{1,0:T(8,128)(2,1)S(1)} %get-tuple-element.102), channel_id=1, source_target_pairs={{2,0},{3,1},{4,2},{5,3},{6,4},{7,5},{8,6},{9,7},{10,8},{11,9},{12,... | collective-permute-start | bytes 1179656 | tf_op jit(solution)/shard_map/ppermute | solution.py:236
  24.4 3.2 %coupled_rows.6 = (bf16[768,256]{1,0:T(8,128)(2,1)S(1)}, bf16[768,256]{1,0:T(8,128)(2,1)S(1)}, bf16[1024,256]{1,0:T(8,128)(2,1)S(1)}, f32[8,128]{1,0:T(8,128)S(1)}) custom-call(s32[1]{0:T(128)} %bitcast.refs_0_, s32[20,4]{1,0:T(8,128)S(1)} %copy.7.refs_1_, s32[20,4]{1,0:T(8,128)S(1)} %collective-permute-done.1.refs_2_, bf16[512,2048]{1,0:T(8,128)(2,1)} %refs_3_.7, ...), custom_call_target="tpu_custom_call" | custom-call | flops 24999999488 | bytes 1 | tf_op jit(solution)/shard_map/coupled_rows/pallas_call | solution.py:33
  27.5 3.2 %coupled_rows.7 = (bf16[768,256]{1,0:T(8,128)(2,1)S(1)}, bf16[768,256]{1,0:T(8,128)(2,1)S(1)}, bf16[1024,256]{1,0:T(8,128)(2,1)S(1)}, f32[8,128]{1,0:T(8,128)S(1)}) custom-call(s32[1]{0:T(128)} %bitcast.refs_0_, s32[20,4]{1,0:T(8,128)S(1)} %copy.7.refs_1_, s32[20,4]{1,0:T(8,128)S(1)} %collective-permute-done.1.refs_2_, bf16[512,2048]{1,0:T(8,128)(2,1)} %refs_3_.7, ...), custom_call_target="tpu_custom_call" | custom-call | flops 24999999488 | bytes 1 | tf_op jit(solution)/shard_map/coupled_rows/pallas_call | solution.py:33
  30.7 7.3 %collective-permute-done.5.refs_5_ = bf16[768,256]{1,0:T(8,128)(2,1)S(1)} collective-permute-done((bf16[768,256]{1,0:T(8,128)(2,1)S(1)}, bf16[768,256]{1,0:T(8,128)(2,1)S(1)}, u32[]{:S(2)}, u32[]{:S(2)}) %collective-permute-start.5) | collective-permute-done | bytes 393248 | tf_op jit(solution)/shard_map/ppermute | solution.py:236
  38.0 2.5 %collective-permute-done.6.refs_6_ = bf16[768,256]{1,0:T(8,128)(2,1)S(1)} collective-permute-done((bf16[768,256]{1,0:T(8,128)(2,1)S(1)}, bf16[768,256]{1,0:T(8,128)(2,1)S(1)}, u32[]{:S(2)}, u32[]{:S(2)}) %collective-permute-start.6) | collective-permute-done | bytes 393248 | tf_op jit(solution)/shard_map/ppermute | solution.py:236
  40.5 4.0 %panel_part.4 = (bf16[512,256]{1,0:T(8,128)(2,1)S(1)}, bf16[512,256]{1,0:T(8,128)(2,1)S(1)}, f32[1024,256]{1,0:T(8,128)S(1)}, f32[8,128]{1,0:T(8,128)S(1)}) custom-call(s32[24]{0:T(128)S(1)} %get-tuple-element.84.refs_0_, bf16[1024,768]{1,0:T(8,128)(2,1)S(1)} %get-tuple-element.85.refs_1_, bf16[1024,768]{1,0:T(8,128)(2,1)S(1)} %get-tuple-element.88.refs_2_, ...), custom_call_target="tpu_custom_call" | custom-call | flops 40000000000 | bytes 1 | tf_op jit(solution)/shard_map/panel_part/pallas_call | solution.py:33
  44.5 0.5 collective-permute-start.7
  45.1 1.6 %collective-permute-start.8 = (bf16[512,256]{1,0:T(8,128)(2,1)S(1)}, bf16[512,256]{1,0:T(8,128)(2,1)S(1)}, u32[]{:S(2)}, u32[]{:S(2)}) collective-permute-start(bf16[512,256]{1,0:T(8,128)(2,1)S(1)} %get-tuple-element.100), channel_id=1, source_target_pairs={{0,4},{1,5},{2,6},{3,7},{4,0},{5,1},{6,2},{7,3},{8,12},{9,13},{10,... | collective-permute-start | bytes 786440 | tf_op jit(solution)/shard_map/ppermute | solution.py:241
  46.6 1.5 %collective-permute-done.10.refs_6_ = bf16[768,256]{1,0:T(8,128)(2,1)S(1)} collective-permute-done((bf16[768,256]{1,0:T(8,128)(2,1)S(1)}, bf16[768,256]{1,0:T(8,128)(2,1)S(1)}, u32[]{:S(2)}, u32[]{:S(2)}) %collective-permute-start.10) | collective-permute-done | bytes 393248 | tf_op jit(solution)/shard_map/ppermute | solution.py:236
  48.1 3.3 %collective-permute-start.15 = (bf16[768,256]{1,0:T(8,128)(2,1)S(1)}, bf16[768,256]{1,0:T(8,128)(2,1)S(1)}, u32[]{:S(2)}, u32[]{:S(2)}) collective-permute-start(bf16[768,256]{1,0:T(8,128)(2,1)S(1)} %get-tuple-element.112), channel_id=1, source_target_pairs={{2,0},{3,1},{4,2},{5,3},{6,4},{7,5},{8,6},{9,7},{10,8},{11,9},{12,... | collective-permute-start | bytes 1179656 | tf_op jit(solution)/shard_map/ppermute | solution.py:236
  51.4 4.0 %panel_part.5 = (bf16[512,256]{1,0:T(8,128)(2,1)S(1)}, bf16[512,256]{1,0:T(8,128)(2,1)S(1)}, f32[1024,256]{1,0:T(8,128)S(1)}, f32[8,128]{1,0:T(8,128)S(1)}) custom-call(s32[24]{0:T(128)S(1)} %get-tuple-element.84.refs_0_, bf16[1024,768]{1,0:T(8,128)(2,1)S(1)} %get-tuple-element.85.refs_1_, bf16[1024,768]{1,0:T(8,128)(2,1)S(1)} %get-tuple-element.88.refs_2_, ...), custom_call_target="tpu_custom_call" | custom-call | flops 40000000000 | bytes 1 | tf_op jit(solution)/shard_map/panel_part/pallas_call | solution.py:33
  55.4 4.8 %collective-permute-start.21 = (bf16[768,256]{1,0:T(8,128)(2,1)S(1)}, bf16[768,256]{1,0:T(8,128)(2,1)S(1)}, u32[]{:S(2)}, u32[]{:S(2)}) collective-permute-start(bf16[768,256]{1,0:T(8,128)(2,1)S(1)} %get-tuple-element.125), channel_id=1, source_target_pairs={{2,0},{3,1},{4,2},{5,3},{6,4},{7,5},{8,6},{9,7},{10,8},{11,9},{12,... | collective-permute-start | bytes 1179656 | tf_op jit(solution)/shard_map/ppermute | solution.py:236
  60.2 0.1 added_split.12
  60.3 9.2 %collective-permute-done.14.refs_5_ = bf16[768,256]{1,0:T(8,128)(2,1)S(1)} collective-permute-done((bf16[768,256]{1,0:T(8,128)(2,1)S(1)}, bf16[768,256]{1,0:T(8,128)(2,1)S(1)}, u32[]{:S(2)}, u32[]{:S(2)}) %collective-permute-start.14) | collective-permute-done | bytes 393248 | tf_op jit(solution)/shard_map/ppermute | solution.py:236
  69.5 5.1 %collective-permute-start.13 = (bf16[512,256]{1,0:T(8,128)(2,1)S(1)}, bf16[512,256]{1,0:T(8,128)(2,1)S(1)}, u32[]{:S(2)}, u32[]{:S(2)}) collective-permute-start(bf16[512,256]{1,0:T(8,128)(2,1)S(1)} %get-tuple-element.110), channel_id=1, source_target_pairs={{0,4},{1,5},{2,6},{3,7},{4,0},{5,1},{6,2},{7,3},{8,12},{9,13},{10,... | collective-permute-start | bytes 786440 | tf_op jit(solution)/shard_map/ppermute | solution.py:241
  74.6 1.0 collective-permute-done.15.refs_6_
  75.6 1.5 %collective-permute-start.11 = (bf16[512,256]{1,0:T(8,128)(2,1)S(1)}, bf16[512,256]{1,0:T(8,128)(2,1)S(1)}, u32[]{:S(2)}, u32[]{:S(2)}) collective-permute-start(bf16[512,256]{1,0:T(8,128)(2,1)S(1)} %get-tuple-element.107), channel_id=1, source_target_pairs={{0,2},{1,3},{2,0},{3,1},{4,6},{5,7},{6,4},{7,5},{8,10},{9,11},{10,... | collective-permute-start | bytes 786440 | tf_op jit(solution)/shard_map/ppermute | solution.py:241
  77.1 4.0 %panel_part.6 = (bf16[512,256]{1,0:T(8,128)(2,1)S(1)}, bf16[512,256]{1,0:T(8,128)(2,1)S(1)}, f32[1024,256]{1,0:T(8,128)S(1)}, f32[8,128]{1,0:T(8,128)S(1)}) custom-call(s32[24]{0:T(128)S(1)} %get-tuple-element.84.refs_0_, bf16[1024,768]{1,0:T(8,128)(2,1)S(1)} %get-tuple-element.85.refs_1_, bf16[1024,768]{1,0:T(8,128)(2,1)S(1)} %get-tuple-element.88.refs_2_, ...), custom_call_target="tpu_custom_call" | custom-call | flops 40000000000 | bytes 1 | tf_op jit(solution)/shard_map/panel_part/pallas_call | solution.py:33
  81.1 0.9 collective-permute-done.12
  82.0 0.4 collective-permute-start.18
  82.3 5.3 %collective-permute-done.13 = bf16[512,256]{1,0:T(8,128)(2,1)S(1)} collective-permute-done((bf16[512,256]{1,0:T(8,128)(2,1)S(1)}, bf16[512,256]{1,0:T(8,128)(2,1)S(1)}, u32[]{:S(2)}, u32[]{:S(2)}) %collective-permute-start.13) | collective-permute-done | bytes 262176 | tf_op jit(solution)/shard_map/ppermute | solution.py:241
  87.6 0.4 collective-permute-start.19
  88.0 0.1 added_split.13
  88.1 1.2 collective-permute-done.11
  89.2 0.1 collective-permute-start.17
  89.4 3.4 %collective-permute-start.16 = (bf16[256,256]{1,0:T(8,128)(2,1)S(1)}, bf16[256,256]{1,0:T(8,128)(2,1)S(1)}, u32[]{:S(2)}, u32[]{:S(2)}) collective-permute-start(bf16[256,256]{1,0:T(8,128)(2,1)S(1)} %get-tuple-element.118), channel_id=1, source_target_pairs={{0,8},{1,9},{2,10},{3,11},{4,12},{5,13},{6,14},{7,15},{8,0},{9,1},... | collective-permute-start | bytes 393224 | tf_op jit(solution)/shard_map/ppermute | solution.py:241
  92.8 4.0 %panel_part.7 = (bf16[512,256]{1,0:T(8,128)(2,1)S(1)}, bf16[512,256]{1,0:T(8,128)(2,1)S(1)}, f32[1024,256]{1,0:T(8,128)S(1)}, f32[8,128]{1,0:T(8,128)S(1)}) custom-call(s32[24]{0:T(128)S(1)} %get-tuple-element.84.refs_0_, bf16[1024,768]{1,0:T(8,128)(2,1)S(1)} %get-tuple-element.85.refs_1_, bf16[1024,768]{1,0:T(8,128)(2,1)S(1)} %get-tuple-element.88.refs_2_, ...), custom_call_target="tpu_custom_call" | custom-call | flops 40000000000 | bytes 1 | tf_op jit(solution)/shard_map/panel_part/pallas_call | solution.py:33
  96.8 1.3 collective-permute-start.24
  98.1 0.8 collective-permute-start.25
  98.9 1.8 %collective-permute-done.19 = bf16[512,256]{1,0:T(8,128)(2,1)S(1)} collective-permute-done((bf16[512,256]{1,0:T(8,128)(2,1)S(1)}, bf16[512,256]{1,0:T(8,128)(2,1)S(1)}, u32[]{:S(2)}, u32[]{:S(2)}) %collective-permute-start.19) | collective-permute-done | bytes 262176 | tf_op jit(solution)/shard_map/ppermute | solution.py:241
  100.7 0.1 added_split.15
  100.8 0.3 collective-permute-start.23
  101.1 4.6 %collective-permute-start.22 = (bf16[256,256]{1,0:T(8,128)(2,1)S(1)}, bf16[256,256]{1,0:T(8,128)(2,1)S(1)}, u32[]{:S(2)}, u32[]{:S(2)}) collective-permute-start(bf16[256,256]{1,0:T(8,128)(2,1)S(1)} %get-tuple-element.133), channel_id=1, source_target_pairs={{0,8},{1,9},{2,10},{3,11},{4,12},{5,13},{6,14},{7,15},{8,0},{9,1},... | collective-permute-start | bytes 393224 | tf_op jit(solution)/shard_map/ppermute | solution.py:241
  105.8 3.3 %collective-permute-done.24 = bf16[512,256]{1,0:T(8,128)(2,1)S(1)} collective-permute-done((bf16[512,256]{1,0:T(8,128)(2,1)S(1)}, bf16[512,256]{1,0:T(8,128)(2,1)S(1)}, u32[]{:S(2)}, u32[]{:S(2)}) %collective-permute-start.24) | collective-permute-done | bytes 262176 | tf_op jit(solution)/shard_map/ppermute | solution.py:241
  109.1 4.2 %collective-permute-done.25 = bf16[512,256]{1,0:T(8,128)(2,1)S(1)} collective-permute-done((bf16[512,256]{1,0:T(8,128)(2,1)S(1)}, bf16[512,256]{1,0:T(8,128)(2,1)S(1)}, u32[]{:S(2)}, u32[]{:S(2)}) %collective-permute-start.25) | collective-permute-done | bytes 262176 | tf_op jit(solution)/shard_map/ppermute | solution.py:241
  113.3 0.1 added_split.18
  113.5 0.9 collective-permute-start.27
  114.3 0.1 added_split.19
  114.4 1.2 collective-permute-start.26
  115.6 0.6 collective-permute-start.30
  116.2 4.3 %collective-permute-done.27 = bf16[512,256]{1,0:T(8,128)(2,1)S(1)} collective-permute-done((bf16[512,256]{1,0:T(8,128)(2,1)S(1)}, bf16[512,256]{1,0:T(8,128)(2,1)S(1)}, u32[]{:S(2)}, u32[]{:S(2)}) %collective-permute-start.27) | collective-permute-done | bytes 262176 | tf_op jit(solution)/shard_map/ppermute | solution.py:241
  120.5 0.1 added_split.21
  120.5 1.3 collective-permute-start.28
  121.8 0.1 collective-permute-start.31
  121.9 5.9 %collective-permute-done.28 = bf16[256,256]{1,0:T(8,128)(2,1)S(1)} collective-permute-done((bf16[256,256]{1,0:T(8,128)(2,1)S(1)}, bf16[256,256]{1,0:T(8,128)(2,1)S(1)}, u32[]{:S(2)}, u32[]{:S(2)}) %collective-permute-start.28) | collective-permute-done | bytes 131104 | tf_op jit(solution)/shard_map/ppermute | solution.py:241
  127.9 0.1 collective-permute-start.32
  128.0 1.3 collective-permute-done.32.refs_8_
  129.3 1.0 put_together.1
  (31 shorter events, 0.3 us)
Async XLA Ops:
  0.0 5.4 %collective-permute-start.2 = (bf16[512,2048]{1,0:T(8,128)(2,1)}, bf16[512,2048]{1,0:T(8,128)(2,1)S(1)}, u32[]{:S(2)}, u32[]{:S(2)}) collective-permute-start(bf16[512,2048]{1,0:T(8,128)(2,1)} %refs_3_.7), channel_id=1, source_target_pairs={{0,1},{1,0},{2,3},{3,2},{4,5},{5,4},{6,7},{7,6},{8,9},{9,8},{10,11... | collective-permute-start | bytes 6291464 | tf_op jit(solution)/shard_map/ppermute | solution.py:241
  0.5 5.0 %collective-permute-start.3 = (bf16[20,64,256]{2,1,0:T(8,128)(2,1)}, bf16[20,64,256]{2,1,0:T(8,128)(2,1)S(1)}, u32[]{:S(2)}, u32[]{:S(2)}) collective-permute-start(bf16[20,64,256]{2,1,0:T(8,128)(2,1)} %refs_5_.7), channel_id=1, source_target_pairs={{0,1},{1,0},{2,3},{3,2},{4,5},{5,4},{6,7},{7,6},{8,9},{9,8},{10,11... | collective-permute-start | bytes 1966088 | tf_op jit(solution)/shard_map/ppermute | solution.py:241
  1.3 3.0 %collective-permute-start.1 = (s32[20,4]{1,0:T(8,128)S(1)}, s32[20,4]{1,0:T(8,128)S(1)}, u32[]{:S(2)}, u32[]{:S(2)}) collective-permute-start(s32[20,4]{1,0:T(8,128)S(1)} %copy.7.refs_1_), channel_id=1, source_target_pairs={{0,1},{1,0},{2,3},{3,2},{4,5},{5,4},{6,7},{7,6},{8,9},{9,8},{10,11... | collective-permute-start | bytes 968 | tf_op jit(solution)/shard_map/ppermute | solution.py:241
  1.7 13.9 %collective-permute-start = (s32[12]{0:T(128)}, s32[12]{0:T(128)S(1)}, u32[]{:S(2)}, u32[]{:S(2)}) collective-permute-start(s32[12]{0:T(128)} %refs_1_.7), channel_id=1, source_target_pairs={{0,1},{1,0},{2,3},{3,2},{4,5},{5,4},{6,7},{7,6},{8,9},{9,8},{10,11... | collective-permute-start | bytes 152 | tf_op jit(solution)/shard_map/ppermute | solution.py:241
  5.4 3.2 %copy-start = (bf16[768,2048]{1,0:T(8,128)(2,1)S(1)}, bf16[768,2048]{1,0:T(8,128)(2,1)}, u32[]{:S(2)}) copy-start(bf16[768,2048]{1,0:T(8,128)(2,1)} %refs_1_.6) | copy-start | bytes 9437188
  8.6 8.4 %collective-permute-start.4 = (bf16[768,2048]{1,0:T(8,128)(2,1)S(1)}, bf16[768,2048]{1,0:T(8,128)(2,1)S(1)}, u32[]{:S(2)}, u32[]{:S(2)}) collective-permute-start(bf16[768,2048]{1,0:T(8,128)(2,1)S(1)} %copy-done), channel_id=1, source_target_pairs={{0,1},{1,0},{2,3},{3,2},{4,5},{5,4},{6,7},{7,6},{8,9},{9,8},{10,11... | collective-permute-start | bytes 9437192 | tf_op jit(solution)/shard_map/ppermute | solution.py:241
  9.1 28.9 %collective-permute-start.5 = (bf16[768,256]{1,0:T(8,128)(2,1)S(1)}, bf16[768,256]{1,0:T(8,128)(2,1)S(1)}, u32[]{:S(2)}, u32[]{:S(2)}) collective-permute-start(bf16[768,256]{1,0:T(8,128)(2,1)S(1)} %get-tuple-element.91), channel_id=1, source_target_pairs={{14,0},{15,1},{0,2},{1,3},{2,4},{3,5},{4,6},{5,7},{6,8},{7,9},{8,1... | collective-permute-start | bytes 1179656 | tf_op jit(solution)/shard_map/ppermute | solution.py:236
  11.7 28.8 %collective-permute-start.6 = (bf16[768,256]{1,0:T(8,128)(2,1)S(1)}, bf16[768,256]{1,0:T(8,128)(2,1)S(1)}, u32[]{:S(2)}, u32[]{:S(2)}) collective-permute-start(bf16[768,256]{1,0:T(8,128)(2,1)S(1)} %get-tuple-element.92), channel_id=1, source_target_pairs={{2,0},{3,1},{4,2},{5,3},{6,4},{7,5},{8,6},{9,7},{10,8},{11,9},{12,... | collective-permute-start | bytes 1179656 | tf_op jit(solution)/shard_map/ppermute | solution.py:236
  14.7 0.9 copy-start.1
  21.1 27.0 %collective-permute-start.10 = (bf16[768,256]{1,0:T(8,128)(2,1)S(1)}, bf16[768,256]{1,0:T(8,128)(2,1)S(1)}, u32[]{:S(2)}, u32[]{:S(2)}) collective-permute-start(bf16[768,256]{1,0:T(8,128)(2,1)S(1)} %get-tuple-element.102), channel_id=1, source_target_pairs={{2,0},{3,1},{4,2},{5,3},{6,4},{7,5},{8,6},{9,7},{10,8},{11,9},{12,... | collective-permute-start | bytes 1179656 | tf_op jit(solution)/shard_map/ppermute | solution.py:236
  24.4 27.0 %collective-permute-start.9 = (bf16[768,256]{1,0:T(8,128)(2,1)S(1)}, bf16[768,256]{1,0:T(8,128)(2,1)S(1)}, u32[]{:S(2)}, u32[]{:S(2)}) collective-permute-start(bf16[768,256]{1,0:T(8,128)(2,1)S(1)} %get-tuple-element.101), channel_id=1, source_target_pairs={{14,0},{15,1},{0,2},{1,3},{2,4},{3,5},{4,6},{5,7},{6,8},{7,9},{8,1... | collective-permute-start | bytes 1179656 | tf_op jit(solution)/shard_map/ppermute | solution.py:236
  44.5 10.8 %collective-permute-start.7 = (bf16[512,256]{1,0:T(8,128)(2,1)S(1)}, bf16[512,256]{1,0:T(8,128)(2,1)S(1)}, u32[]{:S(2)}, u32[]{:S(2)}) collective-permute-start(bf16[512,256]{1,0:T(8,128)(2,1)S(1)} %get-tuple-element.99), channel_id=1, source_target_pairs={{0,4},{1,5},{2,6},{3,7},{4,0},{5,1},{6,2},{7,3},{8,12},{9,13},{10,... | collective-permute-start | bytes 786440 | tf_op jit(solution)/shard_map/ppermute | solution.py:241
  45.1 15.1 %collective-permute-start.8 = (bf16[512,256]{1,0:T(8,128)(2,1)S(1)}, bf16[512,256]{1,0:T(8,128)(2,1)S(1)}, u32[]{:S(2)}, u32[]{:S(2)}) collective-permute-start(bf16[512,256]{1,0:T(8,128)(2,1)S(1)} %get-tuple-element.100), channel_id=1, source_target_pairs={{0,4},{1,5},{2,6},{3,7},{4,0},{5,1},{6,2},{7,3},{8,12},{9,13},{10,... | collective-permute-start | bytes 786440 | tf_op jit(solution)/shard_map/ppermute | solution.py:241
  46.6 22.8 %collective-permute-start.14 = (bf16[768,256]{1,0:T(8,128)(2,1)S(1)}, bf16[768,256]{1,0:T(8,128)(2,1)S(1)}, u32[]{:S(2)}, u32[]{:S(2)}) collective-permute-start(bf16[768,256]{1,0:T(8,128)(2,1)S(1)} %get-tuple-element.111), channel_id=1, source_target_pairs={{14,0},{15,1},{0,2},{1,3},{2,4},{3,5},{4,6},{5,7},{6,8},{7,9},{8,1... | collective-permute-start | bytes 1179656 | tf_op jit(solution)/shard_map/ppermute | solution.py:236
  48.1 27.5 %collective-permute-start.15 = (bf16[768,256]{1,0:T(8,128)(2,1)S(1)}, bf16[768,256]{1,0:T(8,128)(2,1)S(1)}, u32[]{:S(2)}, u32[]{:S(2)}) collective-permute-start(bf16[768,256]{1,0:T(8,128)(2,1)S(1)} %get-tuple-element.112), channel_id=1, source_target_pairs={{2,0},{3,1},{4,2},{5,3},{6,4},{7,5},{8,6},{9,7},{10,8},{11,9},{12,... | collective-permute-start | bytes 1179656 | tf_op jit(solution)/shard_map/ppermute | solution.py:236
  51.4 38.0 %collective-permute-start.20 = (bf16[768,256]{1,0:T(8,128)(2,1)S(1)}, bf16[768,256]{1,0:T(8,128)(2,1)S(1)}, u32[]{:S(2)}, u32[]{:S(2)}) collective-permute-start(bf16[768,256]{1,0:T(8,128)(2,1)S(1)} %get-tuple-element.124), channel_id=1, source_target_pairs={{14,0},{15,1},{0,2},{1,3},{2,4},{3,5},{4,6},{5,7},{6,8},{7,9},{8,1... | collective-permute-start | bytes 1179656 | tf_op jit(solution)/shard_map/ppermute | solution.py:236
  55.4 37.4 %collective-permute-start.21 = (bf16[768,256]{1,0:T(8,128)(2,1)S(1)}, bf16[768,256]{1,0:T(8,128)(2,1)S(1)}, u32[]{:S(2)}, u32[]{:S(2)}) collective-permute-start(bf16[768,256]{1,0:T(8,128)(2,1)S(1)} %get-tuple-element.125), channel_id=1, source_target_pairs={{2,0},{3,1},{4,2},{5,3},{6,4},{7,5},{8,6},{9,7},{10,8},{11,9},{12,... | collective-permute-start | bytes 1179656 | tf_op jit(solution)/shard_map/ppermute | solution.py:236
  60.2 21.8 %collective-permute-start.12 = (bf16[512,256]{1,0:T(8,128)(2,1)S(1)}, bf16[512,256]{1,0:T(8,128)(2,1)S(1)}, u32[]{:S(2)}, u32[]{:S(2)}) collective-permute-start(bf16[512,256]{1,0:T(8,128)(2,1)S(1)} %get-tuple-element.109), channel_id=1, source_target_pairs={{0,4},{1,5},{2,6},{3,7},{4,0},{5,1},{6,2},{7,3},{8,12},{9,13},{10,... | collective-permute-start | bytes 786440 | tf_op jit(solution)/shard_map/ppermute | solution.py:241
  69.5 18.1 %collective-permute-start.13 = (bf16[512,256]{1,0:T(8,128)(2,1)S(1)}, bf16[512,256]{1,0:T(8,128)(2,1)S(1)}, u32[]{:S(2)}, u32[]{:S(2)}) collective-permute-start(bf16[512,256]{1,0:T(8,128)(2,1)S(1)} %get-tuple-element.110), channel_id=1, source_target_pairs={{0,4},{1,5},{2,6},{3,7},{4,0},{5,1},{6,2},{7,3},{8,12},{9,13},{10,... | collective-permute-start | bytes 786440 | tf_op jit(solution)/shard_map/ppermute | solution.py:241
  75.6 13.6 %collective-permute-start.11 = (bf16[512,256]{1,0:T(8,128)(2,1)S(1)}, bf16[512,256]{1,0:T(8,128)(2,1)S(1)}, u32[]{:S(2)}, u32[]{:S(2)}) collective-permute-start(bf16[512,256]{1,0:T(8,128)(2,1)S(1)} %get-tuple-element.107), channel_id=1, source_target_pairs={{0,2},{1,3},{2,0},{3,1},{4,6},{5,7},{6,4},{7,5},{8,10},{9,11},{10,... | collective-permute-start | bytes 786440 | tf_op jit(solution)/shard_map/ppermute | solution.py:241
  82.0 16.1 %collective-permute-start.18 = (bf16[512,256]{1,0:T(8,128)(2,1)S(1)}, bf16[512,256]{1,0:T(8,128)(2,1)S(1)}, u32[]{:S(2)}, u32[]{:S(2)}) collective-permute-start(bf16[512,256]{1,0:T(8,128)(2,1)S(1)} %get-tuple-element.122), channel_id=1, source_target_pairs={{0,4},{1,5},{2,6},{3,7},{4,0},{5,1},{6,2},{7,3},{8,12},{9,13},{10,... | collective-permute-start | bytes 786440 | tf_op jit(solution)/shard_map/ppermute | solution.py:241
  87.6 13.1 %collective-permute-start.19 = (bf16[512,256]{1,0:T(8,128)(2,1)S(1)}, bf16[512,256]{1,0:T(8,128)(2,1)S(1)}, u32[]{:S(2)}, u32[]{:S(2)}) collective-permute-start(bf16[512,256]{1,0:T(8,128)(2,1)S(1)} %get-tuple-element.123), channel_id=1, source_target_pairs={{0,4},{1,5},{2,6},{3,7},{4,0},{5,1},{6,2},{7,3},{8,12},{9,13},{10,... | collective-permute-start | bytes 786440 | tf_op jit(solution)/shard_map/ppermute | solution.py:241
  89.2 11.9 %collective-permute-start.17 = (bf16[512,256]{1,0:T(8,128)(2,1)S(1)}, bf16[512,256]{1,0:T(8,128)(2,1)S(1)}, u32[]{:S(2)}, u32[]{:S(2)}) collective-permute-start(bf16[512,256]{1,0:T(8,128)(2,1)S(1)} %get-tuple-element.120), channel_id=1, source_target_pairs={{0,2},{1,3},{2,0},{3,1},{4,6},{5,7},{6,4},{7,5},{8,10},{9,11},{10,... | collective-permute-start | bytes 786440 | tf_op jit(solution)/shard_map/ppermute | solution.py:241
  89.4 16.4 %collective-permute-start.16 = (bf16[256,256]{1,0:T(8,128)(2,1)S(1)}, bf16[256,256]{1,0:T(8,128)(2,1)S(1)}, u32[]{:S(2)}, u32[]{:S(2)}) collective-permute-start(bf16[256,256]{1,0:T(8,128)(2,1)S(1)} %get-tuple-element.118), channel_id=1, source_target_pairs={{0,8},{1,9},{2,10},{3,11},{4,12},{5,13},{6,14},{7,15},{8,0},{9,1},... | collective-permute-start | bytes 393224 | tf_op jit(solution)/shard_map/ppermute | solution.py:241
  96.8 12.3 %collective-permute-start.24 = (bf16[512,256]{1,0:T(8,128)(2,1)S(1)}, bf16[512,256]{1,0:T(8,128)(2,1)S(1)}, u32[]{:S(2)}, u32[]{:S(2)}) collective-permute-start(bf16[512,256]{1,0:T(8,128)(2,1)S(1)} %get-tuple-element.137), channel_id=1, source_target_pairs={{0,4},{1,5},{2,6},{3,7},{4,0},{5,1},{6,2},{7,3},{8,12},{9,13},{10,... | collective-permute-start | bytes 786440 | tf_op jit(solution)/shard_map/ppermute | solution.py:241
  98.1 15.2 %collective-permute-start.25 = (bf16[512,256]{1,0:T(8,128)(2,1)S(1)}, bf16[512,256]{1,0:T(8,128)(2,1)S(1)}, u32[]{:S(2)}, u32[]{:S(2)}) collective-permute-start(bf16[512,256]{1,0:T(8,128)(2,1)S(1)} %get-tuple-element.138), channel_id=1, source_target_pairs={{0,4},{1,5},{2,6},{3,7},{4,0},{5,1},{6,2},{7,3},{8,12},{9,13},{10,... | collective-permute-start | bytes 786440 | tf_op jit(solution)/shard_map/ppermute | solution.py:241
  100.8 13.6 %collective-permute-start.23 = (bf16[512,256]{1,0:T(8,128)(2,1)S(1)}, bf16[512,256]{1,0:T(8,128)(2,1)S(1)}, u32[]{:S(2)}, u32[]{:S(2)}) collective-permute-start(bf16[512,256]{1,0:T(8,128)(2,1)S(1)} %get-tuple-element.135), channel_id=1, source_target_pairs={{0,2},{1,3},{2,0},{3,1},{4,6},{5,7},{6,4},{7,5},{8,10},{9,11},{10,... | collective-permute-start | bytes 786440 | tf_op jit(solution)/shard_map/ppermute | solution.py:241
  101.1 14.5 %collective-permute-start.22 = (bf16[256,256]{1,0:T(8,128)(2,1)S(1)}, bf16[256,256]{1,0:T(8,128)(2,1)S(1)}, u32[]{:S(2)}, u32[]{:S(2)}) collective-permute-start(bf16[256,256]{1,0:T(8,128)(2,1)S(1)} %get-tuple-element.133), channel_id=1, source_target_pairs={{0,8},{1,9},{2,10},{3,11},{4,12},{5,13},{6,14},{7,15},{8,0},{9,1},... | collective-permute-start | bytes 393224 | tf_op jit(solution)/shard_map/ppermute | solution.py:241
  113.5 7.0 %collective-permute-start.27 = (bf16[512,256]{1,0:T(8,128)(2,1)S(1)}, bf16[512,256]{1,0:T(8,128)(2,1)S(1)}, u32[]{:S(2)}, u32[]{:S(2)}) collective-permute-start(bf16[512,256]{1,0:T(8,128)(2,1)S(1)} %get-tuple-element.146), channel_id=1, source_target_pairs={{0,2},{1,3},{2,0},{3,1},{4,6},{5,7},{6,4},{7,5},{8,10},{9,11},{10,... | collective-permute-start | bytes 786440 | tf_op jit(solution)/shard_map/ppermute | solution.py:241
  114.4 7.4 %collective-permute-start.26 = (bf16[256,256]{1,0:T(8,128)(2,1)S(1)}, bf16[256,256]{1,0:T(8,128)(2,1)S(1)}, u32[]{:S(2)}, u32[]{:S(2)}) collective-permute-start(bf16[256,256]{1,0:T(8,128)(2,1)S(1)} %get-tuple-element.144), channel_id=1, source_target_pairs={{0,8},{1,9},{2,10},{3,11},{4,12},{5,13},{6,14},{7,15},{8,0},{9,1},... | collective-permute-start | bytes 393224 | tf_op jit(solution)/shard_map/ppermute | solution.py:241
  115.6 12.4 %collective-permute-start.29 = (f32[128,256]{1,0:T(8,128)S(1)}, f32[128,256]{1,0:T(8,128)S(1)}, u32[]{:S(2)}, u32[]{:S(2)}) collective-permute-start(f32[128,256]{1,0:T(8,128)S(1)} %get-tuple-element.154), channel_id=1, source_target_pairs={{0,1},{1,0},{2,3},{3,2},{4,5},{5,4},{6,7},{7,6},{8,9},{9,8},{10,11... | collective-permute-start | bytes 393224 | tf_op jit(solution)/shard_map/ppermute | solution.py:241
  115.6 12.4 %collective-permute-start.30 = (f32[128,256]{1,0:T(8,128)S(1)}, f32[128,256]{1,0:T(8,128)S(1)}, u32[]{:S(2)}, u32[]{:S(2)}) collective-permute-start(f32[128,256]{1,0:T(8,128)S(1)} %get-tuple-element.155), channel_id=1, source_target_pairs={{0,1},{1,0},{2,3},{3,2},{4,5},{5,4},{6,7},{7,6},{8,9},{9,8},{10,11... | collective-permute-start | bytes 393224 | tf_op jit(solution)/shard_map/ppermute | solution.py:241
  120.5 7.3 %collective-permute-start.28 = (bf16[256,256]{1,0:T(8,128)(2,1)S(1)}, bf16[256,256]{1,0:T(8,128)(2,1)S(1)}, u32[]{:S(2)}, u32[]{:S(2)}) collective-permute-start(bf16[256,256]{1,0:T(8,128)(2,1)S(1)} %get-tuple-element.151), channel_id=1, source_target_pairs={{0,8},{1,9},{2,10},{3,11},{4,12},{5,13},{6,14},{7,15},{8,0},{9,1},... | collective-permute-start | bytes 393224 | tf_op jit(solution)/shard_map/ppermute | solution.py:241
  121.8 6.2 %collective-permute-start.31 = (f32[128,256]{1,0:T(8,128)S(1)}, f32[128,256]{1,0:T(8,128)S(1)}, u32[]{:S(2)}, u32[]{:S(2)}) collective-permute-start(f32[128,256]{1,0:T(8,128)S(1)} %get-tuple-element.156), channel_id=1, source_target_pairs={{0,1},{1,0},{2,3},{3,2},{4,5},{5,4},{6,7},{7,6},{8,9},{9,8},{10,11... | collective-permute-start | bytes 393224 | tf_op jit(solution)/shard_map/ppermute | solution.py:241
  127.9 1.4 %collective-permute-start.32 = (f32[128,256]{1,0:T(8,128)S(1)}, f32[128,256]{1,0:T(8,128)S(1)}, u32[]{:S(2)}, u32[]{:S(2)}) collective-permute-start(f32[128,256]{1,0:T(8,128)S(1)} %get-tuple-element.157), channel_id=1, source_target_pairs={{0,1},{1,0},{2,3},{3,2},{4,5},{5,4},{6,7},{7,6},{8,9},{9,8},{10,11... | collective-permute-start | bytes 393224 | tf_op jit(solution)/shard_map/ppermute | solution.py:241

commit v8 on v7

--- a/solution.py
+++ b/solution.py
@@ -6,9 +6,9 @@
 from jax.sharding import PartitionSpec as P
 
 CLASSES = 5
-UNITS = (2, 2, 2, 2)
-PARTS = 2
+UNITS = (2, 2, 3, 1)
 EARLY = 4
+ORDERS = {3: [1, 2, 3]}
 PACE = 10**10
 LIMIT = 16 * 2**20
 ANY = pl.BlockSpec(memory_space=pl.ANY)
@@ -100,38 +100,17 @@
     )
 
 
-def turned(side, bit, struct_modes, share, after):
+def turned(struct_modes, after):
     depth, modes = struct_modes.shape
-    half = modes // 2
-    low = 2**bit
-
-    def turn(side_ref, in_ref, kept_out, sent_out):
-        for which, out in ((side_ref[0], kept_out), (1 - side_ref[0], sent_out)):
-            for i in range(half // share):
-                column = (i // low * 2 * low + i % low + which * low) * share
-                block = in_ref[:, pl.ds(pl.multiple_of(column, share), share)]
-                out[i * share : (i + 1) * share, :] = block.T
-
-    if share % 128:
-        sides = struct_modes.T.reshape(-1, 2, low * share, depth)
-        pair = [
-            lax.dynamic_index_in_dim(sides, one, 1, keepdims=False).reshape(half, depth)
-            for one in (side[0], 1 - side[0])
-        ]
-        return [*pair, after[0]]
-    return call(turn, [side], [struct_modes], after, [jax.ShapeDtypeStruct((half, depth), BF16)] * 2, time=2.5)
-
-
-def rows_times(left_own, left_far, picked, out):
-    tall, depth = left_own.shape
-    tile = min(tall, 256)
-
-    @pl.loop(0, tall // tile)
-    def _(i):
-        here = pl.ds(pl.multiple_of(i * tile, tile), tile)
-        product = jnp.dot(left_own[here, :], picked[:depth, :], preferred_element_type=F32)
-        product += jnp.dot(left_far[here, :], picked[depth:, :], preferred_element_type=F32)
-        out[here, :] = product.astype(out.dtype)
+    step = 128 if modes % 128 == 0 else modes
+
+    def turn(in_ref, out_ref):
+        for i in range(0, modes, step):
+            out_ref[i : i + step, :] = in_ref[:, i : i + step].T
+
+    return call(
+        turn, [], [struct_modes], after, [jax.ShapeDtypeStruct((modes, depth), BF16)], time=2.5
+    )
 
 
 def slots_of(core, shifts, per, after):
@@ -153,14 +132,16 @@
     return call(slots, [core, *shifts], [], after, [shape], scalar_out=True)
 
 
-def panel(slots, lefts, pieces, after):
-    tall, depth = lefts[0].shape
+def panel(slots, here, bit, lefts, pieces, share, after):
+    modes, depth = lefts[0].shape
     width = pieces[0].shape[1]
     count = slots.shape[0]
     rows = 2 * depth // count
-
-    def panel_part(slot_ref, own_kept, far_kept, own_sent, far_sent, *refs):
-        parts, away, kept, picked = refs[:3], refs[3 : 3 + PARTS], refs[3 + PARTS], refs[4 + PARTS]
+    run = 2**bit * share
+    tile = min(run, 256)
+
+    def panel_part(slot_ref, here_ref, own, far, *refs):
+        parts, away, kept, picked = refs[:3], refs[3], refs[4], refs[5]
         for b in range(count):
             slot = slot_ref[b]
             base = 0
@@ -173,18 +154,26 @@
                     picked[b * rows : (b + 1) * rows, :] = part[pl.ds(first, rows), :]
 
                 base += many
-        for i in range(PARTS):
-            side = pl.ds(i * (tall // PARTS), tall // PARTS)
-            rows_times(own_sent.at[side, :], far_sent.at[side, :], picked, away[i])
-        rows_times(own_kept, far_kept, picked, kept)
+        for out, side in ((away, 1 - here_ref[0]), (kept, here_ref[0])):
+
+            @pl.loop(0, modes // 2 // tile)
+            def _(i, out=out, side=side):
+                at = i * tile
+                first = (at // run * 2 + side) * run + at % run
+                taken = pl.ds(pl.multiple_of(first, tile), tile)
+                product = jnp.dot(own[taken, :], picked[:depth, :], preferred_element_type=F32)
+                product += jnp.dot(far[taken, :], picked[depth:, :], preferred_element_type=F32)
+                out[pl.ds(pl.multiple_of(at, tile), tile), :] = product.astype(out.dtype)
 
     return call(
         panel_part,
-        [slots],
+        [slots, here],
         [*lefts, *pieces],
         after,
-        [jax.ShapeDtypeStruct((tall // PARTS, width), BF16)] * PARTS
-        + [jax.ShapeDtypeStruct((tall, width), F32)],
+        [
+            jax.ShapeDtypeStruct((modes // 2, width), BF16),
+            jax.ShapeDtypeStruct((modes // 2, width), F32),
+        ],
         [pltpu.VMEM((2 * depth, width), BF16)],
         time=4.0,
     )
@@ -257,8 +246,9 @@
     modes = acoustic_modes.shape[1]
     share = struct_modes.shape[1] // size
     bits = list(range(1, size.bit_length() - 1))
-    order = [2, 1, *bits[2:]]
-    levels = len(order)
+    first = ORDERS
+    levels = len(bits)
+    orders = [[*(first[j] if j in first else [2, 1, 3]), *bits[3:]] for j in range(len(UNITS))]
     widths = [units * (modes // 2 // sum(UNITS)) for units in UNITS]
     starts = [sum(widths[:j]) for j in range(len(widths))]
 
@@ -272,10 +262,10 @@
     acoustics = (acoustic_modes, swapped(acoustic_modes, 0))
     shifts = (face_shift, swapped(face_shift, 0))
     per = coupling.shape[0] // CLASSES
-    state = [dict(bits=sorted([0, *order[1:]], reverse=True)) for _ in widths]
+    state = [dict(bits=sorted([0, *order[1:]], reverse=True)) for order in orders]
     finished = []
     for stage, j in planned(levels):
-        now = state[j]
+        now, order = state[j], orders[j]
         if stage == "coupled":
             ahead, behind, here, last = coupled(
                 core, blocks, acoustics, couplings, starts[j], widths[j], token
@@ -285,14 +275,15 @@
                 later, _ = lax.optimization_barrier((struct_modes, last))
                 now["far"] = swapped(later, 0)
         elif stage == "turned":
-            side = bit_of(order[0])
-            *own, last = turned(side, order[0], struct_modes, share, token)
+            own, last = turned(struct_modes, token)
             slots, last = slots_of(core, shifts, per, [last])
-            *far, last = turned(side, order[0], now["far"], share, [last])
-            kept, sent = zip(own, far)
+            far, last = turned(now["far"], [last])
         elif stage == "panel":
-            *away, now["held"], last = panel(slots, (*kept, *sent), now["pieces"], token)
-            now["got"] = [swapped(one, order[0]) for one in away]
+            bit = order[0]
+            away, now["held"], last = panel(
+                slots, bit_of(bit), bit, (own, far), now["pieces"], share, token
+            )
+            now["got"] = [swapped(away, bit)]
         else:
             bit = order[stage] if stage < levels else 0
             place = now["bits"].index(bit)

time: 131 us -> 128 us (0.977)
  starting transfers between devices: 42.5 us -> 37.4 us
  Pallas kernels: 33.6 us -> 35.6 us
    ppermute x25 -> x21, starting transfers between devices: 25.5 us -> 17.5 us  [swapped(): return lax.ppermute(block, 'mesh', [(i, i ^ 1 << bit) for i in range(size)])]
    ppermute x8, waiting for transfers between devices: 21.5 us -> 24.7 us  [passed_along(): lax.ppermute(block, 'mesh', [((i - distance) % size, i) for i in range(si...]
    ppermute x8, starting transfers between devices: 17 us -> 19.9 us  [passed_along(): lax.ppermute(block, 'mesh', [((i - distance) % size, i) for i in range(si...]
    ppermute x25 -> x21, waiting for transfers between devices: 31.8 us -> 29.1 us  [swapped(): return lax.ppermute(block, 'mesh', [(i, i ^ 1 << bit) for i in range(size)])]
    pallas_call x24, Pallas kernels: 33.6 us -> 35.6 us  [call(): pl.pallas_call(kernel, out_shape=[*out_shape, jax.ShapeDtypeStruct((8, 12...]
  transfers between devices with their start and end apart: 33 -> 29, of which waited for: 16 -> 12; matrix products, arithmetic and copies ran while one was open for 1% -> 1% of each run, Pallas kernels for 25% -> 27%
where the time goes in v8:
time: 128 us
  waiting for transfers between devices  53.8 us (42%)
  starting transfers between devices  37.4 us (29%)
  Pallas kernels  35.6 us (28%)
    pallas_call x24, Pallas kernels, call(): pl.pallas_call(kernel, out_shape=[*out_shape, jax.ShapeDtypeStruct((8, 12...  35.6 us
    ppermute x21, waiting for transfers between devices, swapped(): return lax.ppermute(block, 'mesh', [(i, i ^ 1 << bit) for i in range(size)])  29.1 us
    ppermute x8, waiting for transfers between devices, passed_along(): lax.ppermute(block, 'mesh', [((i - distance) % size, i) for i in range(si...  24.7 us
    ppermute x8, starting transfers between devices, passed_along(): lax.ppermute(block, 'mesh', [((i - distance) % size, i) for i in range(si...  19.9 us
    ppermute x21, starting transfers between devices, swapped(): return lax.ppermute(block, 'mesh', [(i, i ^ 1 << bit) for i in range(size)])  17.5 us
  transfers between devices with their start and end apart: 29, of which 12 were waited for; matrix products, arithmetic and copies ran while one was open for 1% of the time, Pallas kernels for 27%

profile of v8, /device:TPU:0, one launch (start us, length us, event | category | flops | bytes accessed | tf_op | source)
XLA Modules:
  0.0 127.9 jit_solution(1279843510093661344)
XLA Ops:
  0.0 0.5 collective-permute-start.2
  0.5 0.1 collective-permute-start.3
  0.5 0.8 copy.7.refs_1_
  1.3 0.5 collective-permute-start.1
  1.7 0.1 collective-permute-start
  1.8 2.5 %collective-permute-done.1.refs_2_ = s32[20,4]{1,0:T(8,128)S(1)} collective-permute-done((s32[20,4]{1,0:T(8,128)S(1)}, s32[20,4]{1,0:T(8,128)S(1)}, u32[]{:S(2)}, u32[]{:S(2)}) %collective-permute-start.1) | collective-permute-done | bytes 352 | tf_op jit(solution)/shard_map/ppermute | solution.py:230
  4.3 1.1 collective-permute-done.3.refs_6_
  5.4 0.0 collective-permute-done.2.refs_4_
  5.4 3.2 %coupled_rows.4 = (bf16[768,256]{1,0:T(8,128)(2,1)S(1)}, bf16[768,256]{1,0:T(8,128)(2,1)S(1)}, bf16[1024,256]{1,0:T(8,128)(2,1)S(1)}, f32[8,128]{1,0:T(8,128)S(1)}) custom-call(s32[1]{0:T(128)} %bitcast.refs_0_, s32[20,4]{1,0:T(8,128)S(1)} %copy.7.refs_1_, s32[20,4]{1,0:T(8,128)S(1)} %collective-permute-done.1.refs_2_, bf16[512,2048]{1,0:T(8,128)(2,1)} %refs_3_.7, ...), custom_call_target="tpu_custom_call" | custom-call | flops 24999999488 | bytes 1 | tf_op jit(solution)/shard_map/coupled_rows/pallas_call | solution.py:33
  8.6 0.4 collective-permute-start.4
  9.1 2.6 %collective-permute-start.5 = (bf16[768,256]{1,0:T(8,128)(2,1)S(1)}, bf16[768,256]{1,0:T(8,128)(2,1)S(1)}, u32[]{:S(2)}, u32[]{:S(2)}) collective-permute-start(bf16[768,256]{1,0:T(8,128)(2,1)S(1)} %get-tuple-element.83), channel_id=1, source_target_pairs={{14,0},{15,1},{0,2},{1,3},{2,4},{3,5},{4,6},{5,7},{6,8},{7,9},{8,1... | collective-permute-start | bytes 1179656 | tf_op jit(solution)/shard_map/ppermute | solution.py:225
  11.7 3.0 %collective-permute-start.6 = (bf16[768,256]{1,0:T(8,128)(2,1)S(1)}, bf16[768,256]{1,0:T(8,128)(2,1)S(1)}, u32[]{:S(2)}, u32[]{:S(2)}) collective-permute-start(bf16[768,256]{1,0:T(8,128)(2,1)S(1)} %get-tuple-element.84), channel_id=1, source_target_pairs={{2,0},{3,1},{4,2},{5,3},{6,4},{7,5},{8,6},{9,7},{10,8},{11,9},{12,... | collective-permute-start | bytes 1179656 | tf_op jit(solution)/shard_map/ppermute | solution.py:225
  14.7 0.9 turn.2
  15.6 1.3 %slots.1 = (s32[24]{0:T(128)S(1)}, f32[8,128]{1,0:T(8,128)S(1)}) custom-call(s32[1]{0:T(128)} %bitcast.refs_0_, s32[12]{0:T(128)S(1)} %copy-done.1, s32[12]{0:T(128)S(1)} %collective-permute-done.refs_2_, f32[8,128]{1,0:T(8,128)S(1)} %get-tuple-element.77.refs_3_), custom_call_target="tpu_custom_call" | custom-call | flops 10000000000 | bytes 1 | tf_op jit(solution)/shard_map/slots/pallas_call | solution.py:33
  17.0 0.0 collective-permute-done.4.refs_0_
  17.0 0.9 turn.3
  17.9 3.2 %coupled_rows.5 = (bf16[768,256]{1,0:T(8,128)(2,1)S(1)}, bf16[768,256]{1,0:T(8,128)(2,1)S(1)}, bf16[1024,256]{1,0:T(8,128)(2,1)S(1)}, f32[8,128]{1,0:T(8,128)S(1)}) custom-call(s32[1]{0:T(128)} %bitcast.refs_0_, s32[20,4]{1,0:T(8,128)S(1)} %copy.7.refs_1_, s32[20,4]{1,0:T(8,128)S(1)} %collective-permute-done.1.refs_2_, bf16[512,2048]{1,0:T(8,128)(2,1)} %refs_3_.7, ...), custom_call_target="tpu_custom_call" | custom-call | flops 24999999488 | bytes 1 | tf_op jit(solution)/shard_map/coupled_rows/pallas_call | solution.py:33
  21.1 0.3 collective-permute-start.8
  21.3 4.5 %collective-permute-start.9 = (bf16[768,256]{1,0:T(8,128)(2,1)S(1)}, bf16[768,256]{1,0:T(8,128)(2,1)S(1)}, u32[]{:S(2)}, u32[]{:S(2)}) collective-permute-start(bf16[768,256]{1,0:T(8,128)(2,1)S(1)} %get-tuple-element.93), channel_id=1, source_target_pairs={{2,0},{3,1},{4,2},{5,3},{6,4},{7,5},{8,6},{9,7},{10,8},{11,9},{12,... | collective-permute-start | bytes 1179656 | tf_op jit(solution)/shard_map/ppermute | solution.py:225
  25.8 3.9 %coupled_rows.6 = (bf16[768,384]{1,0:T(8,128)(2,1)S(1)}, bf16[768,384]{1,0:T(8,128)(2,1)S(1)}, bf16[1024,384]{1,0:T(8,128)(2,1)S(1)}, f32[8,128]{1,0:T(8,128)S(1)}) custom-call(s32[1]{0:T(128)} %bitcast.refs_0_, s32[20,4]{1,0:T(8,128)S(1)} %copy.7.refs_1_, s32[20,4]{1,0:T(8,128)S(1)} %collective-permute-done.1.refs_2_, bf16[512,2048]{1,0:T(8,128)(2,1)} %refs_3_.7, ...), custom_call_target="tpu_custom_call" | custom-call | flops 24999999488 | bytes 1 | tf_op jit(solution)/shard_map/coupled_rows/pallas_call | solution.py:33
  29.7 2.9 %coupled_rows.7 = (bf16[768,128]{1,0:T(8,128)(2,1)S(1)}, bf16[768,128]{1,0:T(8,128)(2,1)S(1)}, bf16[1024,128]{1,0:T(8,128)(2,1)S(1)}, f32[8,128]{1,0:T(8,128)S(1)}) custom-call(s32[1]{0:T(128)} %bitcast.refs_0_, s32[20,4]{1,0:T(8,128)S(1)} %copy.7.refs_1_, s32[20,4]{1,0:T(8,128)S(1)} %collective-permute-done.1.refs_2_, bf16[512,2048]{1,0:T(8,128)(2,1)} %refs_3_.7, ...), custom_call_target="tpu_custom_call" | custom-call | flops 24999999488 | bytes 1 | tf_op jit(solution)/shard_map/coupled_rows/pallas_call | solution.py:33
  32.6 5.4 %collective-permute-done.5.refs_4_ = bf16[768,256]{1,0:T(8,128)(2,1)S(1)} collective-permute-done((bf16[768,256]{1,0:T(8,128)(2,1)S(1)}, bf16[768,256]{1,0:T(8,128)(2,1)S(1)}, u32[]{:S(2)}, u32[]{:S(2)}) %collective-permute-start.5) | collective-permute-done | bytes 393248 | tf_op jit(solution)/shard_map/ppermute | solution.py:225
  38.0 2.5 %collective-permute-done.6.refs_5_ = bf16[768,256]{1,0:T(8,128)(2,1)S(1)} collective-permute-done((bf16[768,256]{1,0:T(8,128)(2,1)S(1)}, bf16[768,256]{1,0:T(8,128)(2,1)S(1)}, u32[]{:S(2)}, u32[]{:S(2)}) %collective-permute-start.6) | collective-permute-done | bytes 393248 | tf_op jit(solution)/shard_map/ppermute | solution.py:225
  40.5 4.0 %panel_part.4 = (bf16[1024,256]{1,0:T(8,128)(2,1)S(1)}, f32[1024,256]{1,0:T(8,128)S(1)}, f32[8,128]{1,0:T(8,128)S(1)}) custom-call(s32[24]{0:T(128)S(1)} %get-tuple-element.78.refs_0_, s32[1]{0:T(128)} %bitcast.3.refs_1_.refs_0_, bf16[2048,768]{1,0:T(8,128)(2,1)S(1)} %get-tuple-element.79.refs_2_, bf16[2048,768]{1,0:T(8,128)(2,1)S(1)} %get-tuple-element.82.refs_3_, ...), custom_call_target="tpu_custom_call" | custom-call | flops 40000000000 | bytes 1 | tf_op jit(solution)/shard_map/panel_part/pallas_call | solution.py:33
  44.5 0.5 collective-permute-start.7
  45.1 1.1 collective-permute-start.12
  46.1 3.7 %collective-permute-start.13 = (bf16[768,384]{1,0:T(8,128)(2,1)S(1)}, bf16[768,384]{1,0:T(8,128)(2,1)S(1)}, u32[]{:S(2)}, u32[]{:S(2)}) collective-permute-start(bf16[768,384]{1,0:T(8,128)(2,1)S(1)} %get-tuple-element.102), channel_id=1, source_target_pairs={{2,0},{3,1},{4,2},{5,3},{6,4},{7,5},{8,6},{9,7},{10,8},{11,9},{12,... | collective-permute-start | bytes 1769480 | tf_op jit(solution)/shard_map/ppermute | solution.py:225
  49.8 0.0 collective-permute-done.8.refs_4_
  49.8 4.7 %collective-permute-start.18 = (bf16[768,128]{1,0:T(8,128)(2,1)S(1)}, bf16[768,128]{1,0:T(8,128)(2,1)S(1)}, u32[]{:S(2)}, u32[]{:S(2)}) collective-permute-start(bf16[768,128]{1,0:T(8,128)(2,1)S(1)} %get-tuple-element.114), channel_id=1, source_target_pairs={{2,0},{3,1},{4,2},{5,3},{6,4},{7,5},{8,6},{9,7},{10,8},{11,9},{12,... | collective-permute-start | bytes 589832 | tf_op jit(solution)/shard_map/ppermute | solution.py:225
  54.5 4.0 %panel_part.5 = (bf16[1024,256]{1,0:T(8,128)(2,1)S(1)}, f32[1024,256]{1,0:T(8,128)S(1)}, f32[8,128]{1,0:T(8,128)S(1)}) custom-call(s32[24]{0:T(128)S(1)} %get-tuple-element.78.refs_0_, s32[1]{0:T(128)} %bitcast.3.refs_1_.refs_0_, bf16[2048,768]{1,0:T(8,128)(2,1)S(1)} %get-tuple-element.79.refs_2_, bf16[2048,768]{1,0:T(8,128)(2,1)S(1)} %get-tuple-element.82.refs_3_, ...), custom_call_target="tpu_custom_call" | custom-call | flops 40000000000 | bytes 1 | tf_op jit(solution)/shard_map/panel_part/pallas_call | solution.py:33
  58.6 0.9 collective-permute-done.7
  59.5 0.4 collective-permute-start.11
  59.9 0.1 added_split.12
  60.0 16.8 %collective-permute-done.12.refs_4_ = bf16[768,384]{1,0:T(8,128)(2,1)S(1)} collective-permute-done((bf16[768,384]{1,0:T(8,128)(2,1)S(1)}, bf16[768,384]{1,0:T(8,128)(2,1)S(1)}, u32[]{:S(2)}, u32[]{:S(2)}) %collective-permute-start.12) | collective-permute-done | bytes 589856 | tf_op jit(solution)/shard_map/ppermute | solution.py:225
  76.8 2.5 %collective-permute-start.10 = (bf16[512,256]{1,0:T(8,128)(2,1)S(1)}, bf16[512,256]{1,0:T(8,128)(2,1)S(1)}, u32[]{:S(2)}, u32[]{:S(2)}) collective-permute-start(bf16[512,256]{1,0:T(8,128)(2,1)S(1)} %get-tuple-element.98), channel_id=1, source_target_pairs={{0,2},{1,3},{2,0},{3,1},{4,6},{5,7},{6,4},{7,5},{8,10},{9,11},{10,... | collective-permute-start | bytes 786440 | tf_op jit(solution)/shard_map/ppermute | solution.py:230
  79.3 0.0 collective-permute-done.13.refs_5_
  79.3 5.7 %panel_part.6 = (bf16[1024,384]{1,0:T(8,128)(2,1)S(1)}, f32[1024,384]{1,0:T(8,128)S(1)}, f32[8,128]{1,0:T(8,128)S(1)}) custom-call(s32[24]{0:T(128)S(1)} %get-tuple-element.78.refs_0_, s32[1]{0:T(128)} %bitcast.3.refs_1_.refs_0_, bf16[2048,768]{1,0:T(8,128)(2,1)S(1)} %get-tuple-element.79.refs_2_, bf16[2048,768]{1,0:T(8,128)(2,1)S(1)} %get-tuple-element.82.refs_3_, ...), custom_call_target="tpu_custom_call" | custom-call | flops 40000000000 | bytes 1 | tf_op jit(solution)/shard_map/panel_part/pallas_call | solution.py:33
  85.0 1.6 %collective-permute-start.16 = (bf16[1024,384]{1,0:T(8,128)(2,1)S(1)}, bf16[1024,384]{1,0:T(8,128)(2,1)S(1)}, u32[]{:S(2)}, u32[]{:S(2)}) collective-permute-start(bf16[1024,384]{1,0:T(8,128)(2,1)S(1)} %get-tuple-element.112), channel_id=1, source_target_pairs={{0,4},{1,5},{2,6},{3,7},{4,0},{5,1},{6,2},{7,3},{8,12},{9,13},{10,... | collective-permute-start | bytes 2359304 | tf_op jit(solution)/shard_map/ppermute | solution.py:230
  86.5 0.1 added_split.13
  86.6 0.1 collective-permute-start.15
  86.7 1.1 collective-permute-done.10
  87.8 0.1 added_split.14
  87.9 2.0 %collective-permute-start.14 = (bf16[256,256]{1,0:T(8,128)(2,1)S(1)}, bf16[256,256]{1,0:T(8,128)(2,1)S(1)}, u32[]{:S(2)}, u32[]{:S(2)}) collective-permute-start(bf16[256,256]{1,0:T(8,128)(2,1)S(1)} %get-tuple-element.108), channel_id=1, source_target_pairs={{0,8},{1,9},{2,10},{3,11},{4,12},{5,13},{6,14},{7,15},{8,0},{9,1},... | collective-permute-start | bytes 393224 | tf_op jit(solution)/shard_map/ppermute | solution.py:230
  89.9 3.9 %panel_part.7 = (bf16[1024,128]{1,0:T(8,128)(2,1)S(1)}, f32[1024,128]{1,0:T(8,128)S(1)}, f32[8,128]{1,0:T(8,128)S(1)}) custom-call(s32[24]{0:T(128)S(1)} %get-tuple-element.78.refs_0_, s32[1]{0:T(128)} %bitcast.2.refs_0_.refs_1_, bf16[2048,768]{1,0:T(8,128)(2,1)S(1)} %get-tuple-element.79.refs_2_, bf16[2048,768]{1,0:T(8,128)(2,1)S(1)} %get-tuple-element.82.refs_3_, ...), custom_call_target="tpu_custom_call" | custom-call | flops 40000000000 | bytes 1 | tf_op jit(solution)/shard_map/panel_part/pallas_call | solution.py:33
  93.8 1.0 collective-permute-start.21
  94.8 10.2 %collective-permute-done.16 = bf16[1024,384]{1,0:T(8,128)(2,1)S(1)} collective-permute-done((bf16[1024,384]{1,0:T(8,128)(2,1)S(1)}, bf16[1024,384]{1,0:T(8,128)(2,1)S(1)}, u32[]{:S(2)}, u32[]{:S(2)}) %collective-permute-start.16) | collective-permute-done | bytes 786464 | tf_op jit(solution)/shard_map/ppermute | solution.py:230
  105.0 0.2 added_split.15
  105.2 0.6 collective-permute-start.20
  105.8 1.7 %collective-permute-start.19 = (bf16[256,256]{1,0:T(8,128)(2,1)S(1)}, bf16[256,256]{1,0:T(8,128)(2,1)S(1)}, u32[]{:S(2)}, u32[]{:S(2)}) collective-permute-start(bf16[256,256]{1,0:T(8,128)(2,1)S(1)} %get-tuple-element.122), channel_id=1, source_target_pairs={{0,8},{1,9},{2,10},{3,11},{4,12},{5,13},{6,14},{7,15},{8,0},{9,1},... | collective-permute-start | bytes 393224 | tf_op jit(solution)/shard_map/ppermute | solution.py:230
  107.5 0.0 collective-permute-done.14
  107.5 0.0 collective-permute-done.21
  107.5 0.1 added_split.18
  107.6 2.5 %collective-permute-start.23 = (bf16[512,128]{1,0:T(8,128)(2,1)S(1)}, bf16[512,128]{1,0:T(8,128)(2,1)S(1)}, u32[]{:S(2)}, u32[]{:S(2)}) collective-permute-start(bf16[512,128]{1,0:T(8,128)(2,1)S(1)} %get-tuple-element.134), channel_id=1, source_target_pairs={{0,4},{1,5},{2,6},{3,7},{4,0},{5,1},{6,2},{7,3},{8,12},{9,13},{10,... | collective-permute-start | bytes 393224 | tf_op jit(solution)/shard_map/ppermute | solution.py:230
  110.1 2.9 %collective-permute-done.20 = bf16[512,384]{1,0:T(8,128)(2,1)S(1)} collective-permute-done((bf16[512,384]{1,0:T(8,128)(2,1)S(1)}, bf16[512,384]{1,0:T(8,128)(2,1)S(1)}, u32[]{:S(2)}, u32[]{:S(2)}) %collective-permute-start.20) | collective-permute-done | bytes 393248 | tf_op jit(solution)/shard_map/ppermute | solution.py:230
  113.0 0.1 added_split.19
  113.1 2.9 %collective-permute-start.22 = (bf16[256,384]{1,0:T(8,128)(2,1)S(1)}, bf16[256,384]{1,0:T(8,128)(2,1)S(1)}, u32[]{:S(2)}, u32[]{:S(2)}) collective-permute-start(bf16[256,384]{1,0:T(8,128)(2,1)S(1)} %get-tuple-element.132), channel_id=1, source_target_pairs={{0,8},{1,9},{2,10},{3,11},{4,12},{5,13},{6,14},{7,15},{8,0},{9,1},... | collective-permute-start | bytes 589832 | tf_op jit(solution)/shard_map/ppermute | solution.py:230
  116.1 0.1 collective-permute-start.24
  116.2 0.0 collective-permute-start.26
  116.3 8.5 %collective-permute-done.22 = bf16[256,384]{1,0:T(8,128)(2,1)S(1)} collective-permute-done((bf16[256,384]{1,0:T(8,128)(2,1)S(1)}, bf16[256,384]{1,0:T(8,128)(2,1)S(1)}, u32[]{:S(2)}, u32[]{:S(2)}) %collective-permute-start.22) | collective-permute-done | bytes 196640 | tf_op jit(solution)/shard_map/ppermute | solution.py:230
  124.8 0.1 collective-permute-start.27
  124.9 0.6 collective-permute-done.24
  125.5 0.1 collective-permute-start.28
  125.6 1.2 collective-permute-done.28.refs_8_
  126.8 1.0 put_together.1
  (23 shorter events, 0.2 us)
Async XLA Ops:
  0.0 5.4 %collective-permute-start.2 = (bf16[512,2048]{1,0:T(8,128)(2,1)}, bf16[512,2048]{1,0:T(8,128)(2,1)S(1)}, u32[]{:S(2)}, u32[]{:S(2)}) collective-permute-start(bf16[512,2048]{1,0:T(8,128)(2,1)} %refs_3_.7), channel_id=1, source_target_pairs={{0,1},{1,0},{2,3},{3,2},{4,5},{5,4},{6,7},{7,6},{8,9},{9,8},{10,11... | collective-permute-start | bytes 6291464 | tf_op jit(solution)/shard_map/ppermute | solution.py:230
  0.5 5.0 %collective-permute-start.3 = (bf16[20,64,256]{2,1,0:T(8,128)(2,1)}, bf16[20,64,256]{2,1,0:T(8,128)(2,1)S(1)}, u32[]{:S(2)}, u32[]{:S(2)}) collective-permute-start(bf16[20,64,256]{2,1,0:T(8,128)(2,1)} %refs_5_.7), channel_id=1, source_target_pairs={{0,1},{1,0},{2,3},{3,2},{4,5},{5,4},{6,7},{7,6},{8,9},{9,8},{10,11... | collective-permute-start | bytes 1966088 | tf_op jit(solution)/shard_map/ppermute | solution.py:230
  1.3 3.0 %collective-permute-start.1 = (s32[20,4]{1,0:T(8,128)S(1)}, s32[20,4]{1,0:T(8,128)S(1)}, u32[]{:S(2)}, u32[]{:S(2)}) collective-permute-start(s32[20,4]{1,0:T(8,128)S(1)} %copy.7.refs_1_), channel_id=1, source_target_pairs={{0,1},{1,0},{2,3},{3,2},{4,5},{5,4},{6,7},{7,6},{8,9},{9,8},{10,11... | collective-permute-start | bytes 968 | tf_op jit(solution)/shard_map/ppermute | solution.py:230
  1.7 13.9 %collective-permute-start = (s32[12]{0:T(128)}, s32[12]{0:T(128)S(1)}, u32[]{:S(2)}, u32[]{:S(2)}) collective-permute-start(s32[12]{0:T(128)} %refs_1_.5), channel_id=1, source_target_pairs={{0,1},{1,0},{2,3},{3,2},{4,5},{5,4},{6,7},{7,6},{8,9},{9,8},{10,11... | collective-permute-start | bytes 152 | tf_op jit(solution)/shard_map/ppermute | solution.py:230
  5.4 3.2 %copy-start = (bf16[768,2048]{1,0:T(8,128)(2,1)S(1)}, bf16[768,2048]{1,0:T(8,128)(2,1)}, u32[]{:S(2)}) copy-start(bf16[768,2048]{1,0:T(8,128)(2,1)} %refs_0_.1) | copy-start | bytes 9437188
  8.6 8.4 %collective-permute-start.4 = (bf16[768,2048]{1,0:T(8,128)(2,1)S(1)}, bf16[768,2048]{1,0:T(8,128)(2,1)S(1)}, u32[]{:S(2)}, u32[]{:S(2)}) collective-permute-start(bf16[768,2048]{1,0:T(8,128)(2,1)S(1)} %copy-done), channel_id=1, source_target_pairs={{0,1},{1,0},{2,3},{3,2},{4,5},{5,4},{6,7},{7,6},{8,9},{9,8},{10,11... | collective-permute-start | bytes 9437192 | tf_op jit(solution)/shard_map/ppermute | solution.py:230
  9.1 28.9 %collective-permute-start.5 = (bf16[768,256]{1,0:T(8,128)(2,1)S(1)}, bf16[768,256]{1,0:T(8,128)(2,1)S(1)}, u32[]{:S(2)}, u32[]{:S(2)}) collective-permute-start(bf16[768,256]{1,0:T(8,128)(2,1)S(1)} %get-tuple-element.83), channel_id=1, source_target_pairs={{14,0},{15,1},{0,2},{1,3},{2,4},{3,5},{4,6},{5,7},{6,8},{7,9},{8,1... | collective-permute-start | bytes 1179656 | tf_op jit(solution)/shard_map/ppermute | solution.py:225
  11.7 3.9 %copy-start.1 = (s32[12]{0:T(128)S(1)}, s32[12]{0:T(128)}, u32[]{:S(2)}) copy-start(s32[12]{0:T(128)} %refs_1_.5) | copy-start | bytes 148
  11.7 28.8 %collective-permute-start.6 = (bf16[768,256]{1,0:T(8,128)(2,1)S(1)}, bf16[768,256]{1,0:T(8,128)(2,1)S(1)}, u32[]{:S(2)}, u32[]{:S(2)}) collective-permute-start(bf16[768,256]{1,0:T(8,128)(2,1)S(1)} %get-tuple-element.84), channel_id=1, source_target_pairs={{2,0},{3,1},{4,2},{5,3},{6,4},{7,5},{8,6},{9,7},{10,8},{11,9},{12,... | collective-permute-start | bytes 1179656 | tf_op jit(solution)/shard_map/ppermute | solution.py:225
  21.1 28.7 %collective-permute-start.8 = (bf16[768,256]{1,0:T(8,128)(2,1)S(1)}, bf16[768,256]{1,0:T(8,128)(2,1)S(1)}, u32[]{:S(2)}, u32[]{:S(2)}) collective-permute-start(bf16[768,256]{1,0:T(8,128)(2,1)S(1)} %get-tuple-element.92), channel_id=1, source_target_pairs={{14,0},{15,1},{0,2},{1,3},{2,4},{3,5},{4,6},{5,7},{6,8},{7,9},{8,1... | collective-permute-start | bytes 1179656 | tf_op jit(solution)/shard_map/ppermute | solution.py:225
  21.3 28.5 %collective-permute-start.9 = (bf16[768,256]{1,0:T(8,128)(2,1)S(1)}, bf16[768,256]{1,0:T(8,128)(2,1)S(1)}, u32[]{:S(2)}, u32[]{:S(2)}) collective-permute-start(bf16[768,256]{1,0:T(8,128)(2,1)S(1)} %get-tuple-element.93), channel_id=1, source_target_pairs={{2,0},{3,1},{4,2},{5,3},{6,4},{7,5},{8,6},{9,7},{10,8},{11,9},{12,... | collective-permute-start | bytes 1179656 | tf_op jit(solution)/shard_map/ppermute | solution.py:225
  44.5 14.9 %collective-permute-start.7 = (bf16[1024,256]{1,0:T(8,128)(2,1)S(1)}, bf16[1024,256]{1,0:T(8,128)(2,1)S(1)}, u32[]{:S(2)}, u32[]{:S(2)}) collective-permute-start(bf16[1024,256]{1,0:T(8,128)(2,1)S(1)} %get-tuple-element.91), channel_id=1, source_target_pairs={{0,4},{1,5},{2,6},{3,7},{4,0},{5,1},{6,2},{7,3},{8,12},{9,13},{10,... | collective-permute-start | bytes 1572872 | tf_op jit(solution)/shard_map/ppermute | solution.py:230
  45.1 31.7 %collective-permute-start.12 = (bf16[768,384]{1,0:T(8,128)(2,1)S(1)}, bf16[768,384]{1,0:T(8,128)(2,1)S(1)}, u32[]{:S(2)}, u32[]{:S(2)}) collective-permute-start(bf16[768,384]{1,0:T(8,128)(2,1)S(1)} %get-tuple-element.101), channel_id=1, source_target_pairs={{14,0},{15,1},{0,2},{1,3},{2,4},{3,5},{4,6},{5,7},{6,8},{7,9},{8,1... | collective-permute-start | bytes 1769480 | tf_op jit(solution)/shard_map/ppermute | solution.py:225
  46.1 33.1 %collective-permute-start.13 = (bf16[768,384]{1,0:T(8,128)(2,1)S(1)}, bf16[768,384]{1,0:T(8,128)(2,1)S(1)}, u32[]{:S(2)}, u32[]{:S(2)}) collective-permute-start(bf16[768,384]{1,0:T(8,128)(2,1)S(1)} %get-tuple-element.102), channel_id=1, source_target_pairs={{2,0},{3,1},{4,2},{5,3},{6,4},{7,5},{8,6},{9,7},{10,8},{11,9},{12,... | collective-permute-start | bytes 1769480 | tf_op jit(solution)/shard_map/ppermute | solution.py:225
  49.8 40.1 %collective-permute-start.17 = (bf16[768,128]{1,0:T(8,128)(2,1)S(1)}, bf16[768,128]{1,0:T(8,128)(2,1)S(1)}, u32[]{:S(2)}, u32[]{:S(2)}) collective-permute-start(bf16[768,128]{1,0:T(8,128)(2,1)S(1)} %get-tuple-element.113), channel_id=1, source_target_pairs={{14,0},{15,1},{0,2},{1,3},{2,4},{3,5},{4,6},{5,7},{6,8},{7,9},{8,1... | collective-permute-start | bytes 589832 | tf_op jit(solution)/shard_map/ppermute | solution.py:225
  49.8 40.1 %collective-permute-start.18 = (bf16[768,128]{1,0:T(8,128)(2,1)S(1)}, bf16[768,128]{1,0:T(8,128)(2,1)S(1)}, u32[]{:S(2)}, u32[]{:S(2)}) collective-permute-start(bf16[768,128]{1,0:T(8,128)(2,1)S(1)} %get-tuple-element.114), channel_id=1, source_target_pairs={{2,0},{3,1},{4,2},{5,3},{6,4},{7,5},{8,6},{9,7},{10,8},{11,9},{12,... | collective-permute-start | bytes 589832 | tf_op jit(solution)/shard_map/ppermute | solution.py:225
  59.5 27.0 %collective-permute-start.11 = (bf16[1024,256]{1,0:T(8,128)(2,1)S(1)}, bf16[1024,256]{1,0:T(8,128)(2,1)S(1)}, u32[]{:S(2)}, u32[]{:S(2)}) collective-permute-start(bf16[1024,256]{1,0:T(8,128)(2,1)S(1)} %get-tuple-element.100), channel_id=1, source_target_pairs={{0,4},{1,5},{2,6},{3,7},{4,0},{5,1},{6,2},{7,3},{8,12},{9,13},{10,... | collective-permute-start | bytes 1572872 | tf_op jit(solution)/shard_map/ppermute | solution.py:230
  76.8 11.0 %collective-permute-start.10 = (bf16[512,256]{1,0:T(8,128)(2,1)S(1)}, bf16[512,256]{1,0:T(8,128)(2,1)S(1)}, u32[]{:S(2)}, u32[]{:S(2)}) collective-permute-start(bf16[512,256]{1,0:T(8,128)(2,1)S(1)} %get-tuple-element.98), channel_id=1, source_target_pairs={{0,2},{1,3},{2,0},{3,1},{4,6},{5,7},{6,4},{7,5},{8,10},{9,11},{10,... | collective-permute-start | bytes 786440 | tf_op jit(solution)/shard_map/ppermute | solution.py:230
  85.0 20.0 %collective-permute-start.16 = (bf16[1024,384]{1,0:T(8,128)(2,1)S(1)}, bf16[1024,384]{1,0:T(8,128)(2,1)S(1)}, u32[]{:S(2)}, u32[]{:S(2)}) collective-permute-start(bf16[1024,384]{1,0:T(8,128)(2,1)S(1)} %get-tuple-element.112), channel_id=1, source_target_pairs={{0,4},{1,5},{2,6},{3,7},{4,0},{5,1},{6,2},{7,3},{8,12},{9,13},{10,... | collective-permute-start | bytes 2359304 | tf_op jit(solution)/shard_map/ppermute | solution.py:230
  86.6 19.1 %collective-permute-start.15 = (bf16[512,256]{1,0:T(8,128)(2,1)S(1)}, bf16[512,256]{1,0:T(8,128)(2,1)S(1)}, u32[]{:S(2)}, u32[]{:S(2)}) collective-permute-start(bf16[512,256]{1,0:T(8,128)(2,1)S(1)} %get-tuple-element.110), channel_id=1, source_target_pairs={{0,2},{1,3},{2,0},{3,1},{4,6},{5,7},{6,4},{7,5},{8,10},{9,11},{10,... | collective-permute-start | bytes 786440 | tf_op jit(solution)/shard_map/ppermute | solution.py:230
  87.9 19.6 %collective-permute-start.14 = (bf16[256,256]{1,0:T(8,128)(2,1)S(1)}, bf16[256,256]{1,0:T(8,128)(2,1)S(1)}, u32[]{:S(2)}, u32[]{:S(2)}) collective-permute-start(bf16[256,256]{1,0:T(8,128)(2,1)S(1)} %get-tuple-element.108), channel_id=1, source_target_pairs={{0,8},{1,9},{2,10},{3,11},{4,12},{5,13},{6,14},{7,15},{8,0},{9,1},... | collective-permute-start | bytes 393224 | tf_op jit(solution)/shard_map/ppermute | solution.py:230
  93.8 13.7 %collective-permute-start.21 = (bf16[1024,128]{1,0:T(8,128)(2,1)S(1)}, bf16[1024,128]{1,0:T(8,128)(2,1)S(1)}, u32[]{:S(2)}, u32[]{:S(2)}) collective-permute-start(bf16[1024,128]{1,0:T(8,128)(2,1)S(1)} %get-tuple-element.126), channel_id=1, source_target_pairs={{0,2},{1,3},{2,0},{3,1},{4,6},{5,7},{6,4},{7,5},{8,10},{9,11},{10,... | collective-permute-start | bytes 786440 | tf_op jit(solution)/shard_map/ppermute | solution.py:230
  105.2 7.9 %collective-permute-start.20 = (bf16[512,384]{1,0:T(8,128)(2,1)S(1)}, bf16[512,384]{1,0:T(8,128)(2,1)S(1)}, u32[]{:S(2)}, u32[]{:S(2)}) collective-permute-start(bf16[512,384]{1,0:T(8,128)(2,1)S(1)} %get-tuple-element.124), channel_id=1, source_target_pairs={{0,2},{1,3},{2,0},{3,1},{4,6},{5,7},{6,4},{7,5},{8,10},{9,11},{10,... | collective-permute-start | bytes 1179656 | tf_op jit(solution)/shard_map/ppermute | solution.py:230
  105.8 10.2 %collective-permute-start.19 = (bf16[256,256]{1,0:T(8,128)(2,1)S(1)}, bf16[256,256]{1,0:T(8,128)(2,1)S(1)}, u32[]{:S(2)}, u32[]{:S(2)}) collective-permute-start(bf16[256,256]{1,0:T(8,128)(2,1)S(1)} %get-tuple-element.122), channel_id=1, source_target_pairs={{0,8},{1,9},{2,10},{3,11},{4,12},{5,13},{6,14},{7,15},{8,0},{9,1},... | collective-permute-start | bytes 393224 | tf_op jit(solution)/shard_map/ppermute | solution.py:230
  107.6 8.5 %collective-permute-start.23 = (bf16[512,128]{1,0:T(8,128)(2,1)S(1)}, bf16[512,128]{1,0:T(8,128)(2,1)S(1)}, u32[]{:S(2)}, u32[]{:S(2)}) collective-permute-start(bf16[512,128]{1,0:T(8,128)(2,1)S(1)} %get-tuple-element.134), channel_id=1, source_target_pairs={{0,4},{1,5},{2,6},{3,7},{4,0},{5,1},{6,2},{7,3},{8,12},{9,13},{10,... | collective-permute-start | bytes 393224 | tf_op jit(solution)/shard_map/ppermute | solution.py:230
  110.1 15.5 %collective-permute-start.25 = (f32[128,256]{1,0:T(8,128)S(1)}, f32[128,256]{1,0:T(8,128)S(1)}, u32[]{:S(2)}, u32[]{:S(2)}) collective-permute-start(f32[128,256]{1,0:T(8,128)S(1)} %get-tuple-element.142), channel_id=1, source_target_pairs={{0,1},{1,0},{2,3},{3,2},{4,5},{5,4},{6,7},{7,6},{8,9},{9,8},{10,11... | collective-permute-start | bytes 393224 | tf_op jit(solution)/shard_map/ppermute | solution.py:230
  113.1 11.7 %collective-permute-start.22 = (bf16[256,384]{1,0:T(8,128)(2,1)S(1)}, bf16[256,384]{1,0:T(8,128)(2,1)S(1)}, u32[]{:S(2)}, u32[]{:S(2)}) collective-permute-start(bf16[256,384]{1,0:T(8,128)(2,1)S(1)} %get-tuple-element.132), channel_id=1, source_target_pairs={{0,8},{1,9},{2,10},{3,11},{4,12},{5,13},{6,14},{7,15},{8,0},{9,1},... | collective-permute-start | bytes 589832 | tf_op jit(solution)/shard_map/ppermute | solution.py:230
  116.1 9.4 %collective-permute-start.24 = (bf16[256,128]{1,0:T(8,128)(2,1)S(1)}, bf16[256,128]{1,0:T(8,128)(2,1)S(1)}, u32[]{:S(2)}, u32[]{:S(2)}) collective-permute-start(bf16[256,128]{1,0:T(8,128)(2,1)S(1)} %get-tuple-element.139), channel_id=1, source_target_pairs={{0,8},{1,9},{2,10},{3,11},{4,12},{5,13},{6,14},{7,15},{8,0},{9,1},... | collective-permute-start | bytes 196616 | tf_op jit(solution)/shard_map/ppermute | solution.py:230
  116.2 9.4 %collective-permute-start.26 = (f32[128,256]{1,0:T(8,128)S(1)}, f32[128,256]{1,0:T(8,128)S(1)}, u32[]{:S(2)}, u32[]{:S(2)}) collective-permute-start(f32[128,256]{1,0:T(8,128)S(1)} %get-tuple-element.143), channel_id=1, source_target_pairs={{0,1},{1,0},{2,3},{3,2},{4,5},{5,4},{6,7},{7,6},{8,9},{9,8},{10,11... | collective-permute-start | bytes 393224 | tf_op jit(solution)/shard_map/ppermute | solution.py:230
  124.8 2.0 %collective-permute-start.27 = (f32[128,384]{1,0:T(8,128)S(1)}, f32[128,384]{1,0:T(8,128)S(1)}, u32[]{:S(2)}, u32[]{:S(2)}) collective-permute-start(f32[128,384]{1,0:T(8,128)S(1)} %get-tuple-element.144), channel_id=1, source_target_pairs={{0,1},{1,0},{2,3},{3,2},{4,5},{5,4},{6,7},{7,6},{8,9},{9,8},{10,11... | collective-permute-start | bytes 589832 | tf_op jit(solution)/shard_map/ppermute | solution.py:230
  125.5 1.3 %collective-permute-start.28 = (f32[128,128]{1,0:T(8,128)S(1)}, f32[128,128]{1,0:T(8,128)S(1)}, u32[]{:S(2)}, u32[]{:S(2)}) collective-permute-start(f32[128,128]{1,0:T(8,128)S(1)} %get-tuple-element.145), channel_id=1, source_target_pairs={{0,1},{1,0},{2,3},{3,2},{4,5},{5,4},{6,7},{7,6},{8,9},{9,8},{10,11... | collective-permute-start | bytes 196616 | tf_op jit(solution)/shard_map/ppermute | solution.py:230

commit v9 on v8

--- a/solution.py
+++ b/solution.py
@@ -10,7 +10,7 @@
 EARLY = 4
 ORDERS = {3: [1, 2, 3]}
 PACE = 10**10
-LIMIT = 16 * 2**20
+LIMIT = 8 * 2**20
 ANY = pl.BlockSpec(memory_space=pl.ANY)
 BF16, F32 = jnp.bfloat16, jnp.float32
 NEXT = ((0, 0), (1, 0), (1, 1))
@@ -140,8 +140,18 @@
     run = 2**bit * share
     tile = min(run, 256)
 
-    def panel_part(slot_ref, here_ref, own, far, *refs):
-        parts, away, kept, picked = refs[:3], refs[3], refs[4], refs[5]
+    def multiply(out, side, own, far, picked):
+        @pl.loop(0, modes // 2 // tile)
+        def _(i):
+            at = i * tile
+            first = (at // run * 2 + side) * run + at % run
+            taken = pl.ds(pl.multiple_of(first, tile), tile)
+            product = jnp.dot(own[taken, :], picked[:depth, :], preferred_element_type=F32)
+            product += jnp.dot(far[taken, :], picked[depth:, :], preferred_element_type=F32)
+            out[pl.ds(pl.multiple_of(at, tile), tile), :] = product.astype(out.dtype)
+
+    def panel_away(slot_ref, here_ref, own, far, *refs):
+        parts, away, picked = refs[:3], refs[3], refs[4]
         for b in range(count):
             slot = slot_ref[b]
             base = 0
@@ -154,29 +164,24 @@
                     picked[b * rows : (b + 1) * rows, :] = part[pl.ds(first, rows), :]
 
                 base += many
-        for out, side in ((away, 1 - here_ref[0]), (kept, here_ref[0])):
-
-            @pl.loop(0, modes // 2 // tile)
-            def _(i, out=out, side=side):
-                at = i * tile
-                first = (at // run * 2 + side) * run + at % run
-                taken = pl.ds(pl.multiple_of(first, tile), tile)
-                product = jnp.dot(own[taken, :], picked[:depth, :], preferred_element_type=F32)
-                product += jnp.dot(far[taken, :], picked[depth:, :], preferred_element_type=F32)
-                out[pl.ds(pl.multiple_of(at, tile), tile), :] = product.astype(out.dtype)
-
-    return call(
-        panel_part,
+        multiply(away, 1 - here_ref[0], own, far, picked)
+
+    def panel_own(here_ref, own, far, picked, kept):
+        multiply(kept, here_ref[0], own, far, picked)
+
+    half = (modes // 2, width)
+    away, picked, last = call(
+        panel_away,
         [slots, here],
         [*lefts, *pieces],
         after,
-        [
-            jax.ShapeDtypeStruct((modes // 2, width), BF16),
-            jax.ShapeDtypeStruct((modes // 2, width), F32),
-        ],
-        [pltpu.VMEM((2 * depth, width), BF16)],
-        time=4.0,
-    )
+        [jax.ShapeDtypeStruct(half, BF16), jax.ShapeDtypeStruct((2 * depth, width), BF16)],
+        time=5.0,
+    )
+    kept, last = call(
+        panel_own, [here], [*lefts, picked], [last], [jax.ShapeDtypeStruct(half, F32)], time=1.5
+    )
+    return away, kept, last
 
 
 def added(held, got, here, before, wire, after):

time: 128 us -> 128 us (level)
    pallas_call x24 -> x28, Pallas kernels: 35.6 us -> 36.7 us  [call(): pl.pallas_call(kernel, out_shape=[*out_shape, jax.ShapeDtypeStruct((8, 12...]
  transfers between devices with their start and end apart: 29 -> 29, of which waited for: 12 -> 11; matrix products, arithmetic and copies ran while one was open for 1% -> 1% of each run, Pallas kernels for 27% -> 28%
where the time goes in v9:
time: 128 us
  waiting for transfers between devices  52.8 us (41%)
  starting transfers between devices  37.1 us (29%)
  Pallas kernels  36.7 us (29%)
    pallas_call x28, Pallas kernels, call(): pl.pallas_call(kernel, out_shape=[*out_shape, jax.ShapeDtypeStruct((8, 12...  36.7 us
    ppermute x21, waiting for transfers between devices, swapped(): return lax.ppermute(block, 'mesh', [(i, i ^ 1 << bit) for i in range(size)])  28.3 us
    ppermute x8, waiting for transfers between devices, passed_along(): lax.ppermute(block, 'mesh', [((i - distance) % size, i) for i in range(si...  24.5 us
    ppermute x8, starting transfers between devices, passed_along(): lax.ppermute(block, 'mesh', [((i - distance) % size, i) for i in range(si...  19.9 us
    ppermute x21, starting transfers between devices, swapped(): return lax.ppermute(block, 'mesh', [(i, i ^ 1 << bit) for i in range(size)])  17.2 us
  transfers between devices with their start and end apart: 29, of which 11 were waited for; matrix products, arithmetic and copies ran while one was open for 1% of the time, Pallas kernels for 28%

profile of v9, /device:TPU:0, one launch (start us, length us, event | category | flops | bytes accessed | tf_op | source)
XLA Modules:
  0.0 127.7 jit_solution(6295129506208465488)
XLA Ops:
  0.0 0.5 collective-permute-start.1
  0.5 0.1 collective-permute-start.2
  0.5 0.8 copy.7.refs_1_
  1.3 0.5 collective-permute-start
  1.7 0.1 collective-permute-start.4
  1.8 2.5 %collective-permute-done.refs_2_ = s32[20,4]{1,0:T(8,128)S(1)} collective-permute-done((s32[20,4]{1,0:T(8,128)S(1)}, s32[20,4]{1,0:T(8,128)S(1)}, u32[]{:S(2)}, u32[]{:S(2)}) %collective-permute-start) | collective-permute-done | bytes 352 | tf_op jit(solution)/shard_map/ppermute | solution.py:235
  4.3 1.1 collective-permute-done.2.refs_6_
  5.4 3.2 %coupled_rows.4 = (bf16[768,256]{1,0:T(8,128)(2,1)S(1)}, bf16[768,256]{1,0:T(8,128)(2,1)S(1)}, bf16[1024,256]{1,0:T(8,128)(2,1)S(1)}, f32[8,128]{1,0:T(8,128)S(1)}) custom-call(s32[1]{0:T(128)} %bitcast.refs_0_, s32[20,4]{1,0:T(8,128)S(1)} %copy.7.refs_1_, s32[20,4]{1,0:T(8,128)S(1)} %collective-permute-done.refs_2_, bf16[512,2048]{1,0:T(8,128)(2,1)} %refs_3_.7, ...), custom_call_target="tpu_custom_call" | custom-call | flops 24999999488 | bytes 1 | tf_op jit(solution)/shard_map/coupled_rows/pallas_call | solution.py:33
  8.6 0.4 collective-permute-start.3
  9.1 2.6 %collective-permute-start.5 = (bf16[768,256]{1,0:T(8,128)(2,1)S(1)}, bf16[768,256]{1,0:T(8,128)(2,1)S(1)}, u32[]{:S(2)}, u32[]{:S(2)}) collective-permute-start(bf16[768,256]{1,0:T(8,128)(2,1)S(1)} %get-tuple-element.91), channel_id=1, source_target_pairs={{14,0},{15,1},{0,2},{1,3},{2,4},{3,5},{4,6},{5,7},{6,8},{7,9},{8,1... | collective-permute-start | bytes 1179656 | tf_op jit(solution)/shard_map/ppermute | solution.py:230
  11.7 3.0 %collective-permute-start.6 = (bf16[768,256]{1,0:T(8,128)(2,1)S(1)}, bf16[768,256]{1,0:T(8,128)(2,1)S(1)}, u32[]{:S(2)}, u32[]{:S(2)}) collective-permute-start(bf16[768,256]{1,0:T(8,128)(2,1)S(1)} %get-tuple-element.92), channel_id=1, source_target_pairs={{2,0},{3,1},{4,2},{5,3},{6,4},{7,5},{8,6},{9,7},{10,8},{11,9},{12,... | collective-permute-start | bytes 1179656 | tf_op jit(solution)/shard_map/ppermute | solution.py:230
  14.7 0.9 turn.2
  15.6 1.3 %slots.1 = (s32[24]{0:T(128)S(1)}, f32[8,128]{1,0:T(8,128)S(1)}) custom-call(s32[1]{0:T(128)} %bitcast.refs_0_, s32[12]{0:T(128)S(1)} %copy-done.1, s32[12]{0:T(128)S(1)} %collective-permute-done.4.refs_2_, f32[8,128]{1,0:T(8,128)S(1)} %get-tuple-element.87.refs_3_), custom_call_target="tpu_custom_call" | custom-call | flops 10000000000 | bytes 1 | tf_op jit(solution)/shard_map/slots/pallas_call | solution.py:33
  17.0 0.0 collective-permute-done.3.refs_0_
  17.0 0.9 turn.3
  17.9 3.2 %coupled_rows.5 = (bf16[768,256]{1,0:T(8,128)(2,1)S(1)}, bf16[768,256]{1,0:T(8,128)(2,1)S(1)}, bf16[1024,256]{1,0:T(8,128)(2,1)S(1)}, f32[8,128]{1,0:T(8,128)S(1)}) custom-call(s32[1]{0:T(128)} %bitcast.refs_0_, s32[20,4]{1,0:T(8,128)S(1)} %copy.7.refs_1_, s32[20,4]{1,0:T(8,128)S(1)} %collective-permute-done.refs_2_, bf16[512,2048]{1,0:T(8,128)(2,1)} %refs_3_.7, ...), custom_call_target="tpu_custom_call" | custom-call | flops 24999999488 | bytes 1 | tf_op jit(solution)/shard_map/coupled_rows/pallas_call | solution.py:33
  21.1 0.3 collective-permute-start.8
  21.3 4.5 %collective-permute-start.9 = (bf16[768,256]{1,0:T(8,128)(2,1)S(1)}, bf16[768,256]{1,0:T(8,128)(2,1)S(1)}, u32[]{:S(2)}, u32[]{:S(2)}) collective-permute-start(bf16[768,256]{1,0:T(8,128)(2,1)S(1)} %get-tuple-element.103), channel_id=1, source_target_pairs={{2,0},{3,1},{4,2},{5,3},{6,4},{7,5},{8,6},{9,7},{10,8},{11,9},{12,... | collective-permute-start | bytes 1179656 | tf_op jit(solution)/shard_map/ppermute | solution.py:230
  25.8 3.9 %coupled_rows.6 = (bf16[768,384]{1,0:T(8,128)(2,1)S(1)}, bf16[768,384]{1,0:T(8,128)(2,1)S(1)}, bf16[1024,384]{1,0:T(8,128)(2,1)S(1)}, f32[8,128]{1,0:T(8,128)S(1)}) custom-call(s32[1]{0:T(128)} %bitcast.refs_0_, s32[20,4]{1,0:T(8,128)S(1)} %copy.7.refs_1_, s32[20,4]{1,0:T(8,128)S(1)} %collective-permute-done.refs_2_, bf16[512,2048]{1,0:T(8,128)(2,1)} %refs_3_.7, ...), custom_call_target="tpu_custom_call" | custom-call | flops 24999999488 | bytes 1 | tf_op jit(solution)/shard_map/coupled_rows/pallas_call | solution.py:33
  29.7 3.5 %coupled_rows.7 = (bf16[768,128]{1,0:T(8,128)(2,1)}, bf16[768,128]{1,0:T(8,128)(2,1)}, bf16[1024,128]{1,0:T(8,128)(2,1)S(1)}, f32[8,128]{1,0:T(8,128)S(1)}) custom-call(s32[1]{0:T(128)} %bitcast.refs_0_, s32[20,4]{1,0:T(8,128)S(1)} %copy.7.refs_1_, s32[20,4]{1,0:T(8,128)S(1)} %collective-permute-done.refs_2_, bf16[512,2048]{1,0:T(8,128)(2,1)} %refs_3_.7, ...), custom_call_target="tpu_custom_call" | custom-call | flops 24999999488 | bytes 1 | tf_op jit(solution)/shard_map/coupled_rows/pallas_call | solution.py:33
  33.2 4.8 %collective-permute-done.5.refs_4_ = bf16[768,256]{1,0:T(8,128)(2,1)S(1)} collective-permute-done((bf16[768,256]{1,0:T(8,128)(2,1)S(1)}, bf16[768,256]{1,0:T(8,128)(2,1)S(1)}, u32[]{:S(2)}, u32[]{:S(2)}) %collective-permute-start.5) | collective-permute-done | bytes 393248 | tf_op jit(solution)/shard_map/ppermute | solution.py:230
  38.0 2.5 %collective-permute-done.6.refs_5_ = bf16[768,256]{1,0:T(8,128)(2,1)S(1)} collective-permute-done((bf16[768,256]{1,0:T(8,128)(2,1)S(1)}, bf16[768,256]{1,0:T(8,128)(2,1)S(1)}, u32[]{:S(2)}, u32[]{:S(2)}) %collective-permute-start.6) | collective-permute-done | bytes 393248 | tf_op jit(solution)/shard_map/ppermute | solution.py:230
  40.5 2.5 %panel_away.4 = (bf16[1024,256]{1,0:T(8,128)(2,1)S(1)}, bf16[1536,256]{1,0:T(8,128)(2,1)S(1)}, f32[8,128]{1,0:T(8,128)S(1)}) custom-call(s32[24]{0:T(128)S(1)} %get-tuple-element.90.refs_0_, s32[1]{0:T(128)} %bitcast.3.refs_1_.refs_0_, bf16[2048,768]{1,0:T(8,128)(2,1)S(1)} %get-tuple-element.85.refs_2_.refs_1_, ...), custom_call_target="tpu_custom_call" | custom-call | flops 49999998976 | bytes 1 | tf_op jit(solution)/shard_map/panel_away/pallas_call | solution.py:33
  43.1 0.5 collective-permute-start.7
  43.6 1.1 collective-permute-start.12
  44.7 3.7 %collective-permute-start.13 = (bf16[768,384]{1,0:T(8,128)(2,1)S(1)}, bf16[768,384]{1,0:T(8,128)(2,1)S(1)}, u32[]{:S(2)}, u32[]{:S(2)}) collective-permute-start(bf16[768,384]{1,0:T(8,128)(2,1)S(1)} %get-tuple-element.114), channel_id=1, source_target_pairs={{2,0},{3,1},{4,2},{5,3},{6,4},{7,5},{8,6},{9,7},{10,8},{11,9},{12,... | collective-permute-start | bytes 1769480 | tf_op jit(solution)/shard_map/ppermute | solution.py:230
  48.3 1.5 %panel_own.4 = (f32[1024,256]{1,0:T(8,128)S(1)}, f32[8,128]{1,0:T(8,128)S(1)}) custom-call(s32[1]{0:T(128)} %bitcast.3.refs_1_.refs_0_, bf16[2048,768]{1,0:T(8,128)(2,1)S(1)} %get-tuple-element.85.refs_2_.refs_1_, bf16[2048,768]{1,0:T(8,128)(2,1)S(1)} %get-tuple-element.89.refs_3_.refs_2_, bf16[1536,256]{1,0:T(8,128)(2,1)S(1)} %get-tuple-element.98.refs_3_, ...), custom_call_target="tpu_custom_call" | custom-call | flops 15000000512 | bytes 1 | tf_op jit(solution)/shard_map/panel_own/pallas_call | solution.py:33
  49.8 0.0 collective-permute-done.8.refs_4_
  49.8 0.1 collective-permute-start.17
  49.9 4.7 %collective-permute-start.18 = (bf16[768,128]{1,0:T(8,128)(2,1)}, bf16[768,128]{1,0:T(8,128)(2,1)}, u32[]{:S(2)}, u32[]{:S(2)}) collective-permute-start(bf16[768,128]{1,0:T(8,128)(2,1)} %get-tuple-element.128), channel_id=1, source_target_pairs={{2,0},{3,1},{4,2},{5,3},{6,4},{7,5},{8,6},{9,7},{10,8},{11,9},{12,... | collective-permute-start | bytes 589832 | tf_op jit(solution)/shard_map/ppermute | solution.py:230
  54.6 2.5 %panel_away.5 = (bf16[1024,256]{1,0:T(8,128)(2,1)S(1)}, bf16[1536,256]{1,0:T(8,128)(2,1)S(1)}, f32[8,128]{1,0:T(8,128)S(1)}) custom-call(s32[24]{0:T(128)S(1)} %get-tuple-element.90.refs_0_, s32[1]{0:T(128)} %bitcast.3.refs_1_.refs_0_, bf16[2048,768]{1,0:T(8,128)(2,1)S(1)} %get-tuple-element.85.refs_2_.refs_1_, ...), custom_call_target="tpu_custom_call" | custom-call | flops 49999998976 | bytes 1 | tf_op jit(solution)/shard_map/panel_away/pallas_call | solution.py:33
  57.1 1.5 %panel_own.5 = (f32[1024,256]{1,0:T(8,128)S(1)}, f32[8,128]{1,0:T(8,128)S(1)}) custom-call(s32[1]{0:T(128)} %bitcast.3.refs_1_.refs_0_, bf16[2048,768]{1,0:T(8,128)(2,1)S(1)} %get-tuple-element.85.refs_2_.refs_1_, bf16[2048,768]{1,0:T(8,128)(2,1)S(1)} %get-tuple-element.89.refs_3_.refs_2_, bf16[1536,256]{1,0:T(8,128)(2,1)S(1)} %get-tuple-element.106.refs_3_, ...), custom_call_target="tpu_custom_call" | custom-call | flops 15000000512 | bytes 1 | tf_op jit(solution)/shard_map/panel_own/pallas_call | solution.py:33
  58.6 0.1 collective-permute-start.11
  58.7 0.1 added_split.12
  58.8 17.1 %collective-permute-done.12.refs_4_ = bf16[768,384]{1,0:T(8,128)(2,1)S(1)} collective-permute-done((bf16[768,384]{1,0:T(8,128)(2,1)S(1)}, bf16[768,384]{1,0:T(8,128)(2,1)S(1)}, u32[]{:S(2)}, u32[]{:S(2)}) %collective-permute-start.12) | collective-permute-done | bytes 589856 | tf_op jit(solution)/shard_map/ppermute | solution.py:230
  75.9 2.5 %collective-permute-start.10 = (bf16[512,256]{1,0:T(8,128)(2,1)S(1)}, bf16[512,256]{1,0:T(8,128)(2,1)S(1)}, u32[]{:S(2)}, u32[]{:S(2)}) collective-permute-start(bf16[512,256]{1,0:T(8,128)(2,1)S(1)} %get-tuple-element.110), channel_id=1, source_target_pairs={{0,2},{1,3},{2,0},{3,1},{4,6},{5,7},{6,4},{7,5},{8,10},{9,11},{10,... | collective-permute-start | bytes 786440 | tf_op jit(solution)/shard_map/ppermute | solution.py:235
  78.4 0.0 collective-permute-done.13.refs_5_
  78.4 3.4 %panel_away.6 = (bf16[1024,384]{1,0:T(8,128)(2,1)S(1)}, bf16[1536,384]{1,0:T(8,128)(2,1)S(1)}, f32[8,128]{1,0:T(8,128)S(1)}) custom-call(s32[24]{0:T(128)S(1)} %get-tuple-element.90.refs_0_, s32[1]{0:T(128)} %bitcast.3.refs_1_.refs_0_, bf16[2048,768]{1,0:T(8,128)(2,1)S(1)} %get-tuple-element.85.refs_2_.refs_1_, ...), custom_call_target="tpu_custom_call" | custom-call | flops 49999998976 | bytes 1 | tf_op jit(solution)/shard_map/panel_away/pallas_call | solution.py:33
  81.9 1.6 %collective-permute-start.16 = (bf16[1024,384]{1,0:T(8,128)(2,1)S(1)}, bf16[1024,384]{1,0:T(8,128)(2,1)S(1)}, u32[]{:S(2)}, u32[]{:S(2)}) collective-permute-start(bf16[1024,384]{1,0:T(8,128)(2,1)S(1)} %get-tuple-element.126), channel_id=1, source_target_pairs={{0,4},{1,5},{2,6},{3,7},{4,0},{5,1},{6,2},{7,3},{8,12},{9,13},{10,... | collective-permute-start | bytes 2359304 | tf_op jit(solution)/shard_map/ppermute | solution.py:235
  83.5 2.3 %panel_own.6 = (f32[1024,384]{1,0:T(8,128)S(1)}, f32[8,128]{1,0:T(8,128)S(1)}) custom-call(s32[1]{0:T(128)} %bitcast.3.refs_1_.refs_0_, bf16[2048,768]{1,0:T(8,128)(2,1)S(1)} %get-tuple-element.85.refs_2_.refs_1_, bf16[2048,768]{1,0:T(8,128)(2,1)S(1)} %get-tuple-element.89.refs_3_.refs_2_, bf16[1536,384]{1,0:T(8,128)(2,1)S(1)} %get-tuple-element.117.refs_3_, ...), custom_call_target="tpu_custom_call" | custom-call | flops 15000000512 | bytes 1 | tf_op jit(solution)/shard_map/panel_own/pallas_call | solution.py:33
  85.8 0.1 added_split.13
  85.8 0.3 collective-permute-start.15
  86.2 1.6 %collective-permute-done.10 = bf16[512,256]{1,0:T(8,128)(2,1)S(1)} collective-permute-done((bf16[512,256]{1,0:T(8,128)(2,1)S(1)}, bf16[512,256]{1,0:T(8,128)(2,1)S(1)}, u32[]{:S(2)}, u32[]{:S(2)}) %collective-permute-start.10) | collective-permute-done | bytes 262176 | tf_op jit(solution)/shard_map/ppermute | solution.py:235
  87.8 2.0 %collective-permute-start.14 = (bf16[256,256]{1,0:T(8,128)(2,1)S(1)}, bf16[256,256]{1,0:T(8,128)(2,1)S(1)}, u32[]{:S(2)}, u32[]{:S(2)}) collective-permute-start(bf16[256,256]{1,0:T(8,128)(2,1)S(1)} %get-tuple-element.122), channel_id=1, source_target_pairs={{0,8},{1,9},{2,10},{3,11},{4,12},{5,13},{6,14},{7,15},{8,0},{9,1},... | collective-permute-start | bytes 393224 | tf_op jit(solution)/shard_map/ppermute | solution.py:235
  89.8 2.9 %panel_away.7 = (bf16[1024,128]{1,0:T(8,128)(2,1)S(1)}, bf16[1536,128]{1,0:T(8,128)(2,1)S(1)}, f32[8,128]{1,0:T(8,128)S(1)}) custom-call(s32[24]{0:T(128)S(1)} %get-tuple-element.90.refs_0_, s32[1]{0:T(128)} %bitcast.2.refs_0_.refs_1_, bf16[2048,768]{1,0:T(8,128)(2,1)S(1)} %get-tuple-element.85.refs_2_.refs_1_, ...), custom_call_target="tpu_custom_call" | custom-call | flops 49999998976 | bytes 1 | tf_op jit(solution)/shard_map/panel_away/pallas_call | solution.py:33
  92.8 0.9 collective-permute-start.21
  93.7 1.4 %panel_own.7 = (f32[1024,128]{1,0:T(8,128)S(1)}, f32[8,128]{1,0:T(8,128)S(1)}) custom-call(s32[1]{0:T(128)} %bitcast.2.refs_0_.refs_1_, bf16[2048,768]{1,0:T(8,128)(2,1)S(1)} %get-tuple-element.85.refs_2_.refs_1_, bf16[2048,768]{1,0:T(8,128)(2,1)S(1)} %get-tuple-element.89.refs_3_.refs_2_, bf16[1536,128]{1,0:T(8,128)(2,1)S(1)} %get-tuple-element.131.refs_3_, ...), custom_call_target="tpu_custom_call" | custom-call | flops 15000000512 | bytes 1 | tf_op jit(solution)/shard_map/panel_own/pallas_call | solution.py:33
  95.1 8.3 %collective-permute-done.16 = bf16[1024,384]{1,0:T(8,128)(2,1)S(1)} collective-permute-done((bf16[1024,384]{1,0:T(8,128)(2,1)S(1)}, bf16[1024,384]{1,0:T(8,128)(2,1)S(1)}, u32[]{:S(2)}, u32[]{:S(2)}) %collective-permute-start.16) | collective-permute-done | bytes 786464 | tf_op jit(solution)/shard_map/ppermute | solution.py:235
  103.4 0.2 added_split.15
  103.6 1.1 collective-permute-start.20
  104.7 0.1 added_split.16
  104.8 1.0 collective-permute-start.19
  105.8 0.1 added_split.18
  105.9 2.5 %collective-permute-start.23 = (bf16[512,128]{1,0:T(8,128)(2,1)S(1)}, bf16[512,128]{1,0:T(8,128)(2,1)S(1)}, u32[]{:S(2)}, u32[]{:S(2)}) collective-permute-start(bf16[512,128]{1,0:T(8,128)(2,1)S(1)} %get-tuple-element.150), channel_id=1, source_target_pairs={{0,4},{1,5},{2,6},{3,7},{4,0},{5,1},{6,2},{7,3},{8,12},{9,13},{10,... | collective-permute-start | bytes 393224 | tf_op jit(solution)/shard_map/ppermute | solution.py:235
  108.4 4.6 %collective-permute-done.20 = bf16[512,384]{1,0:T(8,128)(2,1)S(1)} collective-permute-done((bf16[512,384]{1,0:T(8,128)(2,1)S(1)}, bf16[512,384]{1,0:T(8,128)(2,1)S(1)}, u32[]{:S(2)}, u32[]{:S(2)}) %collective-permute-start.20) | collective-permute-done | bytes 393248 | tf_op jit(solution)/shard_map/ppermute | solution.py:235
  113.0 0.1 added_split.19
  113.1 2.0 %collective-permute-start.22 = (bf16[256,384]{1,0:T(8,128)(2,1)S(1)}, bf16[256,384]{1,0:T(8,128)(2,1)S(1)}, u32[]{:S(2)}, u32[]{:S(2)}) collective-permute-start(bf16[256,384]{1,0:T(8,128)(2,1)S(1)} %get-tuple-element.148), channel_id=1, source_target_pairs={{0,8},{1,9},{2,10},{3,11},{4,12},{5,13},{6,14},{7,15},{8,0},{9,1},... | collective-permute-start | bytes 589832 | tf_op jit(solution)/shard_map/ppermute | solution.py:235
  115.2 1.0 collective-permute-start.24
  116.2 8.3 %collective-permute-done.22 = bf16[256,384]{1,0:T(8,128)(2,1)S(1)} collective-permute-done((bf16[256,384]{1,0:T(8,128)(2,1)S(1)}, bf16[256,384]{1,0:T(8,128)(2,1)S(1)}, u32[]{:S(2)}, u32[]{:S(2)}) %collective-permute-start.22) | collective-permute-done | bytes 196640 | tf_op jit(solution)/shard_map/ppermute | solution.py:235
  124.6 0.1 collective-permute-start.27
  124.7 0.6 collective-permute-done.24
  125.3 0.1 collective-permute-start.28
  125.4 1.2 collective-permute-done.28.refs_8_
  126.6 1.0 put_together.1
  (27 shorter events, 0.2 us)
Async XLA Ops:
  0.0 5.4 %collective-permute-start.1 = (bf16[512,2048]{1,0:T(8,128)(2,1)}, bf16[512,2048]{1,0:T(8,128)(2,1)S(1)}, u32[]{:S(2)}, u32[]{:S(2)}) collective-permute-start(bf16[512,2048]{1,0:T(8,128)(2,1)} %refs_3_.7), channel_id=1, source_target_pairs={{0,1},{1,0},{2,3},{3,2},{4,5},{5,4},{6,7},{7,6},{8,9},{9,8},{10,11... | collective-permute-start | bytes 6291464 | tf_op jit(solution)/shard_map/ppermute | solution.py:235
  0.5 5.0 %collective-permute-start.2 = (bf16[20,64,256]{2,1,0:T(8,128)(2,1)}, bf16[20,64,256]{2,1,0:T(8,128)(2,1)S(1)}, u32[]{:S(2)}, u32[]{:S(2)}) collective-permute-start(bf16[20,64,256]{2,1,0:T(8,128)(2,1)} %refs_5_.7), channel_id=1, source_target_pairs={{0,1},{1,0},{2,3},{3,2},{4,5},{5,4},{6,7},{7,6},{8,9},{9,8},{10,11... | collective-permute-start | bytes 1966088 | tf_op jit(solution)/shard_map/ppermute | solution.py:235
  1.3 3.0 %collective-permute-start = (s32[20,4]{1,0:T(8,128)S(1)}, s32[20,4]{1,0:T(8,128)S(1)}, u32[]{:S(2)}, u32[]{:S(2)}) collective-permute-start(s32[20,4]{1,0:T(8,128)S(1)} %copy.7.refs_1_), channel_id=1, source_target_pairs={{0,1},{1,0},{2,3},{3,2},{4,5},{5,4},{6,7},{7,6},{8,9},{9,8},{10,11... | collective-permute-start | bytes 968 | tf_op jit(solution)/shard_map/ppermute | solution.py:235
  1.7 13.9 %collective-permute-start.4 = (s32[12]{0:T(128)}, s32[12]{0:T(128)S(1)}, u32[]{:S(2)}, u32[]{:S(2)}) collective-permute-start(s32[12]{0:T(128)} %refs_1_.5), channel_id=1, source_target_pairs={{0,1},{1,0},{2,3},{3,2},{4,5},{5,4},{6,7},{7,6},{8,9},{9,8},{10,11... | collective-permute-start | bytes 152 | tf_op jit(solution)/shard_map/ppermute | solution.py:235
  5.4 3.2 %copy-start = (bf16[768,2048]{1,0:T(8,128)(2,1)S(1)}, bf16[768,2048]{1,0:T(8,128)(2,1)}, u32[]{:S(2)}) copy-start(bf16[768,2048]{1,0:T(8,128)(2,1)} %refs_0_.1) | copy-start | bytes 9437188
  8.6 8.4 %collective-permute-start.3 = (bf16[768,2048]{1,0:T(8,128)(2,1)S(1)}, bf16[768,2048]{1,0:T(8,128)(2,1)S(1)}, u32[]{:S(2)}, u32[]{:S(2)}) collective-permute-start(bf16[768,2048]{1,0:T(8,128)(2,1)S(1)} %copy-done), channel_id=1, source_target_pairs={{0,1},{1,0},{2,3},{3,2},{4,5},{5,4},{6,7},{7,6},{8,9},{9,8},{10,11... | collective-permute-start | bytes 9437192 | tf_op jit(solution)/shard_map/ppermute | solution.py:235
  9.1 28.9 %collective-permute-start.5 = (bf16[768,256]{1,0:T(8,128)(2,1)S(1)}, bf16[768,256]{1,0:T(8,128)(2,1)S(1)}, u32[]{:S(2)}, u32[]{:S(2)}) collective-permute-start(bf16[768,256]{1,0:T(8,128)(2,1)S(1)} %get-tuple-element.91), channel_id=1, source_target_pairs={{14,0},{15,1},{0,2},{1,3},{2,4},{3,5},{4,6},{5,7},{6,8},{7,9},{8,1... | collective-permute-start | bytes 1179656 | tf_op jit(solution)/shard_map/ppermute | solution.py:230
  11.7 3.9 %copy-start.1 = (s32[12]{0:T(128)S(1)}, s32[12]{0:T(128)}, u32[]{:S(2)}) copy-start(s32[12]{0:T(128)} %refs_1_.5) | copy-start | bytes 148
  11.7 28.8 %collective-permute-start.6 = (bf16[768,256]{1,0:T(8,128)(2,1)S(1)}, bf16[768,256]{1,0:T(8,128)(2,1)S(1)}, u32[]{:S(2)}, u32[]{:S(2)}) collective-permute-start(bf16[768,256]{1,0:T(8,128)(2,1)S(1)} %get-tuple-element.92), channel_id=1, source_target_pairs={{2,0},{3,1},{4,2},{5,3},{6,4},{7,5},{8,6},{9,7},{10,8},{11,9},{12,... | collective-permute-start | bytes 1179656 | tf_op jit(solution)/shard_map/ppermute | solution.py:230
  21.1 28.8 %collective-permute-start.8 = (bf16[768,256]{1,0:T(8,128)(2,1)S(1)}, bf16[768,256]{1,0:T(8,128)(2,1)S(1)}, u32[]{:S(2)}, u32[]{:S(2)}) collective-permute-start(bf16[768,256]{1,0:T(8,128)(2,1)S(1)} %get-tuple-element.102), channel_id=1, source_target_pairs={{14,0},{15,1},{0,2},{1,3},{2,4},{3,5},{4,6},{5,7},{6,8},{7,9},{8,1... | collective-permute-start | bytes 1179656 | tf_op jit(solution)/shard_map/ppermute | solution.py:230
  21.3 28.6 %collective-permute-start.9 = (bf16[768,256]{1,0:T(8,128)(2,1)S(1)}, bf16[768,256]{1,0:T(8,128)(2,1)S(1)}, u32[]{:S(2)}, u32[]{:S(2)}) collective-permute-start(bf16[768,256]{1,0:T(8,128)(2,1)S(1)} %get-tuple-element.103), channel_id=1, source_target_pairs={{2,0},{3,1},{4,2},{5,3},{6,4},{7,5},{8,6},{9,7},{10,8},{11,9},{12,... | collective-permute-start | bytes 1179656 | tf_op jit(solution)/shard_map/ppermute | solution.py:230
  43.1 15.6 %collective-permute-start.7 = (bf16[1024,256]{1,0:T(8,128)(2,1)S(1)}, bf16[1024,256]{1,0:T(8,128)(2,1)S(1)}, u32[]{:S(2)}, u32[]{:S(2)}) collective-permute-start(bf16[1024,256]{1,0:T(8,128)(2,1)S(1)} %get-tuple-element.101), channel_id=1, source_target_pairs={{0,4},{1,5},{2,6},{3,7},{4,0},{5,1},{6,2},{7,3},{8,12},{9,13},{10,... | collective-permute-start | bytes 1572872 | tf_op jit(solution)/shard_map/ppermute | solution.py:235
  43.6 32.3 %collective-permute-start.12 = (bf16[768,384]{1,0:T(8,128)(2,1)S(1)}, bf16[768,384]{1,0:T(8,128)(2,1)S(1)}, u32[]{:S(2)}, u32[]{:S(2)}) collective-permute-start(bf16[768,384]{1,0:T(8,128)(2,1)S(1)} %get-tuple-element.113), channel_id=1, source_target_pairs={{14,0},{15,1},{0,2},{1,3},{2,4},{3,5},{4,6},{5,7},{6,8},{7,9},{8,1... | collective-permute-start | bytes 1769480 | tf_op jit(solution)/shard_map/ppermute | solution.py:230
  44.7 33.8 %collective-permute-start.13 = (bf16[768,384]{1,0:T(8,128)(2,1)S(1)}, bf16[768,384]{1,0:T(8,128)(2,1)S(1)}, u32[]{:S(2)}, u32[]{:S(2)}) collective-permute-start(bf16[768,384]{1,0:T(8,128)(2,1)S(1)} %get-tuple-element.114), channel_id=1, source_target_pairs={{2,0},{3,1},{4,2},{5,3},{6,4},{7,5},{8,6},{9,7},{10,8},{11,9},{12,... | collective-permute-start | bytes 1769480 | tf_op jit(solution)/shard_map/ppermute | solution.py:230
  49.8 40.0 %collective-permute-start.17 = (bf16[768,128]{1,0:T(8,128)(2,1)}, bf16[768,128]{1,0:T(8,128)(2,1)}, u32[]{:S(2)}, u32[]{:S(2)}) collective-permute-start(bf16[768,128]{1,0:T(8,128)(2,1)} %get-tuple-element.127), channel_id=1, source_target_pairs={{14,0},{15,1},{0,2},{1,3},{2,4},{3,5},{4,6},{5,7},{6,8},{7,9},{8,1... | collective-permute-start | bytes 589832 | tf_op jit(solution)/shard_map/ppermute | solution.py:230
  49.9 39.9 %collective-permute-start.18 = (bf16[768,128]{1,0:T(8,128)(2,1)}, bf16[768,128]{1,0:T(8,128)(2,1)}, u32[]{:S(2)}, u32[]{:S(2)}) collective-permute-start(bf16[768,128]{1,0:T(8,128)(2,1)} %get-tuple-element.128), channel_id=1, source_target_pairs={{2,0},{3,1},{4,2},{5,3},{6,4},{7,5},{8,6},{9,7},{10,8},{11,9},{12,... | collective-permute-start | bytes 589832 | tf_op jit(solution)/shard_map/ppermute | solution.py:230
  58.6 27.1 %collective-permute-start.11 = (bf16[1024,256]{1,0:T(8,128)(2,1)S(1)}, bf16[1024,256]{1,0:T(8,128)(2,1)S(1)}, u32[]{:S(2)}, u32[]{:S(2)}) collective-permute-start(bf16[1024,256]{1,0:T(8,128)(2,1)S(1)} %get-tuple-element.112), channel_id=1, source_target_pairs={{0,4},{1,5},{2,6},{3,7},{4,0},{5,1},{6,2},{7,3},{8,12},{9,13},{10,... | collective-permute-start | bytes 1572872 | tf_op jit(solution)/shard_map/ppermute | solution.py:235
  75.9 11.9 %collective-permute-start.10 = (bf16[512,256]{1,0:T(8,128)(2,1)S(1)}, bf16[512,256]{1,0:T(8,128)(2,1)S(1)}, u32[]{:S(2)}, u32[]{:S(2)}) collective-permute-start(bf16[512,256]{1,0:T(8,128)(2,1)S(1)} %get-tuple-element.110), channel_id=1, source_target_pairs={{0,2},{1,3},{2,0},{3,1},{4,6},{5,7},{6,4},{7,5},{8,10},{9,11},{10,... | collective-permute-start | bytes 786440 | tf_op jit(solution)/shard_map/ppermute | solution.py:235
  81.9 21.6 %collective-permute-start.16 = (bf16[1024,384]{1,0:T(8,128)(2,1)S(1)}, bf16[1024,384]{1,0:T(8,128)(2,1)S(1)}, u32[]{:S(2)}, u32[]{:S(2)}) collective-permute-start(bf16[1024,384]{1,0:T(8,128)(2,1)S(1)} %get-tuple-element.126), channel_id=1, source_target_pairs={{0,4},{1,5},{2,6},{3,7},{4,0},{5,1},{6,2},{7,3},{8,12},{9,13},{10,... | collective-permute-start | bytes 2359304 | tf_op jit(solution)/shard_map/ppermute | solution.py:235
  85.8 18.8 %collective-permute-start.15 = (bf16[512,256]{1,0:T(8,128)(2,1)S(1)}, bf16[512,256]{1,0:T(8,128)(2,1)S(1)}, u32[]{:S(2)}, u32[]{:S(2)}) collective-permute-start(bf16[512,256]{1,0:T(8,128)(2,1)S(1)} %get-tuple-element.124), channel_id=1, source_target_pairs={{0,2},{1,3},{2,0},{3,1},{4,6},{5,7},{6,4},{7,5},{8,10},{9,11},{10,... | collective-permute-start | bytes 786440 | tf_op jit(solution)/shard_map/ppermute | solution.py:235
  87.8 17.9 %collective-permute-start.14 = (bf16[256,256]{1,0:T(8,128)(2,1)S(1)}, bf16[256,256]{1,0:T(8,128)(2,1)S(1)}, u32[]{:S(2)}, u32[]{:S(2)}) collective-permute-start(bf16[256,256]{1,0:T(8,128)(2,1)S(1)} %get-tuple-element.122), channel_id=1, source_target_pairs={{0,8},{1,9},{2,10},{3,11},{4,12},{5,13},{6,14},{7,15},{8,0},{9,1},... | collective-permute-start | bytes 393224 | tf_op jit(solution)/shard_map/ppermute | solution.py:235
  92.8 13.0 %collective-permute-start.21 = (bf16[1024,128]{1,0:T(8,128)(2,1)S(1)}, bf16[1024,128]{1,0:T(8,128)(2,1)S(1)}, u32[]{:S(2)}, u32[]{:S(2)}) collective-permute-start(bf16[1024,128]{1,0:T(8,128)(2,1)S(1)} %get-tuple-element.142), channel_id=1, source_target_pairs={{0,2},{1,3},{2,0},{3,1},{4,6},{5,7},{6,4},{7,5},{8,10},{9,11},{10,... | collective-permute-start | bytes 786440 | tf_op jit(solution)/shard_map/ppermute | solution.py:235
  103.6 9.4 %collective-permute-start.20 = (bf16[512,384]{1,0:T(8,128)(2,1)S(1)}, bf16[512,384]{1,0:T(8,128)(2,1)S(1)}, u32[]{:S(2)}, u32[]{:S(2)}) collective-permute-start(bf16[512,384]{1,0:T(8,128)(2,1)S(1)} %get-tuple-element.140), channel_id=1, source_target_pairs={{0,2},{1,3},{2,0},{3,1},{4,6},{5,7},{6,4},{7,5},{8,10},{9,11},{10,... | collective-permute-start | bytes 1179656 | tf_op jit(solution)/shard_map/ppermute | solution.py:235
  104.8 10.3 %collective-permute-start.19 = (bf16[256,256]{1,0:T(8,128)(2,1)S(1)}, bf16[256,256]{1,0:T(8,128)(2,1)S(1)}, u32[]{:S(2)}, u32[]{:S(2)}) collective-permute-start(bf16[256,256]{1,0:T(8,128)(2,1)S(1)} %get-tuple-element.138), channel_id=1, source_target_pairs={{0,8},{1,9},{2,10},{3,11},{4,12},{5,13},{6,14},{7,15},{8,0},{9,1},... | collective-permute-start | bytes 393224 | tf_op jit(solution)/shard_map/ppermute | solution.py:235
  105.9 9.3 %collective-permute-start.23 = (bf16[512,128]{1,0:T(8,128)(2,1)S(1)}, bf16[512,128]{1,0:T(8,128)(2,1)S(1)}, u32[]{:S(2)}, u32[]{:S(2)}) collective-permute-start(bf16[512,128]{1,0:T(8,128)(2,1)S(1)} %get-tuple-element.150), channel_id=1, source_target_pairs={{0,4},{1,5},{2,6},{3,7},{4,0},{5,1},{6,2},{7,3},{8,12},{9,13},{10,... | collective-permute-start | bytes 393224 | tf_op jit(solution)/shard_map/ppermute | solution.py:235
  108.4 17.0 %collective-permute-start.25 = (f32[128,256]{1,0:T(8,128)S(1)}, f32[128,256]{1,0:T(8,128)S(1)}, u32[]{:S(2)}, u32[]{:S(2)}) collective-permute-start(f32[128,256]{1,0:T(8,128)S(1)} %get-tuple-element.158), channel_id=1, source_target_pairs={{0,1},{1,0},{2,3},{3,2},{4,5},{5,4},{6,7},{7,6},{8,9},{9,8},{10,11... | collective-permute-start | bytes 393224 | tf_op jit(solution)/shard_map/ppermute | solution.py:235
  113.1 11.5 %collective-permute-start.22 = (bf16[256,384]{1,0:T(8,128)(2,1)S(1)}, bf16[256,384]{1,0:T(8,128)(2,1)S(1)}, u32[]{:S(2)}, u32[]{:S(2)}) collective-permute-start(bf16[256,384]{1,0:T(8,128)(2,1)S(1)} %get-tuple-element.148), channel_id=1, source_target_pairs={{0,8},{1,9},{2,10},{3,11},{4,12},{5,13},{6,14},{7,15},{8,0},{9,1},... | collective-permute-start | bytes 589832 | tf_op jit(solution)/shard_map/ppermute | solution.py:235
  115.2 10.1 %collective-permute-start.24 = (bf16[256,128]{1,0:T(8,128)(2,1)S(1)}, bf16[256,128]{1,0:T(8,128)(2,1)S(1)}, u32[]{:S(2)}, u32[]{:S(2)}) collective-permute-start(bf16[256,128]{1,0:T(8,128)(2,1)S(1)} %get-tuple-element.155), channel_id=1, source_target_pairs={{0,8},{1,9},{2,10},{3,11},{4,12},{5,13},{6,14},{7,15},{8,0},{9,1},... | collective-permute-start | bytes 196616 | tf_op jit(solution)/shard_map/ppermute | solution.py:235
  116.2 9.2 %collective-permute-start.26 = (f32[128,256]{1,0:T(8,128)S(1)}, f32[128,256]{1,0:T(8,128)S(1)}, u32[]{:S(2)}, u32[]{:S(2)}) collective-permute-start(f32[128,256]{1,0:T(8,128)S(1)} %get-tuple-element.159), channel_id=1, source_target_pairs={{0,1},{1,0},{2,3},{3,2},{4,5},{5,4},{6,7},{7,6},{8,9},{9,8},{10,11... | collective-permute-start | bytes 393224 | tf_op jit(solution)/shard_map/ppermute | solution.py:235
  124.6 2.0 %collective-permute-start.27 = (f32[128,384]{1,0:T(8,128)S(1)}, f32[128,384]{1,0:T(8,128)S(1)}, u32[]{:S(2)}, u32[]{:S(2)}) collective-permute-start(f32[128,384]{1,0:T(8,128)S(1)} %get-tuple-element.160), channel_id=1, source_target_pairs={{0,1},{1,0},{2,3},{3,2},{4,5},{5,4},{6,7},{7,6},{8,9},{9,8},{10,11... | collective-permute-start | bytes 589832 | tf_op jit(solution)/shard_map/ppermute | solution.py:235
  125.3 1.3 %collective-permute-start.28 = (f32[128,128]{1,0:T(8,128)S(1)}, f32[128,128]{1,0:T(8,128)S(1)}, u32[]{:S(2)}, u32[]{:S(2)}) collective-permute-start(f32[128,128]{1,0:T(8,128)S(1)} %get-tuple-element.161), channel_id=1, source_target_pairs={{0,1},{1,0},{2,3},{3,2},{4,5},{5,4},{6,7},{7,6},{8,9},{9,8},{10,11... | collective-permute-start | bytes 196616 | tf_op jit(solution)/shard_map/ppermute | solution.py:235

commit v10 on v9

--- a/solution.py
+++ b/solution.py
@@ -6,7 +6,7 @@
 from jax.sharding import PartitionSpec as P
 
 CLASSES = 5
-UNITS = (2, 2, 3, 1)
+UNITS = (2, 2, 2, 2)
 EARLY = 4
 ORDERS = {3: [1, 2, 3]}
 PACE = 10**10

time: 128 us -> 128 us (level)
  Pallas kernels: 36.7 us -> 34.9 us
  starting transfers between devices: 37.1 us -> 38.4 us
    ppermute x21, waiting for transfers between devices: 28.3 us -> 36.9 us  [swapped(): return lax.ppermute(block, 'mesh', [(i, i ^ 1 << bit) for i in range(size)])]
    ppermute x8, waiting for transfers between devices: 24.5 us -> 16.8 us  [passed_along(): lax.ppermute(block, 'mesh', [((i - distance) % size, i) for i in range(si...]
    pallas_call x28, Pallas kernels: 36.7 us -> 34.9 us  [call(): pl.pallas_call(kernel, out_shape=[*out_shape, jax.ShapeDtypeStruct((8, 12...]
  transfers between devices with their start and end apart: 29 -> 29, of which waited for: 11 -> 14; matrix products, arithmetic and copies ran while one was open for 1% -> 1% of each run, Pallas kernels for 28% -> 26%
where the time goes in v10:
time: 128 us
  waiting for transfers between devices  53.8 us (42%)
  starting transfers between devices  38.4 us (30%)
  Pallas kernels  34.9 us (27%)
    ppermute x21, waiting for transfers between devices, swapped(): return lax.ppermute(block, 'mesh', [(i, i ^ 1 << bit) for i in range(size)])  36.9 us
    pallas_call x28, Pallas kernels, call(): pl.pallas_call(kernel, out_shape=[*out_shape, jax.ShapeDtypeStruct((8, 12...  34.9 us
    ppermute x8, starting transfers between devices, passed_along(): lax.ppermute(block, 'mesh', [((i - distance) % size, i) for i in range(si...  19.9 us
    ppermute x21, starting transfers between devices, swapped(): return lax.ppermute(block, 'mesh', [(i, i ^ 1 << bit) for i in range(size)])  18.5 us
    ppermute x8, waiting for transfers between devices, passed_along(): lax.ppermute(block, 'mesh', [((i - distance) % size, i) for i in range(si...  16.8 us
  transfers between devices with their start and end apart: 29, of which 14 were waited for; matrix products, arithmetic and copies ran while one was open for 1% of the time, Pallas kernels for 26%

profile of v10, /device:TPU:0, one launch (start us, length us, event | category | flops | bytes accessed | tf_op | source)
XLA Modules:
  0.0 128.2 jit_solution(248472171427011178)
XLA Ops:
  0.0 0.5 collective-permute-start.1
  0.5 0.8 copy.7.refs_1_
  1.3 0.5 collective-permute-start
  1.8 2.5 %collective-permute-done.refs_2_ = s32[20,4]{1,0:T(8,128)S(1)} collective-permute-done((s32[20,4]{1,0:T(8,128)S(1)}, s32[20,4]{1,0:T(8,128)S(1)}, u32[]{:S(2)}, u32[]{:S(2)}) %collective-permute-start) | collective-permute-done | bytes 352 | tf_op jit(solution)/shard_map/ppermute | solution.py:235
  4.3 1.1 collective-permute-done.2.refs_6_
  5.4 3.2 %coupled_rows.4 = (bf16[768,256]{1,0:T(8,128)(2,1)S(1)}, bf16[768,256]{1,0:T(8,128)(2,1)S(1)}, bf16[1024,256]{1,0:T(8,128)(2,1)S(1)}, f32[8,128]{1,0:T(8,128)S(1)}) custom-call(s32[1]{0:T(128)} %bitcast.refs_0_, s32[20,4]{1,0:T(8,128)S(1)} %copy.7.refs_1_, s32[20,4]{1,0:T(8,128)S(1)} %collective-permute-done.refs_2_, bf16[512,2048]{1,0:T(8,128)(2,1)} %refs_3_.7, ...), custom_call_target="tpu_custom_call" | custom-call | flops 24999999488 | bytes 1 | tf_op jit(solution)/shard_map/coupled_rows/pallas_call | solution.py:33
  8.6 0.4 collective-permute-start.3
  9.1 2.6 %collective-permute-start.5 = (bf16[768,256]{1,0:T(8,128)(2,1)S(1)}, bf16[768,256]{1,0:T(8,128)(2,1)S(1)}, u32[]{:S(2)}, u32[]{:S(2)}) collective-permute-start(bf16[768,256]{1,0:T(8,128)(2,1)S(1)} %get-tuple-element.91), channel_id=1, source_target_pairs={{14,0},{15,1},{0,2},{1,3},{2,4},{3,5},{4,6},{5,7},{6,8},{7,9},{8,1... | collective-permute-start | bytes 1179656 | tf_op jit(solution)/shard_map/ppermute | solution.py:230
  11.7 3.0 %collective-permute-start.6 = (bf16[768,256]{1,0:T(8,128)(2,1)S(1)}, bf16[768,256]{1,0:T(8,128)(2,1)S(1)}, u32[]{:S(2)}, u32[]{:S(2)}) collective-permute-start(bf16[768,256]{1,0:T(8,128)(2,1)S(1)} %get-tuple-element.92), channel_id=1, source_target_pairs={{2,0},{3,1},{4,2},{5,3},{6,4},{7,5},{8,6},{9,7},{10,8},{11,9},{12,... | collective-permute-start | bytes 1179656 | tf_op jit(solution)/shard_map/ppermute | solution.py:230
  14.7 0.9 turn.2
  15.6 1.3 %slots.1 = (s32[24]{0:T(128)S(1)}, f32[8,128]{1,0:T(8,128)S(1)}) custom-call(s32[1]{0:T(128)} %bitcast.refs_0_, s32[12]{0:T(128)S(1)} %copy-done.1, s32[12]{0:T(128)S(1)} %collective-permute-done.4.refs_2_, f32[8,128]{1,0:T(8,128)S(1)} %get-tuple-element.87.refs_3_), custom_call_target="tpu_custom_call" | custom-call | flops 10000000000 | bytes 1 | tf_op jit(solution)/shard_map/slots/pallas_call | solution.py:33
  17.0 0.9 turn.3
  17.9 3.2 %coupled_rows.5 = (bf16[768,256]{1,0:T(8,128)(2,1)S(1)}, bf16[768,256]{1,0:T(8,128)(2,1)S(1)}, bf16[1024,256]{1,0:T(8,128)(2,1)S(1)}, f32[8,128]{1,0:T(8,128)S(1)}) custom-call(s32[1]{0:T(128)} %bitcast.refs_0_, s32[20,4]{1,0:T(8,128)S(1)} %copy.7.refs_1_, s32[20,4]{1,0:T(8,128)S(1)} %collective-permute-done.refs_2_, bf16[512,2048]{1,0:T(8,128)(2,1)} %refs_3_.7, ...), custom_call_target="tpu_custom_call" | custom-call | flops 24999999488 | bytes 1 | tf_op jit(solution)/shard_map/coupled_rows/pallas_call | solution.py:33
  21.1 0.3 collective-permute-start.8
  21.3 4.5 %collective-permute-start.9 = (bf16[768,256]{1,0:T(8,128)(2,1)S(1)}, bf16[768,256]{1,0:T(8,128)(2,1)S(1)}, u32[]{:S(2)}, u32[]{:S(2)}) collective-permute-start(bf16[768,256]{1,0:T(8,128)(2,1)S(1)} %get-tuple-element.103), channel_id=1, source_target_pairs={{2,0},{3,1},{4,2},{5,3},{6,4},{7,5},{8,6},{9,7},{10,8},{11,9},{12,... | collective-permute-start | bytes 1179656 | tf_op jit(solution)/shard_map/ppermute | solution.py:230
  25.8 3.2 %coupled_rows.6 = (bf16[768,256]{1,0:T(8,128)(2,1)S(1)}, bf16[768,256]{1,0:T(8,128)(2,1)S(1)}, bf16[1024,256]{1,0:T(8,128)(2,1)S(1)}, f32[8,128]{1,0:T(8,128)S(1)}) custom-call(s32[1]{0:T(128)} %bitcast.refs_0_, s32[20,4]{1,0:T(8,128)S(1)} %copy.7.refs_1_, s32[20,4]{1,0:T(8,128)S(1)} %collective-permute-done.refs_2_, bf16[512,2048]{1,0:T(8,128)(2,1)} %refs_3_.7, ...), custom_call_target="tpu_custom_call" | custom-call | flops 24999999488 | bytes 1 | tf_op jit(solution)/shard_map/coupled_rows/pallas_call | solution.py:33
  29.0 3.8 %coupled_rows.7 = (bf16[768,256]{1,0:T(8,128)(2,1)}, bf16[768,256]{1,0:T(8,128)(2,1)}, bf16[1024,256]{1,0:T(8,128)(2,1)S(1)}, f32[8,128]{1,0:T(8,128)S(1)}) custom-call(s32[1]{0:T(128)} %bitcast.refs_0_, s32[20,4]{1,0:T(8,128)S(1)} %copy.7.refs_1_, s32[20,4]{1,0:T(8,128)S(1)} %collective-permute-done.refs_2_, bf16[512,2048]{1,0:T(8,128)(2,1)} %refs_3_.7, ...), custom_call_target="tpu_custom_call" | custom-call | flops 24999999488 | bytes 1 | tf_op jit(solution)/shard_map/coupled_rows/pallas_call | solution.py:33
  32.8 5.2 %collective-permute-done.5.refs_4_ = bf16[768,256]{1,0:T(8,128)(2,1)S(1)} collective-permute-done((bf16[768,256]{1,0:T(8,128)(2,1)S(1)}, bf16[768,256]{1,0:T(8,128)(2,1)S(1)}, u32[]{:S(2)}, u32[]{:S(2)}) %collective-permute-start.5) | collective-permute-done | bytes 393248 | tf_op jit(solution)/shard_map/ppermute | solution.py:230
  38.0 2.5 %collective-permute-done.6.refs_5_ = bf16[768,256]{1,0:T(8,128)(2,1)S(1)} collective-permute-done((bf16[768,256]{1,0:T(8,128)(2,1)S(1)}, bf16[768,256]{1,0:T(8,128)(2,1)S(1)}, u32[]{:S(2)}, u32[]{:S(2)}) %collective-permute-start.6) | collective-permute-done | bytes 393248 | tf_op jit(solution)/shard_map/ppermute | solution.py:230
  40.5 2.5 %panel_away.4 = (bf16[1024,256]{1,0:T(8,128)(2,1)S(1)}, bf16[1536,256]{1,0:T(8,128)(2,1)S(1)}, f32[8,128]{1,0:T(8,128)S(1)}) custom-call(s32[24]{0:T(128)S(1)} %get-tuple-element.90.refs_0_, s32[1]{0:T(128)} %bitcast.3.refs_1_.refs_0_, bf16[2048,768]{1,0:T(8,128)(2,1)S(1)} %get-tuple-element.85.refs_2_.refs_1_, ...), custom_call_target="tpu_custom_call" | custom-call | flops 49999998976 | bytes 1 | tf_op jit(solution)/shard_map/panel_away/pallas_call | solution.py:33
  43.1 0.5 collective-permute-start.7
  43.6 1.1 collective-permute-start.12
  44.7 3.7 %collective-permute-start.13 = (bf16[768,256]{1,0:T(8,128)(2,1)S(1)}, bf16[768,256]{1,0:T(8,128)(2,1)S(1)}, u32[]{:S(2)}, u32[]{:S(2)}) collective-permute-start(bf16[768,256]{1,0:T(8,128)(2,1)S(1)} %get-tuple-element.114), channel_id=1, source_target_pairs={{2,0},{3,1},{4,2},{5,3},{6,4},{7,5},{8,6},{9,7},{10,8},{11,9},{12,... | collective-permute-start | bytes 1179656 | tf_op jit(solution)/shard_map/ppermute | solution.py:230
  48.3 1.5 %panel_own.4 = (f32[1024,256]{1,0:T(8,128)S(1)}, f32[8,128]{1,0:T(8,128)S(1)}) custom-call(s32[1]{0:T(128)} %bitcast.3.refs_1_.refs_0_, bf16[2048,768]{1,0:T(8,128)(2,1)S(1)} %get-tuple-element.85.refs_2_.refs_1_, bf16[2048,768]{1,0:T(8,128)(2,1)S(1)} %get-tuple-element.89.refs_3_.refs_2_, bf16[1536,256]{1,0:T(8,128)(2,1)S(1)} %get-tuple-element.98.refs_3_, ...), custom_call_target="tpu_custom_call" | custom-call | flops 15000000512 | bytes 1 | tf_op jit(solution)/shard_map/panel_own/pallas_call | solution.py:33
  49.9 4.7 %collective-permute-start.18 = (bf16[768,256]{1,0:T(8,128)(2,1)}, bf16[768,256]{1,0:T(8,128)(2,1)}, u32[]{:S(2)}, u32[]{:S(2)}) collective-permute-start(bf16[768,256]{1,0:T(8,128)(2,1)} %get-tuple-element.128), channel_id=1, source_target_pairs={{2,0},{3,1},{4,2},{5,3},{6,4},{7,5},{8,6},{9,7},{10,8},{11,9},{12,... | collective-permute-start | bytes 1179656 | tf_op jit(solution)/shard_map/ppermute | solution.py:230
  54.6 2.5 %panel_away.5 = (bf16[1024,256]{1,0:T(8,128)(2,1)S(1)}, bf16[1536,256]{1,0:T(8,128)(2,1)S(1)}, f32[8,128]{1,0:T(8,128)S(1)}) custom-call(s32[24]{0:T(128)S(1)} %get-tuple-element.90.refs_0_, s32[1]{0:T(128)} %bitcast.3.refs_1_.refs_0_, bf16[2048,768]{1,0:T(8,128)(2,1)S(1)} %get-tuple-element.85.refs_2_.refs_1_, ...), custom_call_target="tpu_custom_call" | custom-call | flops 49999998976 | bytes 1 | tf_op jit(solution)/shard_map/panel_away/pallas_call | solution.py:33
  57.1 1.5 %panel_own.5 = (f32[1024,256]{1,0:T(8,128)S(1)}, f32[8,128]{1,0:T(8,128)S(1)}) custom-call(s32[1]{0:T(128)} %bitcast.3.refs_1_.refs_0_, bf16[2048,768]{1,0:T(8,128)(2,1)S(1)} %get-tuple-element.85.refs_2_.refs_1_, bf16[2048,768]{1,0:T(8,128)(2,1)S(1)} %get-tuple-element.89.refs_3_.refs_2_, bf16[1536,256]{1,0:T(8,128)(2,1)S(1)} %get-tuple-element.106.refs_3_, ...), custom_call_target="tpu_custom_call" | custom-call | flops 15000000512 | bytes 1 | tf_op jit(solution)/shard_map/panel_own/pallas_call | solution.py:33
  58.6 0.1 collective-permute-start.11
  58.7 0.1 added_split.12
  58.8 9.1 %collective-permute-done.12.refs_4_ = bf16[768,256]{1,0:T(8,128)(2,1)S(1)} collective-permute-done((bf16[768,256]{1,0:T(8,128)(2,1)S(1)}, bf16[768,256]{1,0:T(8,128)(2,1)S(1)}, u32[]{:S(2)}, u32[]{:S(2)}) %collective-permute-start.12) | collective-permute-done | bytes 393248 | tf_op jit(solution)/shard_map/ppermute | solution.py:230
  68.0 4.0 %collective-permute-start.10 = (bf16[512,256]{1,0:T(8,128)(2,1)S(1)}, bf16[512,256]{1,0:T(8,128)(2,1)S(1)}, u32[]{:S(2)}, u32[]{:S(2)}) collective-permute-start(bf16[512,256]{1,0:T(8,128)(2,1)S(1)} %get-tuple-element.110), channel_id=1, source_target_pairs={{0,2},{1,3},{2,0},{3,1},{4,6},{5,7},{6,4},{7,5},{8,10},{9,11},{10,... | collective-permute-start | bytes 786440 | tf_op jit(solution)/shard_map/ppermute | solution.py:235
  72.0 2.5 %panel_away.6 = (bf16[1024,256]{1,0:T(8,128)(2,1)S(1)}, bf16[1536,256]{1,0:T(8,128)(2,1)S(1)}, f32[8,128]{1,0:T(8,128)S(1)}) custom-call(s32[24]{0:T(128)S(1)} %get-tuple-element.90.refs_0_, s32[1]{0:T(128)} %bitcast.3.refs_1_.refs_0_, bf16[2048,768]{1,0:T(8,128)(2,1)S(1)} %get-tuple-element.85.refs_2_.refs_1_, ...), custom_call_target="tpu_custom_call" | custom-call | flops 49999998976 | bytes 1 | tf_op jit(solution)/shard_map/panel_away/pallas_call | solution.py:33
  74.6 2.3 %collective-permute-start.16 = (bf16[1024,256]{1,0:T(8,128)(2,1)S(1)}, bf16[1024,256]{1,0:T(8,128)(2,1)S(1)}, u32[]{:S(2)}, u32[]{:S(2)}) collective-permute-start(bf16[1024,256]{1,0:T(8,128)(2,1)S(1)} %get-tuple-element.126), channel_id=1, source_target_pairs={{0,4},{1,5},{2,6},{3,7},{4,0},{5,1},{6,2},{7,3},{8,12},{9,13},{10,... | collective-permute-start | bytes 1572872 | tf_op jit(solution)/shard_map/ppermute | solution.py:235
  76.9 1.5 %panel_own.6 = (f32[1024,256]{1,0:T(8,128)S(1)}, f32[8,128]{1,0:T(8,128)S(1)}) custom-call(s32[1]{0:T(128)} %bitcast.3.refs_1_.refs_0_, bf16[2048,768]{1,0:T(8,128)(2,1)S(1)} %get-tuple-element.85.refs_2_.refs_1_, bf16[2048,768]{1,0:T(8,128)(2,1)S(1)} %get-tuple-element.89.refs_3_.refs_2_, bf16[1536,256]{1,0:T(8,128)(2,1)S(1)} %get-tuple-element.117.refs_3_, ...), custom_call_target="tpu_custom_call" | custom-call | flops 15000000512 | bytes 1 | tf_op jit(solution)/shard_map/panel_own/pallas_call | solution.py:33
  78.4 7.7 %collective-permute-done.11 = bf16[1024,256]{1,0:T(8,128)(2,1)S(1)} collective-permute-done((bf16[1024,256]{1,0:T(8,128)(2,1)S(1)}, bf16[1024,256]{1,0:T(8,128)(2,1)S(1)}, u32[]{:S(2)}, u32[]{:S(2)}) %collective-permute-start.11) | collective-permute-done | bytes 524320 | tf_op jit(solution)/shard_map/ppermute | solution.py:235
  86.1 0.1 added_split.13
  86.2 0.1 collective-permute-start.15
  86.4 1.9 %collective-permute-done.10 = bf16[512,256]{1,0:T(8,128)(2,1)S(1)} collective-permute-done((bf16[512,256]{1,0:T(8,128)(2,1)S(1)}, bf16[512,256]{1,0:T(8,128)(2,1)S(1)}, u32[]{:S(2)}, u32[]{:S(2)}) %collective-permute-start.10) | collective-permute-done | bytes 262176 | tf_op jit(solution)/shard_map/ppermute | solution.py:235
  88.3 0.1 added_split.14
  88.3 1.7 %collective-permute-start.14 = (bf16[256,256]{1,0:T(8,128)(2,1)S(1)}, bf16[256,256]{1,0:T(8,128)(2,1)S(1)}, u32[]{:S(2)}, u32[]{:S(2)}) collective-permute-start(bf16[256,256]{1,0:T(8,128)(2,1)S(1)} %get-tuple-element.122), channel_id=1, source_target_pairs={{0,8},{1,9},{2,10},{3,11},{4,12},{5,13},{6,14},{7,15},{8,0},{9,1},... | collective-permute-start | bytes 393224 | tf_op jit(solution)/shard_map/ppermute | solution.py:235
  90.1 3.1 %panel_away.7 = (bf16[1024,256]{1,0:T(8,128)(2,1)S(1)}, bf16[1536,256]{1,0:T(8,128)(2,1)S(1)}, f32[8,128]{1,0:T(8,128)S(1)}) custom-call(s32[24]{0:T(128)S(1)} %get-tuple-element.90.refs_0_, s32[1]{0:T(128)} %bitcast.2.refs_0_.refs_1_, bf16[2048,768]{1,0:T(8,128)(2,1)S(1)} %get-tuple-element.85.refs_2_.refs_1_, ...), custom_call_target="tpu_custom_call" | custom-call | flops 49999998976 | bytes 1 | tf_op jit(solution)/shard_map/panel_away/pallas_call | solution.py:33
  93.2 2.1 %collective-permute-start.21 = (bf16[1024,256]{1,0:T(8,128)(2,1)S(1)}, bf16[1024,256]{1,0:T(8,128)(2,1)S(1)}, u32[]{:S(2)}, u32[]{:S(2)}) collective-permute-start(bf16[1024,256]{1,0:T(8,128)(2,1)S(1)} %get-tuple-element.142), channel_id=1, source_target_pairs={{0,2},{1,3},{2,0},{3,1},{4,6},{5,7},{6,4},{7,5},{8,10},{9,11},{10,... | collective-permute-start | bytes 1572872 | tf_op jit(solution)/shard_map/ppermute | solution.py:235
  95.3 1.5 %panel_own.7 = (f32[1024,256]{1,0:T(8,128)S(1)}, f32[8,128]{1,0:T(8,128)S(1)}) custom-call(s32[1]{0:T(128)} %bitcast.2.refs_0_.refs_1_, bf16[2048,768]{1,0:T(8,128)(2,1)S(1)} %get-tuple-element.85.refs_2_.refs_1_, bf16[2048,768]{1,0:T(8,128)(2,1)S(1)} %get-tuple-element.89.refs_3_.refs_2_, bf16[1536,256]{1,0:T(8,128)(2,1)S(1)} %get-tuple-element.131.refs_3_, ...), custom_call_target="tpu_custom_call" | custom-call | flops 15000000512 | bytes 1 | tf_op jit(solution)/shard_map/panel_own/pallas_call | solution.py:33
  96.7 1.1 collective-permute-done.16
  97.8 0.1 added_split.15
  97.9 1.1 collective-permute-start.20
  99.0 2.2 %collective-permute-start.19 = (bf16[256,256]{1,0:T(8,128)(2,1)S(1)}, bf16[256,256]{1,0:T(8,128)(2,1)S(1)}, u32[]{:S(2)}, u32[]{:S(2)}) collective-permute-start(bf16[256,256]{1,0:T(8,128)(2,1)S(1)} %get-tuple-element.138), channel_id=1, source_target_pairs={{0,8},{1,9},{2,10},{3,11},{4,12},{5,13},{6,14},{7,15},{8,0},{9,1},... | collective-permute-start | bytes 393224 | tf_op jit(solution)/shard_map/ppermute | solution.py:235
  101.3 0.1 collective-permute-start.25
  101.4 6.8 %collective-permute-done.21 = bf16[1024,256]{1,0:T(8,128)(2,1)S(1)} collective-permute-done((bf16[1024,256]{1,0:T(8,128)(2,1)S(1)}, bf16[1024,256]{1,0:T(8,128)(2,1)S(1)}, u32[]{:S(2)}, u32[]{:S(2)}) %collective-permute-start.21) | collective-permute-done | bytes 524320 | tf_op jit(solution)/shard_map/ppermute | solution.py:235
  108.1 0.1 added_split.18
  108.2 1.5 %collective-permute-start.23 = (bf16[512,256]{1,0:T(8,128)(2,1)S(1)}, bf16[512,256]{1,0:T(8,128)(2,1)S(1)}, u32[]{:S(2)}, u32[]{:S(2)}) collective-permute-start(bf16[512,256]{1,0:T(8,128)(2,1)S(1)} %get-tuple-element.150), channel_id=1, source_target_pairs={{0,4},{1,5},{2,6},{3,7},{4,0},{5,1},{6,2},{7,3},{8,12},{9,13},{10,... | collective-permute-start | bytes 786440 | tf_op jit(solution)/shard_map/ppermute | solution.py:235
  109.7 2.5 %collective-permute-done.20 = bf16[512,256]{1,0:T(8,128)(2,1)S(1)} collective-permute-done((bf16[512,256]{1,0:T(8,128)(2,1)S(1)}, bf16[512,256]{1,0:T(8,128)(2,1)S(1)}, u32[]{:S(2)}, u32[]{:S(2)}) %collective-permute-start.20) | collective-permute-done | bytes 262176 | tf_op jit(solution)/shard_map/ppermute | solution.py:235
  112.2 0.1 added_split.19
  112.3 1.0 collective-permute-start.22
  113.3 0.1 collective-permute-start.26
  113.4 2.5 %collective-permute-done.23 = bf16[512,256]{1,0:T(8,128)(2,1)S(1)} collective-permute-done((bf16[512,256]{1,0:T(8,128)(2,1)S(1)}, bf16[512,256]{1,0:T(8,128)(2,1)S(1)}, u32[]{:S(2)}, u32[]{:S(2)}) %collective-permute-start.23) | collective-permute-done | bytes 262176 | tf_op jit(solution)/shard_map/ppermute | solution.py:235
  115.9 0.1 added_split.21
  116.0 0.1 collective-permute-start.24
  116.1 7.9 %collective-permute-done.22 = bf16[256,256]{1,0:T(8,128)(2,1)S(1)} collective-permute-done((bf16[256,256]{1,0:T(8,128)(2,1)S(1)}, bf16[256,256]{1,0:T(8,128)(2,1)S(1)}, u32[]{:S(2)}, u32[]{:S(2)}) %collective-permute-start.22) | collective-permute-done | bytes 131104 | tf_op jit(solution)/shard_map/ppermute | solution.py:235
  124.0 0.1 collective-permute-start.27
  124.1 1.5 %collective-permute-done.24 = bf16[256,256]{1,0:T(8,128)(2,1)S(1)} collective-permute-done((bf16[256,256]{1,0:T(8,128)(2,1)S(1)}, bf16[256,256]{1,0:T(8,128)(2,1)S(1)}, u32[]{:S(2)}, u32[]{:S(2)}) %collective-permute-start.24) | collective-permute-done | bytes 131104 | tf_op jit(solution)/shard_map/ppermute | solution.py:235
  125.7 0.1 collective-permute-start.28
  125.8 1.3 %collective-permute-done.28.refs_8_ = f32[128,256]{1,0:T(8,128)S(1)} collective-permute-done((f32[128,256]{1,0:T(8,128)S(1)}, f32[128,256]{1,0:T(8,128)S(1)}, u32[]{:S(2)}, u32[]{:S(2)}) %collective-permute-start.28) | collective-permute-done | bytes 131104 | tf_op jit(solution)/shard_map/ppermute | solution.py:235
  127.1 1.0 put_together.1
  (27 shorter events, 0.4 us)
Async XLA Ops:
  0.0 5.4 %collective-permute-start.1 = (bf16[512,2048]{1,0:T(8,128)(2,1)}, bf16[512,2048]{1,0:T(8,128)(2,1)S(1)}, u32[]{:S(2)}, u32[]{:S(2)}) collective-permute-start(bf16[512,2048]{1,0:T(8,128)(2,1)} %refs_3_.7), channel_id=1, source_target_pairs={{0,1},{1,0},{2,3},{3,2},{4,5},{5,4},{6,7},{7,6},{8,9},{9,8},{10,11... | collective-permute-start | bytes 6291464 | tf_op jit(solution)/shard_map/ppermute | solution.py:235
  0.5 5.0 %collective-permute-start.2 = (bf16[20,64,256]{2,1,0:T(8,128)(2,1)}, bf16[20,64,256]{2,1,0:T(8,128)(2,1)S(1)}, u32[]{:S(2)}, u32[]{:S(2)}) collective-permute-start(bf16[20,64,256]{2,1,0:T(8,128)(2,1)} %refs_5_.7), channel_id=1, source_target_pairs={{0,1},{1,0},{2,3},{3,2},{4,5},{5,4},{6,7},{7,6},{8,9},{9,8},{10,11... | collective-permute-start | bytes 1966088 | tf_op jit(solution)/shard_map/ppermute | solution.py:235
  1.3 3.0 %collective-permute-start = (s32[20,4]{1,0:T(8,128)S(1)}, s32[20,4]{1,0:T(8,128)S(1)}, u32[]{:S(2)}, u32[]{:S(2)}) collective-permute-start(s32[20,4]{1,0:T(8,128)S(1)} %copy.7.refs_1_), channel_id=1, source_target_pairs={{0,1},{1,0},{2,3},{3,2},{4,5},{5,4},{6,7},{7,6},{8,9},{9,8},{10,11... | collective-permute-start | bytes 968 | tf_op jit(solution)/shard_map/ppermute | solution.py:235
  1.7 13.9 %collective-permute-start.4 = (s32[12]{0:T(128)}, s32[12]{0:T(128)S(1)}, u32[]{:S(2)}, u32[]{:S(2)}) collective-permute-start(s32[12]{0:T(128)} %refs_1_.5), channel_id=1, source_target_pairs={{0,1},{1,0},{2,3},{3,2},{4,5},{5,4},{6,7},{7,6},{8,9},{9,8},{10,11... | collective-permute-start | bytes 152 | tf_op jit(solution)/shard_map/ppermute | solution.py:235
  5.4 3.2 %copy-start = (bf16[768,2048]{1,0:T(8,128)(2,1)S(1)}, bf16[768,2048]{1,0:T(8,128)(2,1)}, u32[]{:S(2)}) copy-start(bf16[768,2048]{1,0:T(8,128)(2,1)} %refs_0_.1) | copy-start | bytes 9437188
  8.6 8.4 %collective-permute-start.3 = (bf16[768,2048]{1,0:T(8,128)(2,1)S(1)}, bf16[768,2048]{1,0:T(8,128)(2,1)S(1)}, u32[]{:S(2)}, u32[]{:S(2)}) collective-permute-start(bf16[768,2048]{1,0:T(8,128)(2,1)S(1)} %copy-done), channel_id=1, source_target_pairs={{0,1},{1,0},{2,3},{3,2},{4,5},{5,4},{6,7},{7,6},{8,9},{9,8},{10,11... | collective-permute-start | bytes 9437192 | tf_op jit(solution)/shard_map/ppermute | solution.py:235
  9.1 28.9 %collective-permute-start.5 = (bf16[768,256]{1,0:T(8,128)(2,1)S(1)}, bf16[768,256]{1,0:T(8,128)(2,1)S(1)}, u32[]{:S(2)}, u32[]{:S(2)}) collective-permute-start(bf16[768,256]{1,0:T(8,128)(2,1)S(1)} %get-tuple-element.91), channel_id=1, source_target_pairs={{14,0},{15,1},{0,2},{1,3},{2,4},{3,5},{4,6},{5,7},{6,8},{7,9},{8,1... | collective-permute-start | bytes 1179656 | tf_op jit(solution)/shard_map/ppermute | solution.py:230
  11.7 3.9 %copy-start.1 = (s32[12]{0:T(128)S(1)}, s32[12]{0:T(128)}, u32[]{:S(2)}) copy-start(s32[12]{0:T(128)} %refs_1_.5) | copy-start | bytes 148
  11.7 28.8 %collective-permute-start.6 = (bf16[768,256]{1,0:T(8,128)(2,1)S(1)}, bf16[768,256]{1,0:T(8,128)(2,1)S(1)}, u32[]{:S(2)}, u32[]{:S(2)}) collective-permute-start(bf16[768,256]{1,0:T(8,128)(2,1)S(1)} %get-tuple-element.92), channel_id=1, source_target_pairs={{2,0},{3,1},{4,2},{5,3},{6,4},{7,5},{8,6},{9,7},{10,8},{11,9},{12,... | collective-permute-start | bytes 1179656 | tf_op jit(solution)/shard_map/ppermute | solution.py:230
  21.1 28.8 %collective-permute-start.8 = (bf16[768,256]{1,0:T(8,128)(2,1)S(1)}, bf16[768,256]{1,0:T(8,128)(2,1)S(1)}, u32[]{:S(2)}, u32[]{:S(2)}) collective-permute-start(bf16[768,256]{1,0:T(8,128)(2,1)S(1)} %get-tuple-element.102), channel_id=1, source_target_pairs={{14,0},{15,1},{0,2},{1,3},{2,4},{3,5},{4,6},{5,7},{6,8},{7,9},{8,1... | collective-permute-start | bytes 1179656 | tf_op jit(solution)/shard_map/ppermute | solution.py:230
  21.3 28.6 %collective-permute-start.9 = (bf16[768,256]{1,0:T(8,128)(2,1)S(1)}, bf16[768,256]{1,0:T(8,128)(2,1)S(1)}, u32[]{:S(2)}, u32[]{:S(2)}) collective-permute-start(bf16[768,256]{1,0:T(8,128)(2,1)S(1)} %get-tuple-element.103), channel_id=1, source_target_pairs={{2,0},{3,1},{4,2},{5,3},{6,4},{7,5},{8,6},{9,7},{10,8},{11,9},{12,... | collective-permute-start | bytes 1179656 | tf_op jit(solution)/shard_map/ppermute | solution.py:230
  43.1 15.6 %collective-permute-start.7 = (bf16[1024,256]{1,0:T(8,128)(2,1)S(1)}, bf16[1024,256]{1,0:T(8,128)(2,1)S(1)}, u32[]{:S(2)}, u32[]{:S(2)}) collective-permute-start(bf16[1024,256]{1,0:T(8,128)(2,1)S(1)} %get-tuple-element.101), channel_id=1, source_target_pairs={{0,4},{1,5},{2,6},{3,7},{4,0},{5,1},{6,2},{7,3},{8,12},{9,13},{10,... | collective-permute-start | bytes 1572872 | tf_op jit(solution)/shard_map/ppermute | solution.py:235
  43.6 24.4 %collective-permute-start.12 = (bf16[768,256]{1,0:T(8,128)(2,1)S(1)}, bf16[768,256]{1,0:T(8,128)(2,1)S(1)}, u32[]{:S(2)}, u32[]{:S(2)}) collective-permute-start(bf16[768,256]{1,0:T(8,128)(2,1)S(1)} %get-tuple-element.113), channel_id=1, source_target_pairs={{14,0},{15,1},{0,2},{1,3},{2,4},{3,5},{4,6},{5,7},{6,8},{7,9},{8,1... | collective-permute-start | bytes 1179656 | tf_op jit(solution)/shard_map/ppermute | solution.py:230
  44.7 27.4 %collective-permute-start.13 = (bf16[768,256]{1,0:T(8,128)(2,1)S(1)}, bf16[768,256]{1,0:T(8,128)(2,1)S(1)}, u32[]{:S(2)}, u32[]{:S(2)}) collective-permute-start(bf16[768,256]{1,0:T(8,128)(2,1)S(1)} %get-tuple-element.114), channel_id=1, source_target_pairs={{2,0},{3,1},{4,2},{5,3},{6,4},{7,5},{8,6},{9,7},{10,8},{11,9},{12,... | collective-permute-start | bytes 1179656 | tf_op jit(solution)/shard_map/ppermute | solution.py:230
  49.8 40.2 %collective-permute-start.17 = (bf16[768,256]{1,0:T(8,128)(2,1)}, bf16[768,256]{1,0:T(8,128)(2,1)}, u32[]{:S(2)}, u32[]{:S(2)}) collective-permute-start(bf16[768,256]{1,0:T(8,128)(2,1)} %get-tuple-element.127), channel_id=1, source_target_pairs={{14,0},{15,1},{0,2},{1,3},{2,4},{3,5},{4,6},{5,7},{6,8},{7,9},{8,1... | collective-permute-start | bytes 1179656 | tf_op jit(solution)/shard_map/ppermute | solution.py:230
  49.9 40.2 %collective-permute-start.18 = (bf16[768,256]{1,0:T(8,128)(2,1)}, bf16[768,256]{1,0:T(8,128)(2,1)}, u32[]{:S(2)}, u32[]{:S(2)}) collective-permute-start(bf16[768,256]{1,0:T(8,128)(2,1)} %get-tuple-element.128), channel_id=1, source_target_pairs={{2,0},{3,1},{4,2},{5,3},{6,4},{7,5},{8,6},{9,7},{10,8},{11,9},{12,... | collective-permute-start | bytes 1179656 | tf_op jit(solution)/shard_map/ppermute | solution.py:230
  58.6 27.5 %collective-permute-start.11 = (bf16[1024,256]{1,0:T(8,128)(2,1)S(1)}, bf16[1024,256]{1,0:T(8,128)(2,1)S(1)}, u32[]{:S(2)}, u32[]{:S(2)}) collective-permute-start(bf16[1024,256]{1,0:T(8,128)(2,1)S(1)} %get-tuple-element.112), channel_id=1, source_target_pairs={{0,4},{1,5},{2,6},{3,7},{4,0},{5,1},{6,2},{7,3},{8,12},{9,13},{10,... | collective-permute-start | bytes 1572872 | tf_op jit(solution)/shard_map/ppermute | solution.py:235
  68.0 20.3 %collective-permute-start.10 = (bf16[512,256]{1,0:T(8,128)(2,1)S(1)}, bf16[512,256]{1,0:T(8,128)(2,1)S(1)}, u32[]{:S(2)}, u32[]{:S(2)}) collective-permute-start(bf16[512,256]{1,0:T(8,128)(2,1)S(1)} %get-tuple-element.110), channel_id=1, source_target_pairs={{0,2},{1,3},{2,0},{3,1},{4,6},{5,7},{6,4},{7,5},{8,10},{9,11},{10,... | collective-permute-start | bytes 786440 | tf_op jit(solution)/shard_map/ppermute | solution.py:235
  74.6 23.2 %collective-permute-start.16 = (bf16[1024,256]{1,0:T(8,128)(2,1)S(1)}, bf16[1024,256]{1,0:T(8,128)(2,1)S(1)}, u32[]{:S(2)}, u32[]{:S(2)}) collective-permute-start(bf16[1024,256]{1,0:T(8,128)(2,1)S(1)} %get-tuple-element.126), channel_id=1, source_target_pairs={{0,4},{1,5},{2,6},{3,7},{4,0},{5,1},{6,2},{7,3},{8,12},{9,13},{10,... | collective-permute-start | bytes 1572872 | tf_op jit(solution)/shard_map/ppermute | solution.py:235
  86.2 12.7 %collective-permute-start.15 = (bf16[512,256]{1,0:T(8,128)(2,1)S(1)}, bf16[512,256]{1,0:T(8,128)(2,1)S(1)}, u32[]{:S(2)}, u32[]{:S(2)}) collective-permute-start(bf16[512,256]{1,0:T(8,128)(2,1)S(1)} %get-tuple-element.124), channel_id=1, source_target_pairs={{0,2},{1,3},{2,0},{3,1},{4,6},{5,7},{6,4},{7,5},{8,10},{9,11},{10,... | collective-permute-start | bytes 786440 | tf_op jit(solution)/shard_map/ppermute | solution.py:235
  88.3 12.9 %collective-permute-start.14 = (bf16[256,256]{1,0:T(8,128)(2,1)S(1)}, bf16[256,256]{1,0:T(8,128)(2,1)S(1)}, u32[]{:S(2)}, u32[]{:S(2)}) collective-permute-start(bf16[256,256]{1,0:T(8,128)(2,1)S(1)} %get-tuple-element.122), channel_id=1, source_target_pairs={{0,8},{1,9},{2,10},{3,11},{4,12},{5,13},{6,14},{7,15},{8,0},{9,1},... | collective-permute-start | bytes 393224 | tf_op jit(solution)/shard_map/ppermute | solution.py:235
  93.2 14.9 %collective-permute-start.21 = (bf16[1024,256]{1,0:T(8,128)(2,1)S(1)}, bf16[1024,256]{1,0:T(8,128)(2,1)S(1)}, u32[]{:S(2)}, u32[]{:S(2)}) collective-permute-start(bf16[1024,256]{1,0:T(8,128)(2,1)S(1)} %get-tuple-element.142), channel_id=1, source_target_pairs={{0,2},{1,3},{2,0},{3,1},{4,6},{5,7},{6,4},{7,5},{8,10},{9,11},{10,... | collective-permute-start | bytes 1572872 | tf_op jit(solution)/shard_map/ppermute | solution.py:235
  97.9 14.3 %collective-permute-start.20 = (bf16[512,256]{1,0:T(8,128)(2,1)S(1)}, bf16[512,256]{1,0:T(8,128)(2,1)S(1)}, u32[]{:S(2)}, u32[]{:S(2)}) collective-permute-start(bf16[512,256]{1,0:T(8,128)(2,1)S(1)} %get-tuple-element.140), channel_id=1, source_target_pairs={{0,2},{1,3},{2,0},{3,1},{4,6},{5,7},{6,4},{7,5},{8,10},{9,11},{10,... | collective-permute-start | bytes 786440 | tf_op jit(solution)/shard_map/ppermute | solution.py:235
  99.0 14.2 %collective-permute-start.19 = (bf16[256,256]{1,0:T(8,128)(2,1)S(1)}, bf16[256,256]{1,0:T(8,128)(2,1)S(1)}, u32[]{:S(2)}, u32[]{:S(2)}) collective-permute-start(bf16[256,256]{1,0:T(8,128)(2,1)S(1)} %get-tuple-element.138), channel_id=1, source_target_pairs={{0,8},{1,9},{2,10},{3,11},{4,12},{5,13},{6,14},{7,15},{8,0},{9,1},... | collective-permute-start | bytes 393224 | tf_op jit(solution)/shard_map/ppermute | solution.py:235
  101.3 24.5 %collective-permute-start.25 = (f32[128,256]{1,0:T(8,128)S(1)}, f32[128,256]{1,0:T(8,128)S(1)}, u32[]{:S(2)}, u32[]{:S(2)}) collective-permute-start(f32[128,256]{1,0:T(8,128)S(1)} %get-tuple-element.158), channel_id=1, source_target_pairs={{0,1},{1,0},{2,3},{3,2},{4,5},{5,4},{6,7},{7,6},{8,9},{9,8},{10,11... | collective-permute-start | bytes 393224 | tf_op jit(solution)/shard_map/ppermute | solution.py:235
  108.2 7.7 %collective-permute-start.23 = (bf16[512,256]{1,0:T(8,128)(2,1)S(1)}, bf16[512,256]{1,0:T(8,128)(2,1)S(1)}, u32[]{:S(2)}, u32[]{:S(2)}) collective-permute-start(bf16[512,256]{1,0:T(8,128)(2,1)S(1)} %get-tuple-element.150), channel_id=1, source_target_pairs={{0,4},{1,5},{2,6},{3,7},{4,0},{5,1},{6,2},{7,3},{8,12},{9,13},{10,... | collective-permute-start | bytes 786440 | tf_op jit(solution)/shard_map/ppermute | solution.py:235
  112.3 11.8 %collective-permute-start.22 = (bf16[256,256]{1,0:T(8,128)(2,1)S(1)}, bf16[256,256]{1,0:T(8,128)(2,1)S(1)}, u32[]{:S(2)}, u32[]{:S(2)}) collective-permute-start(bf16[256,256]{1,0:T(8,128)(2,1)S(1)} %get-tuple-element.148), channel_id=1, source_target_pairs={{0,8},{1,9},{2,10},{3,11},{4,12},{5,13},{6,14},{7,15},{8,0},{9,1},... | collective-permute-start | bytes 393224 | tf_op jit(solution)/shard_map/ppermute | solution.py:235
  113.3 12.5 %collective-permute-start.26 = (f32[128,256]{1,0:T(8,128)S(1)}, f32[128,256]{1,0:T(8,128)S(1)}, u32[]{:S(2)}, u32[]{:S(2)}) collective-permute-start(f32[128,256]{1,0:T(8,128)S(1)} %get-tuple-element.159), channel_id=1, source_target_pairs={{0,1},{1,0},{2,3},{3,2},{4,5},{5,4},{6,7},{7,6},{8,9},{9,8},{10,11... | collective-permute-start | bytes 393224 | tf_op jit(solution)/shard_map/ppermute | solution.py:235
  116.0 9.7 %collective-permute-start.24 = (bf16[256,256]{1,0:T(8,128)(2,1)S(1)}, bf16[256,256]{1,0:T(8,128)(2,1)S(1)}, u32[]{:S(2)}, u32[]{:S(2)}) collective-permute-start(bf16[256,256]{1,0:T(8,128)(2,1)S(1)} %get-tuple-element.155), channel_id=1, source_target_pairs={{0,8},{1,9},{2,10},{3,11},{4,12},{5,13},{6,14},{7,15},{8,0},{9,1},... | collective-permute-start | bytes 393224 | tf_op jit(solution)/shard_map/ppermute | solution.py:235
  124.0 1.8 %collective-permute-start.27 = (f32[128,256]{1,0:T(8,128)S(1)}, f32[128,256]{1,0:T(8,128)S(1)}, u32[]{:S(2)}, u32[]{:S(2)}) collective-permute-start(f32[128,256]{1,0:T(8,128)S(1)} %get-tuple-element.160), channel_id=1, source_target_pairs={{0,1},{1,0},{2,3},{3,2},{4,5},{5,4},{6,7},{7,6},{8,9},{9,8},{10,11... | collective-permute-start | bytes 393224 | tf_op jit(solution)/shard_map/ppermute | solution.py:235
  125.7 1.4 %collective-permute-start.28 = (f32[128,256]{1,0:T(8,128)S(1)}, f32[128,256]{1,0:T(8,128)S(1)}, u32[]{:S(2)}, u32[]{:S(2)}) collective-permute-start(f32[128,256]{1,0:T(8,128)S(1)} %get-tuple-element.161), channel_id=1, source_target_pairs={{0,1},{1,0},{2,3},{3,2},{4,5},{5,4},{6,7},{7,6},{8,9},{9,8},{10,11... | collective-permute-start | bytes 393224 | tf_op jit(solution)/shard_map/ppermute | solution.py:235
